TPU v7x, 32 devices: a whole 2x2x4 slice. The times are simulated.
32 devices in a mesh: stream: 4 (over y, x), span: 8 (over z, core).
Axes of the slice: x: 2, y: 2, z: 4, core: 2. Of those that a mesh axis runs over, the one named last changes fastest.
Arguments:
- right_side: float32 [4, 65536], P(None, ('stream', 'span')), may hold values from -5 to 6
- fine_values: float32 [8, 4, 4, 65536], P(None, None, None, ('stream', 'span')), as said below
- fine_columns: int32 [8, 65536], P(None, ('stream', 'span')), may hold values from 0 to 2303, as said below
- fine_sends: int32 [4, 2048], P(None, ('stream', 'span')), may hold values from 0 to 2047, as said below
- fine_order: int32 [32, 2048], P(('stream', 'span')), may hold values from 0 to 2047, each once within a row
- fine_weights: float32 [4, 4, 65536], P(None, None, ('stream', 'span')), may hold values from -0.6 to 1.2
- middle_values: float32 [8, 4, 4, 16384], P(None, None, None, ('stream', 'span')), as said below
- middle_columns: int32 [8, 16384], P(None, ('stream', 'span')), may hold values from 0 to 767, as said below
- middle_sends: int32 [4, 2048], P(None, ('stream', 'span')), may hold values from 0 to 511, as said below
- middle_order: int32 [32, 512], P(('stream', 'span')), may hold values from 0 to 511, each once within a row
- middle_weights: float32 [4, 4, 16384], P(None, None, ('stream', 'span')), may hold values from -0.6 to 1.2
- coarsest_values: float32 [8, 4, 4, 4096], P(None, None, None, ('stream', 'span')), as said below
- coarsest_columns: int32 [8, 4096], P(None, ('stream', 'span')), may hold values from 0 to 1023, as said below
Outputs:
- solution: float32 [4, 65536], P(None, ('stream', 'span'))
- residual: float32 [4, 65536], P(None, ('stream', 'span'))
Inputs may be any that keep to these rules, and one draw needn't show every extreme that they name: `fine_sends`: entry [d, p * 64 + s] is a local row block of device p sent in direction d (0: lower stream index, 1: higher stream index, 2: lower span index, 3: higher span index). Each list has a length of at most 64, which differs between devices and directions and is 64 on some device; rows may repeat within a list, and the slots at or after the length repeat the list's slot 0 as padding. `middle_sends`: as for the first level, with local row blocks of the second level. `fine_columns`: block k = 0 of row block n names its own local row. Entries below 2048 are local row blocks; an entry 2048 + e * 64 + s names slot s of halo block e. Where halo block e has a sending device, s is below the length of that device's list; where it has none (the block is zero), s may be any slot below 64. `middle_columns`: as for the first level with 512 local row blocks. `coarsest_columns`: block k = 0 names the row block itself within its slab; the others name row blocks of the same slab. `fine_values`: each diagonal entry of the k = 0 block is 1 or more, and the other 31 entries of its row over all 8 blocks have absolute values summing to at most 0.9 times it. `middle_values`: as for the first level. `coarsest_values`: as for the first level.
All inputs are finite; a program needn't handle non-finite values.
Results may differ from a plain program's by a relative error of at most 0.0003.
Values sent between devices are 32-bit elements; how exact they have to be, the bound alone decides.
No kernel may reach another device: no remote copies, remote signals or barrier semaphores. Data moves between devices by JAX's collectives and lax.ppermute only.
A program may use at most 64 MiB of HBM per device.

v0:
```python
import math

import jax
import jax.numpy as jnp
from jax import lax
from jax.sharding import PartitionSpec as P

KSM = 3
KC = 4


CHEB_CENTRE = 1.0
CHEB_RADIUS = 0.9


def padded(cells, sides, width, closed):
    for axis, dim in sides:
        count = lax.axis_size(axis)
        ends = count if closed else count - 1
        head = lax.slice_in_dim(cells, 0, width, axis=dim)
        tail = lax.slice_in_dim(cells, cells.shape[dim] - width, cells.shape[dim], axis=dim)
        cells = jnp.concatenate(
            [
                lax.ppermute(tail, axis, [(i, (i + 1) % count) for i in range(ends)]),
                cells,
                lax.ppermute(head, axis, [((i + 1) % count, i) for i in range(ends)]),
            ],
            axis=dim,
        )
    return cells


def chebyshev(operate, inverse_diag, target, initial, degree):
    sigma_value = CHEB_CENTRE / CHEB_RADIUS
    rho_prev = 1.0 / sigma_value
    if initial is None:
        iterate = jnp.zeros_like(target)
        current = target
    else:
        iterate = initial
        current = target - operate(initial)
    update = inverse_diag * current / CHEB_CENTRE
    iterate = iterate + update
    for _ in range(degree - 1):
        rho_next = 1.0 / (2.0 * sigma_value - rho_prev)
        current = target - operate(iterate)
        update = rho_next * rho_prev * update + 2.0 * rho_next / CHEB_RADIUS * (
            inverse_diag * current
        )
        iterate = iterate + update
        rho_prev = rho_next
    return iterate


def inverse_diagonal(values):
    identity = jnp.eye(4, dtype=values.dtype)
    return 1.0 / jnp.sum(values[0] * identity[:, :, None], axis=1)


def split_parts(vector):
    high_part = vector.astype(jnp.bfloat16)
    rest_part = vector - lax.optimization_barrier(high_part).astype(jnp.float32)
    middle_part = rest_part.astype(jnp.bfloat16)
    low_part = (rest_part - lax.optimization_barrier(middle_part).astype(jnp.float32)).astype(
        jnp.bfloat16
    )
    return jnp.concatenate([high_part, middle_part, low_part], axis=0)


def join_parts(product, row_count):
    return product[:row_count] + product[row_count : 2 * row_count] + product[2 * row_count :]


def pick_columns(vector, index_flat):
    parts = split_parts(vector)
    width = parts.shape[1]
    total = index_flat.shape[0]
    block_size = math.gcd(total, 2048)
    places = jnp.arange(width, dtype=jnp.int32)[:, None]

    def one_block(index_block):
        select = (places == index_block[None, :]).astype(jnp.bfloat16)
        return jnp.dot(parts, select, preferred_element_type=jnp.float32)

    picked = lax.map(one_block, index_flat.reshape(total // block_size, block_size))
    picked = jnp.moveaxis(picked, 0, 1).reshape(parts.shape[0], total)
    return join_parts(picked, vector.shape[0])


def extend(vector, send_rows):
    halo_width = send_rows.shape[1]
    outgoing = pick_columns(vector, send_rows.reshape(-1)).reshape(4, 4, halo_width)
    stream_pair = jnp.concatenate([outgoing[:, 0], outgoing[:, 1]], axis=1)
    span_pair = jnp.concatenate([outgoing[:, 2], outgoing[:, 3]], axis=1)
    stream_ext = padded(stream_pair, (("stream", 1),), halo_width, True)
    span_ext = padded(span_pair, (("span", 1),), halo_width, False)
    return jnp.concatenate(
        [
            vector,
            stream_ext[:, :halo_width],
            stream_ext[:, 3 * halo_width :],
            span_ext[:, :halo_width],
            span_ext[:, 3 * halo_width :],
        ],
        axis=1,
    )


def block_product(values, gathered):
    return jnp.einsum("kijn,jkn->in", values, gathered, precision=lax.Precision.HIGHEST)


def apply_level(vector, values, columns, send_rows):
    extended_vec = extend(vector, send_rows)
    picked = pick_columns(extended_vec, columns.reshape(-1)).reshape(
        4, columns.shape[0], columns.shape[1]
    )
    return block_product(values, picked)


def membership(order_rows):
    row_count = order_rows.shape[0]
    grouped = order_rows.reshape(row_count // 4, 4)
    places = jnp.arange(row_count, dtype=jnp.int32)[:, None, None]
    return jnp.any(places == grouped[None, :, :], axis=2).astype(jnp.bfloat16)


def restrict(fine_vec, weights, member):
    product = jnp.einsum("ijn,in->jn", weights, fine_vec, precision=lax.Precision.HIGHEST)
    parts = split_parts(product)
    return join_parts(jnp.dot(parts, member, preferred_element_type=jnp.float32), 4)


def prolong(coarse, weights, member):
    parts = split_parts(coarse)
    spread = join_parts(
        lax.dot_general(
            parts, member, (((1,), (1,)), ((), ())), preferred_element_type=jnp.float32
        ),
        4,
    )
    return jnp.einsum("ijn,jn->in", weights, spread, precision=lax.Precision.HIGHEST)


def per_device(
    right_side,
    fine_values,
    fine_columns,
    fine_sends,
    fine_order,
    fine_weights,
    middle_values,
    middle_columns,
    middle_sends,
    middle_order,
    middle_weights,
    coarsest_values,
    coarsest_columns,
):

    def fine_apply(vector):
        return apply_level(vector, fine_values, fine_columns, fine_sends)

    def middle_apply(vector):
        return apply_level(vector, middle_values, middle_columns, middle_sends)

    fine_inv = inverse_diagonal(fine_values)
    middle_inv = inverse_diagonal(middle_values)
    fine_member = membership(fine_order[0])
    middle_member = membership(middle_order[0])
    first_iter = chebyshev(fine_apply, fine_inv, right_side, None, KSM)
    fine_resid = right_side - fine_apply(first_iter)
    middle_rhs = restrict(fine_resid, fine_weights, fine_member)
    middle_iter = chebyshev(middle_apply, middle_inv, middle_rhs, None, KSM)
    middle_resid = middle_rhs - middle_apply(middle_iter)
    coarse_rhs = restrict(middle_resid, middle_weights, middle_member)

    def spread_apply(vector):
        slab_vector = lax.all_gather(vector, "span", axis=1, tiled=True)
        picked = pick_columns(slab_vector, coarsest_columns.reshape(-1)).reshape(
            4, coarsest_columns.shape[0], coarsest_columns.shape[1]
        )
        return block_product(coarsest_values, picked)

    coarse_iter = chebyshev(spread_apply, inverse_diagonal(coarsest_values), coarse_rhs, None, KC)
    middle_start = middle_iter + prolong(coarse_iter, middle_weights, middle_member)
    middle_final = chebyshev(middle_apply, middle_inv, middle_rhs, middle_start, KSM)
    fine_start = first_iter + prolong(middle_final, fine_weights, fine_member)
    solution = chebyshev(fine_apply, fine_inv, right_side, fine_start, KSM)
    residual = right_side - fine_apply(solution)
    return (solution, residual)


def solution(mesh):
    in_specs = (
        P(None, ("stream", "span")),
        P(None, None, None, ("stream", "span")),
        P(None, ("stream", "span")),
        P(None, ("stream", "span")),
        P(("stream", "span"), None),
        P(None, None, ("stream", "span")),
        P(None, None, None, ("stream", "span")),
        P(None, ("stream", "span")),
        P(None, ("stream", "span")),
        P(("stream", "span"), None),
        P(None, None, ("stream", "span")),
        P(None, None, None, ("stream", "span")),
        P(None, ("stream", "span")),
    )
    out_specs = (P(None, ("stream", "span")), P(None, ("stream", "span")))
    return jax.shard_map(
        per_device, mesh=mesh, in_specs=in_specs, out_specs=out_specs, check_vma=False
    )
```

profile of v0, /device:TPU:0, one launch (start us, length us, event | category | flops | bytes accessed | tf_op | source)
XLA Modules:
  0.0 379.7 jit_solution(5028634622681309260)
XLA Ops:
  14.8 23.3 %while.39 = (s32[]{:T(128)}, f32[8,12,2048]{2,1,0:T(8,128)S(1)}, s32[8,2048]{1,0:T(8,128)S(1)}, bf16[12,2304]{1,0:T(8,128)(2,1)S(1)}, s32[]{:T(128)}) while((s32[]{:T(128)}, f32[8,12,2048]{2,1,0:T(8,128)S(1)}, s32[8,2048]{1,0:T(8,128)S(1)}, bf16[12,2304]{1,0:T(8,128)(2,1)S(1)}, s32[]{:T(128)}) %tuple.349), condition=%wide.region_2.0_spmd.clone, body=%wide.region_1.0_spmd.clone.sunk | while | flops 117964800 | bytes 229445 | solution.py:85
  43.3 3.7 collective-permute-start.6
  48.8 4.9 %fusion.78 = pred[2048,512]{1,0:T(8,128)(4,1)S(1)} fusion(s32[512,4]{0,1:T(4,128)S(1)} %copy.171), kind=kLoop, calls=%fused_computation.92 | loop fusion | flops 7340032 | bytes 1056768 | tf_op jit(solution)/shard_map/reduce_or | solution.py:125
  54.1 23.3 %while.40 = (s32[]{:T(128)}, f32[8,12,2048]{2,1,0:T(8,128)S(1)}, s32[8,2048]{1,0:T(8,128)S(1)}, bf16[12,2304]{1,0:T(8,128)(2,1)S(1)}, s32[]{:T(128)}) while((s32[]{:T(128)}, f32[8,12,2048]{2,1,0:T(8,128)S(1)}, s32[8,2048]{1,0:T(8,128)S(1)}, bf16[12,2304]{1,0:T(8,128)(2,1)S(1)}, s32[]{:T(128)}) %tuple.350), condition=%wide.region_4.5_spmd.clone, body=%wide.region_3.0_spmd.clone.sunk | while | flops 117964800 | bytes 229445 | solution.py:85
  89.0 30.4 %while.41 = (s32[]{:T(128)}, f32[8,12,2048]{2,1,0:T(8,128)S(1)}, s32[8,2048]{1,0:T(8,128)S(1)}, bf16[12,2304]{1,0:T(8,128)(2,1)}, s32[]{:T(128)}) while((s32[]{:T(128)}, f32[8,12,2048]{2,1,0:T(8,128)S(1)}, s32[8,2048]{1,0:T(8,128)S(1)}, bf16[12,2304]{1,0:T(8,128)(2,1)}, s32[]{:T(128)}) %tuple.351), condition=%wide.region_7.8_spmd.clone, body=%wide.region_6.7_spmd.clone.sunk | while | flops 117964800 | bytes 211013 | solution.py:85
  89.1 3.8 fusion.427
  92.9 3.8 fusion.427
  96.7 3.8 fusion.427
  100.4 3.8 fusion.427
  104.2 3.8 fusion.427
  108.0 3.8 fusion.427
  111.8 3.8 fusion.427
  115.6 3.8 fusion.427
  129.2 3.8 collective-permute-done.15
  139.0 3.7 collective-permute-start.18
  151.8 3.7 collective-permute-start.22
  161.5 13.7 %all_gather.9 = f32[4,1024]{1,0:T(4,128)S(1)} all-gather(f32[4,128]{1,0:T(4,128)S(1)} %get-tuple-element.858), channel_id=1, replica_groups=mesh['stream'=4,'span'=8] {'span'}, dimensions={1}, use_global_device_ids=true | all-gather | bytes 18432 | tf_op jit(solution)/shard_map/all_gather | solution.py:179
  176.1 12.9 %all_gather.10 = f32[4,1024]{1,0:T(4,128)S(1)} all-gather(f32[4,128]{1,0:T(4,128)S(1)} %fusion.313), channel_id=1, replica_groups=mesh['stream'=4,'span'=8] {'span'}, dimensions={1}, use_global_device_ids=true | all-gather | bytes 18432 | tf_op jit(solution)/shard_map/all_gather | solution.py:179
  190.0 12.7 %all_gather.11 = f32[4,1024]{1,0:T(4,128)S(1)} all-gather(f32[4,128]{1,0:T(4,128)S(1)} %fusion.334), channel_id=1, replica_groups=mesh['stream'=4,'span'=8] {'span'}, dimensions={1}, use_global_device_ids=true | all-gather | bytes 18432 | tf_op jit(solution)/shard_map/all_gather | solution.py:179
  230.2 3.7 collective-permute-start.34
  251.6 23.3 %while.48 = (s32[]{:T(128)}, f32[8,12,2048]{2,1,0:T(8,128)S(1)}, s32[8,2048]{1,0:T(8,128)S(1)}, bf16[12,2304]{1,0:T(8,128)(2,1)S(1)}, s32[]{:T(128)}) while((s32[]{:T(128)}, f32[8,12,2048]{2,1,0:T(8,128)S(1)}, s32[8,2048]{1,0:T(8,128)S(1)}, bf16[12,2304]{1,0:T(8,128)(2,1)S(1)}, s32[]{:T(128)}) %tuple.352), condition=%wide.region_24.25_spmd.clone, body=%wide.region_23.24_spmd.clone.sunk | while | flops 117964800 | bytes 229445 | solution.py:85
  286.1 23.3 %while.49 = (s32[]{:T(128)}, f32[8,12,2048]{2,1,0:T(8,128)S(1)}, s32[8,2048]{1,0:T(8,128)S(1)}, bf16[12,2304]{1,0:T(8,128)(2,1)S(1)}, s32[]{:T(128)}) while((s32[]{:T(128)}, f32[8,12,2048]{2,1,0:T(8,128)S(1)}, s32[8,2048]{1,0:T(8,128)S(1)}, bf16[12,2304]{1,0:T(8,128)(2,1)S(1)}, s32[]{:T(128)}) %tuple.353), condition=%wide.region_26.27_spmd.clone, body=%wide.region_25.26_spmd.clone.sunk | while | flops 117964800 | bytes 229445 | solution.py:85
  320.6 23.3 %while.50 = (s32[]{:T(128)}, f32[8,12,2048]{2,1,0:T(8,128)S(1)}, s32[8,2048]{1,0:T(8,128)S(1)}, bf16[12,2304]{1,0:T(8,128)(2,1)S(1)}, s32[]{:T(128)}) while((s32[]{:T(128)}, f32[8,12,2048]{2,1,0:T(8,128)S(1)}, s32[8,2048]{1,0:T(8,128)S(1)}, bf16[12,2304]{1,0:T(8,128)(2,1)S(1)}, s32[]{:T(128)}) %tuple.354), condition=%wide.region_28.29_spmd.clone, body=%wide.region_27.28_spmd.clone.sunk | while | flops 117964800 | bytes 229445 | solution.py:85
  355.2 23.3 %while.51 = (s32[]{:T(128)}, f32[8,12,2048]{2,1,0:T(8,128)S(1)}, s32[8,2048]{1,0:T(8,128)S(1)}, bf16[12,2304]{1,0:T(8,128)(2,1)S(1)}, s32[]{:T(128)}) while((s32[]{:T(128)}, f32[8,12,2048]{2,1,0:T(8,128)S(1)}, s32[8,2048]{1,0:T(8,128)S(1)}, bf16[12,2304]{1,0:T(8,128)(2,1)S(1)}, s32[]{:T(128)}) %tuple.355), condition=%wide.region_30.31_spmd.clone, body=%wide.region_29.30_spmd.clone.sunk | while | flops 117964800 | bytes 229445 | solution.py:85
  (547 shorter events, 296.3 us)
Async XLA Ops:
  3.9 8.4 %collective-permute-start = (f32[4,64]{1,0:T(4,128)S(1)}, f32[4,64]{1,0:T(4,128)S(1)}, u32[]{:S(2)}, u32[]{:S(2)}) collective-permute-start(f32[4,64]{1,0:T(4,128)S(1)} %bitcast.716), channel_id=1, source_target_pairs={{0,8},{8,16},{16,24},{24,0},{1,9},{9,17},{17,25},{25,1},{2,10},{10... | collective-permute-start | bytes 3080 | tf_op jit(solution)/shard_map/ppermute | solution.py:24
  40.3 13.4 %collective-permute-start.4 = (f32[4,64]{1,0:T(4,128)S(1)}, f32[4,64]{1,0:T(4,128)S(1)}, u32[]{:S(2)}, u32[]{:S(2)}) collective-permute-start(f32[4,64]{1,0:T(4,128)S(1)} %bitcast.740), channel_id=1, source_target_pairs={{0,8},{8,16},{16,24},{24,0},{1,9},{9,17},{17,25},{25,1},{2,10},{10... | collective-permute-start | bytes 3080 | tf_op jit(solution)/shard_map/ppermute | solution.py:24
  41.0 12.7 %collective-permute-start.5 = (f32[4,64]{1,0:T(4,128)S(1)}, f32[4,64]{1,0:T(4,128)S(1)}, u32[]{:S(2)}, u32[]{:S(2)}) collective-permute-start(f32[4,64]{1,0:T(4,128)S(1)} %bitcast.729), channel_id=1, source_target_pairs={{8,0},{16,8},{24,16},{0,24},{9,1},{17,9},{25,17},{1,25},{10,2},{18... | collective-permute-start | bytes 3080 | tf_op jit(solution)/shard_map/ppermute | solution.py:26
  43.3 10.4 %collective-permute-start.6 = (f32[4,64]{1,0:T(4,128)S(1)}, f32[4,64]{1,0:T(4,128)S(1)}, u32[]{:S(2)}, u32[]{:S(2)}) collective-permute-start(f32[4,64]{1,0:T(4,128)S(1)} %bitcast.717), channel_id=1, source_target_pairs={{0,1},{1,2},{2,3},{3,4},{4,5},{5,6},{6,7},{8,9},{9,10},{10,11},{11... | collective-permute-start | bytes 3080 | tf_op jit(solution)/shard_map/ppermute | solution.py:24
  47.0 6.7 %collective-permute-start.7 = (f32[4,64]{1,0:T(4,128)S(1)}, f32[4,64]{1,0:T(4,128)S(1)}, u32[]{:S(2)}, u32[]{:S(2)}) collective-permute-start(f32[4,64]{1,0:T(4,128)S(1)} %bitcast.705), channel_id=1, source_target_pairs={{1,0},{2,1},{3,2},{4,3},{5,4},{6,5},{7,6},{9,8},{10,9},{11,10},{12... | collective-permute-start | bytes 3080 | tf_op jit(solution)/shard_map/ppermute | solution.py:26
  78.5 8.7 %collective-permute-start.10 = (f32[4,64]{1,0:T(4,128)S(1)}, f32[4,64]{1,0:T(4,128)S(1)}, u32[]{:S(2)}, u32[]{:S(2)}) collective-permute-start(f32[4,64]{1,0:T(4,128)S(1)} %bitcast.741), channel_id=1, source_target_pairs={{0,1},{1,2},{2,3},{3,4},{4,5},{5,6},{6,7},{8,9},{9,10},{10,11},{11... | collective-permute-start | bytes 3080 | tf_op jit(solution)/shard_map/ppermute | solution.py:24
  121.5 7.7 %collective-permute-start.12 = (f32[4,64]{1,0:T(4,128)S(1)}, f32[4,64]{1,0:T(4,128)S(1)}, u32[]{:S(2)}, u32[]{:S(2)}) collective-permute-start(f32[4,64]{1,0:T(4,128)S(1)} %bitcast.722), channel_id=1, source_target_pairs={{0,8},{8,16},{16,24},{24,0},{1,9},{9,17},{17,25},{25,1},{2,10},{10... | collective-permute-start | bytes 3080 | tf_op jit(solution)/shard_map/ppermute | solution.py:24
  127.0 6.0 %collective-permute-start.15 = (f32[4,64]{1,0:T(4,128)S(1)}, f32[4,64]{1,0:T(4,128)S(1)}, u32[]{:S(2)}, u32[]{:S(2)}) collective-permute-start(f32[4,64]{1,0:T(4,128)S(1)} %bitcast.701), channel_id=1, source_target_pairs={{1,0},{2,1},{3,2},{4,3},{5,4},{6,5},{7,6},{9,8},{10,9},{11,10},{12... | collective-permute-start | bytes 3080 | tf_op jit(solution)/shard_map/ppermute | solution.py:26
  136.0 8.1 %collective-permute-start.16 = (f32[4,64]{1,0:T(4,128)S(1)}, f32[4,64]{1,0:T(4,128)S(1)}, u32[]{:S(2)}, u32[]{:S(2)}) collective-permute-start(f32[4,64]{1,0:T(4,128)S(1)} %bitcast.742), channel_id=1, source_target_pairs={{0,8},{8,16},{16,24},{24,0},{1,9},{9,17},{17,25},{25,1},{2,10},{10... | collective-permute-start | bytes 3080 | tf_op jit(solution)/shard_map/ppermute | solution.py:24
  138.1 6.0 %collective-permute-start.17 = (f32[4,64]{1,0:T(4,128)S(1)}, f32[4,64]{1,0:T(4,128)S(1)}, u32[]{:S(2)}, u32[]{:S(2)}) collective-permute-start(f32[4,64]{1,0:T(4,128)S(1)} %bitcast.731), channel_id=1, source_target_pairs={{8,0},{16,8},{24,16},{0,24},{9,1},{17,9},{25,17},{1,25},{10,2},{18... | collective-permute-start | bytes 3080 | tf_op jit(solution)/shard_map/ppermute | solution.py:26
  148.8 8.1 %collective-permute-start.20 = (f32[4,64]{1,0:T(4,128)S(1)}, f32[4,64]{1,0:T(4,128)S(1)}, u32[]{:S(2)}, u32[]{:S(2)}) collective-permute-start(f32[4,64]{1,0:T(4,128)S(1)} %bitcast.743), channel_id=1, source_target_pairs={{0,8},{8,16},{16,24},{24,0},{1,9},{9,17},{17,25},{25,1},{2,10},{10... | collective-permute-start | bytes 3080 | tf_op jit(solution)/shard_map/ppermute | solution.py:24
  150.0 6.9 %collective-permute-start.21 = (f32[4,64]{1,0:T(4,128)S(1)}, f32[4,64]{1,0:T(4,128)S(1)}, u32[]{:S(2)}, u32[]{:S(2)}) collective-permute-start(f32[4,64]{1,0:T(4,128)S(1)} %bitcast.732), channel_id=1, source_target_pairs={{8,0},{16,8},{24,16},{0,24},{9,1},{17,9},{25,17},{1,25},{10,2},{18... | collective-permute-start | bytes 3080 | tf_op jit(solution)/shard_map/ppermute | solution.py:26
  214.9 7.5 %collective-permute-start.28 = (f32[4,64]{1,0:T(4,128)S(1)}, f32[4,64]{1,0:T(4,128)S(1)}, u32[]{:S(2)}, u32[]{:S(2)}) collective-permute-start(f32[4,64]{1,0:T(4,128)S(1)} %bitcast.746), channel_id=1, source_target_pairs={{0,8},{8,16},{16,24},{24,0},{1,9},{9,17},{17,25},{25,1},{2,10},{10... | collective-permute-start | bytes 3080 | tf_op jit(solution)/shard_map/ppermute | solution.py:24
  215.3 7.1 %collective-permute-start.29 = (f32[4,64]{1,0:T(4,128)S(1)}, f32[4,64]{1,0:T(4,128)S(1)}, u32[]{:S(2)}, u32[]{:S(2)}) collective-permute-start(f32[4,64]{1,0:T(4,128)S(1)} %bitcast.735), channel_id=1, source_target_pairs={{8,0},{16,8},{24,16},{0,24},{9,1},{17,9},{25,17},{1,25},{10,2},{18... | collective-permute-start | bytes 3080 | tf_op jit(solution)/shard_map/ppermute | solution.py:26
  227.2 8.0 %collective-permute-start.32 = (f32[4,64]{1,0:T(4,128)S(1)}, f32[4,64]{1,0:T(4,128)S(1)}, u32[]{:S(2)}, u32[]{:S(2)}) collective-permute-start(f32[4,64]{1,0:T(4,128)S(1)} %bitcast.747), channel_id=1, source_target_pairs={{0,8},{8,16},{16,24},{24,0},{1,9},{9,17},{17,25},{25,1},{2,10},{10... | collective-permute-start | bytes 3080 | tf_op jit(solution)/shard_map/ppermute | solution.py:24
  227.5 7.7 %collective-permute-start.33 = (f32[4,64]{1,0:T(4,128)S(1)}, f32[4,64]{1,0:T(4,128)S(1)}, u32[]{:S(2)}, u32[]{:S(2)}) collective-permute-start(f32[4,64]{1,0:T(4,128)S(1)} %bitcast.736), channel_id=1, source_target_pairs={{8,0},{16,8},{24,16},{0,24},{9,1},{17,9},{25,17},{1,25},{10,2},{18... | collective-permute-start | bytes 3080 | tf_op jit(solution)/shard_map/ppermute | solution.py:26
  241.4 8.4 %collective-permute-start.36 = (f32[4,64]{1,0:T(4,128)S(1)}, f32[4,64]{1,0:T(4,128)S(1)}, u32[]{:S(2)}, u32[]{:S(2)}) collective-permute-start(f32[4,64]{1,0:T(4,128)S(1)} %bitcast.748), channel_id=1, source_target_pairs={{0,8},{8,16},{16,24},{24,0},{1,9},{9,17},{17,25},{25,1},{2,10},{10... | collective-permute-start | bytes 3080 | tf_op jit(solution)/shard_map/ppermute | solution.py:24
  241.7 8.1 %collective-permute-start.37 = (f32[4,64]{1,0:T(4,128)S(1)}, f32[4,64]{1,0:T(4,128)S(1)}, u32[]{:S(2)}, u32[]{:S(2)}) collective-permute-start(f32[4,64]{1,0:T(4,128)S(1)} %bitcast.737), channel_id=1, source_target_pairs={{8,0},{16,8},{24,16},{0,24},{9,1},{17,9},{25,17},{1,25},{10,2},{18... | collective-permute-start | bytes 3080 | tf_op jit(solution)/shard_map/ppermute | solution.py:26
  275.9 8.0 %collective-permute-start.40 = (f32[4,64]{1,0:T(4,128)S(1)}, f32[4,64]{1,0:T(4,128)S(1)}, u32[]{:S(2)}, u32[]{:S(2)}) collective-permute-start(f32[4,64]{1,0:T(4,128)S(1)} %bitcast.749), channel_id=1, source_target_pairs={{0,8},{8,16},{16,24},{24,0},{1,9},{9,17},{17,25},{25,1},{2,10},{10... | collective-permute-start | bytes 3080 | tf_op jit(solution)/shard_map/ppermute | solution.py:24
  276.2 7.7 %collective-permute-start.41 = (f32[4,64]{1,0:T(4,128)S(1)}, f32[4,64]{1,0:T(4,128)S(1)}, u32[]{:S(2)}, u32[]{:S(2)}) collective-permute-start(f32[4,64]{1,0:T(4,128)S(1)} %bitcast.738), channel_id=1, source_target_pairs={{8,0},{16,8},{24,16},{0,24},{9,1},{17,9},{25,17},{1,25},{10,2},{18... | collective-permute-start | bytes 3080 | tf_op jit(solution)/shard_map/ppermute | solution.py:26
  310.5 8.1 %collective-permute-start.44 = (f32[4,64]{1,0:T(4,128)S(1)}, f32[4,64]{1,0:T(4,128)S(1)}, u32[]{:S(2)}, u32[]{:S(2)}) collective-permute-start(f32[4,64]{1,0:T(4,128)S(1)} %bitcast.750), channel_id=1, source_target_pairs={{0,8},{8,16},{16,24},{24,0},{1,9},{9,17},{17,25},{25,1},{2,10},{10... | collective-permute-start | bytes 3080 | tf_op jit(solution)/shard_map/ppermute | solution.py:24
  310.7 7.9 %collective-permute-start.45 = (f32[4,64]{1,0:T(4,128)S(1)}, f32[4,64]{1,0:T(4,128)S(1)}, u32[]{:S(2)}, u32[]{:S(2)}) collective-permute-start(f32[4,64]{1,0:T(4,128)S(1)} %bitcast.739), channel_id=1, source_target_pairs={{8,0},{16,8},{24,16},{0,24},{9,1},{17,9},{25,17},{1,25},{10,2},{18... | collective-permute-start | bytes 3080 | tf_op jit(solution)/shard_map/ppermute | solution.py:26
  345.0 8.0 %collective-permute-start.48 = (f32[4,64]{1,0:T(4,128)S(1)}, f32[4,64]{1,0:T(4,128)S(1)}, u32[]{:S(2)}, u32[]{:S(2)}) collective-permute-start(f32[4,64]{1,0:T(4,128)S(1)} %bitcast.751), channel_id=1, source_target_pairs={{0,8},{8,16},{16,24},{24,0},{1,9},{9,17},{17,25},{25,1},{2,10},{10... | collective-permute-start | bytes 3080 | tf_op jit(solution)/shard_map/ppermute | solution.py:24
  345.3 7.7 %collective-permute-start.49 = (f32[4,64]{1,0:T(4,128)S(1)}, f32[4,64]{1,0:T(4,128)S(1)}, u32[]{:S(2)}, u32[]{:S(2)}) collective-permute-start(f32[4,64]{1,0:T(4,128)S(1)} %bitcast.744), channel_id=1, source_target_pairs={{8,0},{16,8},{24,16},{0,24},{9,1},{17,9},{25,17},{1,25},{10,2},{18... | collective-permute-start | bytes 3080 | tf_op jit(solution)/shard_map/ppermute | solution.py:26
  (45 other events, 230.6 us)
where the time goes:
time: 387 us; the launch traced here: 380 us
  matrix products  190 us (49%)
  starting transfers between devices  99.6 us (26%)
  blocking collectives  39.3 us (10%)
  waiting for transfers between devices  22.4 us (6%)
  other arithmetic  15.1 us (4%)
  local copies, waits for them, and re-layouts  9.37 us (2%)
    dot_general x84, matrix products, one_block(): return jnp.dot(parts, select, preferred_element_type=jnp.float32)  189 us
    ppermute x26, starting transfers between devices, padded(): lax.ppermute(tail, axis, [(i, (i + 1) % count) for i in range(ends)])  53.9 us
    ppermute x26, starting transfers between devices, padded(): lax.ppermute(head, axis, [((i + 1) % count, i) for i in range(ends)])  45.8 us
    all_gather x3, blocking collectives, spread_apply(): slab_vector = lax.all_gather(vector, 'span', axis=1, tiled=True)  39.3 us
    ppermute x26, waiting for transfers between devices, padded(): lax.ppermute(head, axis, [((i + 1) % count, i) for i in range(ends)])  21.7 us
  transfers between devices with their start and end apart: 52, of which 13 were waited for; matrix products, arithmetic and copies ran while one was open for 2% of the time, Pallas kernels for 0%

commit v1 on v0

v1 whole, which is shorter than its diff:
```python
import jax
import jax.numpy as jnp
from jax import lax
from jax.experimental import pallas as pl
from jax.experimental.pallas import tpu as pltpu
from jax.sharding import PartitionSpec as P

KSM = 3
KC = 4
NNZ = 8
LANES = 128
SUBS = 8

CHEB_CENTRE = 1.0
CHEB_RADIUS = 0.9
AXES = ("stream", "span")
F32 = jnp.float32
I32 = jnp.int32


def cheb_factors(degree):
    sigma = CHEB_CENTRE / CHEB_RADIUS
    rho = 1.0 / sigma
    factors = [(0.0, 1.0 / CHEB_CENTRE)]
    for _ in range(degree - 1):
        rho_next = 1.0 / (2.0 * sigma - rho)
        factors.append((rho_next * rho, 2.0 * rho_next / CHEB_RADIUS))
        rho = rho_next
    return factors


def tile_iota(dim):
    return lax.broadcasted_iota(I32, (SUBS, LANES), dim)


def pick(line, lane):
    return jnp.take_along_axis(line, lane, axis=1, mode="promise_in_bounds")


def wide(line):
    return jnp.broadcast_to(line, (SUBS, LANES))


def pick_lines(lines, high, lane, first=0):
    result = jnp.zeros((SUBS, LANES), F32)
    for r, line in enumerate(lines):
        result = jnp.where(high == first + r, pick(line, lane), result)
    return result


def halo_lines(arrivals, edge_ref):
    values = [r[...] for r in arrivals]
    prev_s, next_s, prev_p, next_p = [values[d] + values[4 + d] for d in range(4)]
    left = tile_iota(1) < LANES // 2
    upper = tile_iota(0) < 4
    edge_ref[...] = jnp.where(
        upper, jnp.where(left, prev_s, next_s), jnp.where(left, prev_p, next_p)
    )


def outgoing(lines_of, count, sends):
    high, lane = sends >> 7, sends & (LANES - 1)
    return pick_lines([lines_of(r) for r in range(count)], high, lane)


def duplicate(x):
    return x + pltpu.roll(x, 4, 0)


def fine_start(v_ref, b_ref, s_ref, bo_ref, mo_ref, x_ref, out_ref, pad_ref):
    lines = bo_ref.shape[1]
    for i in range(4):
        for h in range(lines // SUBS):
            rows = pl.ds(h * SUBS, SUBS)
            native = pl.ds(h * SUBS * 4 + i, SUBS, stride=4)
            b = b_ref[native, :]
            m = 1.0 / v_ref[pl.ds((i * lines + h * SUBS) * 4 + i, SUBS, stride=4), :]
            x = m * b
            bo_ref[i, rows, :] = b
            mo_ref[i, rows, :] = m
            x_ref[i, rows, :] = x
            for twice in range(2):
                pad_ref[pl.ds((twice * 4 + i) * lines + h * SUBS, SUBS), :] = x
    out_ref[...] = outgoing(
        lambda r: pad_ref[pl.ds(r, SUBS, stride=lines), :], lines, s_ref[...]
    )


def fine_prepare(v_ref, c_ref, _, vo_ref, co_ref):
    lines = vo_ref.shape[3]
    halves = lines // SUBS

    def body(ki, carry):
        k, i = ki // 4, ki % 4
        for j in range(4):
            for h in range(halves):
                start = ki * (lines * 4) + h * SUBS * 4 + j
                vo_ref[k, i, j, pl.ds(h * SUBS, SUBS), :] = v_ref[
                    pl.ds(start, SUBS, stride=4), :
                ]
        return carry

    lax.fori_loop(0, NNZ * 4, body, 0)
    for k in range(NNZ):
        for h in range(halves):
            co_ref[k, pl.ds(h * SUBS, SUBS), :] = c_ref[
                pl.ds(h * SUBS * NNZ + k, SUBS, stride=NNZ), :
            ]


def fine_local(x_ref, b_ref, v_ref, c_ref, r_ref, line_ref):
    lines = x_ref.shape[1]
    halves = lines // SUBS
    for j in range(4):
        for r in range(lines):
            line_ref[j, r] = wide(x_ref[j, pl.ds(r, 1), :])
    acc = []
    for h in range(halves):
        rows = pl.ds(h * SUBS, SUBS)
        for i in range(4):
            total = b_ref[i, rows, :]
            for j in range(4):
                total = total - v_ref[0, i, j, rows, :] * x_ref[j, rows, :]
            acc.append(total)

    def body(k, acc):
        acc = list(acc)
        for h in range(halves):
            rows = pl.ds(h * SUBS, SUBS)
            col = c_ref[k, rows, :]
            high, lane = col >> 7, col & (LANES - 1)
            for j in range(4):
                got = pick_lines([line_ref[j, r] for r in range(lines)], high, lane)
                for i in range(4):
                    acc[4 * h + i] = acc[4 * h + i] - v_ref[k, i, j, rows, :] * got
        return tuple(acc)

    acc = lax.fori_loop(1, NNZ, body, tuple(acc))
    for h in range(halves):
        for i in range(4):
            r_ref[i, pl.ds(h * SUBS, SUBS), :] = acc[4 * h + i]


def fine_remote(arrivals, r_ref, v_ref, c_ref, edge_ref):
    lines = r_ref.shape[1]
    halves = lines // SUBS
    halo_lines(arrivals, edge_ref)
    edges = [[wide(edge_ref[pl.ds(4 * e + j, 1), :]) for e in range(2)] for j in range(4)]
    result = []
    for h in range(halves):
        rows = pl.ds(h * SUBS, SUBS)
        acc = [r_ref[i, rows, :] for i in range(4)]
        for k in range(1, NNZ):
            col = c_ref[k, rows, :]
            high, lane = col >> 7, col & (LANES - 1)
            for j in range(4):
                got = pick_lines(edges[j], high, lane, lines)
                for i in range(4):
                    acc[i] = acc[i] - v_ref[k, i, j, rows, :] * got
        result.append(acc)
    return result


def fine_step(factors, *refs):
    arrivals = refs[:8]
    (r_ref, v_ref, c_ref, m_ref, x_ref, d_ref, s_ref, xo_ref, do_ref, out_ref, edge_ref, pad_ref) = refs[8:]
    keep, gain = factors
    lines = r_ref.shape[1]
    resid = fine_remote(arrivals, r_ref, v_ref, c_ref, edge_ref)
    for h in range(lines // SUBS):
        rows = pl.ds(h * SUBS, SUBS)
        for i in range(4):
            d = gain * (m_ref[i, rows, :] * resid[h][i])
            if keep:
                d = keep * d_ref[i, rows, :] + d
            x = x_ref[i, rows, :] + d
            do_ref[i, rows, :] = d
            xo_ref[i, rows, :] = x
            for twice in range(2):
                pad_ref[pl.ds((twice * 4 + i) * lines + h * SUBS, SUBS), :] = x
    out_ref[...] = outgoing(
        lambda r: pad_ref[pl.ds(r, SUBS, stride=lines), :], lines, s_ref[...]
    )


def fine_finish(*refs):
    arrivals = refs[:8]
    r_ref, v_ref, c_ref, x_ref, so_ref, ro_ref, edge_ref = refs[8:]
    lines = r_ref.shape[1]
    resid = fine_remote(arrivals, r_ref, v_ref, c_ref, edge_ref)
    for h in range(lines // SUBS):
        for i in range(4):
            native = pl.ds(h * SUBS * 4 + i, SUBS, stride=4)
            so_ref[native, :] = x_ref[i, pl.ds(h * SUBS, SUBS), :]
            ro_ref[native, :] = resid[h][i]


def fine_restrict(*refs):
    arrivals = refs[:8]
    (r_ref, v_ref, c_ref, w_ref, p_ref, m2_ref, s2_ref, b2_ref, x2_ref, out_ref, edge_ref, line_ref, pad_ref) = refs[8:]
    lines = r_ref.shape[1]
    resid = fine_remote(arrivals, r_ref, v_ref, c_ref, edge_ref)
    for h in range(lines // SUBS):
        rows = pl.ds(h * SUBS, SUBS)
        for j in range(4):
            total = w_ref[0, j, rows, :] * resid[h][0]
            for i in range(1, 4):
                total = total + w_ref[i, j, rows, :] * resid[h][i]
            line_ref[j, rows, :] = total
    for j in range(4):
        total = None
        source = [wide(line_ref[j, pl.ds(r, 1), :]) for r in range(lines)]
        for part in range(2):
            place = p_ref[part]
            got = pick_lines(source, place >> 7, place & (LANES - 1))
            total = got if total is None else total + got
        b2 = duplicate(total)
        x2 = m2_ref[j] * b2
        b2_ref[j] = b2
        x2_ref[j] = x2
        middle_pad(pad_ref, j, x2)
    middle_out(out_ref, pad_ref, s2_ref)


def inverse_order(o_row, lines):
    count = lines * LANES
    high, lane = o_row >> 7, o_row & (LANES - 1)
    coarse = lax.broadcasted_iota(I32, (1, count), 1) >> 2
    here = lax.broadcasted_iota(I32, (lines, count), 0) == high
    upper = jnp.where(here, (coarse >> 4).astype(F32), 0.0)
    lower = jnp.where(here, (coarse & 15).astype(F32), 0.0)
    left = jnp.concatenate([upper, lower], axis=0).astype(jnp.bfloat16)
    right = jnp.where(
        lax.broadcasted_iota(I32, (LANES, count), 0) == lane, 1.0, 0.0
    ).astype(jnp.bfloat16)
    found = lax.dot_general(
        left, right, (((1,), (1,)), ((), ())), preferred_element_type=F32
    )
    return (found[:lines] * 16.0 + found[lines:]).astype(I32)


def pick_order(sources, unit):
    lane = tile_iota(1)
    place = 4 * (lane & 31) + unit
    result = jnp.zeros((SUBS, LANES), I32)
    for q, source in enumerate(sources):
        result = jnp.where((lane >> 5) == q, pick(source, place), result)
    return result


def fine_tables(w_ref, row_ref, o_ref, _, wo_ref, agg_ref, place_ref):
    lines = o_ref.shape[0]
    for i in range(4):
        for j in range(4):
            for h in range(lines // SUBS):
                start = (i * lines + h * SUBS) * 4 + j
                wo_ref[i, j, pl.ds(h * SUBS, SUBS), :] = w_ref[pl.ds(start, SUBS, stride=4), :]
    agg_ref[...] = inverse_order(row_ref[...], lines)
    sources = []
    for q in range(4):
        four = o_ref[pl.ds(q, 4, stride=4), :]
        sources.append(jnp.concatenate([four, four], axis=0))
    for part in range(2):
        place_ref[part] = pick_order(sources, (tile_iota(0) >> 2) + 2 * part)


def middle_tables(v_ref, c_ref, w_ref, row_ref, o_ref, _, vo_ref, co_ref, mo_ref, wo_ref, agg_ref, place_ref):
    lines = o_ref.shape[0]

    def body(ki, carry):
        k, i = ki // 4, ki % 4
        kp, i2 = ki // 4, ki % 4
        for j in range(4):
            for odd in range(2):
                start = ((2 * kp + odd) * 4 + i2) * (lines * 4) + j
                vo_ref[k, i, j, pl.ds(4 * odd, 4), :] = v_ref[pl.ds(start, 4, stride=4), :]
        return carry

    lax.fori_loop(0, NNZ // 2 * 4, body, 0)
    for kp in range(NNZ // 2):
        for odd in range(2):
            co_ref[kp, pl.ds(4 * odd, 4), :] = c_ref[pl.ds(2 * kp + odd, 4, stride=NNZ), :]
    for i in range(4):
        four = 1.0 / v_ref[pl.ds(i * lines * 4 + i, 4, stride=4), :]
        mo_ref[i, pl.ds(0, 4), :] = four
        mo_ref[i, pl.ds(4, 4), :] = four
        for j in range(4):
            four = w_ref[pl.ds(i * lines * 4 + j, 4, stride=4), :]
            wo_ref[i, j, pl.ds(0, 4), :] = four
            wo_ref[i, j, pl.ds(4, 4), :] = four
    agg = inverse_order(row_ref[...], lines)
    agg_ref[...] = jnp.concatenate([agg, agg], axis=0)
    sources = [wide(o_ref[pl.ds(q, 1), :]) for q in range(4)]
    place_ref[...] = pick_order(sources, tile_iota(0) & 3)


def middle_pad(pad_ref, j, x):
    for twice in range(2):
        pad_ref[pl.ds((twice * 4 + j) * SUBS, SUBS), :] = x


def middle_out(out_ref, pad_ref, s_ref):
    out_ref[...] = outgoing(
        lambda r: pad_ref[pl.ds(r, SUBS, stride=SUBS), :], 4, s_ref[...]
    )


def middle_residual(arrivals, b_ref, x_ref, v_ref, c_ref, edge_ref):
    halo_lines(arrivals, edge_ref)
    acc = [jnp.zeros((SUBS, LANES), F32) for _ in range(4)]
    for j in range(4):
        source = [wide(x_ref[j, pl.ds(r, 1), :]) for r in range(4)]
        source += [wide(edge_ref[pl.ds(4 * e + j, 1), :]) for e in range(2)]
        for kp in range(NNZ // 2):
            col = c_ref[kp]
            got = pick_lines(source, col >> 7, col & (LANES - 1))
            for i in range(4):
                acc[i] = acc[i] + v_ref[kp, i, j] * got
    return [b_ref[i] - duplicate(acc[i]) for i in range(4)]


def middle_update(factors, resid, m_ref, x_ref, d_ref):
    keep, gain = factors
    xs, ds = [], []
    for i in range(4):
        d = gain * (m_ref[i] * resid[i])
        if keep:
            d = keep * d_ref[i] + d
        ds.append(d)
        xs.append(x_ref[i] + d)
    return xs, ds


def middle_step(factors, *refs):
    arrivals = refs[:8]
    (b_ref, m_ref, x_ref, d_ref, v_ref, c_ref, s_ref, xo_ref, do_ref, out_ref, edge_ref, pad_ref) = refs[8:]
    resid = middle_residual(arrivals, b_ref, x_ref, v_ref, c_ref, edge_ref)
    xs, ds = middle_update(factors, resid, m_ref, x_ref, d_ref)
    for i in range(4):
        xo_ref[i] = xs[i]
        do_ref[i] = ds[i]
        middle_pad(pad_ref, i, xs[i])
    middle_out(out_ref, pad_ref, s_ref)


def middle_restrict(*refs):
    arrivals = refs[:8]
    b_ref, x_ref, v_ref, c_ref, w_ref, p_ref, out_ref, edge_ref, line_ref = refs[8:]
    resid = middle_residual(arrivals, b_ref, x_ref, v_ref, c_ref, edge_ref)
    place = p_ref[...]
    high, lane = place >> 7, place & (LANES - 1)
    for j in range(4):
        total = w_ref[0, j] * resid[0]
        for i in range(1, 4):
            total = total + w_ref[i, j] * resid[i]
        line_ref[j] = total
        source = [wide(line_ref[j, pl.ds(r, 1), :]) for r in range(4)]
        got = pick_lines(source, high, lane)
        got = got + pltpu.roll(got, 2, 0)
        got = got + pltpu.roll(got, 1, 0)
        out_ref[pl.ds(j, 1), :] = got[0:1]
        out_ref[pl.ds(4 + j, 1), :] = got[0:1]


def middle_prolong(factors, *refs):
    arrivals = refs[:8]
    (b_ref, m_ref, x_ref, d_ref, v_ref, c_ref, x1_ref, w_ref, agg_ref, s_ref, xo_ref, out_ref, edge_ref, line_ref, pad_ref) = refs[8:]
    lines = x1_ref.shape[1]
    resid = middle_residual(arrivals, b_ref, x_ref, v_ref, c_ref, edge_ref)
    xs, _ = middle_update(factors, resid, m_ref, x_ref, d_ref)
    for j in range(4):
        line_ref[j] = xs[j]
    for h in range(lines // SUBS):
        rows = pl.ds(h * SUBS, SUBS)
        agg = agg_ref[rows, :]
        high, lane = agg >> 7, agg & (LANES - 1)
        spread = [
            pick_lines([wide(line_ref[j, pl.ds(r, 1), :]) for r in range(4)], high, lane)
            for j in range(4)
        ]
        for i in range(4):
            placed = w_ref[i, 0, rows, :] * spread[0]
            for j in range(1, 4):
                placed = placed + w_ref[i, j, rows, :] * spread[j]
            x = x1_ref[i, rows, :] + placed
            xo_ref[i, rows, :] = x
            for twice in range(2):
                pad_ref[pl.ds((twice * 4 + i) * lines + h * SUBS, SUBS), :] = x
    out_ref[...] = outgoing(
        lambda r: pad_ref[pl.ds(r, SUBS, stride=lines), :], lines, s_ref[...]
    )


def coarse_half(half, *refs):
    for t in range(half):
        refs[2 * half + 1][t] = refs[t][...] + refs[half + t][...]
    for t in range(1, half):
        refs[2 * half + 2][t - 1] = refs[t][...] + refs[half + t][...]


def coarse_tables(group, *refs):
    half = group // 2
    own_ref, me_ref = refs[0], refs[1]
    odd = refs[2]
    even = refs[3:5]
    vo_ref, co_ref, mo_ref, pad_ref = refs[6:]
    pad_ref[0] = own_ref[...]
    for t in range(half):
        pad_ref[2 * t + 1] = odd[t]
    for t in range(half - 1):
        pad_ref[2 * t + 2] = even[0][t] + even[1][t]
    me = me_ref[0]
    for h in range(group // SUBS):
        rows = pl.ds(h * SUBS, SUBS)
        for ki in range(NNZ * 4):
            k, i = ki // 4, ki % 4
            for j in range(4):
                tile = pad_ref[rows, ki * 4 + j, :]
                vo_ref[k, i, j, rows, :] = tile
                if k == 0 and i == j:
                    mo_ref[i, rows, :] = 1.0 / tile
        for k in range(NNZ):
            col = pad_ref[rows, NNZ * 16 + k, :].astype(I32)
            co_ref[k, rows, :] = ((col >> 7) ^ me) * LANES + (col & (LANES - 1))


def coarse_solve(group, *refs):
    half = group // 2
    own_ref = refs[0]
    odd = refs[1 : 1 + 2 * half]
    even = refs[1 + 2 * half : 3 + 2 * half]
    (v_ref, c_ref, m_ref, x2_ref, w_ref, agg_ref, s_ref, xo_ref, out_ref, b_ref, x_ref, d_ref, tmp_ref, pad_ref) = refs[3 + 2 * half :]
    for j in range(4):
        b_ref[j, pl.ds(0, 1), :] = own_ref[pl.ds(j, 1), :]
    for t in range(half):
        tmp_ref[...] = odd[t][...] + odd[half + t][...]
        for j in range(4):
            b_ref[j, pl.ds(2 * t + 1, 1), :] = tmp_ref[pl.ds(j, 1), :]
    for t in range(half - 1):
        tmp_ref[...] = even[0][t] + even[1][t]
        for j in range(4):
            b_ref[j, pl.ds(2 * t + 2, 1), :] = tmp_ref[pl.ds(j, 1), :]
    blocks = group // SUBS
    for j in range(4):
        first = m_ref[j] * b_ref[j]
        x_ref[j] = first
        d_ref[j] = first
    for keep, gain in cheb_factors(KC)[1:]:
        resid = []
        for h in range(blocks):
            rows = pl.ds(h * SUBS, SUBS)
            acc = [b_ref[i, rows, :] for i in range(4)]
            for k in range(NNZ):
                col = c_ref[k, rows, :]
                high, lane = col >> 7, col & (LANES - 1)
                for j in range(4):
                    if k:
                        got = pick_lines(
                            [wide(x_ref[j, pl.ds(r, 1), :]) for r in range(group)], high, lane
                        )
                    else:
                        got = x_ref[j, rows, :]
                    for i in range(4):
                        acc[i] = acc[i] - v_ref[k, i, j, rows, :] * got
            resid.append(acc)
        for h in range(blocks):
            rows = pl.ds(h * SUBS, SUBS)
            for i in range(4):
                d = keep * d_ref[i, rows, :] + gain * (m_ref[i, rows, :] * resid[h][i])
                d_ref[i, rows, :] = d
                x_ref[i, rows, :] = x_ref[i, rows, :] + d
    lane = agg_ref[...]
    spread = [pick(wide(x_ref[j, pl.ds(0, 1), :]), lane) for j in range(4)]
    for i in range(4):
        x = x2_ref[i]
        for j in range(4):
            x = x + w_ref[i, j] * spread[j]
        xo_ref[i] = x
        middle_pad(pad_ref, i, x)
    middle_out(out_ref, pad_ref, s_ref)


def call(body, outs, args, scratch=(), free=(), smem=()):
    specs = []
    for index in range(len(args)):
        if index in free:
            specs.append(pl.BlockSpec(memory_space=pl.ANY))
        elif index in smem:
            specs.append(pl.BlockSpec(memory_space=pltpu.SMEM))
        else:
            specs.append(pl.BlockSpec(memory_space=pltpu.VMEM))
    single = not isinstance(outs, (list, tuple))
    shapes = [outs] if single else list(outs)
    result = pl.pallas_call(
        body,
        out_shape=shapes,
        in_specs=specs,
        out_specs=[pl.BlockSpec(memory_space=pltpu.VMEM) for _ in shapes],
        scratch_shapes=list(scratch),
        compiler_params=pltpu.CompilerParams(vmem_limit_bytes=16 * 2**20),
    )(*args)
    return result[0] if single else result


def shape(*dims, dtype=F32):
    return jax.ShapeDtypeStruct(dims, dtype)


def vmem(*dims, dtype=F32):
    return pltpu.VMEM(dims, dtype)


def native_rows(x):
    lines = x.shape[-1] // LANES
    split = x.reshape(x.shape[:-1] + (lines, LANES))
    return jnp.swapaxes(split, -2, -3).reshape(-1, LANES)


def from_native(rows, lines):
    return jnp.swapaxes(rows.reshape(lines, 4, LANES), 0, 1).reshape(4, lines * LANES)


def send_table(sends):
    stream = jnp.concatenate([sends[1], sends[0]])[None]
    span = jnp.concatenate([sends[3], sends[2]])[None]
    return jnp.concatenate([stream] * 4 + [span] * 4, axis=0)


def colour_of(mesh):
    count = mesh.shape["span"]
    return lambda p: (p // count + p % count) % 2


def exchange(mesh, out):
    slabs, count = mesh.shape["stream"], mesh.shape["span"]
    colour = colour_of(mesh)
    places = [(a, b) for a in range(slabs) for b in range(count)]
    moves = []
    for da, db in ((1, 0), (-1, 0), (0, 1), (0, -1)):
        moves.append(
            [
                (a * count + b, (a + da) % slabs * count + b + db)
                for a, b in places
                if 0 <= b + db < count
            ]
        )
    return [
        lax.ppermute(out, AXES, [pair for pair in move if colour(pair[0]) == side])
        for side in range(2)
        for move in moves
    ]


def span_swaps(mesh, value, masks, in_turn=False):
    slabs, count = mesh.shape["stream"], mesh.shape["span"]
    colour = colour_of(mesh)
    places = [(a, b) for a in range(slabs) for b in range(count)]

    def one_side(value, side):
        return [
            lax.ppermute(
                value,
                AXES,
                [
                    (a * count + b, a * count + (b ^ mask))
                    for a, b in places
                    if colour(a * count + b) == side
                ],
            )
            for mask in masks
        ]

    first = one_side(value, 1)
    if in_turn:
        value, first = lax.optimization_barrier((value, first))
    return one_side(value, 0) + first


def span_gather(mesh, value):
    half = mesh.shape["span"] // 2
    odd = span_swaps(mesh, value, range(1, 2 * half, 2), True)
    held = jnp.stack([odd[t] + odd[half + t] for t in range(1, half)])
    even = span_swaps(mesh, held, (1,))
    return odd, even


def per_device(mesh, right_side, fine_values, fine_columns, fine_sends, fine_order, fine_weights, middle_values, middle_columns, middle_sends, middle_order, middle_weights, coarsest_values, coarsest_columns):
    group = mesh.shape["span"]
    lines = right_side.shape[1] // LANES
    tile = shape(SUBS, LANES)
    vec1 = shape(4, lines, LANES)
    vec2 = shape(4, SUBS, LANES)
    edge = vmem(SUBS, LANES)
    pad1 = vmem(SUBS * lines, LANES)
    pad2 = vmem(SUBS * SUBS, LANES)
    factors = cheb_factors(KSM)
    send1, send2 = send_table(fine_sends), send_table(middle_sends)
    values1 = native_rows(fine_values)
    values2 = native_rows(middle_values)

    b1, m1, x1, out = call(
        fine_start,
        [vec1, vec1, vec1, tile],
        [native_rows(fine_values[0]), native_rows(right_side), send1],
        [pad1],
    )
    d1 = x1

    own3 = jnp.concatenate(
        [coarsest_values.reshape(NNZ * 16, LANES), coarsest_columns.astype(F32)], axis=0
    )
    v1, c1 = call(
        fine_prepare,
        [shape(NNZ, 4, 4, lines, LANES), shape(NNZ, lines, LANES, dtype=I32)],
        [values1, native_columns(fine_columns), out],
        free=(2,),
    )

    def fine_part(x):
        return call(fine_local, vec1, [x, b1, v1, c1], [vmem(4, lines, SUBS, LANES)])

    def fine_next(which, arrived, resid, x, d, after=()):
        args = arrived + [resid, v1, c1, m1, x, d, send1]
        return call(
            lambda *refs: fine_step(factors[which], *(refs[: len(args)] + refs[len(args) + len(after) :])),
            [vec1, vec1, tile],
            args + list(after),
            [edge, pad1],
            free=range(len(args), len(args) + len(after)),
        )

    arrived = exchange(mesh, out)
    own3, _ = lax.optimization_barrier((own3, out))
    swapped3 = span_swaps(mesh, own3, range(1, group, 2))
    resid = fine_part(x1)
    x1, d1, out = fine_next(1, arrived, resid, x1, d1)

    arrived = exchange(mesh, out)
    half = group // 2
    odd3, held3 = call(
        lambda *refs: coarse_half(half, *refs),
        [shape(half, NNZ * 17, LANES), shape(half - 1, NNZ * 17, LANES)],
        swapped3 + [out],
        free=(group,),
    )
    even3 = span_swaps(mesh, held3, (1,))
    resid = fine_part(x1)
    w1, agg1, place1 = call(
        fine_tables,
        [shape(4, 4, lines, LANES), shape(lines, LANES, dtype=I32), shape(2, SUBS, LANES, dtype=I32)],
        [native_rows(fine_weights), fine_order, fine_order.reshape(lines, LANES), out],
        free=(3,),
    )
    x1, d1, out = fine_next(2, arrived, resid, x1, d1, [held3])

    arrived = exchange(mesh, out)
    resid = fine_part(x1)
    v2, c2, m2, w2, agg2, place2 = call(
        middle_tables,
        [
            shape(NNZ // 2, 4, 4, SUBS, LANES),
            shape(NNZ // 2, SUBS, LANES, dtype=I32),
            vec2,
            shape(4, 4, SUBS, LANES),
            shape(SUBS, LANES, dtype=I32),
            shape(SUBS, LANES, dtype=I32),
        ],
        [values2, native_columns(middle_columns), native_rows(middle_weights), middle_order, middle_order.reshape(-1, LANES), out],
        free=(5,),
    )
    b2, x2, out = call(
        fine_restrict,
        [vec2, vec2, tile],
        arrived + [resid, v1, c1, w1, place1, m2, send2],
        [edge, vmem(4, lines, LANES), pad2],
    )
    d2 = x2

    def middle_next(which, arrived, x, d, after=()):
        args = arrived + [b2, m2, x, d, v2, c2, send2]
        return call(
            lambda *refs: middle_step(factors[which], *(refs[: len(args)] + refs[len(args) + len(after) :])),
            [vec2, vec2, tile],
            args + list(after),
            [edge, pad2],
            free=range(len(args), len(args) + len(after)),
        )

    arrived = exchange(mesh, out)
    me = lax.axis_index("span").astype(I32).reshape(1)
    v3, c3, m3 = call(
        lambda *refs: coarse_tables(group, *refs),
        [shape(NNZ, 4, 4, group, LANES), shape(NNZ, group, LANES, dtype=I32), shape(4, group, LANES)],
        [own3, me, odd3] + even3 + [out],
        [vmem(group, NNZ * 17, LANES)],
        free=(5,),
        smem=(1,),
    )
    x2, d2, out = middle_next(1, arrived, x2, d2, [m3])
    arrived = exchange(mesh, out)
    x2, d2, out = middle_next(2, arrived, x2, d2)
    arrived = exchange(mesh, out)
    rhs3 = call(
        middle_restrict,
        tile,
        arrived + [b2, x2, v2, c2, w2, place2],
        [edge, vmem(4, SUBS, LANES)],
    )
    odd, even = span_gather(mesh, rhs3)
    vec3 = vmem(4, group, LANES)
    x2, out = call(
        lambda *refs: coarse_solve(group, *refs),
        [vec2, tile],
        [rhs3] + odd + even + [v3, c3, m3, x2, w2, agg2, send2],
        [vec3, vec3, vec3, edge, pad2],
    )
    arrived = exchange(mesh, out)
    x2, d2, out = middle_next(0, arrived, x2, x2)
    arrived = exchange(mesh, out)
    x2, d2, out = middle_next(1, arrived, x2, d2)
    arrived = exchange(mesh, out)
    x1, out = call(
        lambda *refs: middle_prolong(factors[2], *refs),
        [vec1, tile],
        arrived + [b2, m2, x2, d2, v2, c2, x1, w1, agg1, send1],
        [edge, vmem(4, SUBS, LANES), pad1],
    )
    for which in range(KSM):
        arrived = exchange(mesh, out)
        resid = fine_part(x1)
        x1, d1, out = fine_next(which, arrived, resid, x1, d1)
    arrived = exchange(mesh, out)
    resid = fine_part(x1)
    rows = shape(4 * lines, LANES)
    solved, left = call(fine_finish, [rows, rows], arrived + [resid, v1, c1, x1], [edge])
    return from_native(solved, lines), from_native(left, lines)


def native_columns(columns):
    lines = columns.shape[1] // LANES
    return jnp.swapaxes(columns.reshape(NNZ, lines, LANES), 0, 1).reshape(-1, LANES)


def solution(mesh):
    both = ("stream", "span")
    in_specs = (
        P(None, both),
        P(None, None, None, both),
        P(None, both),
        P(None, both),
        P(both, None),
        P(None, None, both),
        P(None, None, None, both),
        P(None, both),
        P(None, both),
        P(both, None),
        P(None, None, both),
        P(None, None, None, both),
        P(None, both),
    )
    return jax.shard_map(
        lambda *args: per_device(mesh, *args),
        mesh=mesh,
        in_specs=in_specs,
        out_specs=(P(None, both), P(None, both)),
        check_vma=False,
    )
```

time: 387 us -> 277 us (0.72)
  matrix products: 190 us -> 0 us
  starting transfers between devices: 99.6 us -> 212 us
  blocking collectives: 39.3 us -> 0 us
  Pallas kernels: 0 us -> 19.7 us
  other arithmetic: 15.1 us -> 0.18 us
  waiting for transfers between devices: 22.4 us -> 33.1 us
  local copies, waits for them, and re-layouts: 9.37 us -> 5.15 us
    dot_general x88 -> x0, matrix products: 190 us -> none  [the longest x84 189 us: one_block(): return jnp.dot(parts, select, preferred_element_type=jnp.float32)]
    ppermute x52 -> x124, starting transfers between devices: 99.6 us -> 212 us  [the longest x104 175 us: exchange(): lax.ppermute(out, AXES, [pair for pair in move if colour(pair[0]) == side])]
    all_gather x3 -> x0, blocking collectives: 39.3 us -> none  [spread_apply(): slab_vector = lax.all_gather(vector, 'span', axis=1, tiled=True)]
    pallas_call x0 -> x27, Pallas kernels: none -> 19.7 us  [call(): pl.pallas_call(body, out_shape=shapes, in_specs=specs, out_specs=[pl.Bloc...]
    ppermute x52 -> x124, waiting for transfers between devices: 22.4 us -> 33.1 us  [the longest x104 25 us: exchange(): lax.ppermute(out, AXES, [pair for pair in move if colour(pair[0]) == side])]
    reduce_or x2 -> x0, other arithmetic: 4.99 us -> none  [membership(): return jnp.any(places == grouped[None, :, :], axis=2).astype(jnp.bfloat16)]
  transfers between devices with their start and end apart: 52 -> 124, of which waited for: 13 -> 18; matrix products, arithmetic and copies ran while one was open for 2% -> 0% of each run, Pallas kernels for 0% -> 5%
where the time goes in v1:
time: 277 us; the launch traced here: 272 us
  starting transfers between devices  212 us (77%)
  waiting for transfers between devices  33.1 us (12%)
  Pallas kernels  19.7 us (7%)
  local copies, waits for them, and re-layouts  5.15 us (2%)
    ppermute x104, starting transfers between devices, exchange(): lax.ppermute(out, AXES, [pair for pair in move if colour(pair[0]) == side])  175 us
    ppermute x20, starting transfers between devices, one_side(): lax.ppermute(value, AXES, [(a * count + b, a * count + (b ^ mask)) for a,...  37.1 us
    ppermute x104, waiting for transfers between devices, exchange(): lax.ppermute(out, AXES, [pair for pair in move if colour(pair[0]) == side])  25 us
    pallas_call x27, Pallas kernels, call(): pl.pallas_call(body, out_shape=shapes, in_specs=specs, out_specs=[pl.Bloc...  19.7 us
    ppermute x20, waiting for transfers between devices, one_side(): lax.ppermute(value, AXES, [(a * count + b, a * count + (b ^ mask)) for a,...  8.08 us
  transfers between devices with their start and end apart: 124, of which 18 were waited for; matrix products, arithmetic and copies ran while one was open for 0% of the time, Pallas kernels for 5%

profile of v1, /device:TPU:0, one launch (start us, length us, event | category | flops | bytes accessed | tf_op | source)
XLA Modules:
  0.0 272.5 jit_solution(7342758650665711268)
XLA Ops:
  9.3 5.7 %collective-permute-done.7.refs_7_ = f32[8,128]{1,0:T(8,128)S(1)} collective-permute-done((f32[8,128]{1,0:T(8,128)S(1)}, f32[8,128]{1,0:T(8,128)S(1)}, u32[]{:S(2)}, u32[]{:S(2)}) %collective-permute-start.7) | collective-permute-done | bytes 4128 | tf_op jit(solution)/shard_map/ppermute | solution.py:548
  17.6 2.9 %collective-permute-done.5.refs_5_ = f32[8,128]{1,0:T(8,128)S(1)} collective-permute-done((f32[8,128]{1,0:T(8,128)S(1)}, f32[8,128]{1,0:T(8,128)S(1)}, u32[]{:S(2)}, u32[]{:S(2)}) %collective-permute-start.5) | collective-permute-done | bytes 4128 | tf_op jit(solution)/shard_map/ppermute | solution.py:548
  24.3 2.9 %collective-permute-start.1 = (f32[8,128]{1,0:T(8,128)S(1)}, f32[8,128]{1,0:T(8,128)S(1)}, u32[]{:S(2)}, u32[]{:S(2)}) collective-permute-start(f32[8,128]{1,0:T(8,128)S(1)} %get-tuple-element.62._), channel_id=1, source_target_pairs={{0,24},{2,26},{4,28},{6,30},{9,1},{11,3},{13,5},{15,7},{16,8},{18,... | collective-permute-start | bytes 12296 | tf_op jit(solution)/shard_map/ppermute | solution.py:548
  37.6 2.9 %collective-permute-done.13.refs_5_ = f32[8,128]{1,0:T(8,128)S(1)} collective-permute-done((f32[8,128]{1,0:T(8,128)S(1)}, f32[8,128]{1,0:T(8,128)S(1)}, u32[]{:S(2)}, u32[]{:S(2)}) %collective-permute-start.13) | collective-permute-done | bytes 4128 | tf_op jit(solution)/shard_map/ppermute | solution.py:548
  40.5 4.7 %collective-permute-start.19 = (f32[136,128]{1,0:T(8,128)S(1)}, f32[136,128]{1,0:T(8,128)S(1)}, u32[]{:S(2)}, u32[]{:S(2)}) collective-permute-start(f32[136,128]{1,0:T(8,128)S(1)} %pad_maximum_fusion.refs_0_), channel_id=1, source_target_pairs={{0,7},{2,5},{4,3},{6,1},{9,14},{11,12},{13,10},{15,8},{16,23},{18,... | collective-permute-start | bytes 208904 | tf_op jit(solution)/shard_map/ppermute | solution.py:561
  51.2 3.5 %collective-permute-start.10 = (f32[8,128]{1,0:T(8,128)S(1)}, f32[8,128]{1,0:T(8,128)S(1)}, u32[]{:S(2)}, u32[]{:S(2)}) collective-permute-start(f32[8,128]{1,0:T(8,128)S(1)} %get-tuple-element.68.refs_8_._), channel_id=1, source_target_pairs={{0,1},{2,3},{4,5},{6,7},{9,10},{11,12},{13,14},{16,17},{18,19},{20... | collective-permute-start | bytes 12296 | tf_op jit(solution)/shard_map/ppermute | solution.py:548
  54.7 3.3 %collective-permute-start.9 = (f32[8,128]{1,0:T(8,128)S(1)}, f32[8,128]{1,0:T(8,128)S(1)}, u32[]{:S(2)}, u32[]{:S(2)}) collective-permute-start(f32[8,128]{1,0:T(8,128)S(1)} %get-tuple-element.68.refs_8_._), channel_id=1, source_target_pairs={{0,24},{2,26},{4,28},{6,30},{9,1},{11,3},{13,5},{15,7},{16,8},{18,... | collective-permute-start | bytes 12296 | tf_op jit(solution)/shard_map/ppermute | solution.py:548
  67.8 6.0 %collective-permute-start.40 = (f32[3,136,128]{2,1,0:T(8,128)S(1)}, f32[3,136,128]{2,1,0:T(8,128)S(1)}, u32[]{:S(2)}, u32[]{:S(2)}) collective-permute-start(f32[3,136,128]{2,1,0:T(8,128)S(1)} %get-tuple-element.72.refs_15_), channel_id=1, source_target_pairs={{0,1},{2,3},{4,5},{6,7},{9,8},{11,10},{13,12},{15,14},{16,17},{18,... | collective-permute-start | bytes 626696 | tf_op jit(solution)/shard_map/ppermute | solution.py:561
  75.2 2.5 collective-permute-start.25
  88.5 3.4 %collective-permute-done.37.refs_5_ = f32[8,128]{1,0:T(8,128)S(1)} collective-permute-done((f32[8,128]{1,0:T(8,128)S(1)}, f32[8,128]{1,0:T(8,128)S(1)}, u32[]{:S(2)}, u32[]{:S(2)}) %collective-permute-start.37) | collective-permute-done | bytes 4128 | tf_op jit(solution)/shard_map/ppermute | solution.py:548
  91.9 3.9 %collective-permute-start.34 = (f32[8,128]{1,0:T(8,128)S(1)}, f32[8,128]{1,0:T(8,128)S(1)}, u32[]{:S(2)}, u32[]{:S(2)}) collective-permute-start(f32[8,128]{1,0:T(8,128)S(1)} %get-tuple-element.78.refs_5_), channel_id=1, source_target_pairs={{0,1},{2,3},{4,5},{6,7},{9,10},{11,12},{13,14},{16,17},{18,19},{20... | collective-permute-start | bytes 12296 | tf_op jit(solution)/shard_map/ppermute | solution.py:548
  105.3 6.7 %collective-permute-start.44 = (f32[8,128]{1,0:T(8,128)S(1)}, f32[8,128]{1,0:T(8,128)S(1)}, u32[]{:S(2)}, u32[]{:S(2)}) collective-permute-start(f32[8,128]{1,0:T(8,128)S(1)} %get-tuple-element.85), channel_id=1, source_target_pairs={{0,1},{2,3},{4,5},{6,7},{9,10},{11,12},{13,14},{16,17},{18,19},{20... | collective-permute-start | bytes 12296 | tf_op jit(solution)/shard_map/ppermute | solution.py:548
  122.0 6.7 %collective-permute-start.52 = (f32[8,128]{1,0:T(8,128)S(1)}, f32[8,128]{1,0:T(8,128)S(1)}, u32[]{:S(2)}, u32[]{:S(2)}) collective-permute-start(f32[8,128]{1,0:T(8,128)S(1)} %get-tuple-element.88), channel_id=1, source_target_pairs={{0,1},{2,3},{4,5},{6,7},{9,10},{11,12},{13,14},{16,17},{18,19},{20... | collective-permute-start | bytes 12296 | tf_op jit(solution)/shard_map/ppermute | solution.py:548
  141.5 2.2 collective-permute-done.59.refs_6_
  144.2 2.2 collective-permute-start.65
  151.6 3.4 %collective-permute-start.66 = (f32[3,8,128]{2,1,0:T(8,128)S(1)}, f32[3,8,128]{2,1,0:T(8,128)S(1)}, u32[]{:S(2)}, u32[]{:S(2)}) collective-permute-start(f32[3,8,128]{2,1,0:T(8,128)S(1)} %pad_maximum_fusion.1), channel_id=1, source_target_pairs={{0,1},{2,3},{4,5},{6,7},{9,8},{11,10},{13,12},{15,14},{16,17},{18,... | collective-permute-start | bytes 36872 | tf_op jit(solution)/shard_map/ppermute | solution.py:561
  163.7 5.0 %collective-permute-start.70 = (f32[8,128]{1,0:T(8,128)S(1)}, f32[8,128]{1,0:T(8,128)S(1)}, u32[]{:S(2)}, u32[]{:S(2)}) collective-permute-start(f32[8,128]{1,0:T(8,128)S(1)} %get-tuple-element.100), channel_id=1, source_target_pairs={{0,1},{2,3},{4,5},{6,7},{9,10},{11,12},{13,14},{16,17},{18,19},{20... | collective-permute-start | bytes 12296 | tf_op jit(solution)/shard_map/ppermute | solution.py:548
  168.7 1.8 collective-permute-start.69
  178.6 6.2 %collective-permute-start.78 = (f32[8,128]{1,0:T(8,128)S(1)}, f32[8,128]{1,0:T(8,128)S(1)}, u32[]{:S(2)}, u32[]{:S(2)}) collective-permute-start(f32[8,128]{1,0:T(8,128)S(1)} %get-tuple-element.102), channel_id=1, source_target_pairs={{0,1},{2,3},{4,5},{6,7},{9,10},{11,12},{13,14},{16,17},{18,19},{20... | collective-permute-start | bytes 12296 | tf_op jit(solution)/shard_map/ppermute | solution.py:548
  194.4 6.7 %collective-permute-start.86 = (f32[8,128]{1,0:T(8,128)S(1)}, f32[8,128]{1,0:T(8,128)S(1)}, u32[]{:S(2)}, u32[]{:S(2)}) collective-permute-start(f32[8,128]{1,0:T(8,128)S(1)} %get-tuple-element.105), channel_id=1, source_target_pairs={{0,1},{2,3},{4,5},{6,7},{9,10},{11,12},{13,14},{16,17},{18,19},{20... | collective-permute-start | bytes 12296 | tf_op jit(solution)/shard_map/ppermute | solution.py:548
  210.7 6.7 %collective-permute-start.94 = (f32[8,128]{1,0:T(8,128)S(1)}, f32[8,128]{1,0:T(8,128)S(1)}, u32[]{:S(2)}, u32[]{:S(2)}) collective-permute-start(f32[8,128]{1,0:T(8,128)S(1)} %get-tuple-element.109), channel_id=1, source_target_pairs={{0,1},{2,3},{4,5},{6,7},{9,10},{11,12},{13,14},{16,17},{18,19},{20... | collective-permute-start | bytes 12296 | tf_op jit(solution)/shard_map/ppermute | solution.py:548
  227.2 6.7 %collective-permute-start.102 = (f32[8,128]{1,0:T(8,128)S(1)}, f32[8,128]{1,0:T(8,128)S(1)}, u32[]{:S(2)}, u32[]{:S(2)}) collective-permute-start(f32[8,128]{1,0:T(8,128)S(1)} %get-tuple-element.112), channel_id=1, source_target_pairs={{0,1},{2,3},{4,5},{6,7},{9,10},{11,12},{13,14},{16,17},{18,19},{20... | collective-permute-start | bytes 12296 | tf_op jit(solution)/shard_map/ppermute | solution.py:548
  243.7 6.7 %collective-permute-start.110 = (f32[8,128]{1,0:T(8,128)S(1)}, f32[8,128]{1,0:T(8,128)S(1)}, u32[]{:S(2)}, u32[]{:S(2)}) collective-permute-start(f32[8,128]{1,0:T(8,128)S(1)} %get-tuple-element.115), channel_id=1, source_target_pairs={{0,1},{2,3},{4,5},{6,7},{9,10},{11,12},{13,14},{16,17},{18,19},{20... | collective-permute-start | bytes 12296 | tf_op jit(solution)/shard_map/ppermute | solution.py:548
  260.7 6.7 %collective-permute-start.118 = (f32[8,128]{1,0:T(8,128)S(1)}, f32[8,128]{1,0:T(8,128)S(1)}, u32[]{:S(2)}, u32[]{:S(2)}) collective-permute-start(f32[8,128]{1,0:T(8,128)S(1)} %get-tuple-element.118), channel_id=1, source_target_pairs={{0,1},{2,3},{4,5},{6,7},{9,10},{11,12},{13,14},{16,17},{18,19},{20... | collective-permute-start | bytes 12296 | tf_op jit(solution)/shard_map/ppermute | solution.py:548
  (288 shorter events, 160.4 us)
Async XLA Ops:
  3.4 41.8 %collective-permute-start.23 = (f32[136,128]{1,0:T(8,128)S(1)}, f32[136,128]{1,0:T(8,128)S(1)}, u32[]{:S(2)}, u32[]{:S(2)}) collective-permute-start(f32[136,128]{1,0:T(8,128)S(1)} %pad_maximum_fusion.refs_0_), channel_id=1, source_target_pairs={{1,6},{3,4},{5,2},{7,0},{8,15},{10,13},{12,11},{14,9},{17,22},{19,... | collective-permute-start | bytes 208904 | tf_op jit(solution)/shard_map/ppermute | solution.py:561
  4.7 41.8 %collective-permute-start.22 = (f32[136,128]{1,0:T(8,128)S(1)}, f32[136,128]{1,0:T(8,128)S(1)}, u32[]{:S(2)}, u32[]{:S(2)}) collective-permute-start(f32[136,128]{1,0:T(8,128)S(1)} %pad_maximum_fusion.refs_0_), channel_id=1, source_target_pairs={{1,4},{3,6},{5,0},{7,2},{8,13},{10,15},{12,9},{14,11},{17,20},{19,... | collective-permute-start | bytes 208904 | tf_op jit(solution)/shard_map/ppermute | solution.py:561
  6.0 41.9 %collective-permute-start.21 = (f32[136,128]{1,0:T(8,128)S(1)}, f32[136,128]{1,0:T(8,128)S(1)}, u32[]{:S(2)}, u32[]{:S(2)}) collective-permute-start(f32[136,128]{1,0:T(8,128)S(1)} %pad_maximum_fusion.refs_0_), channel_id=1, source_target_pairs={{1,2},{3,0},{5,6},{7,4},{8,11},{10,9},{12,15},{14,13},{17,18},{19,... | collective-permute-start | bytes 208904 | tf_op jit(solution)/shard_map/ppermute | solution.py:561
  36.3 12.9 %collective-permute-start.20 = (f32[136,128]{1,0:T(8,128)S(1)}, f32[136,128]{1,0:T(8,128)S(1)}, u32[]{:S(2)}, u32[]{:S(2)}) collective-permute-start(f32[136,128]{1,0:T(8,128)S(1)} %pad_maximum_fusion.refs_0_), channel_id=1, source_target_pairs={{1,0},{3,2},{5,4},{7,6},{8,9},{10,11},{12,13},{14,15},{17,16},{19,... | collective-permute-start | bytes 208904 | tf_op jit(solution)/shard_map/ppermute | solution.py:561
  49.2 11.6 %collective-permute-start.12 = (f32[8,128]{1,0:T(8,128)S(1)}, f32[8,128]{1,0:T(8,128)S(1)}, u32[]{:S(2)}, u32[]{:S(2)}) collective-permute-start(f32[8,128]{1,0:T(8,128)S(1)} %get-tuple-element.68.refs_8_._), channel_id=1, source_target_pairs={{1,9},{3,11},{5,13},{7,15},{8,16},{10,18},{12,20},{14,22},{17,25},... | collective-permute-start | bytes 12296 | tf_op jit(solution)/shard_map/ppermute | solution.py:548
  65.8 11.8 %collective-permute-start.27 = (f32[8,128]{1,0:T(8,128)S(1)}, f32[8,128]{1,0:T(8,128)S(1)}, u32[]{:S(2)}, u32[]{:S(2)}) collective-permute-start(f32[8,128]{1,0:T(8,128)S(1)} %get-tuple-element.73._), channel_id=1, source_target_pairs={{2,1},{4,3},{6,5},{9,8},{11,10},{13,12},{15,14},{18,17},{20,19},{2... | collective-permute-start | bytes 12296 | tf_op jit(solution)/shard_map/ppermute | solution.py:548
  66.5 29.3 %collective-permute-start.41 = (f32[3,136,128]{2,1,0:T(8,128)S(1)}, f32[3,136,128]{2,1,0:T(8,128)S(1)}, u32[]{:S(2)}, u32[]{:S(2)}) collective-permute-start(f32[3,136,128]{2,1,0:T(8,128)S(1)} %get-tuple-element.72.refs_15_), channel_id=1, source_target_pairs={{1,0},{3,2},{5,4},{7,6},{8,9},{10,11},{12,13},{14,15},{17,16},{19,... | collective-permute-start | bytes 626696 | tf_op jit(solution)/shard_map/ppermute | solution.py:561
  67.8 29.3 %collective-permute-start.40 = (f32[3,136,128]{2,1,0:T(8,128)S(1)}, f32[3,136,128]{2,1,0:T(8,128)S(1)}, u32[]{:S(2)}, u32[]{:S(2)}) collective-permute-start(f32[3,136,128]{2,1,0:T(8,128)S(1)} %get-tuple-element.72.refs_15_), channel_id=1, source_target_pairs={{0,1},{2,3},{4,5},{6,7},{9,8},{11,10},{13,12},{15,14},{16,17},{18,... | collective-permute-start | bytes 626696 | tf_op jit(solution)/shard_map/ppermute | solution.py:561
  86.5 12.3 %collective-permute-start.36 = (f32[8,128]{1,0:T(8,128)S(1)}, f32[8,128]{1,0:T(8,128)S(1)}, u32[]{:S(2)}, u32[]{:S(2)}) collective-permute-start(f32[8,128]{1,0:T(8,128)S(1)} %get-tuple-element.78.refs_5_), channel_id=1, source_target_pairs={{1,9},{3,11},{5,13},{7,15},{8,16},{10,18},{12,20},{14,22},{17,25},... | collective-permute-start | bytes 12296 | tf_op jit(solution)/shard_map/ppermute | solution.py:548
  102.0 11.3 %collective-permute-start.47 = (f32[8,128]{1,0:T(8,128)S(1)}, f32[8,128]{1,0:T(8,128)S(1)}, u32[]{:S(2)}, u32[]{:S(2)}) collective-permute-start(f32[8,128]{1,0:T(8,128)S(1)} %get-tuple-element.85), channel_id=1, source_target_pairs={{1,25},{3,27},{5,29},{7,31},{8,0},{10,2},{12,4},{14,6},{17,9},{19,... | collective-permute-start | bytes 12296 | tf_op jit(solution)/shard_map/ppermute | solution.py:548
  103.3 11.3 %collective-permute-start.46 = (f32[8,128]{1,0:T(8,128)S(1)}, f32[8,128]{1,0:T(8,128)S(1)}, u32[]{:S(2)}, u32[]{:S(2)}) collective-permute-start(f32[8,128]{1,0:T(8,128)S(1)} %get-tuple-element.85), channel_id=1, source_target_pairs={{1,9},{3,11},{5,13},{7,15},{8,16},{10,18},{12,20},{14,22},{17,25},... | collective-permute-start | bytes 12296 | tf_op jit(solution)/shard_map/ppermute | solution.py:548
  118.7 11.3 %collective-permute-start.55 = (f32[8,128]{1,0:T(8,128)S(1)}, f32[8,128]{1,0:T(8,128)S(1)}, u32[]{:S(2)}, u32[]{:S(2)}) collective-permute-start(f32[8,128]{1,0:T(8,128)S(1)} %get-tuple-element.88), channel_id=1, source_target_pairs={{1,25},{3,27},{5,29},{7,31},{8,0},{10,2},{12,4},{14,6},{17,9},{19,... | collective-permute-start | bytes 12296 | tf_op jit(solution)/shard_map/ppermute | solution.py:548
  120.0 11.3 %collective-permute-start.54 = (f32[8,128]{1,0:T(8,128)S(1)}, f32[8,128]{1,0:T(8,128)S(1)}, u32[]{:S(2)}, u32[]{:S(2)}) collective-permute-start(f32[8,128]{1,0:T(8,128)S(1)} %get-tuple-element.88), channel_id=1, source_target_pairs={{1,9},{3,11},{5,13},{7,15},{8,16},{10,18},{12,20},{14,22},{17,25},... | collective-permute-start | bytes 12296 | tf_op jit(solution)/shard_map/ppermute | solution.py:548
  191.1 11.3 %collective-permute-start.89 = (f32[8,128]{1,0:T(8,128)S(1)}, f32[8,128]{1,0:T(8,128)S(1)}, u32[]{:S(2)}, u32[]{:S(2)}) collective-permute-start(f32[8,128]{1,0:T(8,128)S(1)} %get-tuple-element.105), channel_id=1, source_target_pairs={{1,25},{3,27},{5,29},{7,31},{8,0},{10,2},{12,4},{14,6},{17,9},{19,... | collective-permute-start | bytes 12296 | tf_op jit(solution)/shard_map/ppermute | solution.py:548
  192.4 11.3 %collective-permute-start.88 = (f32[8,128]{1,0:T(8,128)S(1)}, f32[8,128]{1,0:T(8,128)S(1)}, u32[]{:S(2)}, u32[]{:S(2)}) collective-permute-start(f32[8,128]{1,0:T(8,128)S(1)} %get-tuple-element.105), channel_id=1, source_target_pairs={{1,9},{3,11},{5,13},{7,15},{8,16},{10,18},{12,20},{14,22},{17,25},... | collective-permute-start | bytes 12296 | tf_op jit(solution)/shard_map/ppermute | solution.py:548
  207.4 11.3 %collective-permute-start.97 = (f32[8,128]{1,0:T(8,128)S(1)}, f32[8,128]{1,0:T(8,128)S(1)}, u32[]{:S(2)}, u32[]{:S(2)}) collective-permute-start(f32[8,128]{1,0:T(8,128)S(1)} %get-tuple-element.109), channel_id=1, source_target_pairs={{1,25},{3,27},{5,29},{7,31},{8,0},{10,2},{12,4},{14,6},{17,9},{19,... | collective-permute-start | bytes 12296 | tf_op jit(solution)/shard_map/ppermute | solution.py:548
  208.7 12.8 %collective-permute-start.96 = (f32[8,128]{1,0:T(8,128)S(1)}, f32[8,128]{1,0:T(8,128)S(1)}, u32[]{:S(2)}, u32[]{:S(2)}) collective-permute-start(f32[8,128]{1,0:T(8,128)S(1)} %get-tuple-element.109), channel_id=1, source_target_pairs={{1,9},{3,11},{5,13},{7,15},{8,16},{10,18},{12,20},{14,22},{17,25},... | collective-permute-start | bytes 12296 | tf_op jit(solution)/shard_map/ppermute | solution.py:548
  210.0 11.5 %collective-permute-start.95 = (f32[8,128]{1,0:T(8,128)S(1)}, f32[8,128]{1,0:T(8,128)S(1)}, u32[]{:S(2)}, u32[]{:S(2)}) collective-permute-start(f32[8,128]{1,0:T(8,128)S(1)} %get-tuple-element.109), channel_id=1, source_target_pairs={{2,1},{4,3},{6,5},{9,8},{11,10},{13,12},{15,14},{18,17},{20,19},{2... | collective-permute-start | bytes 12296 | tf_op jit(solution)/shard_map/ppermute | solution.py:548
  225.2 12.8 %collective-permute-start.104 = (f32[8,128]{1,0:T(8,128)S(1)}, f32[8,128]{1,0:T(8,128)S(1)}, u32[]{:S(2)}, u32[]{:S(2)}) collective-permute-start(f32[8,128]{1,0:T(8,128)S(1)} %get-tuple-element.112), channel_id=1, source_target_pairs={{1,9},{3,11},{5,13},{7,15},{8,16},{10,18},{12,20},{14,22},{17,25},... | collective-permute-start | bytes 12296 | tf_op jit(solution)/shard_map/ppermute | solution.py:548
  226.5 11.5 %collective-permute-start.103 = (f32[8,128]{1,0:T(8,128)S(1)}, f32[8,128]{1,0:T(8,128)S(1)}, u32[]{:S(2)}, u32[]{:S(2)}) collective-permute-start(f32[8,128]{1,0:T(8,128)S(1)} %get-tuple-element.112), channel_id=1, source_target_pairs={{2,1},{4,3},{6,5},{9,8},{11,10},{13,12},{15,14},{18,17},{20,19},{2... | collective-permute-start | bytes 12296 | tf_op jit(solution)/shard_map/ppermute | solution.py:548
  241.7 12.8 %collective-permute-start.112 = (f32[8,128]{1,0:T(8,128)S(1)}, f32[8,128]{1,0:T(8,128)S(1)}, u32[]{:S(2)}, u32[]{:S(2)}) collective-permute-start(f32[8,128]{1,0:T(8,128)S(1)} %get-tuple-element.115), channel_id=1, source_target_pairs={{1,9},{3,11},{5,13},{7,15},{8,16},{10,18},{12,20},{14,22},{17,25},... | collective-permute-start | bytes 12296 | tf_op jit(solution)/shard_map/ppermute | solution.py:548
  243.0 11.5 %collective-permute-start.111 = (f32[8,128]{1,0:T(8,128)S(1)}, f32[8,128]{1,0:T(8,128)S(1)}, u32[]{:S(2)}, u32[]{:S(2)}) collective-permute-start(f32[8,128]{1,0:T(8,128)S(1)} %get-tuple-element.115), channel_id=1, source_target_pairs={{2,1},{4,3},{6,5},{9,8},{11,10},{13,12},{15,14},{18,17},{20,19},{2... | collective-permute-start | bytes 12296 | tf_op jit(solution)/shard_map/ppermute | solution.py:548
  258.7 12.8 %collective-permute-start.120 = (f32[8,128]{1,0:T(8,128)S(1)}, f32[8,128]{1,0:T(8,128)S(1)}, u32[]{:S(2)}, u32[]{:S(2)}) collective-permute-start(f32[8,128]{1,0:T(8,128)S(1)} %get-tuple-element.118), channel_id=1, source_target_pairs={{1,9},{3,11},{5,13},{7,15},{8,16},{10,18},{12,20},{14,22},{17,25},... | collective-permute-start | bytes 12296 | tf_op jit(solution)/shard_map/ppermute | solution.py:548
  260.0 11.5 %collective-permute-start.119 = (f32[8,128]{1,0:T(8,128)S(1)}, f32[8,128]{1,0:T(8,128)S(1)}, u32[]{:S(2)}, u32[]{:S(2)}) collective-permute-start(f32[8,128]{1,0:T(8,128)S(1)} %get-tuple-element.118), channel_id=1, source_target_pairs={{2,1},{4,3},{6,5},{9,8},{11,10},{13,12},{15,14},{18,17},{20,19},{2... | collective-permute-start | bytes 12296 | tf_op jit(solution)/shard_map/ppermute | solution.py:548
  (112 other events, 740.2 us)

commit v2 on v1

--- a/solution.py
+++ b/solution.py
@@ -49,13 +49,13 @@
 
 
 def halo_lines(arrivals, edge_ref):
-    values = [r[...] for r in arrivals]
-    prev_s, next_s, prev_p, next_p = [values[d] + values[4 + d] for d in range(4)]
+    prev_s, next_s, prev_p, next_p, inside = [r[...] for r in arrivals]
     left = tile_iota(1) < LANES // 2
     upper = tile_iota(0) < 4
-    edge_ref[...] = jnp.where(
+    values = jnp.where(
         upper, jnp.where(left, prev_s, next_s), jnp.where(left, prev_p, next_p)
     )
+    edge_ref[...] = jnp.where(inside > 0.0, values, 0.0)
 
 
 def outgoing(lines_of, count, sends):
@@ -162,8 +162,8 @@
 
 
 def fine_step(factors, *refs):
-    arrivals = refs[:8]
-    (r_ref, v_ref, c_ref, m_ref, x_ref, d_ref, s_ref, xo_ref, do_ref, out_ref, edge_ref, pad_ref) = refs[8:]
+    arrivals = refs[:5]
+    (r_ref, v_ref, c_ref, m_ref, x_ref, d_ref, s_ref, xo_ref, do_ref, out_ref, edge_ref, pad_ref) = refs[5:]
     keep, gain = factors
     lines = r_ref.shape[1]
     resid = fine_remote(arrivals, r_ref, v_ref, c_ref, edge_ref)
@@ -184,8 +184,8 @@
 
 
 def fine_finish(*refs):
-    arrivals = refs[:8]
-    r_ref, v_ref, c_ref, x_ref, so_ref, ro_ref, edge_ref = refs[8:]
+    arrivals = refs[:5]
+    r_ref, v_ref, c_ref, x_ref, so_ref, ro_ref, edge_ref = refs[5:]
     lines = r_ref.shape[1]
     resid = fine_remote(arrivals, r_ref, v_ref, c_ref, edge_ref)
     for h in range(lines // SUBS):
@@ -196,8 +196,8 @@
 
 
 def fine_restrict(*refs):
-    arrivals = refs[:8]
-    (r_ref, v_ref, c_ref, w_ref, p_ref, m2_ref, s2_ref, b2_ref, x2_ref, out_ref, edge_ref, line_ref, pad_ref) = refs[8:]
+    arrivals = refs[:5]
+    (r_ref, v_ref, c_ref, w_ref, p_ref, m2_ref, s2_ref, b2_ref, x2_ref, out_ref, edge_ref, line_ref, pad_ref) = refs[5:]
     lines = r_ref.shape[1]
     resid = fine_remote(arrivals, r_ref, v_ref, c_ref, edge_ref)
     for h in range(lines // SUBS):
@@ -332,8 +332,8 @@
 
 
 def middle_step(factors, *refs):
-    arrivals = refs[:8]
-    (b_ref, m_ref, x_ref, d_ref, v_ref, c_ref, s_ref, xo_ref, do_ref, out_ref, edge_ref, pad_ref) = refs[8:]
+    arrivals = refs[:5]
+    (b_ref, m_ref, x_ref, d_ref, v_ref, c_ref, s_ref, xo_ref, do_ref, out_ref, edge_ref, pad_ref) = refs[5:]
     resid = middle_residual(arrivals, b_ref, x_ref, v_ref, c_ref, edge_ref)
     xs, ds = middle_update(factors, resid, m_ref, x_ref, d_ref)
     for i in range(4):
@@ -344,8 +344,8 @@
 
 
 def middle_restrict(*refs):
-    arrivals = refs[:8]
-    b_ref, x_ref, v_ref, c_ref, w_ref, p_ref, out_ref, edge_ref, line_ref = refs[8:]
+    arrivals = refs[:5]
+    b_ref, x_ref, v_ref, c_ref, w_ref, p_ref, out_ref, edge_ref, line_ref = refs[5:]
     resid = middle_residual(arrivals, b_ref, x_ref, v_ref, c_ref, edge_ref)
     place = p_ref[...]
     high, lane = place >> 7, place & (LANES - 1)
@@ -363,8 +363,8 @@
 
 
 def middle_prolong(factors, *refs):
-    arrivals = refs[:8]
-    (b_ref, m_ref, x_ref, d_ref, v_ref, c_ref, x1_ref, w_ref, agg_ref, s_ref, xo_ref, out_ref, edge_ref, line_ref, pad_ref) = refs[8:]
+    arrivals = refs[:5]
+    (b_ref, m_ref, x_ref, d_ref, v_ref, c_ref, x1_ref, w_ref, agg_ref, s_ref, xo_ref, out_ref, edge_ref, line_ref, pad_ref) = refs[5:]
     lines = x1_ref.shape[1]
     resid = middle_residual(arrivals, b_ref, x_ref, v_ref, c_ref, edge_ref)
     xs, _ = middle_update(factors, resid, m_ref, x_ref, d_ref)
@@ -391,25 +391,14 @@
     )
 
 
-def coarse_half(half, *refs):
-    for t in range(half):
-        refs[2 * half + 1][t] = refs[t][...] + refs[half + t][...]
-    for t in range(1, half):
-        refs[2 * half + 2][t - 1] = refs[t][...] + refs[half + t][...]
-
-
 def coarse_tables(group, *refs):
-    half = group // 2
-    own_ref, me_ref = refs[0], refs[1]
-    odd = refs[2]
-    even = refs[3:5]
-    vo_ref, co_ref, mo_ref, pad_ref = refs[6:]
-    pad_ref[0] = own_ref[...]
-    for t in range(half):
-        pad_ref[2 * t + 1] = odd[t]
-    for t in range(half - 1):
-        pad_ref[2 * t + 2] = even[0][t] + even[1][t]
-    me = me_ref[0]
+    vo_ref, co_ref, mo_ref, pad_ref = refs[-4:]
+    me = refs[0][0]
+    place = 0
+    for piece in refs[1:-5]:
+        for t in range(piece.shape[0]):
+            pad_ref[place] = piece[t]
+            place += 1
     for h in range(group // SUBS):
         rows = pl.ds(h * SUBS, SUBS)
         for ki in range(NNZ * 4):
@@ -421,25 +410,19 @@
                     mo_ref[i, rows, :] = 1.0 / tile
         for k in range(NNZ):
             col = pad_ref[rows, NNZ * 16 + k, :].astype(I32)
-            co_ref[k, rows, :] = ((col >> 7) ^ me) * LANES + (col & (LANES - 1))
+            back = me - (col >> 7)
+            back = jnp.where(back < 0, back + group, back)
+            co_ref[k, rows, :] = back * LANES + (col & (LANES - 1))
 
 
 def coarse_solve(group, *refs):
-    half = group // 2
-    own_ref = refs[0]
-    odd = refs[1 : 1 + 2 * half]
-    even = refs[1 + 2 * half : 3 + 2 * half]
-    (v_ref, c_ref, m_ref, x2_ref, w_ref, agg_ref, s_ref, xo_ref, out_ref, b_ref, x_ref, d_ref, tmp_ref, pad_ref) = refs[3 + 2 * half :]
-    for j in range(4):
-        b_ref[j, pl.ds(0, 1), :] = own_ref[pl.ds(j, 1), :]
-    for t in range(half):
-        tmp_ref[...] = odd[t][...] + odd[half + t][...]
-        for j in range(4):
-            b_ref[j, pl.ds(2 * t + 1, 1), :] = tmp_ref[pl.ds(j, 1), :]
-    for t in range(half - 1):
-        tmp_ref[...] = even[0][t] + even[1][t]
-        for j in range(4):
-            b_ref[j, pl.ds(2 * t + 2, 1), :] = tmp_ref[pl.ds(j, 1), :]
+    (v_ref, c_ref, m_ref, x2_ref, w_ref, agg_ref, s_ref, xo_ref, out_ref, b_ref, x_ref, d_ref, pad_ref) = refs[-13:]
+    place = 0
+    for piece in refs[:-13]:
+        for t in range(piece.shape[0]):
+            for j in range(4):
+                b_ref[j, pl.ds(place, 1), :] = piece[t, pl.ds(j, 1), :]
+            place += 1
     blocks = group // SUBS
     for j in range(4):
         first = m_ref[j] * b_ref[j]
@@ -526,62 +509,31 @@
     return jnp.concatenate([stream] * 4 + [span] * 4, axis=0)
 
 
-def colour_of(mesh):
+def exchange(mesh, out, inside):
     count = mesh.shape["span"]
-    return lambda p: (p // count + p % count) % 2
-
-
-def exchange(mesh, out):
+    total = mesh.shape["stream"] * count
+    moved = [
+        lax.ppermute(out, AXES, [(p, (p + shift) % total) for p in range(total)])
+        for shift in (count, -count, 1, -1)
+    ]
+    return moved + [inside]
+
+
+def span_shift(mesh, value, shift):
     slabs, count = mesh.shape["stream"], mesh.shape["span"]
-    colour = colour_of(mesh)
-    places = [(a, b) for a in range(slabs) for b in range(count)]
-    moves = []
-    for da, db in ((1, 0), (-1, 0), (0, 1), (0, -1)):
-        moves.append(
-            [
-                (a * count + b, (a + da) % slabs * count + b + db)
-                for a, b in places
-                if 0 <= b + db < count
-            ]
-        )
-    return [
-        lax.ppermute(out, AXES, [pair for pair in move if colour(pair[0]) == side])
-        for side in range(2)
-        for move in moves
+    pairs = [
+        (a * count + b, a * count + (b + shift) % count)
+        for a in range(slabs)
+        for b in range(count)
     ]
-
-
-def span_swaps(mesh, value, masks, in_turn=False):
-    slabs, count = mesh.shape["stream"], mesh.shape["span"]
-    colour = colour_of(mesh)
-    places = [(a, b) for a in range(slabs) for b in range(count)]
-
-    def one_side(value, side):
-        return [
-            lax.ppermute(
-                value,
-                AXES,
-                [
-                    (a * count + b, a * count + (b ^ mask))
-                    for a, b in places
-                    if colour(a * count + b) == side
-                ],
-            )
-            for mask in masks
-        ]
-
-    first = one_side(value, 1)
-    if in_turn:
-        value, first = lax.optimization_barrier((value, first))
-    return one_side(value, 0) + first
-
-
-def span_gather(mesh, value):
-    half = mesh.shape["span"] // 2
-    odd = span_swaps(mesh, value, range(1, 2 * half, 2), True)
-    held = jnp.stack([odd[t] + odd[half + t] for t in range(1, half)])
-    even = span_swaps(mesh, held, (1,))
-    return odd, even
+    return lax.ppermute(value, AXES, pairs)
+
+
+def span_stage(mesh, pieces):
+    group = mesh.shape["span"]
+    have = sum(piece.shape[0] for piece in pieces)
+    held = jnp.concatenate(pieces)[: min(have, group - have)]
+    return pieces + [span_shift(mesh, held, have)]
 
 
 def per_device(mesh, right_side, fine_values, fine_columns, fine_sends, fine_order, fine_weights, middle_values, middle_columns, middle_sends, middle_order, middle_weights, coarsest_values, coarsest_columns):
@@ -594,6 +546,10 @@
     pad1 = vmem(SUBS * lines, LANES)
     pad2 = vmem(SUBS * SUBS, LANES)
     factors = cheb_factors(KSM)
+    me = lax.axis_index("span").astype(I32)
+    row, lane = (lax.broadcasted_iota(I32, (SUBS, LANES), d) for d in range(2))
+    outside = (row >= 4) & jnp.where(lane < LANES // 2, me == 0, me == group - 1)
+    inside = jnp.where(outside, 0.0, 1.0).astype(F32)
     send1, send2 = send_table(fine_sends), send_table(middle_sends)
     values1 = native_rows(fine_values)
     values2 = native_rows(middle_values)
@@ -629,21 +585,15 @@
             free=range(len(args), len(args) + len(after)),
         )
 
-    arrived = exchange(mesh, out)
+    arrived = exchange(mesh, out, inside)
     own3, _ = lax.optimization_barrier((own3, out))
-    swapped3 = span_swaps(mesh, own3, range(1, group, 2))
+    pieces3 = span_stage(mesh, [own3[None]])
     resid = fine_part(x1)
     x1, d1, out = fine_next(1, arrived, resid, x1, d1)
 
-    arrived = exchange(mesh, out)
-    half = group // 2
-    odd3, held3 = call(
-        lambda *refs: coarse_half(half, *refs),
-        [shape(half, NNZ * 17, LANES), shape(half - 1, NNZ * 17, LANES)],
-        swapped3 + [out],
-        free=(group,),
-    )
-    even3 = span_swaps(mesh, held3, (1,))
+    arrived = exchange(mesh, out, inside)
+    pieces3, _ = lax.optimization_barrier((pieces3, out))
+    pieces3 = span_stage(mesh, pieces3)
     resid = fine_part(x1)
     w1, agg1, place1 = call(
         fine_tables,
@@ -651,9 +601,12 @@
         [native_rows(fine_weights), fine_order, fine_order.reshape(lines, LANES), out],
         free=(3,),
     )
-    x1, d1, out = fine_next(2, arrived, resid, x1, d1, [held3])
-
-    arrived = exchange(mesh, out)
+    x1, d1, out = fine_next(2, arrived, resid, x1, d1, [pieces3[1]])
+
+    arrived = exchange(mesh, out, inside)
+    pieces3, _ = lax.optimization_barrier((pieces3, out))
+    while sum(piece.shape[0] for piece in pieces3) < group:
+        pieces3 = span_stage(mesh, pieces3)
     resid = fine_part(x1)
     v2, c2, m2, w2, agg2, place2 = call(
         middle_tables,
@@ -686,39 +639,40 @@
             free=range(len(args), len(args) + len(after)),
         )
 
-    arrived = exchange(mesh, out)
-    me = lax.axis_index("span").astype(I32).reshape(1)
+    arrived = exchange(mesh, out, inside)
     v3, c3, m3 = call(
         lambda *refs: coarse_tables(group, *refs),
         [shape(NNZ, 4, 4, group, LANES), shape(NNZ, group, LANES, dtype=I32), shape(4, group, LANES)],
-        [own3, me, odd3] + even3 + [out],
+        [me.reshape(1)] + pieces3 + [out],
         [vmem(group, NNZ * 17, LANES)],
-        free=(5,),
-        smem=(1,),
+        free=(1 + len(pieces3),),
+        smem=(0,),
     )
     x2, d2, out = middle_next(1, arrived, x2, d2, [m3])
-    arrived = exchange(mesh, out)
+    arrived = exchange(mesh, out, inside)
     x2, d2, out = middle_next(2, arrived, x2, d2)
-    arrived = exchange(mesh, out)
+    arrived = exchange(mesh, out, inside)
     rhs3 = call(
         middle_restrict,
         tile,
         arrived + [b2, x2, v2, c2, w2, place2],
         [edge, vmem(4, SUBS, LANES)],
     )
-    odd, even = span_gather(mesh, rhs3)
+    pieces = [rhs3[None]]
+    while sum(piece.shape[0] for piece in pieces) < group:
+        pieces = span_stage(mesh, pieces)
     vec3 = vmem(4, group, LANES)
     x2, out = call(
         lambda *refs: coarse_solve(group, *refs),
         [vec2, tile],
-        [rhs3] + odd + even + [v3, c3, m3, x2, w2, agg2, send2],
-        [vec3, vec3, vec3, edge, pad2],
-    )
-    arrived = exchange(mesh, out)
+        pieces + [v3, c3, m3, x2, w2, agg2, send2],
+        [vec3, vec3, vec3, pad2],
+    )
+    arrived = exchange(mesh, out, inside)
     x2, d2, out = middle_next(0, arrived, x2, x2)
-    arrived = exchange(mesh, out)
+    arrived = exchange(mesh, out, inside)
     x2, d2, out = middle_next(1, arrived, x2, d2)
-    arrived = exchange(mesh, out)
+    arrived = exchange(mesh, out, inside)
     x1, out = call(
         lambda *refs: middle_prolong(factors[2], *refs),
         [vec1, tile],
@@ -726,10 +680,10 @@
         [edge, vmem(4, SUBS, LANES), pad1],
     )
     for which in range(KSM):
-        arrived = exchange(mesh, out)
+        arrived = exchange(mesh, out, inside)
         resid = fine_part(x1)
         x1, d1, out = fine_next(which, arrived, resid, x1, d1)
-    arrived = exchange(mesh, out)
+    arrived = exchange(mesh, out, inside)
     resid = fine_part(x1)
     rows = shape(4 * lines, LANES)
     solved, left = call(fine_finish, [rows, rows], arrived + [resid, v1, c1, x1], [edge])

time: 277 us -> 158 us (0.57); the launches traced: 272 us -> 158 us
  starting transfers between devices: 212 us -> 107 us
  waiting for transfers between devices: 33.1 us -> 23.8 us
    ppermute x124 -> x58, starting transfers between devices: 212 us -> 107 us  [the longest x52 107 us: exchange(): lax.ppermute(out, AXES, [(p, (p + shift) % total) for p in range(total)])]
    ppermute x124 -> x58, waiting for transfers between devices: 33.1 us -> 23.8 us  [the longest x6 16.2 us: span_shift(): return lax.ppermute(value, AXES, pairs)]
    pallas_call x27 -> x26, Pallas kernels: 19.7 us -> 19.6 us  [call(): pl.pallas_call(body, out_shape=shapes, in_specs=specs, out_specs=[pl.Bloc...]
  transfers between devices with their start and end apart: 124 -> 58, of which waited for: 18 -> 10; matrix products, arithmetic and copies ran while one was open for 0% -> 0% of each run, Pallas kernels for 5% -> 8%
where the time goes in v2:
time: 158 us
  starting transfers between devices  107 us (68%)
  waiting for transfers between devices  23.8 us (15%)
  Pallas kernels  19.6 us (12%)
  local copies, waits for them, and re-layouts  5.59 us (4%)
    ppermute x52, starting transfers between devices, exchange(): lax.ppermute(out, AXES, [(p, (p + shift) % total) for p in range(total)])  107 us
    pallas_call x26, Pallas kernels, call(): pl.pallas_call(body, out_shape=shapes, in_specs=specs, out_specs=[pl.Bloc...  19.6 us
    ppermute x6, waiting for transfers between devices, span_shift(): return lax.ppermute(value, AXES, pairs)  16.2 us
    ppermute x52, waiting for transfers between devices, exchange(): lax.ppermute(out, AXES, [(p, (p + shift) % total) for p in range(total)])  7.6 us
    unnamed x24, local copies, waits for them, and re-layouts  3.78 us
  transfers between devices with their start and end apart: 58, of which 10 were waited for; matrix products, arithmetic and copies ran while one was open for 0% of the time, Pallas kernels for 8%

profile of v2, /device:TPU:0, one launch (start us, length us, event | category | flops | bytes accessed | tf_op | source)
XLA Modules:
  0.0 157.9 jit_solution(6229024549743002684)
XLA Ops:
  2.6 3.0 %collective-permute-start = (f32[8,128]{1,0:T(8,128)S(1)}, f32[8,128]{1,0:T(8,128)S(1)}, u32[]{:S(2)}, u32[]{:S(2)}) collective-permute-start(f32[8,128]{1,0:T(8,128)S(1)} %get-tuple-element.60._), channel_id=1, source_target_pairs={{0,8},{1,9},{2,10},{3,11},{4,12},{5,13},{6,14},{7,15},{8,16},{9,17... | collective-permute-start | bytes 12296 | tf_op jit(solution)/shard_map/ppermute | solution.py:516
  6.7 5.3 %collective-permute-start.3 = (f32[8,128]{1,0:T(8,128)S(1)}, f32[8,128]{1,0:T(8,128)S(1)}, u32[]{:S(2)}, u32[]{:S(2)}) collective-permute-start(f32[8,128]{1,0:T(8,128)S(1)} %get-tuple-element.60._), channel_id=1, source_target_pairs={{0,31},{1,0},{2,1},{3,2},{4,3},{5,4},{6,5},{7,6},{8,7},{9,8},{10,9... | collective-permute-start | bytes 12296 | tf_op jit(solution)/shard_map/ppermute | solution.py:516
  17.8 2.8 %collective-permute-start.5 = (f32[8,128]{1,0:T(8,128)S(1)}, f32[8,128]{1,0:T(8,128)S(1)}, u32[]{:S(2)}, u32[]{:S(2)}) collective-permute-start(f32[8,128]{1,0:T(8,128)S(1)} %get-tuple-element.66._), channel_id=1, source_target_pairs={{0,24},{1,25},{2,26},{3,27},{4,28},{5,29},{6,30},{7,31},{8,0},{9,1... | collective-permute-start | bytes 12296 | tf_op jit(solution)/shard_map/ppermute | solution.py:516
  20.7 5.3 %collective-permute-start.7 = (f32[8,128]{1,0:T(8,128)S(1)}, f32[8,128]{1,0:T(8,128)S(1)}, u32[]{:S(2)}, u32[]{:S(2)}) collective-permute-start(f32[8,128]{1,0:T(8,128)S(1)} %get-tuple-element.66._), channel_id=1, source_target_pairs={{0,31},{1,0},{2,1},{3,2},{4,3},{5,4},{6,5},{7,6},{8,7},{9,8},{10,9... | collective-permute-start | bytes 12296 | tf_op jit(solution)/shard_map/ppermute | solution.py:516
  28.6 5.3 %collective-permute-start.12 = (f32[8,128]{1,0:T(8,128)S(1)}, f32[8,128]{1,0:T(8,128)S(1)}, u32[]{:S(2)}, u32[]{:S(2)}) collective-permute-start(f32[8,128]{1,0:T(8,128)S(1)} %get-tuple-element.71._), channel_id=1, source_target_pairs={{0,31},{1,0},{2,1},{3,2},{4,3},{5,4},{6,5},{7,6},{8,7},{9,8},{10,9... | collective-permute-start | bytes 12296 | tf_op jit(solution)/shard_map/ppermute | solution.py:516
  42.6 5.3 %collective-permute-start.16 = (f32[8,128]{1,0:T(8,128)S(1)}, f32[8,128]{1,0:T(8,128)S(1)}, u32[]{:S(2)}, u32[]{:S(2)}) collective-permute-start(f32[8,128]{1,0:T(8,128)S(1)} %get-tuple-element.76.refs_5_), channel_id=1, source_target_pairs={{0,31},{1,0},{2,1},{3,2},{4,3},{5,4},{6,5},{7,6},{8,7},{9,8},{10,9... | collective-permute-start | bytes 12296 | tf_op jit(solution)/shard_map/ppermute | solution.py:516
  52.6 5.3 %collective-permute-start.22 = (f32[8,128]{1,0:T(8,128)S(1)}, f32[8,128]{1,0:T(8,128)S(1)}, u32[]{:S(2)}, u32[]{:S(2)}) collective-permute-start(f32[8,128]{1,0:T(8,128)S(1)} %get-tuple-element.86), channel_id=1, source_target_pairs={{0,31},{1,0},{2,1},{3,2},{4,3},{5,4},{6,5},{7,6},{8,7},{9,8},{10,9... | collective-permute-start | bytes 12296 | tf_op jit(solution)/shard_map/ppermute | solution.py:516
  60.1 2.9 %collective-permute-start.24 = (f32[8,128]{1,0:T(8,128)S(1)}, f32[8,128]{1,0:T(8,128)S(1)}, u32[]{:S(2)}, u32[]{:S(2)}) collective-permute-start(f32[8,128]{1,0:T(8,128)S(1)} %get-tuple-element.89), channel_id=1, source_target_pairs={{0,24},{1,25},{2,26},{3,27},{4,28},{5,29},{6,30},{7,31},{8,0},{9,1... | collective-permute-start | bytes 12296 | tf_op jit(solution)/shard_map/ppermute | solution.py:516
  63.0 5.3 %collective-permute-start.26 = (f32[8,128]{1,0:T(8,128)S(1)}, f32[8,128]{1,0:T(8,128)S(1)}, u32[]{:S(2)}, u32[]{:S(2)}) collective-permute-start(f32[8,128]{1,0:T(8,128)S(1)} %get-tuple-element.89), channel_id=1, source_target_pairs={{0,31},{1,0},{2,1},{3,2},{4,3},{5,4},{6,5},{7,6},{8,7},{9,8},{10,9... | collective-permute-start | bytes 12296 | tf_op jit(solution)/shard_map/ppermute | solution.py:516
  70.1 4.8 %collective-permute-done.27.refs_1_ = f32[1,8,128]{2,1,0:T(8,128)S(1)} collective-permute-done((f32[1,8,128]{2,1,0:T(8,128)S(1)}, f32[1,8,128]{2,1,0:T(8,128)S(1)}, u32[]{:S(2)}, u32[]{:S(2)}) %collective-permute-start.27) | collective-permute-done | bytes 4128 | tf_op jit(solution)/shard_map/ppermute | solution.py:529
  74.9 5.4 %collective-permute-done.28.refs_2_ = f32[2,8,128]{2,1,0:T(8,128)S(1)} collective-permute-done((f32[2,8,128]{2,1,0:T(8,128)S(1)}, f32[2,8,128]{2,1,0:T(8,128)S(1)}, u32[]{:S(2)}, u32[]{:S(2)}) %collective-permute-start.28) | collective-permute-done | bytes 8224 | tf_op jit(solution)/shard_map/ppermute | solution.py:529
  80.4 4.6 %collective-permute-done.29.refs_3_ = f32[4,8,128]{2,1,0:T(8,128)S(1)} collective-permute-done((f32[4,8,128]{2,1,0:T(8,128)S(1)}, f32[4,8,128]{2,1,0:T(8,128)S(1)}, u32[]{:S(2)}, u32[]{:S(2)}) %collective-permute-start.29) | collective-permute-done | bytes 16416 | tf_op jit(solution)/shard_map/ppermute | solution.py:529
  89.2 5.3 %collective-permute-start.33 = (f32[8,128]{1,0:T(8,128)S(1)}, f32[8,128]{1,0:T(8,128)S(1)}, u32[]{:S(2)}, u32[]{:S(2)}) collective-permute-start(f32[8,128]{1,0:T(8,128)S(1)} %get-tuple-element.96), channel_id=1, source_target_pairs={{0,31},{1,0},{2,1},{3,2},{4,3},{5,4},{6,5},{7,6},{8,7},{9,8},{10,9... | collective-permute-start | bytes 12296 | tf_op jit(solution)/shard_map/ppermute | solution.py:516
  99.1 5.3 %collective-permute-start.37 = (f32[8,128]{1,0:T(8,128)S(1)}, f32[8,128]{1,0:T(8,128)S(1)}, u32[]{:S(2)}, u32[]{:S(2)}) collective-permute-start(f32[8,128]{1,0:T(8,128)S(1)} %get-tuple-element.98), channel_id=1, source_target_pairs={{0,31},{1,0},{2,1},{3,2},{4,3},{5,4},{6,5},{7,6},{8,7},{9,8},{10,9... | collective-permute-start | bytes 12296 | tf_op jit(solution)/shard_map/ppermute | solution.py:516
  106.1 2.9 %collective-permute-start.39 = (f32[8,128]{1,0:T(8,128)S(1)}, f32[8,128]{1,0:T(8,128)S(1)}, u32[]{:S(2)}, u32[]{:S(2)}) collective-permute-start(f32[8,128]{1,0:T(8,128)S(1)} %get-tuple-element.101), channel_id=1, source_target_pairs={{0,24},{1,25},{2,26},{3,27},{4,28},{5,29},{6,30},{7,31},{8,0},{9,1... | collective-permute-start | bytes 12296 | tf_op jit(solution)/shard_map/ppermute | solution.py:516
  109.1 5.3 %collective-permute-start.41 = (f32[8,128]{1,0:T(8,128)S(1)}, f32[8,128]{1,0:T(8,128)S(1)}, u32[]{:S(2)}, u32[]{:S(2)}) collective-permute-start(f32[8,128]{1,0:T(8,128)S(1)} %get-tuple-element.101), channel_id=1, source_target_pairs={{0,31},{1,0},{2,1},{3,2},{4,3},{5,4},{6,5},{7,6},{8,7},{9,8},{10,9... | collective-permute-start | bytes 12296 | tf_op jit(solution)/shard_map/ppermute | solution.py:516
  116.2 2.9 %collective-permute-start.43 = (f32[8,128]{1,0:T(8,128)S(1)}, f32[8,128]{1,0:T(8,128)S(1)}, u32[]{:S(2)}, u32[]{:S(2)}) collective-permute-start(f32[8,128]{1,0:T(8,128)S(1)} %get-tuple-element.105), channel_id=1, source_target_pairs={{0,24},{1,25},{2,26},{3,27},{4,28},{5,29},{6,30},{7,31},{8,0},{9,1... | collective-permute-start | bytes 12296 | tf_op jit(solution)/shard_map/ppermute | solution.py:516
  119.2 5.3 %collective-permute-start.45 = (f32[8,128]{1,0:T(8,128)S(1)}, f32[8,128]{1,0:T(8,128)S(1)}, u32[]{:S(2)}, u32[]{:S(2)}) collective-permute-start(f32[8,128]{1,0:T(8,128)S(1)} %get-tuple-element.105), channel_id=1, source_target_pairs={{0,31},{1,0},{2,1},{3,2},{4,3},{5,4},{6,5},{7,6},{8,7},{9,8},{10,9... | collective-permute-start | bytes 12296 | tf_op jit(solution)/shard_map/ppermute | solution.py:516
  126.4 2.9 %collective-permute-start.47 = (f32[8,128]{1,0:T(8,128)S(1)}, f32[8,128]{1,0:T(8,128)S(1)}, u32[]{:S(2)}, u32[]{:S(2)}) collective-permute-start(f32[8,128]{1,0:T(8,128)S(1)} %get-tuple-element.108), channel_id=1, source_target_pairs={{0,24},{1,25},{2,26},{3,27},{4,28},{5,29},{6,30},{7,31},{8,0},{9,1... | collective-permute-start | bytes 12296 | tf_op jit(solution)/shard_map/ppermute | solution.py:516
  129.3 5.3 %collective-permute-start.49 = (f32[8,128]{1,0:T(8,128)S(1)}, f32[8,128]{1,0:T(8,128)S(1)}, u32[]{:S(2)}, u32[]{:S(2)}) collective-permute-start(f32[8,128]{1,0:T(8,128)S(1)} %get-tuple-element.108), channel_id=1, source_target_pairs={{0,31},{1,0},{2,1},{3,2},{4,3},{5,4},{6,5},{7,6},{8,7},{9,8},{10,9... | collective-permute-start | bytes 12296 | tf_op jit(solution)/shard_map/ppermute | solution.py:516
  136.6 2.9 %collective-permute-start.51 = (f32[8,128]{1,0:T(8,128)S(1)}, f32[8,128]{1,0:T(8,128)S(1)}, u32[]{:S(2)}, u32[]{:S(2)}) collective-permute-start(f32[8,128]{1,0:T(8,128)S(1)} %get-tuple-element.111), channel_id=1, source_target_pairs={{0,24},{1,25},{2,26},{3,27},{4,28},{5,29},{6,30},{7,31},{8,0},{9,1... | collective-permute-start | bytes 12296 | tf_op jit(solution)/shard_map/ppermute | solution.py:516
  139.5 5.3 %collective-permute-start.53 = (f32[8,128]{1,0:T(8,128)S(1)}, f32[8,128]{1,0:T(8,128)S(1)}, u32[]{:S(2)}, u32[]{:S(2)}) collective-permute-start(f32[8,128]{1,0:T(8,128)S(1)} %get-tuple-element.111), channel_id=1, source_target_pairs={{0,31},{1,0},{2,1},{3,2},{4,3},{5,4},{6,5},{7,6},{8,7},{9,8},{10,9... | collective-permute-start | bytes 12296 | tf_op jit(solution)/shard_map/ppermute | solution.py:516
  147.3 2.9 %collective-permute-start.55 = (f32[8,128]{1,0:T(8,128)S(1)}, f32[8,128]{1,0:T(8,128)S(1)}, u32[]{:S(2)}, u32[]{:S(2)}) collective-permute-start(f32[8,128]{1,0:T(8,128)S(1)} %get-tuple-element.114), channel_id=1, source_target_pairs={{0,24},{1,25},{2,26},{3,27},{4,28},{5,29},{6,30},{7,31},{8,0},{9,1... | collective-permute-start | bytes 12296 | tf_op jit(solution)/shard_map/ppermute | solution.py:516
  150.2 5.3 %collective-permute-start.57 = (f32[8,128]{1,0:T(8,128)S(1)}, f32[8,128]{1,0:T(8,128)S(1)}, u32[]{:S(2)}, u32[]{:S(2)}) collective-permute-start(f32[8,128]{1,0:T(8,128)S(1)} %get-tuple-element.114), channel_id=1, source_target_pairs={{0,31},{1,0},{2,1},{3,2},{4,3},{5,4},{6,5},{7,6},{8,7},{9,8},{10,9... | collective-permute-start | bytes 12296 | tf_op jit(solution)/shard_map/ppermute | solution.py:516
  (158 shorter events, 49.1 us)
Async XLA Ops:
  2.6 13.3 %collective-permute-start = (f32[8,128]{1,0:T(8,128)S(1)}, f32[8,128]{1,0:T(8,128)S(1)}, u32[]{:S(2)}, u32[]{:S(2)}) collective-permute-start(f32[8,128]{1,0:T(8,128)S(1)} %get-tuple-element.60._), channel_id=1, source_target_pairs={{0,8},{1,9},{2,10},{3,11},{4,12},{5,13},{6,14},{7,15},{8,16},{9,17... | collective-permute-start | bytes 12296 | tf_op jit(solution)/shard_map/ppermute | solution.py:516
  5.6 10.3 %collective-permute-start.1 = (f32[8,128]{1,0:T(8,128)S(1)}, f32[8,128]{1,0:T(8,128)S(1)}, u32[]{:S(2)}, u32[]{:S(2)}) collective-permute-start(f32[8,128]{1,0:T(8,128)S(1)} %get-tuple-element.60._), channel_id=1, source_target_pairs={{0,24},{1,25},{2,26},{3,27},{4,28},{5,29},{6,30},{7,31},{8,0},{9,1... | collective-permute-start | bytes 12296 | tf_op jit(solution)/shard_map/ppermute | solution.py:516
  6.6 9.3 %collective-permute-start.2 = (f32[8,128]{1,0:T(8,128)S(1)}, f32[8,128]{1,0:T(8,128)S(1)}, u32[]{:S(2)}, u32[]{:S(2)}) collective-permute-start(f32[8,128]{1,0:T(8,128)S(1)} %get-tuple-element.60._), channel_id=1, source_target_pairs={{0,1},{1,2},{2,3},{3,4},{4,5},{5,6},{6,7},{7,8},{8,9},{9,10},{10,1... | collective-permute-start | bytes 12296 | tf_op jit(solution)/shard_map/ppermute | solution.py:516
  6.7 9.3 %collective-permute-start.3 = (f32[8,128]{1,0:T(8,128)S(1)}, f32[8,128]{1,0:T(8,128)S(1)}, u32[]{:S(2)}, u32[]{:S(2)}) collective-permute-start(f32[8,128]{1,0:T(8,128)S(1)} %get-tuple-element.60._), channel_id=1, source_target_pairs={{0,31},{1,0},{2,1},{3,2},{4,3},{5,4},{6,5},{7,6},{8,7},{9,8},{10,9... | collective-permute-start | bytes 12296 | tf_op jit(solution)/shard_map/ppermute | solution.py:516
  17.6 10.3 %collective-permute-start.17 = (f32[2,136,128]{2,1,0:T(8,128)S(1)}, f32[2,136,128]{2,1,0:T(8,128)S(1)}, u32[]{:S(2)}, u32[]{:S(2)}) collective-permute-start(f32[2,136,128]{2,1,0:T(8,128)S(1)} %pad_maximum_fusion.1), channel_id=1, source_target_pairs={{0,2},{1,3},{2,4},{3,5},{4,6},{5,7},{6,0},{7,1},{8,10},{9,11},{10,... | collective-permute-start | bytes 417800 | tf_op jit(solution)/shard_map/ppermute | solution.py:529
  17.7 9.8 %collective-permute-start.4 = (f32[8,128]{1,0:T(8,128)S(1)}, f32[8,128]{1,0:T(8,128)S(1)}, u32[]{:S(2)}, u32[]{:S(2)}) collective-permute-start(f32[8,128]{1,0:T(8,128)S(1)} %get-tuple-element.66._), channel_id=1, source_target_pairs={{0,8},{1,9},{2,10},{3,11},{4,12},{5,13},{6,14},{7,15},{8,16},{9,17... | collective-permute-start | bytes 12296 | tf_op jit(solution)/shard_map/ppermute | solution.py:516
  17.8 9.7 %collective-permute-start.5 = (f32[8,128]{1,0:T(8,128)S(1)}, f32[8,128]{1,0:T(8,128)S(1)}, u32[]{:S(2)}, u32[]{:S(2)}) collective-permute-start(f32[8,128]{1,0:T(8,128)S(1)} %get-tuple-element.66._), channel_id=1, source_target_pairs={{0,24},{1,25},{2,26},{3,27},{4,28},{5,29},{6,30},{7,31},{8,0},{9,1... | collective-permute-start | bytes 12296 | tf_op jit(solution)/shard_map/ppermute | solution.py:516
  28.0 20.0 %collective-permute-start.18 = (f32[4,136,128]{2,1,0:T(8,128)S(1)}, f32[4,136,128]{2,1,0:T(8,128)S(1)}, u32[]{:S(2)}, u32[]{:S(2)}) collective-permute-start(f32[4,136,128]{2,1,0:T(8,128)S(1)} %pad_maximum_fusion), channel_id=1, source_target_pairs={{0,4},{1,5},{2,6},{3,7},{4,0},{5,1},{6,2},{7,3},{8,12},{9,13},{10,... | collective-permute-start | bytes 835592 | tf_op jit(solution)/shard_map/ppermute | solution.py:529
  28.6 10.5 %collective-permute-start.10 = (f32[8,128]{1,0:T(8,128)S(1)}, f32[8,128]{1,0:T(8,128)S(1)}, u32[]{:S(2)}, u32[]{:S(2)}) collective-permute-start(f32[8,128]{1,0:T(8,128)S(1)} %get-tuple-element.71._), channel_id=1, source_target_pairs={{0,24},{1,25},{2,26},{3,27},{4,28},{5,29},{6,30},{7,31},{8,0},{9,1... | collective-permute-start | bytes 12296 | tf_op jit(solution)/shard_map/ppermute | solution.py:516
  28.6 10.5 %collective-permute-start.11 = (f32[8,128]{1,0:T(8,128)S(1)}, f32[8,128]{1,0:T(8,128)S(1)}, u32[]{:S(2)}, u32[]{:S(2)}) collective-permute-start(f32[8,128]{1,0:T(8,128)S(1)} %get-tuple-element.71._), channel_id=1, source_target_pairs={{0,1},{1,2},{2,3},{3,4},{4,5},{5,6},{6,7},{7,8},{8,9},{9,10},{10,1... | collective-permute-start | bytes 12296 | tf_op jit(solution)/shard_map/ppermute | solution.py:516
  28.6 10.5 %collective-permute-start.12 = (f32[8,128]{1,0:T(8,128)S(1)}, f32[8,128]{1,0:T(8,128)S(1)}, u32[]{:S(2)}, u32[]{:S(2)}) collective-permute-start(f32[8,128]{1,0:T(8,128)S(1)} %get-tuple-element.71._), channel_id=1, source_target_pairs={{0,31},{1,0},{2,1},{3,2},{4,3},{5,4},{6,5},{7,6},{8,7},{9,8},{10,9... | collective-permute-start | bytes 12296 | tf_op jit(solution)/shard_map/ppermute | solution.py:516
  39.7 8.7 %collective-permute-start.13 = (f32[8,128]{1,0:T(8,128)S(1)}, f32[8,128]{1,0:T(8,128)S(1)}, u32[]{:S(2)}, u32[]{:S(2)}) collective-permute-start(f32[8,128]{1,0:T(8,128)S(1)} %get-tuple-element.76.refs_5_), channel_id=1, source_target_pairs={{0,8},{1,9},{2,10},{3,11},{4,12},{5,13},{6,14},{7,15},{8,16},{9,17... | collective-permute-start | bytes 12296 | tf_op jit(solution)/shard_map/ppermute | solution.py:516
  49.6 8.3 %collective-permute-start.19 = (f32[8,128]{1,0:T(8,128)S(1)}, f32[8,128]{1,0:T(8,128)S(1)}, u32[]{:S(2)}, u32[]{:S(2)}) collective-permute-start(f32[8,128]{1,0:T(8,128)S(1)} %get-tuple-element.86), channel_id=1, source_target_pairs={{0,8},{1,9},{2,10},{3,11},{4,12},{5,13},{6,14},{7,15},{8,16},{9,17... | collective-permute-start | bytes 12296 | tf_op jit(solution)/shard_map/ppermute | solution.py:516
  86.3 8.3 %collective-permute-start.30 = (f32[8,128]{1,0:T(8,128)S(1)}, f32[8,128]{1,0:T(8,128)S(1)}, u32[]{:S(2)}, u32[]{:S(2)}) collective-permute-start(f32[8,128]{1,0:T(8,128)S(1)} %get-tuple-element.96), channel_id=1, source_target_pairs={{0,8},{1,9},{2,10},{3,11},{4,12},{5,13},{6,14},{7,15},{8,16},{9,17... | collective-permute-start | bytes 12296 | tf_op jit(solution)/shard_map/ppermute | solution.py:516
  96.2 8.3 %collective-permute-start.34 = (f32[8,128]{1,0:T(8,128)S(1)}, f32[8,128]{1,0:T(8,128)S(1)}, u32[]{:S(2)}, u32[]{:S(2)}) collective-permute-start(f32[8,128]{1,0:T(8,128)S(1)} %get-tuple-element.98), channel_id=1, source_target_pairs={{0,8},{1,9},{2,10},{3,11},{4,12},{5,13},{6,14},{7,15},{8,16},{9,17... | collective-permute-start | bytes 12296 | tf_op jit(solution)/shard_map/ppermute | solution.py:516
  106.1 8.3 %collective-permute-start.38 = (f32[8,128]{1,0:T(8,128)S(1)}, f32[8,128]{1,0:T(8,128)S(1)}, u32[]{:S(2)}, u32[]{:S(2)}) collective-permute-start(f32[8,128]{1,0:T(8,128)S(1)} %get-tuple-element.101), channel_id=1, source_target_pairs={{0,8},{1,9},{2,10},{3,11},{4,12},{5,13},{6,14},{7,15},{8,16},{9,17... | collective-permute-start | bytes 12296 | tf_op jit(solution)/shard_map/ppermute | solution.py:516
  116.2 9.8 %collective-permute-start.42 = (f32[8,128]{1,0:T(8,128)S(1)}, f32[8,128]{1,0:T(8,128)S(1)}, u32[]{:S(2)}, u32[]{:S(2)}) collective-permute-start(f32[8,128]{1,0:T(8,128)S(1)} %get-tuple-element.105), channel_id=1, source_target_pairs={{0,8},{1,9},{2,10},{3,11},{4,12},{5,13},{6,14},{7,15},{8,16},{9,17... | collective-permute-start | bytes 12296 | tf_op jit(solution)/shard_map/ppermute | solution.py:516
  116.2 9.8 %collective-permute-start.43 = (f32[8,128]{1,0:T(8,128)S(1)}, f32[8,128]{1,0:T(8,128)S(1)}, u32[]{:S(2)}, u32[]{:S(2)}) collective-permute-start(f32[8,128]{1,0:T(8,128)S(1)} %get-tuple-element.105), channel_id=1, source_target_pairs={{0,24},{1,25},{2,26},{3,27},{4,28},{5,29},{6,30},{7,31},{8,0},{9,1... | collective-permute-start | bytes 12296 | tf_op jit(solution)/shard_map/ppermute | solution.py:516
  126.4 9.8 %collective-permute-start.46 = (f32[8,128]{1,0:T(8,128)S(1)}, f32[8,128]{1,0:T(8,128)S(1)}, u32[]{:S(2)}, u32[]{:S(2)}) collective-permute-start(f32[8,128]{1,0:T(8,128)S(1)} %get-tuple-element.108), channel_id=1, source_target_pairs={{0,8},{1,9},{2,10},{3,11},{4,12},{5,13},{6,14},{7,15},{8,16},{9,17... | collective-permute-start | bytes 12296 | tf_op jit(solution)/shard_map/ppermute | solution.py:516
  126.4 9.8 %collective-permute-start.47 = (f32[8,128]{1,0:T(8,128)S(1)}, f32[8,128]{1,0:T(8,128)S(1)}, u32[]{:S(2)}, u32[]{:S(2)}) collective-permute-start(f32[8,128]{1,0:T(8,128)S(1)} %get-tuple-element.108), channel_id=1, source_target_pairs={{0,24},{1,25},{2,26},{3,27},{4,28},{5,29},{6,30},{7,31},{8,0},{9,1... | collective-permute-start | bytes 12296 | tf_op jit(solution)/shard_map/ppermute | solution.py:516
  136.6 9.8 %collective-permute-start.50 = (f32[8,128]{1,0:T(8,128)S(1)}, f32[8,128]{1,0:T(8,128)S(1)}, u32[]{:S(2)}, u32[]{:S(2)}) collective-permute-start(f32[8,128]{1,0:T(8,128)S(1)} %get-tuple-element.111), channel_id=1, source_target_pairs={{0,8},{1,9},{2,10},{3,11},{4,12},{5,13},{6,14},{7,15},{8,16},{9,17... | collective-permute-start | bytes 12296 | tf_op jit(solution)/shard_map/ppermute | solution.py:516
  136.6 9.8 %collective-permute-start.51 = (f32[8,128]{1,0:T(8,128)S(1)}, f32[8,128]{1,0:T(8,128)S(1)}, u32[]{:S(2)}, u32[]{:S(2)}) collective-permute-start(f32[8,128]{1,0:T(8,128)S(1)} %get-tuple-element.111), channel_id=1, source_target_pairs={{0,24},{1,25},{2,26},{3,27},{4,28},{5,29},{6,30},{7,31},{8,0},{9,1... | collective-permute-start | bytes 12296 | tf_op jit(solution)/shard_map/ppermute | solution.py:516
  147.3 9.8 %collective-permute-start.54 = (f32[8,128]{1,0:T(8,128)S(1)}, f32[8,128]{1,0:T(8,128)S(1)}, u32[]{:S(2)}, u32[]{:S(2)}) collective-permute-start(f32[8,128]{1,0:T(8,128)S(1)} %get-tuple-element.114), channel_id=1, source_target_pairs={{0,8},{1,9},{2,10},{3,11},{4,12},{5,13},{6,14},{7,15},{8,16},{9,17... | collective-permute-start | bytes 12296 | tf_op jit(solution)/shard_map/ppermute | solution.py:516
  147.3 9.8 %collective-permute-start.55 = (f32[8,128]{1,0:T(8,128)S(1)}, f32[8,128]{1,0:T(8,128)S(1)}, u32[]{:S(2)}, u32[]{:S(2)}) collective-permute-start(f32[8,128]{1,0:T(8,128)S(1)} %get-tuple-element.114), channel_id=1, source_target_pairs={{0,24},{1,25},{2,26},{3,27},{4,28},{5,29},{6,30},{7,31},{8,0},{9,1... | collective-permute-start | bytes 12296 | tf_op jit(solution)/shard_map/ppermute | solution.py:516
  (46 other events, 263.3 us)

commit v3 on v2

--- a/solution.py
+++ b/solution.py
@@ -49,7 +49,9 @@
 
 
 def halo_lines(arrivals, edge_ref):
-    prev_s, next_s, prev_p, next_p, inside = [r[...] for r in arrivals]
+    all_ref, place_ref, inside_ref = arrivals
+    prev_s, next_s, prev_p, next_p = [all_ref[place_ref[d]] for d in range(4)]
+    inside = inside_ref[...]
     left = tile_iota(1) < LANES // 2
     upper = tile_iota(0) < 4
     values = jnp.where(
@@ -162,8 +164,8 @@
 
 
 def fine_step(factors, *refs):
-    arrivals = refs[:5]
-    (r_ref, v_ref, c_ref, m_ref, x_ref, d_ref, s_ref, xo_ref, do_ref, out_ref, edge_ref, pad_ref) = refs[5:]
+    arrivals = refs[:3]
+    (r_ref, v_ref, c_ref, m_ref, x_ref, d_ref, s_ref, xo_ref, do_ref, out_ref, edge_ref, pad_ref) = refs[3:]
     keep, gain = factors
     lines = r_ref.shape[1]
     resid = fine_remote(arrivals, r_ref, v_ref, c_ref, edge_ref)
@@ -184,8 +186,8 @@
 
 
 def fine_finish(*refs):
-    arrivals = refs[:5]
-    r_ref, v_ref, c_ref, x_ref, so_ref, ro_ref, edge_ref = refs[5:]
+    arrivals = refs[:3]
+    r_ref, v_ref, c_ref, x_ref, so_ref, ro_ref, edge_ref = refs[3:]
     lines = r_ref.shape[1]
     resid = fine_remote(arrivals, r_ref, v_ref, c_ref, edge_ref)
     for h in range(lines // SUBS):
@@ -196,8 +198,8 @@
 
 
 def fine_restrict(*refs):
-    arrivals = refs[:5]
-    (r_ref, v_ref, c_ref, w_ref, p_ref, m2_ref, s2_ref, b2_ref, x2_ref, out_ref, edge_ref, line_ref, pad_ref) = refs[5:]
+    arrivals = refs[:3]
+    (r_ref, v_ref, c_ref, w_ref, p_ref, m2_ref, s2_ref, b2_ref, x2_ref, out_ref, edge_ref, line_ref, pad_ref) = refs[3:]
     lines = r_ref.shape[1]
     resid = fine_remote(arrivals, r_ref, v_ref, c_ref, edge_ref)
     for h in range(lines // SUBS):
@@ -332,8 +334,8 @@
 
 
 def middle_step(factors, *refs):
-    arrivals = refs[:5]
-    (b_ref, m_ref, x_ref, d_ref, v_ref, c_ref, s_ref, xo_ref, do_ref, out_ref, edge_ref, pad_ref) = refs[5:]
+    arrivals = refs[:3]
+    (b_ref, m_ref, x_ref, d_ref, v_ref, c_ref, s_ref, xo_ref, do_ref, out_ref, edge_ref, pad_ref) = refs[3:]
     resid = middle_residual(arrivals, b_ref, x_ref, v_ref, c_ref, edge_ref)
     xs, ds = middle_update(factors, resid, m_ref, x_ref, d_ref)
     for i in range(4):
@@ -344,8 +346,8 @@
 
 
 def middle_restrict(*refs):
-    arrivals = refs[:5]
-    b_ref, x_ref, v_ref, c_ref, w_ref, p_ref, out_ref, edge_ref, line_ref = refs[5:]
+    arrivals = refs[:3]
+    b_ref, x_ref, v_ref, c_ref, w_ref, p_ref, out_ref, edge_ref, line_ref = refs[3:]
     resid = middle_residual(arrivals, b_ref, x_ref, v_ref, c_ref, edge_ref)
     place = p_ref[...]
     high, lane = place >> 7, place & (LANES - 1)
@@ -363,8 +365,8 @@
 
 
 def middle_prolong(factors, *refs):
-    arrivals = refs[:5]
-    (b_ref, m_ref, x_ref, d_ref, v_ref, c_ref, x1_ref, w_ref, agg_ref, s_ref, xo_ref, out_ref, edge_ref, line_ref, pad_ref) = refs[5:]
+    arrivals = refs[:3]
+    (b_ref, m_ref, x_ref, d_ref, v_ref, c_ref, x1_ref, w_ref, agg_ref, s_ref, xo_ref, out_ref, edge_ref, line_ref, pad_ref) = refs[3:]
     lines = x1_ref.shape[1]
     resid = middle_residual(arrivals, b_ref, x_ref, v_ref, c_ref, edge_ref)
     xs, _ = middle_update(factors, resid, m_ref, x_ref, d_ref)
@@ -465,6 +467,7 @@
 
 def call(body, outs, args, scratch=(), free=(), smem=()):
     specs = []
+    smem = tuple(smem) + tuple(t for t, arg in enumerate(args) if arg.shape == (4,))
     for index in range(len(args)):
         if index in free:
             specs.append(pl.BlockSpec(memory_space=pl.ANY))
@@ -509,14 +512,10 @@
     return jnp.concatenate([stream] * 4 + [span] * 4, axis=0)
 
 
-def exchange(mesh, out, inside):
-    count = mesh.shape["span"]
-    total = mesh.shape["stream"] * count
-    moved = [
-        lax.ppermute(out, AXES, [(p, (p + shift) % total) for p in range(total)])
-        for shift in (count, -count, 1, -1)
-    ]
-    return moved + [inside]
+def exchange(mesh, out, near):
+    total = mesh.shape["stream"] * mesh.shape["span"]
+    copies = jnp.broadcast_to(out[None], (total, SUBS, LANES))
+    return [lax.all_to_all(copies, AXES, 0, 0, tiled=True)] + near
 
 
 def span_shift(mesh, value, shift):
@@ -550,6 +549,10 @@
     row, lane = (lax.broadcasted_iota(I32, (SUBS, LANES), d) for d in range(2))
     outside = (row >= 4) & jnp.where(lane < LANES // 2, me == 0, me == group - 1)
     inside = jnp.where(outside, 0.0, 1.0).astype(F32)
+    total = mesh.shape["stream"] * group
+    here = lax.axis_index("stream").astype(I32) * group + me
+    place = jnp.stack([here - group, here + group, here - 1, here + 1])
+    near = [jnp.where(place < 0, place + total, jnp.where(place >= total, place - total, place)), inside]
     send1, send2 = send_table(fine_sends), send_table(middle_sends)
     values1 = native_rows(fine_values)
     values2 = native_rows(middle_values)
@@ -585,13 +588,13 @@
             free=range(len(args), len(args) + len(after)),
         )
 
-    arrived = exchange(mesh, out, inside)
+    arrived = exchange(mesh, out, near)
     own3, _ = lax.optimization_barrier((own3, out))
     pieces3 = span_stage(mesh, [own3[None]])
     resid = fine_part(x1)
     x1, d1, out = fine_next(1, arrived, resid, x1, d1)
 
-    arrived = exchange(mesh, out, inside)
+    arrived = exchange(mesh, out, near)
     pieces3, _ = lax.optimization_barrier((pieces3, out))
     pieces3 = span_stage(mesh, pieces3)
     resid = fine_part(x1)
@@ -603,7 +606,7 @@
     )
     x1, d1, out = fine_next(2, arrived, resid, x1, d1, [pieces3[1]])
 
-    arrived = exchange(mesh, out, inside)
+    arrived = exchange(mesh, out, near)
     pieces3, _ = lax.optimization_barrier((pieces3, out))
     while sum(piece.shape[0] for piece in pieces3) < group:
         pieces3 = span_stage(mesh, pieces3)
@@ -639,7 +642,7 @@
             free=range(len(args), len(args) + len(after)),
         )
 
-    arrived = exchange(mesh, out, inside)
+    arrived = exchange(mesh, out, near)
     v3, c3, m3 = call(
         lambda *refs: coarse_tables(group, *refs),
         [shape(NNZ, 4, 4, group, LANES), shape(NNZ, group, LANES, dtype=I32), shape(4, group, LANES)],
@@ -649,9 +652,9 @@
         smem=(0,),
     )
     x2, d2, out = middle_next(1, arrived, x2, d2, [m3])
-    arrived = exchange(mesh, out, inside)
+    arrived = exchange(mesh, out, near)
     x2, d2, out = middle_next(2, arrived, x2, d2)
-    arrived = exchange(mesh, out, inside)
+    arrived = exchange(mesh, out, near)
     rhs3 = call(
         middle_restrict,
         tile,
@@ -668,11 +671,11 @@
         pieces + [v3, c3, m3, x2, w2, agg2, send2],
         [vec3, vec3, vec3, pad2],
     )
-    arrived = exchange(mesh, out, inside)
+    arrived = exchange(mesh, out, near)
     x2, d2, out = middle_next(0, arrived, x2, x2)
-    arrived = exchange(mesh, out, inside)
+    arrived = exchange(mesh, out, near)
     x2, d2, out = middle_next(1, arrived, x2, d2)
-    arrived = exchange(mesh, out, inside)
+    arrived = exchange(mesh, out, near)
     x1, out = call(
         lambda *refs: middle_prolong(factors[2], *refs),
         [vec1, tile],
@@ -680,10 +683,10 @@
         [edge, vmem(4, SUBS, LANES), pad1],
     )
     for which in range(KSM):
-        arrived = exchange(mesh, out, inside)
+        arrived = exchange(mesh, out, near)
         resid = fine_part(x1)
         x1, d1, out = fine_next(which, arrived, resid, x1, d1)
-    arrived = exchange(mesh, out, inside)
+    arrived = exchange(mesh, out, near)
     resid = fine_part(x1)
     rows = shape(4 * lines, LANES)
     solved, left = call(fine_finish, [rows, rows], arrived + [resid, v1, c1, x1], [edge])

time: 158 us -> 188 us (1.19)
  starting transfers between devices: 107 us -> 37.4 us
  blocking collectives: 0 us -> 49.4 us
  waiting for transfers between devices: 23.8 us -> 62.3 us
  Pallas kernels: 19.6 us -> 26.6 us
  local copies, waits for them, and re-layouts: 5.59 us -> 10.5 us
    ppermute x52 -> x0, starting transfers between devices: 107 us -> none  [exchange(): lax.ppermute(out, AXES, [(p, (p + shift) % total) for p in range(total)])]
    all_to_all x0 -> x5, blocking collectives: none -> 49.4 us  [exchange(): return [lax.all_to_all(copies, AXES, 0, 0, tiled=True)] + near]
    all_to_all x0 -> x8, waiting for transfers between devices: none -> 39.7 us  [exchange(): return [lax.all_to_all(copies, AXES, 0, 0, tiled=True)] + near]
    all_to_all x0 -> x8, starting transfers between devices: none -> 34.1 us  [exchange(): return [lax.all_to_all(copies, AXES, 0, 0, tiled=True)] + near]
    ppermute x52 -> x0, waiting for transfers between devices: 7.6 us -> none  [exchange(): lax.ppermute(out, AXES, [(p, (p + shift) % total) for p in range(total)])]
    pallas_call x26, Pallas kernels: 19.6 us -> 26.6 us  [call(): pl.pallas_call(body, out_shape=shapes, in_specs=specs, out_specs=[pl.Bloc...]
    ppermute x6, waiting for transfers between devices: 16.2 us -> 22.6 us  [span_shift(): return lax.ppermute(value, AXES, pairs)]
    broadcast_in_dim x0 -> x13, local copies, waits for them, and re-layouts: none -> 5.49 us  [exchange(): copies = jnp.broadcast_to(out[None], (total, SUBS, LANES))]
  transfers between devices with their start and end apart: 58 -> 14, of which waited for: 10 -> 12; matrix products, arithmetic and copies ran while one was open for 0% -> 1% of each run, Pallas kernels for 8% -> 7%
where the time goes in v3:
time: 188 us
  waiting for transfers between devices  62.3 us (33%)
  blocking collectives  49.4 us (26%)
  starting transfers between devices  37.4 us (20%)
  Pallas kernels  26.6 us (14%)
  local copies, waits for them, and re-layouts  10.5 us (6%)
    all_to_all x5, blocking collectives, exchange(): return [lax.all_to_all(copies, AXES, 0, 0, tiled=True)] + near  49.4 us
    all_to_all x8, waiting for transfers between devices, exchange(): return [lax.all_to_all(copies, AXES, 0, 0, tiled=True)] + near  39.7 us
    all_to_all x8, starting transfers between devices, exchange(): return [lax.all_to_all(copies, AXES, 0, 0, tiled=True)] + near  34.1 us
    pallas_call x26, Pallas kernels, call(): pl.pallas_call(body, out_shape=shapes, in_specs=specs, out_specs=[pl.Bloc...  26.6 us
    ppermute x6, waiting for transfers between devices, span_shift(): return lax.ppermute(value, AXES, pairs)  22.6 us
    broadcast_in_dim x13, local copies, waits for them, and re-layouts, exchange(): copies = jnp.broadcast_to(out[None], (total, SUBS, LANES))  5.49 us
  transfers between devices with their start and end apart: 14, of which 12 were waited for; matrix products, arithmetic and copies ran while one was open for 1% of the time, Pallas kernels for 7%

profile of v3, /device:TPU:0, one launch (start us, length us, event | category | flops | bytes accessed | tf_op | source)
XLA Modules:
  0.0 187.6 jit_solution(11710443923596948526)
XLA Ops:
  3.3 7.3 %all-to-all-start = ((f32[32,8,128]{2,1,0:T(8,128)}), f32[32,8,128]{2,1,0:T(8,128)S(1)}, u32[]{:S(2)}, u32[]{:S(2)}) async-start(f32[32,8,128]{2,1,0:T(8,128)} %broadcast_in_dim.56), calls=%async_computation | async-start | bytes 262144 | tf_op jit(solution)/shard_map/all_to_all | solution.py:518
  14.5 4.3 %all-to-all-done.refs_0_ = f32[32,8,128]{2,1,0:T(8,128)S(1)} async-done(((f32[32,8,128]{2,1,0:T(8,128)}), f32[32,8,128]{2,1,0:T(8,128)S(1)}, u32[]{:S(2)}, u32[]{:S(2)}) %all-to-all-start) | async-done | bytes 131104 | tf_op jit(solution)/shard_map/all_to_all | solution.py:518
  20.3 2.7 %all-to-all-start.1 = ((f32[32,8,128]{2,1,0:T(8,128)}), f32[32,8,128]{2,1,0:T(8,128)S(1)}, u32[]{:S(2)}, u32[]{:S(2)}) async-start(f32[32,8,128]{2,1,0:T(8,128)} %broadcast_in_dim.61), calls=%async_computation.1 | async-start | bytes 262144 | tf_op jit(solution)/shard_map/all_to_all | solution.py:518
  23.2 7.4 %collective-permute-done.refs_10_.refs_2_ = f32[1,136,128]{2,1,0:T(8,128)S(1)} collective-permute-done((f32[1,136,128]{2,1,0:T(8,128)S(1)}, f32[1,136,128]{2,1,0:T(8,128)S(1)}, u32[]{:S(2)}, u32[]{:S(2)}) %collective-permute-start) | collective-permute-done | bytes 69664 | tf_op jit(solution)/shard_map/ppermute | solution.py:528
  33.8 6.0 %all-to-all-start.2 = ((f32[32,8,128]{2,1,0:T(8,128)}), f32[32,8,128]{2,1,0:T(8,128)S(1)}, u32[]{:S(2)}, u32[]{:S(2)}) async-start(f32[32,8,128]{2,1,0:T(8,128)} %broadcast_in_dim.63), calls=%async_computation.2 | async-start | bytes 262144 | tf_op jit(solution)/shard_map/all_to_all | solution.py:518
  39.8 2.7 %collective-permute-start.2 = (f32[4,136,128]{2,1,0:T(8,128)S(1)}, f32[4,136,128]{2,1,0:T(8,128)S(1)}, u32[]{:S(2)}, u32[]{:S(2)}) collective-permute-start(f32[4,136,128]{2,1,0:T(8,128)S(1)} %pad_maximum_fusion), channel_id=1, source_target_pairs={{0,4},{1,5},{2,6},{3,7},{4,0},{5,1},{6,2},{7,3},{8,12},{9,13},{10,... | collective-permute-start | bytes 835592 | tf_op jit(solution)/shard_map/ppermute | solution.py:528
  49.8 7.9 %all-to-all-start.3 = ((f32[32,8,128]{2,1,0:T(8,128)}), f32[32,8,128]{2,1,0:T(8,128)S(1)}, u32[]{:S(2)}, u32[]{:S(2)}) async-start(f32[32,8,128]{2,1,0:T(8,128)} %broadcast_in_dim.124), calls=%async_computation.3 | async-start | bytes 262144 | tf_op jit(solution)/shard_map/all_to_all | solution.py:518
  58.7 7.1 %all-to-all-done.3.refs_0_ = f32[32,8,128]{2,1,0:T(8,128)S(1)} async-done(((f32[32,8,128]{2,1,0:T(8,128)}), f32[32,8,128]{2,1,0:T(8,128)S(1)}, u32[]{:S(2)}, u32[]{:S(2)}) %all-to-all-start.3) | async-done | bytes 131104 | tf_op jit(solution)/shard_map/all_to_all | solution.py:518
  66.7 9.9 %all_to_all.65.refs_0_ = f32[32,8,128]{2,1,0:T(8,128)S(1)} all-to-all(f32[32,8,128]{2,1,0:T(8,128)S(1)} %broadcast_in_dim.125), channel_id=1, replica_groups=mesh['stream'=4,'span'=8] {'stream','span'}, dimensions={0} | all-to-all | bytes 262144 | tf_op jit(solution)/shard_map/all_to_all | solution.py:518
  78.0 9.9 %all_to_all.66.refs_0_ = f32[32,8,128]{2,1,0:T(8,128)S(1)} all-to-all(f32[32,8,128]{2,1,0:T(8,128)S(1)} %broadcast_in_dim.126), channel_id=1, replica_groups=mesh['stream'=4,'span'=8] {'stream','span'}, dimensions={0} | all-to-all | bytes 262144 | tf_op jit(solution)/shard_map/all_to_all | solution.py:518
  89.1 4.5 %collective-permute-done.3.refs_1_ = f32[1,8,128]{2,1,0:T(8,128)S(1)} collective-permute-done((f32[1,8,128]{2,1,0:T(8,128)S(1)}, f32[1,8,128]{2,1,0:T(8,128)S(1)}, u32[]{:S(2)}, u32[]{:S(2)}) %collective-permute-start.3) | collective-permute-done | bytes 4128 | tf_op jit(solution)/shard_map/ppermute | solution.py:528
  93.6 5.4 %collective-permute-done.4.refs_2_ = f32[2,8,128]{2,1,0:T(8,128)S(1)} collective-permute-done((f32[2,8,128]{2,1,0:T(8,128)S(1)}, f32[2,8,128]{2,1,0:T(8,128)S(1)}, u32[]{:S(2)}, u32[]{:S(2)}) %collective-permute-start.4) | collective-permute-done | bytes 8224 | tf_op jit(solution)/shard_map/ppermute | solution.py:528
  99.1 4.6 %collective-permute-done.5.refs_3_ = f32[4,8,128]{2,1,0:T(8,128)S(1)} collective-permute-done((f32[4,8,128]{2,1,0:T(8,128)S(1)}, f32[4,8,128]{2,1,0:T(8,128)S(1)}, u32[]{:S(2)}, u32[]{:S(2)}) %collective-permute-start.5) | collective-permute-done | bytes 16416 | tf_op jit(solution)/shard_map/ppermute | solution.py:528
  105.0 9.9 %all_to_all.67.refs_0_ = f32[32,8,128]{2,1,0:T(8,128)S(1)} all-to-all(f32[32,8,128]{2,1,0:T(8,128)S(1)} %broadcast_in_dim.128), channel_id=1, replica_groups=mesh['stream'=4,'span'=8] {'stream','span'}, dimensions={0} | all-to-all | bytes 262144 | tf_op jit(solution)/shard_map/all_to_all | solution.py:518
  115.7 9.9 %all_to_all.68.refs_0_ = f32[32,8,128]{2,1,0:T(8,128)S(1)} all-to-all(f32[32,8,128]{2,1,0:T(8,128)S(1)} %broadcast_in_dim.129), channel_id=1, replica_groups=mesh['stream'=4,'span'=8] {'stream','span'}, dimensions={0} | all-to-all | bytes 262144 | tf_op jit(solution)/shard_map/all_to_all | solution.py:518
  126.5 9.9 %all_to_all.69.refs_0_ = f32[32,8,128]{2,1,0:T(8,128)S(1)} all-to-all(f32[32,8,128]{2,1,0:T(8,128)S(1)} %broadcast_in_dim.130), channel_id=1, replica_groups=mesh['stream'=4,'span'=8] {'stream','span'}, dimensions={0} | all-to-all | bytes 262144 | tf_op jit(solution)/shard_map/all_to_all | solution.py:518
  138.1 2.6 %all-to-all-start.9 = ((f32[32,8,128]{2,1,0:T(8,128)}), f32[32,8,128]{2,1,0:T(8,128)S(1)}, u32[]{:S(2)}, u32[]{:S(2)}) async-start(f32[32,8,128]{2,1,0:T(8,128)} %broadcast_in_dim.131), calls=%async_computation.9 | async-start | bytes 262144 | tf_op jit(solution)/shard_map/all_to_all | solution.py:518
  142.1 6.7 %all-to-all-done.9.refs_0_ = f32[32,8,128]{2,1,0:T(8,128)S(1)} async-done(((f32[32,8,128]{2,1,0:T(8,128)}), f32[32,8,128]{2,1,0:T(8,128)S(1)}, u32[]{:S(2)}, u32[]{:S(2)}) %all-to-all-start.9) | async-done | bytes 131104 | tf_op jit(solution)/shard_map/all_to_all | solution.py:518
  150.3 2.6 %all-to-all-start.10 = ((f32[32,8,128]{2,1,0:T(8,128)}), f32[32,8,128]{2,1,0:T(8,128)S(1)}, u32[]{:S(2)}, u32[]{:S(2)}) async-start(f32[32,8,128]{2,1,0:T(8,128)} %broadcast_in_dim.132), calls=%async_computation.10 | async-start | bytes 262144 | tf_op jit(solution)/shard_map/all_to_all | solution.py:518
  154.4 6.7 %all-to-all-done.10.refs_0_ = f32[32,8,128]{2,1,0:T(8,128)S(1)} async-done(((f32[32,8,128]{2,1,0:T(8,128)}), f32[32,8,128]{2,1,0:T(8,128)S(1)}, u32[]{:S(2)}, u32[]{:S(2)}) %all-to-all-start.10) | async-done | bytes 131104 | tf_op jit(solution)/shard_map/all_to_all | solution.py:518
  162.6 2.6 %all-to-all-start.11 = ((f32[32,8,128]{2,1,0:T(8,128)}), f32[32,8,128]{2,1,0:T(8,128)S(1)}, u32[]{:S(2)}, u32[]{:S(2)}) async-start(f32[32,8,128]{2,1,0:T(8,128)} %broadcast_in_dim.133), calls=%async_computation.11 | async-start | bytes 262144 | tf_op jit(solution)/shard_map/all_to_all | solution.py:518
  166.7 6.7 %all-to-all-done.11.refs_0_ = f32[32,8,128]{2,1,0:T(8,128)S(1)} async-done(((f32[32,8,128]{2,1,0:T(8,128)}), f32[32,8,128]{2,1,0:T(8,128)S(1)}, u32[]{:S(2)}, u32[]{:S(2)}) %all-to-all-start.11) | async-done | bytes 131104 | tf_op jit(solution)/shard_map/all_to_all | solution.py:518
  175.4 2.6 %all-to-all-start.12 = ((f32[32,8,128]{2,1,0:T(8,128)}), f32[32,8,128]{2,1,0:T(8,128)S(1)}, u32[]{:S(2)}, u32[]{:S(2)}) async-start(f32[32,8,128]{2,1,0:T(8,128)} %broadcast_in_dim.134), calls=%async_computation.12 | async-start | bytes 262144 | tf_op jit(solution)/shard_map/all_to_all | solution.py:518
  179.5 6.7 %all-to-all-done.12.refs_0_ = f32[32,8,128]{2,1,0:T(8,128)S(1)} async-done(((f32[32,8,128]{2,1,0:T(8,128)}), f32[32,8,128]{2,1,0:T(8,128)S(1)}, u32[]{:S(2)}, u32[]{:S(2)}) %all-to-all-start.12) | async-done | bytes 131104 | tf_op jit(solution)/shard_map/all_to_all | solution.py:518
  (89 shorter events, 40.4 us)
Async XLA Ops:
  1.5 1.0 copy-start.6
  3.3 8.0 %copy-start.3 = (s32[8,2048]{1,0:T(8,128)S(1)}, s32[8,2048]{1,0:T(8,128)}, u32[]{:S(2)}) copy-start(s32[8,2048]{1,0:T(8,128)} %param.15) | copy-start | bytes 196612
  3.3 15.5 %all-to-all-start = ((f32[32,8,128]{2,1,0:T(8,128)}), f32[32,8,128]{2,1,0:T(8,128)S(1)}, u32[]{:S(2)}, u32[]{:S(2)}) async-start(f32[32,8,128]{2,1,0:T(8,128)} %broadcast_in_dim.56), calls=%async_computation | async-start | bytes 262144 | tf_op jit(solution)/shard_map/all_to_all | solution.py:518
  11.3 1.2 copy-start
  20.3 2.7 %copy-start.9 = (f32[8,4,4,128]{3,2,1,0:T(4,128)S(1)}, f32[8,4,4,128]{3,2,1,0:T(4,128)}, u32[]{:S(2)}) copy-start(f32[8,4,4,128]{3,2,1,0:T(4,128)} %param.24) | copy-start | bytes 196612
  20.3 11.9 %all-to-all-start.1 = ((f32[32,8,128]{2,1,0:T(8,128)}), f32[32,8,128]{2,1,0:T(8,128)S(1)}, u32[]{:S(2)}, u32[]{:S(2)}) async-start(f32[32,8,128]{2,1,0:T(8,128)} %broadcast_in_dim.61), calls=%async_computation.1 | async-start | bytes 262144 | tf_op jit(solution)/shard_map/all_to_all | solution.py:518
  23.0 7.5 %collective-permute-start = (f32[1,136,128]{2,1,0:T(8,128)S(1)}, f32[1,136,128]{2,1,0:T(8,128)S(1)}, u32[]{:S(2)}, u32[]{:S(2)}) collective-permute-start(f32[1,136,128]{2,1,0:T(8,128)S(1)} %bitcast.85), channel_id=1, source_target_pairs={{0,1},{1,2},{2,3},{3,4},{4,5},{5,6},{6,7},{7,0},{8,9},{9,10},{10,1... | collective-permute-start | bytes 208904 | tf_op jit(solution)/shard_map/ppermute | solution.py:528
  32.1 7.7 %collective-permute-start.1 = (f32[2,136,128]{2,1,0:T(8,128)S(1)}, f32[2,136,128]{2,1,0:T(8,128)S(1)}, u32[]{:S(2)}, u32[]{:S(2)}) collective-permute-start(f32[2,136,128]{2,1,0:T(8,128)S(1)} %pad_maximum_fusion.1), channel_id=1, source_target_pairs={{0,2},{1,3},{2,4},{3,5},{4,6},{5,7},{6,0},{7,1},{8,10},{9,11},{10,... | collective-permute-start | bytes 417800 | tf_op jit(solution)/shard_map/ppermute | solution.py:528
  33.8 6.0 %copy-start.11 = (s32[4,64]{1,0:T(4,128)S(1)}, s32[4,64]{1,0:T(4,128)}, u32[]{:S(2)}) copy-start(s32[4,64]{1,0:T(4,128)} %param.21) | copy-start | bytes 3076
  33.8 14.2 %all-to-all-start.2 = ((f32[32,8,128]{2,1,0:T(8,128)}), f32[32,8,128]{2,1,0:T(8,128)S(1)}, u32[]{:S(2)}, u32[]{:S(2)}) async-start(f32[32,8,128]{2,1,0:T(8,128)} %broadcast_in_dim.63), calls=%async_computation.2 | async-start | bytes 262144 | tf_op jit(solution)/shard_map/all_to_all | solution.py:518
  39.8 2.9 %copy-start.2 = (f32[4,4,2048]{2,1,0:T(4,128)S(1)}, f32[4,4,2048]{2,1,0:T(4,128)}, u32[]{:S(2)}) copy-start(f32[4,4,2048]{2,1,0:T(4,128)} %param.18) | copy-start | bytes 393220
  39.8 18.4 %collective-permute-start.2 = (f32[4,136,128]{2,1,0:T(8,128)S(1)}, f32[4,136,128]{2,1,0:T(8,128)S(1)}, u32[]{:S(2)}, u32[]{:S(2)}) collective-permute-start(f32[4,136,128]{2,1,0:T(8,128)S(1)} %pad_maximum_fusion), channel_id=1, source_target_pairs={{0,4},{1,5},{2,6},{3,7},{4,0},{5,1},{6,2},{7,3},{8,12},{9,13},{10,... | collective-permute-start | bytes 835592 | tf_op jit(solution)/shard_map/ppermute | solution.py:528
  42.7 0.7 copy-start.5
  43.7 1.6 copy-start.1
  43.7 1.6 copy-start.4
  43.7 1.6 copy-start.7
  49.8 16.0 %all-to-all-start.3 = ((f32[32,8,128]{2,1,0:T(8,128)}), f32[32,8,128]{2,1,0:T(8,128)S(1)}, u32[]{:S(2)}, u32[]{:S(2)}) async-start(f32[32,8,128]{2,1,0:T(8,128)} %broadcast_in_dim.124), calls=%async_computation.3 | async-start | bytes 262144 | tf_op jit(solution)/shard_map/all_to_all | solution.py:518
  88.8 4.9 %collective-permute-start.3 = (f32[1,8,128]{2,1,0:T(8,128)S(1)}, f32[1,8,128]{2,1,0:T(8,128)S(1)}, u32[]{:S(2)}, u32[]{:S(2)}) collective-permute-start(f32[1,8,128]{2,1,0:T(8,128)S(1)} %bitcast.92), channel_id=1, source_target_pairs={{0,1},{1,2},{2,3},{3,4},{4,5},{5,6},{6,7},{7,0},{8,9},{9,10},{10,1... | collective-permute-start | bytes 12296 | tf_op jit(solution)/shard_map/ppermute | solution.py:528
  93.6 5.4 %collective-permute-start.4 = (f32[2,8,128]{2,1,0:T(8,128)S(1)}, f32[2,8,128]{2,1,0:T(8,128)S(1)}, u32[]{:S(2)}, u32[]{:S(2)}) collective-permute-start(f32[2,8,128]{2,1,0:T(8,128)S(1)} %pad_maximum_fusion.4), channel_id=1, source_target_pairs={{0,2},{1,3},{2,4},{3,5},{4,6},{5,7},{6,0},{7,1},{8,10},{9,11},{10,... | collective-permute-start | bytes 24584 | tf_op jit(solution)/shard_map/ppermute | solution.py:528
  99.1 4.6 %collective-permute-start.5 = (f32[4,8,128]{2,1,0:T(8,128)S(1)}, f32[4,8,128]{2,1,0:T(8,128)S(1)}, u32[]{:S(2)}, u32[]{:S(2)}) collective-permute-start(f32[4,8,128]{2,1,0:T(8,128)S(1)} %pad_maximum_fusion.3), channel_id=1, source_target_pairs={{0,4},{1,5},{2,6},{3,7},{4,0},{5,1},{6,2},{7,3},{8,12},{9,13},{10,... | collective-permute-start | bytes 49160 | tf_op jit(solution)/shard_map/ppermute | solution.py:528
  138.1 10.7 %all-to-all-start.9 = ((f32[32,8,128]{2,1,0:T(8,128)}), f32[32,8,128]{2,1,0:T(8,128)S(1)}, u32[]{:S(2)}, u32[]{:S(2)}) async-start(f32[32,8,128]{2,1,0:T(8,128)} %broadcast_in_dim.131), calls=%async_computation.9 | async-start | bytes 262144 | tf_op jit(solution)/shard_map/all_to_all | solution.py:518
  150.3 10.7 %all-to-all-start.10 = ((f32[32,8,128]{2,1,0:T(8,128)}), f32[32,8,128]{2,1,0:T(8,128)S(1)}, u32[]{:S(2)}, u32[]{:S(2)}) async-start(f32[32,8,128]{2,1,0:T(8,128)} %broadcast_in_dim.132), calls=%async_computation.10 | async-start | bytes 262144 | tf_op jit(solution)/shard_map/all_to_all | solution.py:518
  162.6 10.7 %all-to-all-start.11 = ((f32[32,8,128]{2,1,0:T(8,128)}), f32[32,8,128]{2,1,0:T(8,128)S(1)}, u32[]{:S(2)}, u32[]{:S(2)}) async-start(f32[32,8,128]{2,1,0:T(8,128)} %broadcast_in_dim.133), calls=%async_computation.11 | async-start | bytes 262144 | tf_op jit(solution)/shard_map/all_to_all | solution.py:518
  175.4 10.7 %all-to-all-start.12 = ((f32[32,8,128]{2,1,0:T(8,128)}), f32[32,8,128]{2,1,0:T(8,128)S(1)}, u32[]{:S(2)}, u32[]{:S(2)}) async-start(f32[32,8,128]{2,1,0:T(8,128)} %broadcast_in_dim.134), calls=%async_computation.12 | async-start | bytes 262144 | tf_op jit(solution)/shard_map/all_to_all | solution.py:518
  (2 other events, 1.4 us)

commit v4 on v2

--- a/solution.py
+++ b/solution.py
@@ -49,13 +49,11 @@
 
 
 def halo_lines(arrivals, edge_ref):
-    prev_s, next_s, prev_p, next_p, inside = [r[...] for r in arrivals]
-    left = tile_iota(1) < LANES // 2
+    s_odd, p_odd, s_even, p_even, which = [r[...] for r in arrivals]
     upper = tile_iota(0) < 4
-    values = jnp.where(
-        upper, jnp.where(left, prev_s, next_s), jnp.where(left, prev_p, next_p)
-    )
-    edge_ref[...] = jnp.where(inside > 0.0, values, 0.0)
+    even = jnp.where(upper, s_even, p_even)
+    odd = jnp.where(upper, s_odd, p_odd)
+    edge_ref[...] = jnp.where(which == 1, even, jnp.where(which == 2, odd, 0.0))
 
 
 def outgoing(lines_of, count, sends):
@@ -63,11 +61,19 @@
     return pick_lines([lines_of(r) for r in range(count)], high, lane)
 
 
+def send_table(s_ref):
+    stream = jnp.concatenate([s_ref[pl.ds(1, 1), :], s_ref[pl.ds(0, 1), :]], axis=1)
+    span = jnp.concatenate([s_ref[pl.ds(3, 1), :], s_ref[pl.ds(2, 1), :]], axis=1)
+    return jnp.where(tile_iota(0) < 4, stream, span)
+
+
 def duplicate(x):
     return x + pltpu.roll(x, 4, 0)
 
 
-def fine_start(v_ref, b_ref, s_ref, bo_ref, mo_ref, x_ref, out_ref, pad_ref):
+def fine_start(v_ref, b_ref, s_ref, bo_ref, mo_ref, x_ref, so_ref, out_ref, pad_ref):
+    sends = send_table(s_ref)
+    so_ref[...] = sends
     lines = bo_ref.shape[1]
     for i in range(4):
         for h in range(lines // SUBS):
@@ -82,7 +88,7 @@
             for twice in range(2):
                 pad_ref[pl.ds((twice * 4 + i) * lines + h * SUBS, SUBS), :] = x
     out_ref[...] = outgoing(
-        lambda r: pad_ref[pl.ds(r, SUBS, stride=lines), :], lines, s_ref[...]
+        lambda r: pad_ref[pl.ds(r, SUBS, stride=lines), :], lines, sends
     )
 
 
@@ -264,8 +270,9 @@
         place_ref[part] = pick_order(sources, (tile_iota(0) >> 2) + 2 * part)
 
 
-def middle_tables(v_ref, c_ref, w_ref, row_ref, o_ref, _, vo_ref, co_ref, mo_ref, wo_ref, agg_ref, place_ref):
+def middle_tables(v_ref, c_ref, w_ref, row_ref, o_ref, s_ref, _, so_ref, vo_ref, co_ref, mo_ref, wo_ref, agg_ref, place_ref):
     lines = o_ref.shape[0]
+    so_ref[...] = send_table(s_ref)
 
     def body(ki, carry):
         k, i = ki // 4, ki % 4
@@ -394,11 +401,9 @@
 def coarse_tables(group, *refs):
     vo_ref, co_ref, mo_ref, pad_ref = refs[-4:]
     me = refs[0][0]
-    place = 0
-    for piece in refs[1:-5]:
-        for t in range(piece.shape[0]):
+    for piece, places in zip(refs[1:-5], span_places(group)):
+        for t, place in enumerate(places):
             pad_ref[place] = piece[t]
-            place += 1
     for h in range(group // SUBS):
         rows = pl.ds(h * SUBS, SUBS)
         for ki in range(NNZ * 4):
@@ -410,19 +415,15 @@
                     mo_ref[i, rows, :] = 1.0 / tile
         for k in range(NNZ):
             col = pad_ref[rows, NNZ * 16 + k, :].astype(I32)
-            back = me - (col >> 7)
-            back = jnp.where(back < 0, back + group, back)
-            co_ref[k, rows, :] = back * LANES + (col & (LANES - 1))
+            co_ref[k, rows, :] = ((col >> 7) ^ me) * LANES + (col & (LANES - 1))
 
 
 def coarse_solve(group, *refs):
     (v_ref, c_ref, m_ref, x2_ref, w_ref, agg_ref, s_ref, xo_ref, out_ref, b_ref, x_ref, d_ref, pad_ref) = refs[-13:]
-    place = 0
-    for piece in refs[:-13]:
-        for t in range(piece.shape[0]):
+    for piece, places in zip(refs[:-13], span_places(group)):
+        for t, place in enumerate(places):
             for j in range(4):
                 b_ref[j, pl.ds(place, 1), :] = piece[t, pl.ds(j, 1), :]
-            place += 1
     blocks = group // SUBS
     for j in range(4):
         first = m_ref[j] * b_ref[j]
@@ -503,37 +504,51 @@
     return jnp.swapaxes(rows.reshape(lines, 4, LANES), 0, 1).reshape(4, lines * LANES)
 
 
-def send_table(sends):
-    stream = jnp.concatenate([sends[1], sends[0]])[None]
-    span = jnp.concatenate([sends[3], sends[2]])[None]
-    return jnp.concatenate([stream] * 4 + [span] * 4, axis=0)
-
-
-def exchange(mesh, out, inside):
-    count = mesh.shape["span"]
-    total = mesh.shape["stream"] * count
-    moved = [
-        lax.ppermute(out, AXES, [(p, (p + shift) % total) for p in range(total)])
-        for shift in (count, -count, 1, -1)
+def exchange(mesh, out, which):
+    slabs, count = mesh.shape["stream"], mesh.shape["span"]
+
+    def partner(index, size, odd, closed):
+        other = index ^ 1 if not odd else (index + 1 if index % 2 else index - 1)
+        return other % size if closed or 0 <= other < size else index
+
+    def swap(odd_s, odd_p):
+        pairs = []
+        for a in range(slabs):
+            for b in range(count):
+                to_a = a if odd_s is None else partner(a, slabs, odd_s, True)
+                to_b = b if odd_p is None else partner(b, count, odd_p, False)
+                pairs.append((a * count + b, to_a * count + to_b))
+        return lax.ppermute(out, AXES, pairs)
+
+    return [swap(True, None), swap(None, True), swap(False, None), swap(None, False), which]
+
+
+def halo_choice(a, b, count):
+    row, lane = (lax.broadcasted_iota(I32, (SUBS, LANES), d) for d in range(2))
+    left = lane < LANES // 2
+    index = jnp.where(row < 4, a, b)
+    even = left == (index % 2 == 1)
+    outside = (row >= 4) & jnp.where(left, b == 0, b == count - 1)
+    return jnp.where(outside, 0, jnp.where(even, 1, 2)).astype(I32)
+
+
+def span_places(group):
+    places = [[0]]
+    mask = group // 2
+    while mask:
+        places.append([mask ^ m for piece in places for m in piece])
+        mask //= 2
+    return places
+
+
+def span_stage(mesh, pieces):
+    slabs, count = mesh.shape["stream"], mesh.shape["span"]
+    held = jnp.concatenate(pieces)
+    mask = count // 2 // held.shape[0]
+    pairs = [
+        (a * count + b, a * count + (b ^ mask)) for a in range(slabs) for b in range(count)
     ]
-    return moved + [inside]
-
-
-def span_shift(mesh, value, shift):
-    slabs, count = mesh.shape["stream"], mesh.shape["span"]
-    pairs = [
-        (a * count + b, a * count + (b + shift) % count)
-        for a in range(slabs)
-        for b in range(count)
-    ]
-    return lax.ppermute(value, AXES, pairs)
-
-
-def span_stage(mesh, pieces):
-    group = mesh.shape["span"]
-    have = sum(piece.shape[0] for piece in pieces)
-    held = jnp.concatenate(pieces)[: min(have, group - have)]
-    return pieces + [span_shift(mesh, held, have)]
+    return pieces + [lax.ppermute(held, AXES, pairs)]
 
 
 def per_device(mesh, right_side, fine_values, fine_columns, fine_sends, fine_order, fine_weights, middle_values, middle_columns, middle_sends, middle_order, middle_weights, coarsest_values, coarsest_columns):
@@ -547,17 +562,14 @@
     pad2 = vmem(SUBS * SUBS, LANES)
     factors = cheb_factors(KSM)
     me = lax.axis_index("span").astype(I32)
-    row, lane = (lax.broadcasted_iota(I32, (SUBS, LANES), d) for d in range(2))
-    outside = (row >= 4) & jnp.where(lane < LANES // 2, me == 0, me == group - 1)
-    inside = jnp.where(outside, 0.0, 1.0).astype(F32)
-    send1, send2 = send_table(fine_sends), send_table(middle_sends)
+    choice = halo_choice(lax.axis_index("stream").astype(I32), me, group)
     values1 = native_rows(fine_values)
     values2 = native_rows(middle_values)
 
-    b1, m1, x1, out = call(
+    b1, m1, x1, send1, out = call(
         fine_start,
-        [vec1, vec1, vec1, tile],
-        [native_rows(fine_values[0]), native_rows(right_side), send1],
+        [vec1, vec1, vec1, shape(SUBS, LANES, dtype=I32), tile],
+        [values1, native_rows(right_side), fine_sends],
         [pad1],
     )
     d1 = x1
@@ -585,13 +597,13 @@
             free=range(len(args), len(args) + len(after)),
         )
 
-    arrived = exchange(mesh, out, inside)
+    arrived = exchange(mesh, out, choice)
     own3, _ = lax.optimization_barrier((own3, out))
     pieces3 = span_stage(mesh, [own3[None]])
     resid = fine_part(x1)
     x1, d1, out = fine_next(1, arrived, resid, x1, d1)
 
-    arrived = exchange(mesh, out, inside)
+    arrived = exchange(mesh, out, choice)
     pieces3, _ = lax.optimization_barrier((pieces3, out))
     pieces3 = span_stage(mesh, pieces3)
     resid = fine_part(x1)
@@ -603,14 +615,15 @@
     )
     x1, d1, out = fine_next(2, arrived, resid, x1, d1, [pieces3[1]])
 
-    arrived = exchange(mesh, out, inside)
+    arrived = exchange(mesh, out, choice)
     pieces3, _ = lax.optimization_barrier((pieces3, out))
     while sum(piece.shape[0] for piece in pieces3) < group:
         pieces3 = span_stage(mesh, pieces3)
     resid = fine_part(x1)
-    v2, c2, m2, w2, agg2, place2 = call(
+    send2, v2, c2, m2, w2, agg2, place2 = call(
         middle_tables,
         [
+            shape(SUBS, LANES, dtype=I32),
             shape(NNZ // 2, 4, 4, SUBS, LANES),
             shape(NNZ // 2, SUBS, LANES, dtype=I32),
             vec2,
@@ -618,8 +631,8 @@
             shape(SUBS, LANES, dtype=I32),
             shape(SUBS, LANES, dtype=I32),
         ],
-        [values2, native_columns(middle_columns), native_rows(middle_weights), middle_order, middle_order.reshape(-1, LANES), out],
-        free=(5,),
+        [values2, native_columns(middle_columns), native_rows(middle_weights), middle_order, middle_order.reshape(-1, LANES), middle_sends, out],
+        free=(6,),
     )
     b2, x2, out = call(
         fine_restrict,
@@ -639,7 +652,7 @@
             free=range(len(args), len(args) + len(after)),
         )
 
-    arrived = exchange(mesh, out, inside)
+    arrived = exchange(mesh, out, choice)
     v3, c3, m3 = call(
         lambda *refs: coarse_tables(group, *refs),
         [shape(NNZ, 4, 4, group, LANES), shape(NNZ, group, LANES, dtype=I32), shape(4, group, LANES)],
@@ -649,9 +662,9 @@
         smem=(0,),
     )
     x2, d2, out = middle_next(1, arrived, x2, d2, [m3])
-    arrived = exchange(mesh, out, inside)
+    arrived = exchange(mesh, out, choice)
     x2, d2, out = middle_next(2, arrived, x2, d2)
-    arrived = exchange(mesh, out, inside)
+    arrived = exchange(mesh, out, choice)
     rhs3 = call(
         middle_restrict,
         tile,
@@ -668,11 +681,11 @@
         pieces + [v3, c3, m3, x2, w2, agg2, send2],
         [vec3, vec3, vec3, pad2],
     )
-    arrived = exchange(mesh, out, inside)
+    arrived = exchange(mesh, out, choice)
     x2, d2, out = middle_next(0, arrived, x2, x2)
-    arrived = exchange(mesh, out, inside)
+    arrived = exchange(mesh, out, choice)
     x2, d2, out = middle_next(1, arrived, x2, d2)
-    arrived = exchange(mesh, out, inside)
+    arrived = exchange(mesh, out, choice)
     x1, out = call(
         lambda *refs: middle_prolong(factors[2], *refs),
         [vec1, tile],
@@ -680,10 +693,10 @@
         [edge, vmem(4, SUBS, LANES), pad1],
     )
     for which in range(KSM):
-        arrived = exchange(mesh, out, inside)
+        arrived = exchange(mesh, out, choice)
         resid = fine_part(x1)
         x1, d1, out = fine_next(which, arrived, resid, x1, d1)
-    arrived = exchange(mesh, out, inside)
+    arrived = exchange(mesh, out, choice)
     resid = fine_part(x1)
     rows = shape(4 * lines, LANES)
     solved, left = call(fine_finish, [rows, rows], arrived + [resid, v1, c1, x1], [edge])

time: 158 us -> 126 us (0.80)
  starting transfers between devices: 107 us -> 88.4 us
  waiting for transfers between devices: 23.8 us -> 11.1 us
  local copies, waits for them, and re-layouts: 5.59 us -> 3.35 us
    ppermute x58, starting transfers between devices: 107 us -> 88.4 us  [the longest x52 79.9 us: swap(): return lax.ppermute(out, AXES, pairs)]
    ppermute x58, waiting for transfers between devices: 23.8 us -> 11.1 us  [the longest x6 6.41 us: span_stage(): return pieces + [lax.ppermute(held, AXES, pairs)]]
    unnamed x24 -> x26, local copies, waits for them, and re-layouts: 3.78 us -> 3.35 us
  transfers between devices with their start and end apart: 58 -> 58, of which waited for: 10 -> 10; matrix products, arithmetic and copies ran while one was open for 0% -> 1% of each run, Pallas kernels for 8% -> 11%
where the time goes in v4:
time: 126 us; the launch traced here: 125 us
  starting transfers between devices  88.4 us (70%)
  Pallas kernels  19.8 us (16%)
  waiting for transfers between devices  11.1 us (9%)
  local copies, waits for them, and re-layouts  3.35 us (3%)
    ppermute x52, starting transfers between devices, swap(): return lax.ppermute(out, AXES, pairs)  79.9 us
    pallas_call x26, Pallas kernels, call(): pl.pallas_call(body, out_shape=shapes, in_specs=specs, out_specs=[pl.Bloc...  19.8 us
    ppermute x6, starting transfers between devices, span_stage(): return pieces + [lax.ppermute(held, AXES, pairs)]  8.54 us
    ppermute x6, waiting for transfers between devices, span_stage(): return pieces + [lax.ppermute(held, AXES, pairs)]  6.41 us
    ppermute x52, waiting for transfers between devices, swap(): return lax.ppermute(out, AXES, pairs)  4.67 us
    unnamed x26, local copies, waits for them, and re-layouts  3.35 us
  transfers between devices with their start and end apart: 58, of which 10 were waited for; matrix products, arithmetic and copies ran while one was open for 1% of the time, Pallas kernels for 11%

profile of v4, /device:TPU:0, one launch (start us, length us, event | category | flops | bytes accessed | tf_op | source)
XLA Modules:
  0.0 124.9 jit_solution(2833714778880897853)
XLA Ops:
  3.5 4.0 %collective-permute-start = (f32[8,128]{1,0:T(8,128)S(1)}, f32[8,128]{1,0:T(8,128)S(1)}, u32[]{:S(2)}, u32[]{:S(2)}) collective-permute-start(f32[8,128]{1,0:T(8,128)S(1)} %get-tuple-element.62._), channel_id=1, source_target_pairs={{0,24},{1,25},{2,26},{3,27},{4,28},{5,29},{6,30},{7,31},{8,16},{9,... | collective-permute-start | bytes 12296 | tf_op jit(solution)/shard_map/ppermute | solution.py:521
  8.7 2.7 %collective-permute-start.3 = (f32[8,128]{1,0:T(8,128)S(1)}, f32[8,128]{1,0:T(8,128)S(1)}, u32[]{:S(2)}, u32[]{:S(2)}) collective-permute-start(f32[8,128]{1,0:T(8,128)S(1)} %get-tuple-element.62._), channel_id=1, source_target_pairs={{0,1},{1,0},{2,3},{3,2},{4,5},{5,4},{6,7},{7,6},{8,9},{9,8},{10,11... | collective-permute-start | bytes 12296 | tf_op jit(solution)/shard_map/ppermute | solution.py:521
  12.2 2.6 %collective-permute-start.8 = (f32[1,136,128]{2,1,0:T(8,128)S(1)}, f32[1,136,128]{2,1,0:T(8,128)S(1)}, u32[]{:S(2)}, u32[]{:S(2)}) collective-permute-start(f32[1,136,128]{2,1,0:T(8,128)S(1)} %bitcast.53), channel_id=1, source_target_pairs={{0,4},{1,5},{2,6},{3,7},{4,0},{5,1},{6,2},{7,3},{8,12},{9,13},{10,... | collective-permute-start | bytes 208904 | tf_op jit(solution)/shard_map/ppermute | solution.py:551
  17.2 1.7 %collective-permute-done.8.refs_12_.refs_2_ = f32[1,136,128]{2,1,0:T(8,128)S(1)} collective-permute-done((f32[1,136,128]{2,1,0:T(8,128)S(1)}, f32[1,136,128]{2,1,0:T(8,128)S(1)}, u32[]{:S(2)}, u32[]{:S(2)}) %collective-permute-start.8) | collective-permute-done | bytes 69664 | tf_op jit(solution)/shard_map/ppermute | solution.py:551
  21.8 3.0 %collective-permute-start.7 = (f32[8,128]{1,0:T(8,128)S(1)}, f32[8,128]{1,0:T(8,128)S(1)}, u32[]{:S(2)}, u32[]{:S(2)}) collective-permute-start(f32[8,128]{1,0:T(8,128)S(1)} %get-tuple-element.69._), channel_id=1, source_target_pairs={{0,1},{1,0},{2,3},{3,2},{4,5},{5,4},{6,7},{7,6},{8,9},{9,8},{10,11... | collective-permute-start | bytes 12296 | tf_op jit(solution)/shard_map/ppermute | solution.py:521
  29.1 2.7 %collective-permute-start.12 = (f32[8,128]{1,0:T(8,128)S(1)}, f32[8,128]{1,0:T(8,128)S(1)}, u32[]{:S(2)}, u32[]{:S(2)}) collective-permute-start(f32[8,128]{1,0:T(8,128)S(1)} %get-tuple-element.74._), channel_id=1, source_target_pairs={{0,1},{1,0},{2,3},{3,2},{4,5},{5,4},{6,7},{7,6},{8,9},{9,8},{10,11... | collective-permute-start | bytes 12296 | tf_op jit(solution)/shard_map/ppermute | solution.py:521
  31.8 2.1 %collective-permute-start.9 = (f32[8,128]{1,0:T(8,128)S(1)}, f32[8,128]{1,0:T(8,128)S(1)}, u32[]{:S(2)}, u32[]{:S(2)}) collective-permute-start(f32[8,128]{1,0:T(8,128)S(1)} %get-tuple-element.74._), channel_id=1, source_target_pairs={{0,24},{1,25},{2,26},{3,27},{4,28},{5,29},{6,30},{7,31},{8,16},{9,... | collective-permute-start | bytes 12296 | tf_op jit(solution)/shard_map/ppermute | solution.py:521
  40.6 1.8 %collective-permute-start.16 = (f32[8,128]{1,0:T(8,128)S(1)}, f32[8,128]{1,0:T(8,128)S(1)}, u32[]{:S(2)}, u32[]{:S(2)}) collective-permute-start(f32[8,128]{1,0:T(8,128)S(1)} %get-tuple-element.80.refs_5_), channel_id=1, source_target_pairs={{0,1},{1,0},{2,3},{3,2},{4,5},{5,4},{6,7},{7,6},{8,9},{9,8},{10,11... | collective-permute-start | bytes 12296 | tf_op jit(solution)/shard_map/ppermute | solution.py:521
  47.2 2.9 %collective-permute-start.22 = (f32[8,128]{1,0:T(8,128)S(1)}, f32[8,128]{1,0:T(8,128)S(1)}, u32[]{:S(2)}, u32[]{:S(2)}) collective-permute-start(f32[8,128]{1,0:T(8,128)S(1)} %get-tuple-element.90), channel_id=1, source_target_pairs={{0,1},{1,0},{2,3},{3,2},{4,5},{5,4},{6,7},{7,6},{8,9},{9,8},{10,11... | collective-permute-start | bytes 12296 | tf_op jit(solution)/shard_map/ppermute | solution.py:521
  53.6 1.6 %collective-permute-start.25 = (f32[8,128]{1,0:T(8,128)S(1)}, f32[8,128]{1,0:T(8,128)S(1)}, u32[]{:S(2)}, u32[]{:S(2)}) collective-permute-start(f32[8,128]{1,0:T(8,128)S(1)} %get-tuple-element.93), channel_id=1, source_target_pairs={{0,8},{1,9},{2,10},{3,11},{4,12},{5,13},{6,14},{7,15},{8,0},{9,1},... | collective-permute-start | bytes 12296 | tf_op jit(solution)/shard_map/ppermute | solution.py:521
  55.1 2.9 %collective-permute-start.26 = (f32[8,128]{1,0:T(8,128)S(1)}, f32[8,128]{1,0:T(8,128)S(1)}, u32[]{:S(2)}, u32[]{:S(2)}) collective-permute-start(f32[8,128]{1,0:T(8,128)S(1)} %get-tuple-element.93), channel_id=1, source_target_pairs={{0,1},{1,0},{2,3},{3,2},{4,5},{5,4},{6,7},{7,6},{8,9},{9,8},{10,11... | collective-permute-start | bytes 12296 | tf_op jit(solution)/shard_map/ppermute | solution.py:521
  59.2 2.7 %collective-permute-start.27 = (f32[1,8,128]{2,1,0:T(8,128)S(1)}, f32[1,8,128]{2,1,0:T(8,128)S(1)}, u32[]{:S(2)}, u32[]{:S(2)}) collective-permute-start(f32[1,8,128]{2,1,0:T(8,128)S(1)} %bitcast.59), channel_id=1, source_target_pairs={{0,4},{1,5},{2,6},{3,7},{4,0},{5,1},{6,2},{7,3},{8,12},{9,13},{10,... | collective-permute-start | bytes 12296 | tf_op jit(solution)/shard_map/ppermute | solution.py:551
  61.8 1.9 %collective-permute-done.27.refs_1_ = f32[1,8,128]{2,1,0:T(8,128)S(1)} collective-permute-done((f32[1,8,128]{2,1,0:T(8,128)S(1)}, f32[1,8,128]{2,1,0:T(8,128)S(1)}, u32[]{:S(2)}, u32[]{:S(2)}) %collective-permute-start.27) | collective-permute-done | bytes 4128 | tf_op jit(solution)/shard_map/ppermute | solution.py:551
  63.7 2.4 %collective-permute-start.28 = (f32[2,8,128]{2,1,0:T(8,128)S(1)}, f32[2,8,128]{2,1,0:T(8,128)S(1)}, u32[]{:S(2)}, u32[]{:S(2)}) collective-permute-start(f32[2,8,128]{2,1,0:T(8,128)S(1)} %pad_maximum_fusion.4), channel_id=1, source_target_pairs={{0,2},{1,3},{2,0},{3,1},{4,6},{5,7},{6,4},{7,5},{8,10},{9,11},{10,... | collective-permute-start | bytes 24584 | tf_op jit(solution)/shard_map/ppermute | solution.py:551
  66.1 1.6 %collective-permute-done.28.refs_2_ = f32[2,8,128]{2,1,0:T(8,128)S(1)} collective-permute-done((f32[2,8,128]{2,1,0:T(8,128)S(1)}, f32[2,8,128]{2,1,0:T(8,128)S(1)}, u32[]{:S(2)}, u32[]{:S(2)}) %collective-permute-start.28) | collective-permute-done | bytes 8224 | tf_op jit(solution)/shard_map/ppermute | solution.py:551
  73.5 2.9 %collective-permute-start.33 = (f32[8,128]{1,0:T(8,128)S(1)}, f32[8,128]{1,0:T(8,128)S(1)}, u32[]{:S(2)}, u32[]{:S(2)}) collective-permute-start(f32[8,128]{1,0:T(8,128)S(1)} %get-tuple-element.100), channel_id=1, source_target_pairs={{0,1},{1,0},{2,3},{3,2},{4,5},{5,4},{6,7},{7,6},{8,9},{9,8},{10,11... | collective-permute-start | bytes 12296 | tf_op jit(solution)/shard_map/ppermute | solution.py:521
  80.9 2.6 %collective-permute-start.37 = (f32[8,128]{1,0:T(8,128)S(1)}, f32[8,128]{1,0:T(8,128)S(1)}, u32[]{:S(2)}, u32[]{:S(2)}) collective-permute-start(f32[8,128]{1,0:T(8,128)S(1)} %get-tuple-element.102), channel_id=1, source_target_pairs={{0,1},{1,0},{2,3},{3,2},{4,5},{5,4},{6,7},{7,6},{8,9},{9,8},{10,11... | collective-permute-start | bytes 12296 | tf_op jit(solution)/shard_map/ppermute | solution.py:521
  84.6 1.8 %collective-permute-start.38 = (f32[8,128]{1,0:T(8,128)S(1)}, f32[8,128]{1,0:T(8,128)S(1)}, u32[]{:S(2)}, u32[]{:S(2)}) collective-permute-start(f32[8,128]{1,0:T(8,128)S(1)} %get-tuple-element.105), channel_id=1, source_target_pairs={{0,24},{1,25},{2,26},{3,27},{4,28},{5,29},{6,30},{7,31},{8,16},{9,... | collective-permute-start | bytes 12296 | tf_op jit(solution)/shard_map/ppermute | solution.py:521
  88.2 3.2 %collective-permute-start.41 = (f32[8,128]{1,0:T(8,128)S(1)}, f32[8,128]{1,0:T(8,128)S(1)}, u32[]{:S(2)}, u32[]{:S(2)}) collective-permute-start(f32[8,128]{1,0:T(8,128)S(1)} %get-tuple-element.105), channel_id=1, source_target_pairs={{0,1},{1,0},{2,3},{3,2},{4,5},{5,4},{6,7},{7,6},{8,9},{9,8},{10,11... | collective-permute-start | bytes 12296 | tf_op jit(solution)/shard_map/ppermute | solution.py:521
  96.1 2.6 %collective-permute-start.45 = (f32[8,128]{1,0:T(8,128)S(1)}, f32[8,128]{1,0:T(8,128)S(1)}, u32[]{:S(2)}, u32[]{:S(2)}) collective-permute-start(f32[8,128]{1,0:T(8,128)S(1)} %get-tuple-element.109), channel_id=1, source_target_pairs={{0,1},{1,0},{2,3},{3,2},{4,5},{5,4},{6,7},{7,6},{8,9},{9,8},{10,11... | collective-permute-start | bytes 12296 | tf_op jit(solution)/shard_map/ppermute | solution.py:521
  100.6 1.8 %collective-permute-start.46 = (f32[8,128]{1,0:T(8,128)S(1)}, f32[8,128]{1,0:T(8,128)S(1)}, u32[]{:S(2)}, u32[]{:S(2)}) collective-permute-start(f32[8,128]{1,0:T(8,128)S(1)} %get-tuple-element.112), channel_id=1, source_target_pairs={{0,24},{1,25},{2,26},{3,27},{4,28},{5,29},{6,30},{7,31},{8,16},{9,... | collective-permute-start | bytes 12296 | tf_op jit(solution)/shard_map/ppermute | solution.py:521
  104.3 2.6 %collective-permute-start.49 = (f32[8,128]{1,0:T(8,128)S(1)}, f32[8,128]{1,0:T(8,128)S(1)}, u32[]{:S(2)}, u32[]{:S(2)}) collective-permute-start(f32[8,128]{1,0:T(8,128)S(1)} %get-tuple-element.112), channel_id=1, source_target_pairs={{0,1},{1,0},{2,3},{3,2},{4,5},{5,4},{6,7},{7,6},{8,9},{9,8},{10,11... | collective-permute-start | bytes 12296 | tf_op jit(solution)/shard_map/ppermute | solution.py:521
  111.9 2.3 %collective-permute-start.53 = (f32[8,128]{1,0:T(8,128)S(1)}, f32[8,128]{1,0:T(8,128)S(1)}, u32[]{:S(2)}, u32[]{:S(2)}) collective-permute-start(f32[8,128]{1,0:T(8,128)S(1)} %get-tuple-element.115), channel_id=1, source_target_pairs={{0,1},{1,0},{2,3},{3,2},{4,5},{5,4},{6,7},{7,6},{8,9},{9,8},{10,11... | collective-permute-start | bytes 12296 | tf_op jit(solution)/shard_map/ppermute | solution.py:521
  119.9 2.6 %collective-permute-start.57 = (f32[8,128]{1,0:T(8,128)S(1)}, f32[8,128]{1,0:T(8,128)S(1)}, u32[]{:S(2)}, u32[]{:S(2)}) collective-permute-start(f32[8,128]{1,0:T(8,128)S(1)} %get-tuple-element.118), channel_id=1, source_target_pairs={{0,1},{1,0},{2,3},{3,2},{4,5},{5,4},{6,7},{7,6},{8,9},{9,8},{10,11... | collective-permute-start | bytes 12296 | tf_op jit(solution)/shard_map/ppermute | solution.py:521
  (155 shorter events, 64.9 us)
Async XLA Ops:
  3.5 13.4 %collective-permute-start = (f32[8,128]{1,0:T(8,128)S(1)}, f32[8,128]{1,0:T(8,128)S(1)}, u32[]{:S(2)}, u32[]{:S(2)}) collective-permute-start(f32[8,128]{1,0:T(8,128)S(1)} %get-tuple-element.62._), channel_id=1, source_target_pairs={{0,24},{1,25},{2,26},{3,27},{4,28},{5,29},{6,30},{7,31},{8,16},{9,... | collective-permute-start | bytes 12296 | tf_op jit(solution)/shard_map/ppermute | solution.py:521
  7.4 9.4 %collective-permute-start.1 = (f32[8,128]{1,0:T(8,128)S(1)}, f32[8,128]{1,0:T(8,128)S(1)}, u32[]{:S(2)}, u32[]{:S(2)}) collective-permute-start(f32[8,128]{1,0:T(8,128)S(1)} %get-tuple-element.62._), channel_id=1, source_target_pairs={{0,0},{1,2},{2,1},{3,4},{4,3},{5,6},{6,5},{7,7},{8,8},{9,10},{10,9... | collective-permute-start | bytes 12296 | tf_op jit(solution)/shard_map/ppermute | solution.py:521
  8.1 8.8 %collective-permute-start.2 = (f32[8,128]{1,0:T(8,128)S(1)}, f32[8,128]{1,0:T(8,128)S(1)}, u32[]{:S(2)}, u32[]{:S(2)}) collective-permute-start(f32[8,128]{1,0:T(8,128)S(1)} %get-tuple-element.62._), channel_id=1, source_target_pairs={{0,8},{1,9},{2,10},{3,11},{4,12},{5,13},{6,14},{7,15},{8,0},{9,1},... | collective-permute-start | bytes 12296 | tf_op jit(solution)/shard_map/ppermute | solution.py:521
  8.7 8.2 %collective-permute-start.3 = (f32[8,128]{1,0:T(8,128)S(1)}, f32[8,128]{1,0:T(8,128)S(1)}, u32[]{:S(2)}, u32[]{:S(2)}) collective-permute-start(f32[8,128]{1,0:T(8,128)S(1)} %get-tuple-element.62._), channel_id=1, source_target_pairs={{0,1},{1,0},{2,3},{3,2},{4,5},{5,4},{6,7},{7,6},{8,9},{9,8},{10,11... | collective-permute-start | bytes 12296 | tf_op jit(solution)/shard_map/ppermute | solution.py:521
  12.2 6.7 %collective-permute-start.8 = (f32[1,136,128]{2,1,0:T(8,128)S(1)}, f32[1,136,128]{2,1,0:T(8,128)S(1)}, u32[]{:S(2)}, u32[]{:S(2)}) collective-permute-start(f32[1,136,128]{2,1,0:T(8,128)S(1)} %bitcast.53), channel_id=1, source_target_pairs={{0,4},{1,5},{2,6},{3,7},{4,0},{5,1},{6,2},{7,3},{8,12},{9,13},{10,... | collective-permute-start | bytes 208904 | tf_op jit(solution)/shard_map/ppermute | solution.py:551
  18.9 7.8 %collective-permute-start.17 = (f32[2,136,128]{2,1,0:T(8,128)S(1)}, f32[2,136,128]{2,1,0:T(8,128)S(1)}, u32[]{:S(2)}, u32[]{:S(2)}) collective-permute-start(f32[2,136,128]{2,1,0:T(8,128)S(1)} %pad_maximum_fusion.1), channel_id=1, source_target_pairs={{0,2},{1,3},{2,0},{3,1},{4,6},{5,7},{6,4},{7,5},{8,10},{9,11},{10,... | collective-permute-start | bytes 417800 | tf_op jit(solution)/shard_map/ppermute | solution.py:551
  19.1 7.2 %collective-permute-start.4 = (f32[8,128]{1,0:T(8,128)S(1)}, f32[8,128]{1,0:T(8,128)S(1)}, u32[]{:S(2)}, u32[]{:S(2)}) collective-permute-start(f32[8,128]{1,0:T(8,128)S(1)} %get-tuple-element.69._), channel_id=1, source_target_pairs={{0,24},{1,25},{2,26},{3,27},{4,28},{5,29},{6,30},{7,31},{8,16},{9,... | collective-permute-start | bytes 12296 | tf_op jit(solution)/shard_map/ppermute | solution.py:521
  20.5 5.8 %collective-permute-start.5 = (f32[8,128]{1,0:T(8,128)S(1)}, f32[8,128]{1,0:T(8,128)S(1)}, u32[]{:S(2)}, u32[]{:S(2)}) collective-permute-start(f32[8,128]{1,0:T(8,128)S(1)} %get-tuple-element.69._), channel_id=1, source_target_pairs={{0,0},{1,2},{2,1},{3,4},{4,3},{5,6},{6,5},{7,7},{8,8},{9,10},{10,9... | collective-permute-start | bytes 12296 | tf_op jit(solution)/shard_map/ppermute | solution.py:521
  26.8 15.6 %collective-permute-start.18 = (f32[4,136,128]{2,1,0:T(8,128)S(1)}, f32[4,136,128]{2,1,0:T(8,128)S(1)}, u32[]{:S(2)}, u32[]{:S(2)}) collective-permute-start(f32[4,136,128]{2,1,0:T(8,128)S(1)} %pad_maximum_fusion), channel_id=1, source_target_pairs={{0,1},{1,0},{2,3},{3,2},{4,5},{5,4},{6,7},{7,6},{8,9},{9,8},{10,11... | collective-permute-start | bytes 835592 | tf_op jit(solution)/shard_map/ppermute | solution.py:551
  27.5 9.4 %collective-permute-start.10 = (f32[8,128]{1,0:T(8,128)S(1)}, f32[8,128]{1,0:T(8,128)S(1)}, u32[]{:S(2)}, u32[]{:S(2)}) collective-permute-start(f32[8,128]{1,0:T(8,128)S(1)} %get-tuple-element.74._), channel_id=1, source_target_pairs={{0,0},{1,2},{2,1},{3,4},{4,3},{5,6},{6,5},{7,7},{8,8},{9,10},{10,9... | collective-permute-start | bytes 12296 | tf_op jit(solution)/shard_map/ppermute | solution.py:521
  28.1 8.7 %collective-permute-start.11 = (f32[8,128]{1,0:T(8,128)S(1)}, f32[8,128]{1,0:T(8,128)S(1)}, u32[]{:S(2)}, u32[]{:S(2)}) collective-permute-start(f32[8,128]{1,0:T(8,128)S(1)} %get-tuple-element.74._), channel_id=1, source_target_pairs={{0,8},{1,9},{2,10},{3,11},{4,12},{5,13},{6,14},{7,15},{8,0},{9,1},... | collective-permute-start | bytes 12296 | tf_op jit(solution)/shard_map/ppermute | solution.py:521
  29.1 7.8 %collective-permute-start.12 = (f32[8,128]{1,0:T(8,128)S(1)}, f32[8,128]{1,0:T(8,128)S(1)}, u32[]{:S(2)}, u32[]{:S(2)}) collective-permute-start(f32[8,128]{1,0:T(8,128)S(1)} %get-tuple-element.74._), channel_id=1, source_target_pairs={{0,1},{1,0},{2,3},{3,2},{4,5},{5,4},{6,7},{7,6},{8,9},{9,8},{10,11... | collective-permute-start | bytes 12296 | tf_op jit(solution)/shard_map/ppermute | solution.py:521
  43.6 6.5 %collective-permute-start.19 = (f32[8,128]{1,0:T(8,128)S(1)}, f32[8,128]{1,0:T(8,128)S(1)}, u32[]{:S(2)}, u32[]{:S(2)}) collective-permute-start(f32[8,128]{1,0:T(8,128)S(1)} %get-tuple-element.90), channel_id=1, source_target_pairs={{0,24},{1,25},{2,26},{3,27},{4,28},{5,29},{6,30},{7,31},{8,16},{9,... | collective-permute-start | bytes 12296 | tf_op jit(solution)/shard_map/ppermute | solution.py:521
  51.8 6.2 %collective-permute-start.23 = (f32[8,128]{1,0:T(8,128)S(1)}, f32[8,128]{1,0:T(8,128)S(1)}, u32[]{:S(2)}, u32[]{:S(2)}) collective-permute-start(f32[8,128]{1,0:T(8,128)S(1)} %get-tuple-element.93), channel_id=1, source_target_pairs={{0,24},{1,25},{2,26},{3,27},{4,28},{5,29},{6,30},{7,31},{8,16},{9,... | collective-permute-start | bytes 12296 | tf_op jit(solution)/shard_map/ppermute | solution.py:521
  70.2 6.2 %collective-permute-start.30 = (f32[8,128]{1,0:T(8,128)S(1)}, f32[8,128]{1,0:T(8,128)S(1)}, u32[]{:S(2)}, u32[]{:S(2)}) collective-permute-start(f32[8,128]{1,0:T(8,128)S(1)} %get-tuple-element.100), channel_id=1, source_target_pairs={{0,24},{1,25},{2,26},{3,27},{4,28},{5,29},{6,30},{7,31},{8,16},{9,... | collective-permute-start | bytes 12296 | tf_op jit(solution)/shard_map/ppermute | solution.py:521
  77.5 5.9 %collective-permute-start.34 = (f32[8,128]{1,0:T(8,128)S(1)}, f32[8,128]{1,0:T(8,128)S(1)}, u32[]{:S(2)}, u32[]{:S(2)}) collective-permute-start(f32[8,128]{1,0:T(8,128)S(1)} %get-tuple-element.102), channel_id=1, source_target_pairs={{0,24},{1,25},{2,26},{3,27},{4,28},{5,29},{6,30},{7,31},{8,16},{9,... | collective-permute-start | bytes 12296 | tf_op jit(solution)/shard_map/ppermute | solution.py:521
  84.6 6.8 %collective-permute-start.38 = (f32[8,128]{1,0:T(8,128)S(1)}, f32[8,128]{1,0:T(8,128)S(1)}, u32[]{:S(2)}, u32[]{:S(2)}) collective-permute-start(f32[8,128]{1,0:T(8,128)S(1)} %get-tuple-element.105), channel_id=1, source_target_pairs={{0,24},{1,25},{2,26},{3,27},{4,28},{5,29},{6,30},{7,31},{8,16},{9,... | collective-permute-start | bytes 12296 | tf_op jit(solution)/shard_map/ppermute | solution.py:521
  92.7 7.5 %collective-permute-start.42 = (f32[8,128]{1,0:T(8,128)S(1)}, f32[8,128]{1,0:T(8,128)S(1)}, u32[]{:S(2)}, u32[]{:S(2)}) collective-permute-start(f32[8,128]{1,0:T(8,128)S(1)} %get-tuple-element.109), channel_id=1, source_target_pairs={{0,24},{1,25},{2,26},{3,27},{4,28},{5,29},{6,30},{7,31},{8,16},{9,... | collective-permute-start | bytes 12296 | tf_op jit(solution)/shard_map/ppermute | solution.py:521
  93.9 6.3 %collective-permute-start.43 = (f32[8,128]{1,0:T(8,128)S(1)}, f32[8,128]{1,0:T(8,128)S(1)}, u32[]{:S(2)}, u32[]{:S(2)}) collective-permute-start(f32[8,128]{1,0:T(8,128)S(1)} %get-tuple-element.109), channel_id=1, source_target_pairs={{0,0},{1,2},{2,1},{3,4},{4,3},{5,6},{6,5},{7,7},{8,8},{9,10},{10,9... | collective-permute-start | bytes 12296 | tf_op jit(solution)/shard_map/ppermute | solution.py:521
  100.6 7.8 %collective-permute-start.46 = (f32[8,128]{1,0:T(8,128)S(1)}, f32[8,128]{1,0:T(8,128)S(1)}, u32[]{:S(2)}, u32[]{:S(2)}) collective-permute-start(f32[8,128]{1,0:T(8,128)S(1)} %get-tuple-element.112), channel_id=1, source_target_pairs={{0,24},{1,25},{2,26},{3,27},{4,28},{5,29},{6,30},{7,31},{8,16},{9,... | collective-permute-start | bytes 12296 | tf_op jit(solution)/shard_map/ppermute | solution.py:521
  102.4 6.0 %collective-permute-start.47 = (f32[8,128]{1,0:T(8,128)S(1)}, f32[8,128]{1,0:T(8,128)S(1)}, u32[]{:S(2)}, u32[]{:S(2)}) collective-permute-start(f32[8,128]{1,0:T(8,128)S(1)} %get-tuple-element.112), channel_id=1, source_target_pairs={{0,0},{1,2},{2,1},{3,4},{4,3},{5,6},{6,5},{7,7},{8,8},{9,10},{10,9... | collective-permute-start | bytes 12296 | tf_op jit(solution)/shard_map/ppermute | solution.py:521
  108.7 7.0 %collective-permute-start.50 = (f32[8,128]{1,0:T(8,128)S(1)}, f32[8,128]{1,0:T(8,128)S(1)}, u32[]{:S(2)}, u32[]{:S(2)}) collective-permute-start(f32[8,128]{1,0:T(8,128)S(1)} %get-tuple-element.115), channel_id=1, source_target_pairs={{0,24},{1,25},{2,26},{3,27},{4,28},{5,29},{6,30},{7,31},{8,16},{9,... | collective-permute-start | bytes 12296 | tf_op jit(solution)/shard_map/ppermute | solution.py:521
  116.7 7.3 %collective-permute-start.54 = (f32[8,128]{1,0:T(8,128)S(1)}, f32[8,128]{1,0:T(8,128)S(1)}, u32[]{:S(2)}, u32[]{:S(2)}) collective-permute-start(f32[8,128]{1,0:T(8,128)S(1)} %get-tuple-element.118), channel_id=1, source_target_pairs={{0,24},{1,25},{2,26},{3,27},{4,28},{5,29},{6,30},{7,31},{8,16},{9,... | collective-permute-start | bytes 12296 | tf_op jit(solution)/shard_map/ppermute | solution.py:521
  118.1 5.9 %collective-permute-start.55 = (f32[8,128]{1,0:T(8,128)S(1)}, f32[8,128]{1,0:T(8,128)S(1)}, u32[]{:S(2)}, u32[]{:S(2)}) collective-permute-start(f32[8,128]{1,0:T(8,128)S(1)} %get-tuple-element.118), channel_id=1, source_target_pairs={{0,0},{1,2},{2,1},{3,4},{4,3},{5,6},{6,5},{7,7},{8,8},{9,10},{10,9... | collective-permute-start | bytes 12296 | tf_op jit(solution)/shard_map/ppermute | solution.py:521
  (47 other events, 194.3 us)

commit v5 on v4

--- a/solution.py
+++ b/solution.py
@@ -167,9 +167,11 @@
     return result
 
 
-def fine_step(factors, *refs):
+def fine_step(factors, last, *refs):
     arrivals = refs[:5]
-    (r_ref, v_ref, c_ref, m_ref, x_ref, d_ref, s_ref, xo_ref, do_ref, out_ref, edge_ref, pad_ref) = refs[5:]
+    r_ref, v_ref, c_ref, m_ref, x_ref, d_ref, s_ref, xo_ref, out_ref = refs[5:14]
+    do_ref = refs[14] if last is False else None
+    edge_ref, pad_ref = refs[-2:]
     keep, gain = factors
     lines = r_ref.shape[1]
     resid = fine_remote(arrivals, r_ref, v_ref, c_ref, edge_ref)
@@ -180,7 +182,8 @@
             if keep:
                 d = keep * d_ref[i, rows, :] + d
             x = x_ref[i, rows, :] + d
-            do_ref[i, rows, :] = d
+            if not last:
+                do_ref[i, rows, :] = d
             xo_ref[i, rows, :] = x
             for twice in range(2):
                 pad_ref[pl.ds((twice * 4 + i) * lines + h * SUBS, SUBS), :] = x
@@ -338,14 +341,17 @@
     return xs, ds
 
 
-def middle_step(factors, *refs):
+def middle_step(factors, last, *refs):
     arrivals = refs[:5]
-    (b_ref, m_ref, x_ref, d_ref, v_ref, c_ref, s_ref, xo_ref, do_ref, out_ref, edge_ref, pad_ref) = refs[5:]
+    b_ref, m_ref, x_ref, d_ref, v_ref, c_ref, s_ref, xo_ref, out_ref = refs[5:14]
+    do_ref = refs[14] if last is False else None
+    edge_ref, pad_ref = refs[-2:]
     resid = middle_residual(arrivals, b_ref, x_ref, v_ref, c_ref, edge_ref)
     xs, ds = middle_update(factors, resid, m_ref, x_ref, d_ref)
     for i in range(4):
         xo_ref[i] = xs[i]
-        do_ref[i] = ds[i]
+        if not last:
+            do_ref[i] = ds[i]
         middle_pad(pad_ref, i, xs[i])
     middle_out(out_ref, pad_ref, s_ref)
 
@@ -401,9 +407,8 @@
 def coarse_tables(group, *refs):
     vo_ref, co_ref, mo_ref, pad_ref = refs[-4:]
     me = refs[0][0]
-    for piece, places in zip(refs[1:-5], span_places(group)):
-        for t, place in enumerate(places):
-            pad_ref[place] = piece[t]
+    for q in range(group):
+        pad_ref[me ^ q] = refs[1][q]
     for h in range(group // SUBS):
         rows = pl.ds(h * SUBS, SUBS)
         for ki in range(NNZ * 4):
@@ -507,20 +512,27 @@
 def exchange(mesh, out, which):
     slabs, count = mesh.shape["stream"], mesh.shape["span"]
 
-    def partner(index, size, odd, closed):
-        other = index ^ 1 if not odd else (index + 1 if index % 2 else index - 1)
-        return other % size if closed or 0 <= other < size else index
-
-    def swap(odd_s, odd_p):
+    def swap(partner):
         pairs = []
         for a in range(slabs):
             for b in range(count):
-                to_a = a if odd_s is None else partner(a, slabs, odd_s, True)
-                to_b = b if odd_p is None else partner(b, count, odd_p, False)
+                to_a, to_b = partner(a, b)
                 pairs.append((a * count + b, to_a * count + to_b))
         return lax.ppermute(out, AXES, pairs)
 
-    return [swap(True, None), swap(None, True), swap(False, None), swap(None, False), which]
+    def odd(index):
+        return index + 1 if index % 2 else index - 1
+
+    def span_odd(a, b):
+        return (a, odd(b)) if 0 <= odd(b) < count else (a ^ 1, b)
+
+    return [
+        swap(lambda a, b: (odd(a) % slabs, b)),
+        swap(span_odd),
+        swap(lambda a, b: (a ^ 1, b)),
+        swap(lambda a, b: (a, b ^ 1)),
+        which,
+    ]
 
 
 def halo_choice(a, b, count):
@@ -589,23 +601,25 @@
 
     def fine_next(which, arrived, resid, x, d, after=()):
         args = arrived + [resid, v1, c1, m1, x, d, send1]
-        return call(
-            lambda *refs: fine_step(factors[which], *(refs[: len(args)] + refs[len(args) + len(after) :])),
-            [vec1, vec1, tile],
+        last = which == KSM - 1
+        result = call(
+            lambda *refs: fine_step(
+                factors[which], last, *(refs[: len(args)] + refs[len(args) + len(after) :])
+            ),
+            [vec1, tile] + ([] if last else [vec1]),
             args + list(after),
             [edge, pad1],
             free=range(len(args), len(args) + len(after)),
         )
+        return result[0], (None if last else result[2]), result[1]
 
     arrived = exchange(mesh, out, choice)
     own3, _ = lax.optimization_barrier((own3, out))
-    pieces3 = span_stage(mesh, [own3[None]])
+    slab3 = lax.all_gather(own3, "span", axis=0)
     resid = fine_part(x1)
     x1, d1, out = fine_next(1, arrived, resid, x1, d1)
 
     arrived = exchange(mesh, out, choice)
-    pieces3, _ = lax.optimization_barrier((pieces3, out))
-    pieces3 = span_stage(mesh, pieces3)
     resid = fine_part(x1)
     w1, agg1, place1 = call(
         fine_tables,
@@ -613,12 +627,9 @@
         [native_rows(fine_weights), fine_order, fine_order.reshape(lines, LANES), out],
         free=(3,),
     )
-    x1, d1, out = fine_next(2, arrived, resid, x1, d1, [pieces3[1]])
-
-    arrived = exchange(mesh, out, choice)
-    pieces3, _ = lax.optimization_barrier((pieces3, out))
-    while sum(piece.shape[0] for piece in pieces3) < group:
-        pieces3 = span_stage(mesh, pieces3)
+    x1, d1, out = fine_next(2, arrived, resid, x1, d1, [])
+
+    arrived = exchange(mesh, out, choice)
     resid = fine_part(x1)
     send2, v2, c2, m2, w2, agg2, place2 = call(
         middle_tables,
@@ -644,21 +655,25 @@
 
     def middle_next(which, arrived, x, d, after=()):
         args = arrived + [b2, m2, x, d, v2, c2, send2]
-        return call(
-            lambda *refs: middle_step(factors[which], *(refs[: len(args)] + refs[len(args) + len(after) :])),
-            [vec2, vec2, tile],
+        last = which == KSM - 1
+        result = call(
+            lambda *refs: middle_step(
+                factors[which], last, *(refs[: len(args)] + refs[len(args) + len(after) :])
+            ),
+            [vec2, tile] + ([] if last else [vec2]),
             args + list(after),
             [edge, pad2],
             free=range(len(args), len(args) + len(after)),
         )
+        return result[0], (None if last else result[2]), result[1]
 
     arrived = exchange(mesh, out, choice)
     v3, c3, m3 = call(
         lambda *refs: coarse_tables(group, *refs),
         [shape(NNZ, 4, 4, group, LANES), shape(NNZ, group, LANES, dtype=I32), shape(4, group, LANES)],
-        [me.reshape(1)] + pieces3 + [out],
+        [me.reshape(1), slab3, out],
         [vmem(group, NNZ * 17, LANES)],
-        free=(1 + len(pieces3),),
+        free=(2,),
         smem=(0,),
     )
     x2, d2, out = middle_next(1, arrived, x2, d2, [m3])
@@ -692,6 +707,7 @@
         arrived + [b2, m2, x2, d2, v2, c2, x1, w1, agg1, send1],
         [edge, vmem(4, SUBS, LANES), pad1],
     )
+    d1 = x1
     for which in range(KSM):
         arrived = exchange(mesh, out, choice)
         resid = fine_part(x1)

time: 126 us -> 115 us (0.913)
  starting transfers between devices: 88.4 us -> 54.5 us
  blocking collectives: 0 us -> 15 us
  waiting for transfers between devices: 11.1 us -> 21.4 us
    ppermute x52, starting transfers between devices: 79.9 us -> 54.1 us  [swap(): return lax.ppermute(out, AXES, pairs)]
    all_gather x0 -> x1, blocking collectives: none -> 15 us  [per_device(): slab3 = lax.all_gather(own3, 'span', axis=0)]
    ppermute x6 -> x3, starting transfers between devices: 8.54 us -> 0.41 us  [span_stage(): return pieces + [lax.ppermute(held, AXES, pairs)]]
    ppermute x52, waiting for transfers between devices: 4.67 us -> 12.5 us  [swap(): return lax.ppermute(out, AXES, pairs)]
    ppermute x6 -> x3, waiting for transfers between devices: 6.41 us -> 8.99 us  [span_stage(): return pieces + [lax.ppermute(held, AXES, pairs)]]
    unnamed x26 -> x28, local copies, waits for them, and re-layouts: 3.35 us -> 4.03 us
  transfers between devices with their start and end apart: 58 -> 55, of which waited for: 10 -> 21; matrix products, arithmetic and copies ran while one was open for 1% -> 0% of each run, Pallas kernels for 11% -> 11%
where the time goes in v5:
time: 115 us
  starting transfers between devices  54.5 us (47%)
  waiting for transfers between devices  21.4 us (19%)
  Pallas kernels  18.7 us (16%)
  blocking collectives  15 us (13%)
  local copies, waits for them, and re-layouts  4.03 us (4%)
    ppermute x52, starting transfers between devices, swap(): return lax.ppermute(out, AXES, pairs)  54.1 us
    pallas_call x26, Pallas kernels, call(): pl.pallas_call(body, out_shape=shapes, in_specs=specs, out_specs=[pl.Bloc...  18.7 us
    all_gather x1, blocking collectives, per_device(): slab3 = lax.all_gather(own3, 'span', axis=0)  15 us
    ppermute x52, waiting for transfers between devices, swap(): return lax.ppermute(out, AXES, pairs)  12.5 us
    ppermute x3, waiting for transfers between devices, span_stage(): return pieces + [lax.ppermute(held, AXES, pairs)]  8.99 us
    unnamed x28, local copies, waits for them, and re-layouts  4.03 us
  transfers between devices with their start and end apart: 55, of which 21 were waited for; matrix products, arithmetic and copies ran while one was open for 0% of the time, Pallas kernels for 11%

profile of v5, /device:TPU:0, one launch (start us, length us, event | category | flops | bytes accessed | tf_op | source)
XLA Modules:
  0.0 114.7 jit_solution(687918355464021132)
XLA Ops:
  3.5 4.0 %collective-permute-start = (f32[8,128]{1,0:T(8,128)S(1)}, f32[8,128]{1,0:T(8,128)S(1)}, u32[]{:S(2)}, u32[]{:S(2)}) collective-permute-start(f32[8,128]{1,0:T(8,128)S(1)} %get-tuple-element.56._), channel_id=1, source_target_pairs={{0,24},{1,25},{2,26},{3,27},{4,28},{5,29},{6,30},{7,31},{8,16},{9,... | collective-permute-start | bytes 12296 | tf_op jit(solution)/shard_map/ppermute | solution.py:521
  17.8 1.6 %collective-permute-start.10 = (f32[8,128]{1,0:T(8,128)S(1)}, f32[8,128]{1,0:T(8,128)S(1)}, u32[]{:S(2)}, u32[]{:S(2)}) collective-permute-start(f32[8,128]{1,0:T(8,128)S(1)} %get-tuple-element.66._), channel_id=1, source_target_pairs={{0,8},{1,9},{2,10},{3,11},{4,12},{5,13},{6,14},{7,15},{8,0},{9,1},... | collective-permute-start | bytes 12296 | tf_op jit(solution)/shard_map/ppermute | solution.py:521
  27.1 1.5 %collective-permute-start.13 = (f32[8,128]{1,0:T(8,128)S(1)}, f32[8,128]{1,0:T(8,128)S(1)}, u32[]{:S(2)}, u32[]{:S(2)}) collective-permute-start(f32[8,128]{1,0:T(8,128)S(1)} %get-tuple-element.72.refs_2_), channel_id=1, source_target_pairs={{0,8},{1,2},{2,1},{3,4},{4,3},{5,6},{6,5},{7,15},{8,0},{9,10},{10,... | collective-permute-start | bytes 12296 | tf_op jit(solution)/shard_map/ppermute | solution.py:521
  29.1 15.0 %all-gather = f32[1088,128]{1,0:T(8,128)S(1)} all-gather(f32[136,128]{1,0:T(8,128)S(1)} %pad_maximum_fusion), channel_id=2, replica_groups=mesh['stream'=4,'span'=8] {'span'}, dimensions={0}, use_global_device_ids=true | all-gather | bytes 626688 | tf_op jit(solution)/shard_map/all_gather | solution.py:618
  44.9 2.7 %collective-permute-start.16 = (f32[8,128]{1,0:T(8,128)S(1)}, f32[8,128]{1,0:T(8,128)S(1)}, u32[]{:S(2)}, u32[]{:S(2)}) collective-permute-start(f32[8,128]{1,0:T(8,128)S(1)} %get-tuple-element.79), channel_id=1, source_target_pairs={{0,24},{1,25},{2,26},{3,27},{4,28},{5,29},{6,30},{7,31},{8,16},{9,... | collective-permute-start | bytes 12296 | tf_op jit(solution)/shard_map/ppermute | solution.py:521
  48.0 1.6 %collective-permute-start.18 = (f32[8,128]{1,0:T(8,128)S(1)}, f32[8,128]{1,0:T(8,128)S(1)}, u32[]{:S(2)}, u32[]{:S(2)}) collective-permute-start(f32[8,128]{1,0:T(8,128)S(1)} %get-tuple-element.79), channel_id=1, source_target_pairs={{0,8},{1,9},{2,10},{3,11},{4,12},{5,13},{6,14},{7,15},{8,0},{9,1},... | collective-permute-start | bytes 12296 | tf_op jit(solution)/shard_map/ppermute | solution.py:521
  49.6 1.6 %collective-permute-done.17.refs_1_ = f32[8,128]{1,0:T(8,128)S(1)} collective-permute-done((f32[8,128]{1,0:T(8,128)S(1)}, f32[8,128]{1,0:T(8,128)S(1)}, u32[]{:S(2)}, u32[]{:S(2)}) %collective-permute-start.17) | collective-permute-done | bytes 4128 | tf_op jit(solution)/shard_map/ppermute | solution.py:521
  53.8 1.7 %collective-permute-start.22 = (f32[8,128]{1,0:T(8,128)S(1)}, f32[8,128]{1,0:T(8,128)S(1)}, u32[]{:S(2)}, u32[]{:S(2)}) collective-permute-start(f32[8,128]{1,0:T(8,128)S(1)} %get-tuple-element.82), channel_id=1, source_target_pairs={{0,8},{1,9},{2,10},{3,11},{4,12},{5,13},{6,14},{7,15},{8,0},{9,1},... | collective-permute-start | bytes 12296 | tf_op jit(solution)/shard_map/ppermute | solution.py:521
  57.8 4.5 %collective-permute-done.24.refs_1_ = f32[1,8,128]{2,1,0:T(8,128)S(1)} collective-permute-done((f32[1,8,128]{2,1,0:T(8,128)S(1)}, f32[1,8,128]{2,1,0:T(8,128)S(1)}, u32[]{:S(2)}, u32[]{:S(2)}) %collective-permute-start.24) | collective-permute-done | bytes 4128 | tf_op jit(solution)/shard_map/ppermute | solution.py:563
  62.7 3.3 %collective-permute-done.25.refs_2_ = f32[2,8,128]{2,1,0:T(8,128)S(1)} collective-permute-done((f32[2,8,128]{2,1,0:T(8,128)S(1)}, f32[2,8,128]{2,1,0:T(8,128)S(1)}, u32[]{:S(2)}, u32[]{:S(2)}) %collective-permute-start.25) | collective-permute-done | bytes 8224 | tf_op jit(solution)/shard_map/ppermute | solution.py:563
  68.4 2.7 %collective-permute-start.27 = (f32[8,128]{1,0:T(8,128)S(1)}, f32[8,128]{1,0:T(8,128)S(1)}, u32[]{:S(2)}, u32[]{:S(2)}) collective-permute-start(f32[8,128]{1,0:T(8,128)S(1)} %get-tuple-element.89), channel_id=1, source_target_pairs={{0,24},{1,25},{2,26},{3,27},{4,28},{5,29},{6,30},{7,31},{8,16},{9,... | collective-permute-start | bytes 12296 | tf_op jit(solution)/shard_map/ppermute | solution.py:521
  71.5 1.5 %collective-permute-start.29 = (f32[8,128]{1,0:T(8,128)S(1)}, f32[8,128]{1,0:T(8,128)S(1)}, u32[]{:S(2)}, u32[]{:S(2)}) collective-permute-start(f32[8,128]{1,0:T(8,128)S(1)} %get-tuple-element.89), channel_id=1, source_target_pairs={{0,8},{1,9},{2,10},{3,11},{4,12},{5,13},{6,14},{7,15},{8,0},{9,1},... | collective-permute-start | bytes 12296 | tf_op jit(solution)/shard_map/ppermute | solution.py:521
  73.1 1.6 %collective-permute-done.28.refs_1_ = f32[8,128]{1,0:T(8,128)S(1)} collective-permute-done((f32[8,128]{1,0:T(8,128)S(1)}, f32[8,128]{1,0:T(8,128)S(1)}, u32[]{:S(2)}, u32[]{:S(2)}) %collective-permute-start.28) | collective-permute-done | bytes 4128 | tf_op jit(solution)/shard_map/ppermute | solution.py:521
  77.3 1.7 %collective-permute-start.33 = (f32[8,128]{1,0:T(8,128)S(1)}, f32[8,128]{1,0:T(8,128)S(1)}, u32[]{:S(2)}, u32[]{:S(2)}) collective-permute-start(f32[8,128]{1,0:T(8,128)S(1)} %get-tuple-element.91), channel_id=1, source_target_pairs={{0,8},{1,9},{2,10},{3,11},{4,12},{5,13},{6,14},{7,15},{8,0},{9,1},... | collective-permute-start | bytes 12296 | tf_op jit(solution)/shard_map/ppermute | solution.py:521
  81.3 2.7 %collective-permute-start.35 = (f32[8,128]{1,0:T(8,128)S(1)}, f32[8,128]{1,0:T(8,128)S(1)}, u32[]{:S(2)}, u32[]{:S(2)}) collective-permute-start(f32[8,128]{1,0:T(8,128)S(1)} %get-tuple-element.94), channel_id=1, source_target_pairs={{0,24},{1,25},{2,26},{3,27},{4,28},{5,29},{6,30},{7,31},{8,16},{9,... | collective-permute-start | bytes 12296 | tf_op jit(solution)/shard_map/ppermute | solution.py:521
  84.4 1.5 %collective-permute-start.37 = (f32[8,128]{1,0:T(8,128)S(1)}, f32[8,128]{1,0:T(8,128)S(1)}, u32[]{:S(2)}, u32[]{:S(2)}) collective-permute-start(f32[8,128]{1,0:T(8,128)S(1)} %get-tuple-element.94), channel_id=1, source_target_pairs={{0,8},{1,9},{2,10},{3,11},{4,12},{5,13},{6,14},{7,15},{8,0},{9,1},... | collective-permute-start | bytes 12296 | tf_op jit(solution)/shard_map/ppermute | solution.py:521
  85.9 1.6 %collective-permute-done.36.refs_1_ = f32[8,128]{1,0:T(8,128)S(1)} collective-permute-done((f32[8,128]{1,0:T(8,128)S(1)}, f32[8,128]{1,0:T(8,128)S(1)}, u32[]{:S(2)}, u32[]{:S(2)}) %collective-permute-start.36) | collective-permute-done | bytes 4128 | tf_op jit(solution)/shard_map/ppermute | solution.py:521
  88.5 1.5 %collective-permute-start.39 = (f32[8,128]{1,0:T(8,128)S(1)}, f32[8,128]{1,0:T(8,128)S(1)}, u32[]{:S(2)}, u32[]{:S(2)}) collective-permute-start(f32[8,128]{1,0:T(8,128)S(1)} %get-tuple-element.98), channel_id=1, source_target_pairs={{0,24},{1,25},{2,26},{3,27},{4,28},{5,29},{6,30},{7,31},{8,16},{9,... | collective-permute-start | bytes 12296 | tf_op jit(solution)/shard_map/ppermute | solution.py:521
  90.3 1.7 %collective-permute-start.41 = (f32[8,128]{1,0:T(8,128)S(1)}, f32[8,128]{1,0:T(8,128)S(1)}, u32[]{:S(2)}, u32[]{:S(2)}) collective-permute-start(f32[8,128]{1,0:T(8,128)S(1)} %get-tuple-element.98), channel_id=1, source_target_pairs={{0,8},{1,9},{2,10},{3,11},{4,12},{5,13},{6,14},{7,15},{8,0},{9,1},... | collective-permute-start | bytes 12296 | tf_op jit(solution)/shard_map/ppermute | solution.py:521
  94.3 2.7 %collective-permute-start.43 = (f32[8,128]{1,0:T(8,128)S(1)}, f32[8,128]{1,0:T(8,128)S(1)}, u32[]{:S(2)}, u32[]{:S(2)}) collective-permute-start(f32[8,128]{1,0:T(8,128)S(1)} %get-tuple-element.100), channel_id=1, source_target_pairs={{0,24},{1,25},{2,26},{3,27},{4,28},{5,29},{6,30},{7,31},{8,16},{9,... | collective-permute-start | bytes 12296 | tf_op jit(solution)/shard_map/ppermute | solution.py:521
  97.4 1.5 %collective-permute-start.45 = (f32[8,128]{1,0:T(8,128)S(1)}, f32[8,128]{1,0:T(8,128)S(1)}, u32[]{:S(2)}, u32[]{:S(2)}) collective-permute-start(f32[8,128]{1,0:T(8,128)S(1)} %get-tuple-element.100), channel_id=1, source_target_pairs={{0,8},{1,9},{2,10},{3,11},{4,12},{5,13},{6,14},{7,15},{8,0},{9,1},... | collective-permute-start | bytes 12296 | tf_op jit(solution)/shard_map/ppermute | solution.py:521
  103.2 1.7 %collective-permute-start.49 = (f32[8,128]{1,0:T(8,128)S(1)}, f32[8,128]{1,0:T(8,128)S(1)}, u32[]{:S(2)}, u32[]{:S(2)}) collective-permute-start(f32[8,128]{1,0:T(8,128)S(1)} %get-tuple-element.103), channel_id=1, source_target_pairs={{0,8},{1,9},{2,10},{3,11},{4,12},{5,13},{6,14},{7,15},{8,0},{9,1},... | collective-permute-start | bytes 12296 | tf_op jit(solution)/shard_map/ppermute | solution.py:521
  107.1 2.7 %collective-permute-start.51 = (f32[8,128]{1,0:T(8,128)S(1)}, f32[8,128]{1,0:T(8,128)S(1)}, u32[]{:S(2)}, u32[]{:S(2)}) collective-permute-start(f32[8,128]{1,0:T(8,128)S(1)} %get-tuple-element.106), channel_id=1, source_target_pairs={{0,24},{1,25},{2,26},{3,27},{4,28},{5,29},{6,30},{7,31},{8,16},{9,... | collective-permute-start | bytes 12296 | tf_op jit(solution)/shard_map/ppermute | solution.py:521
  110.3 1.5 %collective-permute-start.53 = (f32[8,128]{1,0:T(8,128)S(1)}, f32[8,128]{1,0:T(8,128)S(1)}, u32[]{:S(2)}, u32[]{:S(2)}) collective-permute-start(f32[8,128]{1,0:T(8,128)S(1)} %get-tuple-element.106), channel_id=1, source_target_pairs={{0,8},{1,9},{2,10},{3,11},{4,12},{5,13},{6,14},{7,15},{8,0},{9,1},... | collective-permute-start | bytes 12296 | tf_op jit(solution)/shard_map/ppermute | solution.py:521
  (150 shorter events, 49.8 us)
Async XLA Ops:
  3.5 8.0 %collective-permute-start = (f32[8,128]{1,0:T(8,128)S(1)}, f32[8,128]{1,0:T(8,128)S(1)}, u32[]{:S(2)}, u32[]{:S(2)}) collective-permute-start(f32[8,128]{1,0:T(8,128)S(1)} %get-tuple-element.56._), channel_id=1, source_target_pairs={{0,24},{1,25},{2,26},{3,27},{4,28},{5,29},{6,30},{7,31},{8,16},{9,... | collective-permute-start | bytes 12296 | tf_op jit(solution)/shard_map/ppermute | solution.py:521
  7.4 4.1 %collective-permute-start.1 = (f32[8,128]{1,0:T(8,128)S(1)}, f32[8,128]{1,0:T(8,128)S(1)}, u32[]{:S(2)}, u32[]{:S(2)}) collective-permute-start(f32[8,128]{1,0:T(8,128)S(1)} %get-tuple-element.56._), channel_id=1, source_target_pairs={{0,8},{1,2},{2,1},{3,4},{4,3},{5,6},{6,5},{7,15},{8,0},{9,10},{10,... | collective-permute-start | bytes 12296 | tf_op jit(solution)/shard_map/ppermute | solution.py:521
  11.9 5.0 %collective-permute-start.4 = (f32[8,128]{1,0:T(8,128)S(1)}, f32[8,128]{1,0:T(8,128)S(1)}, u32[]{:S(2)}, u32[]{:S(2)}) collective-permute-start(f32[8,128]{1,0:T(8,128)S(1)} %get-tuple-element.63._), channel_id=1, source_target_pairs={{0,24},{1,25},{2,26},{3,27},{4,28},{5,29},{6,30},{7,31},{8,16},{9,... | collective-permute-start | bytes 12296 | tf_op jit(solution)/shard_map/ppermute | solution.py:521
  17.8 8.3 %collective-permute-start.10 = (f32[8,128]{1,0:T(8,128)S(1)}, f32[8,128]{1,0:T(8,128)S(1)}, u32[]{:S(2)}, u32[]{:S(2)}) collective-permute-start(f32[8,128]{1,0:T(8,128)S(1)} %get-tuple-element.66._), channel_id=1, source_target_pairs={{0,8},{1,9},{2,10},{3,11},{4,12},{5,13},{6,14},{7,15},{8,0},{9,1},... | collective-permute-start | bytes 12296 | tf_op jit(solution)/shard_map/ppermute | solution.py:521
  19.4 6.7 %collective-permute-start.11 = (f32[8,128]{1,0:T(8,128)S(1)}, f32[8,128]{1,0:T(8,128)S(1)}, u32[]{:S(2)}, u32[]{:S(2)}) collective-permute-start(f32[8,128]{1,0:T(8,128)S(1)} %get-tuple-element.66._), channel_id=1, source_target_pairs={{0,1},{1,0},{2,3},{3,2},{4,5},{5,4},{6,7},{7,6},{8,9},{9,8},{10,11... | collective-permute-start | bytes 12296 | tf_op jit(solution)/shard_map/ppermute | solution.py:521
  19.4 6.7 %collective-permute-start.8 = (f32[8,128]{1,0:T(8,128)S(1)}, f32[8,128]{1,0:T(8,128)S(1)}, u32[]{:S(2)}, u32[]{:S(2)}) collective-permute-start(f32[8,128]{1,0:T(8,128)S(1)} %get-tuple-element.66._), channel_id=1, source_target_pairs={{0,24},{1,25},{2,26},{3,27},{4,28},{5,29},{6,30},{7,31},{8,16},{9,... | collective-permute-start | bytes 12296 | tf_op jit(solution)/shard_map/ppermute | solution.py:521
  20.9 5.2 %collective-permute-start.9 = (f32[8,128]{1,0:T(8,128)S(1)}, f32[8,128]{1,0:T(8,128)S(1)}, u32[]{:S(2)}, u32[]{:S(2)}) collective-permute-start(f32[8,128]{1,0:T(8,128)S(1)} %get-tuple-element.66._), channel_id=1, source_target_pairs={{0,8},{1,2},{2,1},{3,4},{4,3},{5,6},{6,5},{7,15},{8,0},{9,10},{10,... | collective-permute-start | bytes 12296 | tf_op jit(solution)/shard_map/ppermute | solution.py:521
  26.7 17.8 %collective-permute-start.12 = (f32[8,128]{1,0:T(8,128)S(1)}, f32[8,128]{1,0:T(8,128)S(1)}, u32[]{:S(2)}, u32[]{:S(2)}) collective-permute-start(f32[8,128]{1,0:T(8,128)S(1)} %get-tuple-element.72.refs_2_), channel_id=1, source_target_pairs={{0,24},{1,25},{2,26},{3,27},{4,28},{5,29},{6,30},{7,31},{8,16},{9,... | collective-permute-start | bytes 12296 | tf_op jit(solution)/shard_map/ppermute | solution.py:521
  27.1 17.4 %collective-permute-start.13 = (f32[8,128]{1,0:T(8,128)S(1)}, f32[8,128]{1,0:T(8,128)S(1)}, u32[]{:S(2)}, u32[]{:S(2)}) collective-permute-start(f32[8,128]{1,0:T(8,128)S(1)} %get-tuple-element.72.refs_2_), channel_id=1, source_target_pairs={{0,8},{1,2},{2,1},{3,4},{4,3},{5,6},{6,5},{7,15},{8,0},{9,10},{10,... | collective-permute-start | bytes 12296 | tf_op jit(solution)/shard_map/ppermute | solution.py:521
  28.6 15.9 %collective-permute-start.14 = (f32[8,128]{1,0:T(8,128)S(1)}, f32[8,128]{1,0:T(8,128)S(1)}, u32[]{:S(2)}, u32[]{:S(2)}) collective-permute-start(f32[8,128]{1,0:T(8,128)S(1)} %get-tuple-element.72.refs_2_), channel_id=1, source_target_pairs={{0,8},{1,9},{2,10},{3,11},{4,12},{5,13},{6,14},{7,15},{8,0},{9,1},... | collective-permute-start | bytes 12296 | tf_op jit(solution)/shard_map/ppermute | solution.py:521
  29.1 15.4 %collective-permute-start.15 = (f32[8,128]{1,0:T(8,128)S(1)}, f32[8,128]{1,0:T(8,128)S(1)}, u32[]{:S(2)}, u32[]{:S(2)}) collective-permute-start(f32[8,128]{1,0:T(8,128)S(1)} %get-tuple-element.72.refs_2_), channel_id=1, source_target_pairs={{0,1},{1,0},{2,3},{3,2},{4,5},{5,4},{6,7},{7,6},{8,9},{9,8},{10,11... | collective-permute-start | bytes 12296 | tf_op jit(solution)/shard_map/ppermute | solution.py:521
  44.9 4.7 %collective-permute-start.16 = (f32[8,128]{1,0:T(8,128)S(1)}, f32[8,128]{1,0:T(8,128)S(1)}, u32[]{:S(2)}, u32[]{:S(2)}) collective-permute-start(f32[8,128]{1,0:T(8,128)S(1)} %get-tuple-element.79), channel_id=1, source_target_pairs={{0,24},{1,25},{2,26},{3,27},{4,28},{5,29},{6,30},{7,31},{8,16},{9,... | collective-permute-start | bytes 12296 | tf_op jit(solution)/shard_map/ppermute | solution.py:521
  47.5 3.6 %collective-permute-start.17 = (f32[8,128]{1,0:T(8,128)S(1)}, f32[8,128]{1,0:T(8,128)S(1)}, u32[]{:S(2)}, u32[]{:S(2)}) collective-permute-start(f32[8,128]{1,0:T(8,128)S(1)} %get-tuple-element.79), channel_id=1, source_target_pairs={{0,8},{1,2},{2,1},{3,4},{4,3},{5,6},{6,5},{7,15},{8,0},{9,10},{10,... | collective-permute-start | bytes 12296 | tf_op jit(solution)/shard_map/ppermute | solution.py:521
  52.0 4.5 %collective-permute-start.20 = (f32[8,128]{1,0:T(8,128)S(1)}, f32[8,128]{1,0:T(8,128)S(1)}, u32[]{:S(2)}, u32[]{:S(2)}) collective-permute-start(f32[8,128]{1,0:T(8,128)S(1)} %get-tuple-element.82), channel_id=1, source_target_pairs={{0,24},{1,25},{2,26},{3,27},{4,28},{5,29},{6,30},{7,31},{8,16},{9,... | collective-permute-start | bytes 12296 | tf_op jit(solution)/shard_map/ppermute | solution.py:521
  57.8 4.6 %collective-permute-start.24 = (f32[1,8,128]{2,1,0:T(8,128)S(1)}, f32[1,8,128]{2,1,0:T(8,128)S(1)}, u32[]{:S(2)}, u32[]{:S(2)}) collective-permute-start(f32[1,8,128]{2,1,0:T(8,128)S(1)} %bitcast.56), channel_id=1, source_target_pairs={{0,4},{1,5},{2,6},{3,7},{4,0},{5,1},{6,2},{7,3},{8,12},{9,13},{10,... | collective-permute-start | bytes 12296 | tf_op jit(solution)/shard_map/ppermute | solution.py:563
  62.3 3.7 %collective-permute-start.25 = (f32[2,8,128]{2,1,0:T(8,128)S(1)}, f32[2,8,128]{2,1,0:T(8,128)S(1)}, u32[]{:S(2)}, u32[]{:S(2)}) collective-permute-start(f32[2,8,128]{2,1,0:T(8,128)S(1)} %pad_maximum_fusion.2), channel_id=1, source_target_pairs={{0,2},{1,3},{2,0},{3,1},{4,6},{5,7},{6,4},{7,5},{8,10},{9,11},{10,... | collective-permute-start | bytes 24584 | tf_op jit(solution)/shard_map/ppermute | solution.py:563
  68.4 4.7 %collective-permute-start.27 = (f32[8,128]{1,0:T(8,128)S(1)}, f32[8,128]{1,0:T(8,128)S(1)}, u32[]{:S(2)}, u32[]{:S(2)}) collective-permute-start(f32[8,128]{1,0:T(8,128)S(1)} %get-tuple-element.89), channel_id=1, source_target_pairs={{0,24},{1,25},{2,26},{3,27},{4,28},{5,29},{6,30},{7,31},{8,16},{9,... | collective-permute-start | bytes 12296 | tf_op jit(solution)/shard_map/ppermute | solution.py:521
  71.1 3.6 %collective-permute-start.28 = (f32[8,128]{1,0:T(8,128)S(1)}, f32[8,128]{1,0:T(8,128)S(1)}, u32[]{:S(2)}, u32[]{:S(2)}) collective-permute-start(f32[8,128]{1,0:T(8,128)S(1)} %get-tuple-element.89), channel_id=1, source_target_pairs={{0,8},{1,2},{2,1},{3,4},{4,3},{5,6},{6,5},{7,15},{8,0},{9,10},{10,... | collective-permute-start | bytes 12296 | tf_op jit(solution)/shard_map/ppermute | solution.py:521
  75.5 4.5 %collective-permute-start.31 = (f32[8,128]{1,0:T(8,128)S(1)}, f32[8,128]{1,0:T(8,128)S(1)}, u32[]{:S(2)}, u32[]{:S(2)}) collective-permute-start(f32[8,128]{1,0:T(8,128)S(1)} %get-tuple-element.91), channel_id=1, source_target_pairs={{0,24},{1,25},{2,26},{3,27},{4,28},{5,29},{6,30},{7,31},{8,16},{9,... | collective-permute-start | bytes 12296 | tf_op jit(solution)/shard_map/ppermute | solution.py:521
  81.3 4.7 %collective-permute-start.35 = (f32[8,128]{1,0:T(8,128)S(1)}, f32[8,128]{1,0:T(8,128)S(1)}, u32[]{:S(2)}, u32[]{:S(2)}) collective-permute-start(f32[8,128]{1,0:T(8,128)S(1)} %get-tuple-element.94), channel_id=1, source_target_pairs={{0,24},{1,25},{2,26},{3,27},{4,28},{5,29},{6,30},{7,31},{8,16},{9,... | collective-permute-start | bytes 12296 | tf_op jit(solution)/shard_map/ppermute | solution.py:521
  88.5 5.1 %collective-permute-start.39 = (f32[8,128]{1,0:T(8,128)S(1)}, f32[8,128]{1,0:T(8,128)S(1)}, u32[]{:S(2)}, u32[]{:S(2)}) collective-permute-start(f32[8,128]{1,0:T(8,128)S(1)} %get-tuple-element.98), channel_id=1, source_target_pairs={{0,24},{1,25},{2,26},{3,27},{4,28},{5,29},{6,30},{7,31},{8,16},{9,... | collective-permute-start | bytes 12296 | tf_op jit(solution)/shard_map/ppermute | solution.py:521
  94.3 6.2 %collective-permute-start.43 = (f32[8,128]{1,0:T(8,128)S(1)}, f32[8,128]{1,0:T(8,128)S(1)}, u32[]{:S(2)}, u32[]{:S(2)}) collective-permute-start(f32[8,128]{1,0:T(8,128)S(1)} %get-tuple-element.100), channel_id=1, source_target_pairs={{0,24},{1,25},{2,26},{3,27},{4,28},{5,29},{6,30},{7,31},{8,16},{9,... | collective-permute-start | bytes 12296 | tf_op jit(solution)/shard_map/ppermute | solution.py:521
  101.4 5.1 %collective-permute-start.47 = (f32[8,128]{1,0:T(8,128)S(1)}, f32[8,128]{1,0:T(8,128)S(1)}, u32[]{:S(2)}, u32[]{:S(2)}) collective-permute-start(f32[8,128]{1,0:T(8,128)S(1)} %get-tuple-element.103), channel_id=1, source_target_pairs={{0,24},{1,25},{2,26},{3,27},{4,28},{5,29},{6,30},{7,31},{8,16},{9,... | collective-permute-start | bytes 12296 | tf_op jit(solution)/shard_map/ppermute | solution.py:521
  107.1 6.2 %collective-permute-start.51 = (f32[8,128]{1,0:T(8,128)S(1)}, f32[8,128]{1,0:T(8,128)S(1)}, u32[]{:S(2)}, u32[]{:S(2)}) collective-permute-start(f32[8,128]{1,0:T(8,128)S(1)} %get-tuple-element.106), channel_id=1, source_target_pairs={{0,24},{1,25},{2,26},{3,27},{4,28},{5,29},{6,30},{7,31},{8,16},{9,... | collective-permute-start | bytes 12296 | tf_op jit(solution)/shard_map/ppermute | solution.py:521
  (45 other events, 127.3 us)

commit v6 on v5

--- a/solution.py
+++ b/solution.py
@@ -71,9 +71,30 @@
     return x + pltpu.roll(x, 4, 0)
 
 
-def fine_start(v_ref, b_ref, s_ref, bo_ref, mo_ref, x_ref, so_ref, out_ref, pad_ref):
+def fine_start(*refs):
+    sources = refs[:7]
+    (bo_ref, mo_ref, x_ref, so_ref, s2o_ref, co_ref, o3_ref, out_ref, pad_ref) = refs[7:16]
+    held, sems = refs[16:23], refs[23]
+    copies = [
+        pltpu.make_async_copy(source.at[pl.ds(0, there.shape[0]), :], there, sems.at[t])
+        for t, (source, there) in enumerate(zip(sources, held))
+    ]
+    for copy in copies:
+        copy.start()
+    for copy in copies:
+        copy.wait()
+    v_ref, b_ref, s_ref, s2_ref, c_ref, v3_ref, c3_ref = held
     sends = send_table(s_ref)
     so_ref[...] = sends
+    s2o_ref[...] = send_table(s2_ref)
+    count = v3_ref.shape[0]
+    o3_ref[0, pl.ds(0, count), :] = v3_ref[...]
+    o3_ref[0, pl.ds(count, NNZ), :] = c3_ref[...].astype(F32)
+    for k in range(NNZ):
+        for h in range(co_ref.shape[1] // SUBS):
+            co_ref[k, pl.ds(h * SUBS, SUBS), :] = c_ref[
+                pl.ds(h * SUBS * NNZ + k, SUBS, stride=NNZ), :
+            ]
     lines = bo_ref.shape[1]
     for i in range(4):
         for h in range(lines // SUBS):
@@ -92,7 +113,7 @@
     )
 
 
-def fine_prepare(v_ref, c_ref, _, vo_ref, co_ref):
+def fine_prepare(v_ref, _, vo_ref):
     lines = vo_ref.shape[3]
     halves = lines // SUBS
 
@@ -107,11 +128,6 @@
         return carry
 
     lax.fori_loop(0, NNZ * 4, body, 0)
-    for k in range(NNZ):
-        for h in range(halves):
-            co_ref[k, pl.ds(h * SUBS, SUBS), :] = c_ref[
-                pl.ds(h * SUBS * NNZ + k, SUBS, stride=NNZ), :
-            ]
 
 
 def fine_local(x_ref, b_ref, v_ref, c_ref, r_ref, line_ref):
@@ -257,43 +273,47 @@
     return result
 
 
-def fine_tables(w_ref, row_ref, o_ref, _, wo_ref, agg_ref, place_ref):
+def fine_tables(w_ref, o_ref, v2_ref, _, wo_ref, place_ref, m2_ref):
     lines = o_ref.shape[0]
     for i in range(4):
         for j in range(4):
             for h in range(lines // SUBS):
                 start = (i * lines + h * SUBS) * 4 + j
                 wo_ref[i, j, pl.ds(h * SUBS, SUBS), :] = w_ref[pl.ds(start, SUBS, stride=4), :]
-    agg_ref[...] = inverse_order(row_ref[...], lines)
     sources = []
     for q in range(4):
         four = o_ref[pl.ds(q, 4, stride=4), :]
         sources.append(jnp.concatenate([four, four], axis=0))
     for part in range(2):
         place_ref[part] = pick_order(sources, (tile_iota(0) >> 2) + 2 * part)
-
-
-def middle_tables(v_ref, c_ref, w_ref, row_ref, o_ref, s_ref, _, so_ref, vo_ref, co_ref, mo_ref, wo_ref, agg_ref, place_ref):
-    lines = o_ref.shape[0]
-    so_ref[...] = send_table(s_ref)
-
+    for i in range(4):
+        four = 1.0 / v2_ref[pl.ds(i * 16 + i, 4, stride=4), :]
+        m2_ref[i, pl.ds(0, 4), :] = four
+        m2_ref[i, pl.ds(4, 4), :] = four
+
+
+def fine_inverse(row_ref, _, agg_ref):
+    agg_ref[...] = inverse_order(row_ref[...], agg_ref.shape[0])
+
+
+def middle_blocks(v_ref, c_ref, _, vo_ref, co_ref):
     def body(ki, carry):
         k, i = ki // 4, ki % 4
-        kp, i2 = ki // 4, ki % 4
         for j in range(4):
             for odd in range(2):
-                start = ((2 * kp + odd) * 4 + i2) * (lines * 4) + j
+                start = ((2 * k + odd) * 4 + i) * 16 + j
                 vo_ref[k, i, j, pl.ds(4 * odd, 4), :] = v_ref[pl.ds(start, 4, stride=4), :]
         return carry
 
     lax.fori_loop(0, NNZ // 2 * 4, body, 0)
-    for kp in range(NNZ // 2):
+    for k in range(NNZ // 2):
         for odd in range(2):
-            co_ref[kp, pl.ds(4 * odd, 4), :] = c_ref[pl.ds(2 * kp + odd, 4, stride=NNZ), :]
+            co_ref[k, pl.ds(4 * odd, 4), :] = c_ref[pl.ds(2 * k + odd, 4, stride=NNZ), :]
+
+
+def middle_tables(w_ref, row_ref, o_ref, _, wo_ref, agg_ref, place_ref):
+    lines = o_ref.shape[0]
     for i in range(4):
-        four = 1.0 / v_ref[pl.ds(i * lines * 4 + i, 4, stride=4), :]
-        mo_ref[i, pl.ds(0, 4), :] = four
-        mo_ref[i, pl.ds(4, 4), :] = four
         for j in range(4):
             four = w_ref[pl.ds(i * lines * 4 + j, 4, stride=4), :]
             wo_ref[i, j, pl.ds(0, 4), :] = four
@@ -407,8 +427,9 @@
 def coarse_tables(group, *refs):
     vo_ref, co_ref, mo_ref, pad_ref = refs[-4:]
     me = refs[0][0]
-    for q in range(group):
-        pad_ref[me ^ q] = refs[1][q]
+    for piece, places in zip(refs[1:-5], span_places(group)):
+        for t, place in enumerate(places):
+            pad_ref[place] = piece[t]
     for h in range(group // SUBS):
         rows = pl.ds(h * SUBS, SUBS)
         for ki in range(NNZ * 4):
@@ -425,8 +446,8 @@
 
 def coarse_solve(group, *refs):
     (v_ref, c_ref, m_ref, x2_ref, w_ref, agg_ref, s_ref, xo_ref, out_ref, b_ref, x_ref, d_ref, pad_ref) = refs[-13:]
-    for piece, places in zip(refs[:-13], span_places(group)):
-        for t, place in enumerate(places):
+    for odd, piece in enumerate(refs[:-13]):
+        for t, place in enumerate(range(odd, group, 2)):
             for j in range(4):
                 b_ref[j, pl.ds(place, 1), :] = piece[t, pl.ds(j, 1), :]
     blocks = group // SUBS
@@ -469,10 +490,12 @@
     middle_out(out_ref, pad_ref, s_ref)
 
 
-def call(body, outs, args, scratch=(), free=(), smem=()):
+def call(body, outs, args, scratch=(), free=(), smem=(), hbm=(), limit=16):
     specs = []
     for index in range(len(args)):
-        if index in free:
+        if index in hbm:
+            specs.append(pl.BlockSpec(memory_space=pltpu.HBM))
+        elif index in free:
             specs.append(pl.BlockSpec(memory_space=pl.ANY))
         elif index in smem:
             specs.append(pl.BlockSpec(memory_space=pltpu.SMEM))
@@ -486,7 +509,7 @@
         in_specs=specs,
         out_specs=[pl.BlockSpec(memory_space=pltpu.VMEM) for _ in shapes],
         scratch_shapes=list(scratch),
-        compiler_params=pltpu.CompilerParams(vmem_limit_bytes=16 * 2**20),
+        compiler_params=pltpu.CompilerParams(vmem_limit_bytes=limit * 2**20),
     )(*args)
     return result[0] if single else result
 
@@ -553,14 +576,23 @@
     return places
 
 
-def span_stage(mesh, pieces):
+def span_swap(mesh, value, mask):
     slabs, count = mesh.shape["stream"], mesh.shape["span"]
-    held = jnp.concatenate(pieces)
-    mask = count // 2 // held.shape[0]
     pairs = [
         (a * count + b, a * count + (b ^ mask)) for a in range(slabs) for b in range(count)
     ]
-    return pieces + [lax.ppermute(held, AXES, pairs)]
+    return lax.ppermute(value, AXES, pairs)
+
+
+def span_stage(mesh, pieces, out):
+    pieces, _ = lax.optimization_barrier((pieces, out))
+    held = jnp.concatenate(pieces)
+    return pieces + [span_swap(mesh, held, mesh.shape["span"] // 2 // held.shape[0])]
+
+
+def span_gather(mesh, value):
+    even = jnp.stack([value] + [span_swap(mesh, value, m) for m in range(2, mesh.shape["span"], 2)])
+    return [even, span_swap(mesh, even, 1)]
 
 
 def per_device(mesh, right_side, fine_values, fine_columns, fine_sends, fine_order, fine_weights, middle_values, middle_columns, middle_sends, middle_order, middle_weights, coarsest_values, coarsest_columns):
@@ -578,23 +610,36 @@
     values1 = native_rows(fine_values)
     values2 = native_rows(middle_values)
 
-    b1, m1, x1, send1, out = call(
+    starts = [
+        values1,
+        native_rows(right_side),
+        fine_sends,
+        middle_sends,
+        native_columns(fine_columns),
+        coarsest_values.reshape(NNZ * 16, LANES),
+        coarsest_columns,
+    ]
+    int_tile = shape(SUBS, LANES, dtype=I32)
+    b1, m1, x1, send1, send2, c1, own3, out = call(
         fine_start,
-        [vec1, vec1, vec1, shape(SUBS, LANES, dtype=I32), tile],
-        [values1, native_rows(right_side), fine_sends],
-        [pad1],
+        [
+            vec1,
+            vec1,
+            vec1,
+            int_tile,
+            int_tile,
+            shape(NNZ, lines, LANES, dtype=I32),
+            shape(1, NNZ * 17, LANES),
+            tile,
+        ],
+        [pltpu.with_memory_space_constraint(x, pltpu.HBM) for x in starts],
+        [pad1, vmem(16 * lines, LANES)]
+        + [vmem(*x.shape, dtype=x.dtype) for x in starts[1:]]
+        + [pltpu.SemaphoreType.DMA((len(starts),))],
+        hbm=range(len(starts)),
     )
     d1 = x1
-
-    own3 = jnp.concatenate(
-        [coarsest_values.reshape(NNZ * 16, LANES), coarsest_columns.astype(F32)], axis=0
-    )
-    v1, c1 = call(
-        fine_prepare,
-        [shape(NNZ, 4, 4, lines, LANES), shape(NNZ, lines, LANES, dtype=I32)],
-        [values1, native_columns(fine_columns), out],
-        free=(2,),
-    )
+    v1 = call(fine_prepare, shape(NNZ, 4, 4, lines, LANES), [values1, out], free=(1,))
 
     def fine_part(x):
         return call(fine_local, vec1, [x, b1, v1, c1], [vmem(4, lines, SUBS, LANES)])
@@ -614,37 +659,29 @@
         return result[0], (None if last else result[2]), result[1]
 
     arrived = exchange(mesh, out, choice)
-    own3, _ = lax.optimization_barrier((own3, out))
-    slab3 = lax.all_gather(own3, "span", axis=0)
+    pieces3 = span_stage(mesh, [own3], out)
     resid = fine_part(x1)
     x1, d1, out = fine_next(1, arrived, resid, x1, d1)
 
     arrived = exchange(mesh, out, choice)
     resid = fine_part(x1)
-    w1, agg1, place1 = call(
+    w1, place1, m2 = call(
         fine_tables,
-        [shape(4, 4, lines, LANES), shape(lines, LANES, dtype=I32), shape(2, SUBS, LANES, dtype=I32)],
-        [native_rows(fine_weights), fine_order, fine_order.reshape(lines, LANES), out],
+        [
+            shape(4, 4, lines, LANES),
+            shape(2, SUBS, LANES, dtype=I32),
+            vec2,
+        ],
+        [native_rows(fine_weights), fine_order.reshape(lines, LANES), values2, out],
         free=(3,),
     )
-    x1, d1, out = fine_next(2, arrived, resid, x1, d1, [])
-
-    arrived = exchange(mesh, out, choice)
+    x1, d1, out = fine_next(2, arrived, resid, x1, d1, [m2])
+
+    arrived = exchange(mesh, out, choice)
+    stages = len(span_places(group)) - 1
+    for _ in range(stages - 2):
+        pieces3 = span_stage(mesh, pieces3, out)
     resid = fine_part(x1)
-    send2, v2, c2, m2, w2, agg2, place2 = call(
-        middle_tables,
-        [
-            shape(SUBS, LANES, dtype=I32),
-            shape(NNZ // 2, 4, 4, SUBS, LANES),
-            shape(NNZ // 2, SUBS, LANES, dtype=I32),
-            vec2,
-            shape(4, 4, SUBS, LANES),
-            shape(SUBS, LANES, dtype=I32),
-            shape(SUBS, LANES, dtype=I32),
-        ],
-        [values2, native_columns(middle_columns), native_rows(middle_weights), middle_order, middle_order.reshape(-1, LANES), middle_sends, out],
-        free=(6,),
-    )
     b2, x2, out = call(
         fine_restrict,
         [vec2, vec2, tile],
@@ -668,32 +705,50 @@
         return result[0], (None if last else result[2]), result[1]
 
     arrived = exchange(mesh, out, choice)
+    pieces3 = span_stage(mesh, pieces3, out)
+    v2, c2 = call(
+        middle_blocks,
+        [shape(NNZ // 2, 4, 4, SUBS, LANES), shape(NNZ // 2, SUBS, LANES, dtype=I32)],
+        [values2, native_columns(middle_columns), out],
+        free=(2,),
+    )
+    x2, d2, out = middle_next(1, arrived, x2, d2)
+
+    arrived = exchange(mesh, out, choice)
+    w2, agg2, place2 = call(
+        middle_tables,
+        [
+            shape(4, 4, SUBS, LANES),
+            shape(SUBS, LANES, dtype=I32),
+            shape(SUBS, LANES, dtype=I32),
+        ],
+        [native_rows(middle_weights), middle_order, middle_order.reshape(-1, LANES), out],
+        free=(3,),
+    )
     v3, c3, m3 = call(
         lambda *refs: coarse_tables(group, *refs),
         [shape(NNZ, 4, 4, group, LANES), shape(NNZ, group, LANES, dtype=I32), shape(4, group, LANES)],
-        [me.reshape(1), slab3, out],
+        [me.reshape(1)] + pieces3 + [out],
         [vmem(group, NNZ * 17, LANES)],
-        free=(2,),
+        free=(1 + len(pieces3),),
         smem=(0,),
     )
-    x2, d2, out = middle_next(1, arrived, x2, d2, [m3])
-    arrived = exchange(mesh, out, choice)
-    x2, d2, out = middle_next(2, arrived, x2, d2)
-    arrived = exchange(mesh, out, choice)
+    x2, d2, out = middle_next(2, arrived, x2, d2, [agg2, m3])
+
+    arrived = exchange(mesh, out, choice)
+    agg1 = call(fine_inverse, shape(lines, LANES, dtype=I32), [fine_order, out], free=(1,))
     rhs3 = call(
-        middle_restrict,
+        lambda *refs: middle_restrict(*(refs[:11] + refs[12:])),
         tile,
-        arrived + [b2, x2, v2, c2, w2, place2],
+        arrived + [b2, x2, v2, c2, w2, place2, agg1],
         [edge, vmem(4, SUBS, LANES)],
-    )
-    pieces = [rhs3[None]]
-    while sum(piece.shape[0] for piece in pieces) < group:
-        pieces = span_stage(mesh, pieces)
+        free=(11,),
+    )
     vec3 = vmem(4, group, LANES)
     x2, out = call(
         lambda *refs: coarse_solve(group, *refs),
         [vec2, tile],
-        pieces + [v3, c3, m3, x2, w2, agg2, send2],
+        span_gather(mesh, rhs3) + [v3, c3, m3, x2, w2, agg2, send2],
         [vec3, vec3, vec3, pad2],
     )
     arrived = exchange(mesh, out, choice)

time: 115 us -> 100 us (0.87)
  blocking collectives: 15 us -> 0 us
  local copies, waits for them, and re-layouts: 4.03 us -> 0.03 us
  starting transfers between devices: 54.5 us -> 57.2 us
    all_gather x1 -> x0, blocking collectives: 15 us -> none  [per_device(): slab3 = lax.all_gather(own3, 'span', axis=0)]
    ppermute x3 -> x7, starting transfers between devices: 0.41 us -> 7.63 us  [span_swap(): return lax.ppermute(value, AXES, pairs)]
    ppermute x52, waiting for transfers between devices: 12.5 us -> 19.2 us  [swap(): return lax.ppermute(out, AXES, pairs)]
    ppermute x3 -> x7, waiting for transfers between devices: 8.99 us -> 2.81 us  [span_swap(): return lax.ppermute(value, AXES, pairs)]
    ppermute x52, starting transfers between devices: 54.1 us -> 49.5 us  [swap(): return lax.ppermute(out, AXES, pairs)]
    unnamed x28 -> x14, local copies, waits for them, and re-layouts: 4.03 us -> 0.03 us
    pallas_call x26 -> x28, Pallas kernels: 18.7 us -> 19.8 us  [call(): pl.pallas_call(body, out_shape=shapes, in_specs=specs, out_specs=[pl.Bloc...]
  transfers between devices with their start and end apart: 55 -> 59, of which waited for: 21 -> 26; matrix products, arithmetic and copies ran while one was open for 0% -> 0% of each run, Pallas kernels for 11% -> 14%
where the time goes in v6:
time: 100 us
  starting transfers between devices  57.2 us (57%)
  waiting for transfers between devices  22 us (22%)
  Pallas kernels  19.8 us (20%)
  between operations  1 us (1%)
    ppermute x52, starting transfers between devices, swap(): return lax.ppermute(out, AXES, pairs)  49.5 us
    pallas_call x28, Pallas kernels, call(): pl.pallas_call(body, out_shape=shapes, in_specs=specs, out_specs=[pl.Bloc...  19.8 us
    ppermute x52, waiting for transfers between devices, swap(): return lax.ppermute(out, AXES, pairs)  19.2 us
    ppermute x7, starting transfers between devices, span_swap(): return lax.ppermute(value, AXES, pairs)  7.63 us
    ppermute x7, waiting for transfers between devices, span_swap(): return lax.ppermute(value, AXES, pairs)  2.81 us
  transfers between devices with their start and end apart: 59, of which 26 were waited for; matrix products, arithmetic and copies ran while one was open for 0% of the time, Pallas kernels for 14%

profile of v6, /device:TPU:0, one launch (start us, length us, event | category | flops | bytes accessed | tf_op | source)
XLA Modules:
  0.0 100.2 jit_solution(17059652708576333267)
XLA Ops:
  0.6 1.3 %shard_map.140 = (f32[4,16,128]{2,1,0:T(8,128)S(1)}, f32[4,16,128]{2,1,0:T(8,128)S(1)}, f32[4,16,128]{2,1,0:T(8,128)S(1)}, s32[8,128]{1,0:T(8,128)S(1)}, s32[8,1...) custom-call(f32[2048,128]{1,0:T(8,128)} %bitcast.53, ...), custom_call_target="tpu_custom_call" | custom-call | tf_op jit(solution)/shard_map/pallas_call | solution.py:506
  1.9 4.0 %collective-permute-start = (f32[8,128]{1,0:T(8,128)S(1)}, f32[8,128]{1,0:T(8,128)S(1)}, u32[]{:S(2)}, u32[]{:S(2)}) collective-permute-start(f32[8,128]{1,0:T(8,128)S(1)} %get-tuple-element.60._), channel_id=1, source_target_pairs={{0,24},{1,25},{2,26},{3,27},{4,28},{5,29},{6,30},{7,31},{8,16},{9,... | collective-permute-start | bytes 12296 | tf_op jit(solution)/shard_map/ppermute | solution.py:544
  6.4 1.5 %collective-permute-start.2 = (f32[8,128]{1,0:T(8,128)S(1)}, f32[8,128]{1,0:T(8,128)S(1)}, u32[]{:S(2)}, u32[]{:S(2)}) collective-permute-start(f32[8,128]{1,0:T(8,128)S(1)} %get-tuple-element.60._), channel_id=1, source_target_pairs={{0,8},{1,9},{2,10},{3,11},{4,12},{5,13},{6,14},{7,15},{8,0},{9,1},... | collective-permute-start | bytes 12296 | tf_op jit(solution)/shard_map/ppermute | solution.py:544
  7.9 2.5 %collective-permute-start.20 = (f32[1,136,128]{2,1,0:T(8,128)S(1)}, f32[1,136,128]{2,1,0:T(8,128)S(1)}, u32[]{:S(2)}, u32[]{:S(2)}) collective-permute-start(f32[1,136,128]{2,1,0:T(8,128)S(1)} %get-tuple-element.88.refs_1_), channel_id=1, source_target_pairs={{0,4},{1,5},{2,6},{3,7},{4,0},{5,1},{6,2},{7,3},{8,12},{9,13},{10,... | collective-permute-start | bytes 208904 | tf_op jit(solution)/shard_map/ppermute | solution.py:584
  10.9 1.5 %shard_map.142.refs_5_ = f32[4,16,128]{2,1,0:T(8,128)S(1)} custom-call(f32[4,16,128]{2,1,0:T(8,128)S(1)} %get-tuple-element.61.x_ref.refs_9_.refs_10_, f32[4,16,128]{2,1,0:T(8,128)S(1)} %get-tuple-element.62.b_ref, f32[8,4,4,16,128]{4,3,2,1,0:T(8,128)S(1)} %shard_map.141.v_ref.refs_6_, s32[8,16,128]{2,1,0:T(8,128)S(1)} %get-tuple-element.63.c_ref.refs_7_), custom_call_target="tpu_custom_call" | custom-call | tf_op jit(solution)/shard_map/pallas_call | solution.py:506
  12.8 1.4 %collective-permute-start.4 = (f32[8,128]{1,0:T(8,128)S(1)}, f32[8,128]{1,0:T(8,128)S(1)}, u32[]{:S(2)}, u32[]{:S(2)}) collective-permute-start(f32[8,128]{1,0:T(8,128)S(1)} %get-tuple-element.66._), channel_id=1, source_target_pairs={{0,24},{1,25},{2,26},{3,27},{4,28},{5,29},{6,30},{7,31},{8,16},{9,... | collective-permute-start | bytes 12296 | tf_op jit(solution)/shard_map/ppermute | solution.py:544
  14.8 1.5 %collective-permute-start.6 = (f32[8,128]{1,0:T(8,128)S(1)}, f32[8,128]{1,0:T(8,128)S(1)}, u32[]{:S(2)}, u32[]{:S(2)}) collective-permute-start(f32[8,128]{1,0:T(8,128)S(1)} %get-tuple-element.66._), channel_id=1, source_target_pairs={{0,8},{1,9},{2,10},{3,11},{4,12},{5,13},{6,14},{7,15},{8,0},{9,1},... | collective-permute-start | bytes 12296 | tf_op jit(solution)/shard_map/ppermute | solution.py:544
  16.3 1.5 %shard_map.144.refs_5_ = f32[4,16,128]{2,1,0:T(8,128)S(1)} custom-call(f32[4,16,128]{2,1,0:T(8,128)S(1)} %get-tuple-element.67.x_ref.refs_9_, f32[4,16,128]{2,1,0:T(8,128)S(1)} %get-tuple-element.62.b_ref, f32[8,4,4,16,128]{4,3,2,1,0:T(8,128)S(1)} %shard_map.141.v_ref.refs_6_, s32[8,16,128]{2,1,0:T(8,128)S(1)} %get-tuple-element.63.c_ref.refs_7_), custom_call_target="tpu_custom_call" | custom-call | tf_op jit(solution)/shard_map/pallas_call | solution.py:506
  20.4 2.0 %collective-permute-start.8 = (f32[8,128]{1,0:T(8,128)S(1)}, f32[8,128]{1,0:T(8,128)S(1)}, u32[]{:S(2)}, u32[]{:S(2)}) collective-permute-start(f32[8,128]{1,0:T(8,128)S(1)} %get-tuple-element.70), channel_id=1, source_target_pairs={{0,24},{1,25},{2,26},{3,27},{4,28},{5,29},{6,30},{7,31},{8,16},{9,... | collective-permute-start | bytes 12296 | tf_op jit(solution)/shard_map/ppermute | solution.py:544
  23.4 1.5 %shard_map.147.refs_5_ = f32[4,16,128]{2,1,0:T(8,128)S(1)} custom-call(f32[4,16,128]{2,1,0:T(8,128)S(1)} %get-tuple-element.71.x_ref.refs_11_, f32[4,16,128]{2,1,0:T(8,128)S(1)} %get-tuple-element.62.b_ref, f32[8,4,4,16,128]{4,3,2,1,0:T(8,128)S(1)} %shard_map.141.v_ref.refs_6_, s32[8,16,128]{2,1,0:T(8,128)S(1)} %get-tuple-element.63.c_ref.refs_7_), custom_call_target="tpu_custom_call" | custom-call | tf_op jit(solution)/shard_map/pallas_call | solution.py:506
  32.6 2.0 %collective-permute-start.16 = (f32[8,128]{1,0:T(8,128)S(1)}, f32[8,128]{1,0:T(8,128)S(1)}, u32[]{:S(2)}, u32[]{:S(2)}) collective-permute-start(f32[8,128]{1,0:T(8,128)S(1)} %get-tuple-element.80._.refs_5_), channel_id=1, source_target_pairs={{0,24},{1,25},{2,26},{3,27},{4,28},{5,29},{6,30},{7,31},{8,16},{9,... | collective-permute-start | bytes 12296 | tf_op jit(solution)/shard_map/ppermute | solution.py:544
  42.9 1.2 %collective-permute-done.23.refs_0_ = f32[8,128]{1,0:T(8,128)S(1)} collective-permute-done((f32[8,128]{1,0:T(8,128)S(1)}, f32[8,128]{1,0:T(8,128)S(1)}, u32[]{:S(2)}, u32[]{:S(2)}) %collective-permute-start.23) | collective-permute-done | bytes 4128 | tf_op jit(solution)/shard_map/ppermute | solution.py:544
  46.1 3.9 %collective-permute-start.29 = (f32[8,128]{1,0:T(8,128)S(1)}, f32[8,128]{1,0:T(8,128)S(1)}, u32[]{:S(2)}, u32[]{:S(2)}) collective-permute-start(f32[8,128]{1,0:T(8,128)S(1)} %shard_map.155), channel_id=1, source_target_pairs={{0,6},{1,7},{2,4},{3,5},{4,2},{5,3},{6,0},{7,1},{8,14},{9,15},{10,... | collective-permute-start | bytes 12296 | tf_op jit(solution)/shard_map/ppermute | solution.py:584
  50.2 1.4 %collective-permute-done.29 = f32[8,128]{1,0:T(8,128)S(1)} collective-permute-done((f32[8,128]{1,0:T(8,128)S(1)}, f32[8,128]{1,0:T(8,128)S(1)}, u32[]{:S(2)}, u32[]{:S(2)}) %collective-permute-start.29) | collective-permute-done | bytes 4128 | tf_op jit(solution)/shard_map/ppermute | solution.py:584
  52.8 1.2 %shard_map.156 = (f32[4,8,128]{2,1,0:T(8,128)S(1)}, f32[8,128]{1,0:T(8,128)S(1)}) custom-call(f32[4,8,128]{2,1,0:T(8,128)S(1)} %pad_maximum_fusion.2.refs_0_, f32[4,8,128]{2,1,0:T(8,128)S(1)} %collective-permute-done.30.refs_1_, f32[8,4,4,8,128]{4,3,2,1,0:T(8,128)S(1)} %get-tuple-element.96.refs_2_, s32[8,8,128]{2,1,0:T(8,128)S(1)} %get-tuple-element.97.refs_3_, ...), custom_call_target="tpu_custom_call" | custom-call | tf_op jit(solution)/shard_map/pallas_call | solution.py:506
  54.0 2.0 %collective-permute-start.31 = (f32[8,128]{1,0:T(8,128)S(1)}, f32[8,128]{1,0:T(8,128)S(1)}, u32[]{:S(2)}, u32[]{:S(2)}) collective-permute-start(f32[8,128]{1,0:T(8,128)S(1)} %get-tuple-element.98), channel_id=1, source_target_pairs={{0,24},{1,25},{2,26},{3,27},{4,28},{5,29},{6,30},{7,31},{8,16},{9,... | collective-permute-start | bytes 12296 | tf_op jit(solution)/shard_map/ppermute | solution.py:544
  64.0 1.5 %collective-permute-done.35.refs_0_ = f32[8,128]{1,0:T(8,128)S(1)} collective-permute-done((f32[8,128]{1,0:T(8,128)S(1)}, f32[8,128]{1,0:T(8,128)S(1)}, u32[]{:S(2)}, u32[]{:S(2)}) %collective-permute-start.35) | collective-permute-done | bytes 4128 | tf_op jit(solution)/shard_map/ppermute | solution.py:544
  66.9 2.0 %collective-permute-start.39 = (f32[8,128]{1,0:T(8,128)S(1)}, f32[8,128]{1,0:T(8,128)S(1)}, u32[]{:S(2)}, u32[]{:S(2)}) collective-permute-start(f32[8,128]{1,0:T(8,128)S(1)} %get-tuple-element.103), channel_id=1, source_target_pairs={{0,24},{1,25},{2,26},{3,27},{4,28},{5,29},{6,30},{7,31},{8,16},{9,... | collective-permute-start | bytes 12296 | tf_op jit(solution)/shard_map/ppermute | solution.py:544
  77.0 1.5 %shard_map.160.refs_5_ = f32[4,16,128]{2,1,0:T(8,128)S(1)} custom-call(f32[4,16,128]{2,1,0:T(8,128)S(1)} %get-tuple-element.107.x_ref.refs_9_.refs_10_, f32[4,16,128]{2,1,0:T(8,128)S(1)} %get-tuple-element.62.b_ref, f32[8,4,4,16,128]{4,3,2,1,0:T(8,128)S(1)} %shard_map.141.v_ref.refs_6_, s32[8,16,128]{2,1,0:T(8,128)S(1)} %get-tuple-element.63.c_ref.refs_7_), custom_call_target="tpu_custom_call" | custom-call | tf_op jit(solution)/shard_map/pallas_call | solution.py:506
  79.9 2.0 %collective-permute-start.47 = (f32[8,128]{1,0:T(8,128)S(1)}, f32[8,128]{1,0:T(8,128)S(1)}, u32[]{:S(2)}, u32[]{:S(2)}) collective-permute-start(f32[8,128]{1,0:T(8,128)S(1)} %get-tuple-element.108), channel_id=1, source_target_pairs={{0,24},{1,25},{2,26},{3,27},{4,28},{5,29},{6,30},{7,31},{8,16},{9,... | collective-permute-start | bytes 12296 | tf_op jit(solution)/shard_map/ppermute | solution.py:544
  83.9 1.5 %shard_map.162.refs_5_ = f32[4,16,128]{2,1,0:T(8,128)S(1)} custom-call(f32[4,16,128]{2,1,0:T(8,128)S(1)} %get-tuple-element.109.x_ref.refs_9_, f32[4,16,128]{2,1,0:T(8,128)S(1)} %get-tuple-element.62.b_ref, f32[8,4,4,16,128]{4,3,2,1,0:T(8,128)S(1)} %shard_map.141.v_ref.refs_6_, s32[8,16,128]{2,1,0:T(8,128)S(1)} %get-tuple-element.63.c_ref.refs_7_), custom_call_target="tpu_custom_call" | custom-call | tf_op jit(solution)/shard_map/pallas_call | solution.py:506
  89.9 1.5 %shard_map.164.refs_5_ = f32[4,16,128]{2,1,0:T(8,128)S(1)} custom-call(f32[4,16,128]{2,1,0:T(8,128)S(1)} %get-tuple-element.112.x_ref.refs_9_, f32[4,16,128]{2,1,0:T(8,128)S(1)} %get-tuple-element.62.b_ref, f32[8,4,4,16,128]{4,3,2,1,0:T(8,128)S(1)} %shard_map.141.v_ref.refs_6_, s32[8,16,128]{2,1,0:T(8,128)S(1)} %get-tuple-element.63.c_ref.refs_7_), custom_call_target="tpu_custom_call" | custom-call | tf_op jit(solution)/shard_map/pallas_call | solution.py:506
  92.8 2.0 %collective-permute-start.55 = (f32[8,128]{1,0:T(8,128)S(1)}, f32[8,128]{1,0:T(8,128)S(1)}, u32[]{:S(2)}, u32[]{:S(2)}) collective-permute-start(f32[8,128]{1,0:T(8,128)S(1)} %get-tuple-element.114), channel_id=1, source_target_pairs={{0,24},{1,25},{2,26},{3,27},{4,28},{5,29},{6,30},{7,31},{8,16},{9,... | collective-permute-start | bytes 12296 | tf_op jit(solution)/shard_map/ppermute | solution.py:544
  96.8 1.5 %shard_map.166.refs_5_ = f32[4,16,128]{2,1,0:T(8,128)S(1)} custom-call(f32[4,16,128]{2,1,0:T(8,128)S(1)} %get-tuple-element.115.x_ref.refs_8_, f32[4,16,128]{2,1,0:T(8,128)S(1)} %get-tuple-element.62.b_ref, f32[8,4,4,16,128]{4,3,2,1,0:T(8,128)S(1)} %shard_map.141.v_ref.refs_6_, s32[8,16,128]{2,1,0:T(8,128)S(1)} %get-tuple-element.63.c_ref.refs_7_), custom_call_target="tpu_custom_call" | custom-call | tf_op jit(solution)/shard_map/pallas_call | solution.py:506
  (144 shorter events, 55.2 us)
Async XLA Ops:
  1.9 10.5 %collective-permute-start = (f32[8,128]{1,0:T(8,128)S(1)}, f32[8,128]{1,0:T(8,128)S(1)}, u32[]{:S(2)}, u32[]{:S(2)}) collective-permute-start(f32[8,128]{1,0:T(8,128)S(1)} %get-tuple-element.60._), channel_id=1, source_target_pairs={{0,24},{1,25},{2,26},{3,27},{4,28},{5,29},{6,30},{7,31},{8,16},{9,... | collective-permute-start | bytes 12296 | tf_op jit(solution)/shard_map/ppermute | solution.py:544
  5.9 6.5 %collective-permute-start.1 = (f32[8,128]{1,0:T(8,128)S(1)}, f32[8,128]{1,0:T(8,128)S(1)}, u32[]{:S(2)}, u32[]{:S(2)}) collective-permute-start(f32[8,128]{1,0:T(8,128)S(1)} %get-tuple-element.60._), channel_id=1, source_target_pairs={{0,8},{1,2},{2,1},{3,4},{4,3},{5,6},{6,5},{7,15},{8,0},{9,10},{10,... | collective-permute-start | bytes 12296 | tf_op jit(solution)/shard_map/ppermute | solution.py:544
  6.4 6.0 %collective-permute-start.2 = (f32[8,128]{1,0:T(8,128)S(1)}, f32[8,128]{1,0:T(8,128)S(1)}, u32[]{:S(2)}, u32[]{:S(2)}) collective-permute-start(f32[8,128]{1,0:T(8,128)S(1)} %get-tuple-element.60._), channel_id=1, source_target_pairs={{0,8},{1,9},{2,10},{3,11},{4,12},{5,13},{6,14},{7,15},{8,0},{9,1},... | collective-permute-start | bytes 12296 | tf_op jit(solution)/shard_map/ppermute | solution.py:544
  7.9 4.5 %collective-permute-start.3 = (f32[8,128]{1,0:T(8,128)S(1)}, f32[8,128]{1,0:T(8,128)S(1)}, u32[]{:S(2)}, u32[]{:S(2)}) collective-permute-start(f32[8,128]{1,0:T(8,128)S(1)} %get-tuple-element.60._), channel_id=1, source_target_pairs={{0,1},{1,0},{2,3},{3,2},{4,5},{5,4},{6,7},{7,6},{8,9},{9,8},{10,11... | collective-permute-start | bytes 12296 | tf_op jit(solution)/shard_map/ppermute | solution.py:544
  7.9 10.8 %collective-permute-start.20 = (f32[1,136,128]{2,1,0:T(8,128)S(1)}, f32[1,136,128]{2,1,0:T(8,128)S(1)}, u32[]{:S(2)}, u32[]{:S(2)}) collective-permute-start(f32[1,136,128]{2,1,0:T(8,128)S(1)} %get-tuple-element.88.refs_1_), channel_id=1, source_target_pairs={{0,4},{1,5},{2,6},{3,7},{4,0},{5,1},{6,2},{7,3},{8,12},{9,13},{10,... | collective-permute-start | bytes 208904 | tf_op jit(solution)/shard_map/ppermute | solution.py:584
  12.8 5.1 %collective-permute-start.4 = (f32[8,128]{1,0:T(8,128)S(1)}, f32[8,128]{1,0:T(8,128)S(1)}, u32[]{:S(2)}, u32[]{:S(2)}) collective-permute-start(f32[8,128]{1,0:T(8,128)S(1)} %get-tuple-element.66._), channel_id=1, source_target_pairs={{0,24},{1,25},{2,26},{3,27},{4,28},{5,29},{6,30},{7,31},{8,16},{9,... | collective-permute-start | bytes 12296 | tf_op jit(solution)/shard_map/ppermute | solution.py:544
  18.8 7.8 %collective-permute-start.21 = (f32[2,136,128]{2,1,0:T(8,128)S(1)}, f32[2,136,128]{2,1,0:T(8,128)S(1)}, u32[]{:S(2)}, u32[]{:S(2)}) collective-permute-start(f32[2,136,128]{2,1,0:T(8,128)S(1)} %pad_maximum_fusion.1), channel_id=1, source_target_pairs={{0,2},{1,3},{2,0},{3,1},{4,6},{5,7},{6,4},{7,5},{8,10},{9,11},{10,... | collective-permute-start | bytes 417800 | tf_op jit(solution)/shard_map/ppermute | solution.py:584
  19.4 5.5 %collective-permute-start.10 = (f32[8,128]{1,0:T(8,128)S(1)}, f32[8,128]{1,0:T(8,128)S(1)}, u32[]{:S(2)}, u32[]{:S(2)}) collective-permute-start(f32[8,128]{1,0:T(8,128)S(1)} %get-tuple-element.70), channel_id=1, source_target_pairs={{0,8},{1,9},{2,10},{3,11},{4,12},{5,13},{6,14},{7,15},{8,0},{9,1},... | collective-permute-start | bytes 12296 | tf_op jit(solution)/shard_map/ppermute | solution.py:544
  20.4 4.5 %collective-permute-start.11 = (f32[8,128]{1,0:T(8,128)S(1)}, f32[8,128]{1,0:T(8,128)S(1)}, u32[]{:S(2)}, u32[]{:S(2)}) collective-permute-start(f32[8,128]{1,0:T(8,128)S(1)} %get-tuple-element.70), channel_id=1, source_target_pairs={{0,1},{1,0},{2,3},{3,2},{4,5},{5,4},{6,7},{7,6},{8,9},{9,8},{10,11... | collective-permute-start | bytes 12296 | tf_op jit(solution)/shard_map/ppermute | solution.py:544
  20.4 4.5 %collective-permute-start.8 = (f32[8,128]{1,0:T(8,128)S(1)}, f32[8,128]{1,0:T(8,128)S(1)}, u32[]{:S(2)}, u32[]{:S(2)}) collective-permute-start(f32[8,128]{1,0:T(8,128)S(1)} %get-tuple-element.70), channel_id=1, source_target_pairs={{0,24},{1,25},{2,26},{3,27},{4,28},{5,29},{6,30},{7,31},{8,16},{9,... | collective-permute-start | bytes 12296 | tf_op jit(solution)/shard_map/ppermute | solution.py:544
  26.6 10.3 %collective-permute-start.22 = (f32[4,136,128]{2,1,0:T(8,128)S(1)}, f32[4,136,128]{2,1,0:T(8,128)S(1)}, u32[]{:S(2)}, u32[]{:S(2)}) collective-permute-start(f32[4,136,128]{2,1,0:T(8,128)S(1)} %pad_maximum_fusion), channel_id=1, source_target_pairs={{0,1},{1,0},{2,3},{3,2},{4,5},{5,4},{6,7},{7,6},{8,9},{9,8},{10,11... | collective-permute-start | bytes 835592 | tf_op jit(solution)/shard_map/ppermute | solution.py:584
  26.7 4.6 %collective-permute-start.12 = (f32[8,128]{1,0:T(8,128)S(1)}, f32[8,128]{1,0:T(8,128)S(1)}, u32[]{:S(2)}, u32[]{:S(2)}) collective-permute-start(f32[8,128]{1,0:T(8,128)S(1)} %get-tuple-element.75._), channel_id=1, source_target_pairs={{0,24},{1,25},{2,26},{3,27},{4,28},{5,29},{6,30},{7,31},{8,16},{9,... | collective-permute-start | bytes 12296 | tf_op jit(solution)/shard_map/ppermute | solution.py:544
  32.6 4.6 %collective-permute-start.16 = (f32[8,128]{1,0:T(8,128)S(1)}, f32[8,128]{1,0:T(8,128)S(1)}, u32[]{:S(2)}, u32[]{:S(2)}) collective-permute-start(f32[8,128]{1,0:T(8,128)S(1)} %get-tuple-element.80._.refs_5_), channel_id=1, source_target_pairs={{0,24},{1,25},{2,26},{3,27},{4,28},{5,29},{6,30},{7,31},{8,16},{9,... | collective-permute-start | bytes 12296 | tf_op jit(solution)/shard_map/ppermute | solution.py:544
  39.6 4.5 %collective-permute-start.23 = (f32[8,128]{1,0:T(8,128)S(1)}, f32[8,128]{1,0:T(8,128)S(1)}, u32[]{:S(2)}, u32[]{:S(2)}) collective-permute-start(f32[8,128]{1,0:T(8,128)S(1)} %get-tuple-element.92._), channel_id=1, source_target_pairs={{0,24},{1,25},{2,26},{3,27},{4,28},{5,29},{6,30},{7,31},{8,16},{9,... | collective-permute-start | bytes 12296 | tf_op jit(solution)/shard_map/ppermute | solution.py:544
  45.5 4.5 %collective-permute-start.27 = (f32[8,128]{1,0:T(8,128)S(1)}, f32[8,128]{1,0:T(8,128)S(1)}, u32[]{:S(2)}, u32[]{:S(2)}) collective-permute-start(f32[8,128]{1,0:T(8,128)S(1)} %shard_map.155), channel_id=1, source_target_pairs={{0,2},{1,3},{2,0},{3,1},{4,6},{5,7},{6,4},{7,5},{8,10},{9,11},{10,... | collective-permute-start | bytes 12296 | tf_op jit(solution)/shard_map/ppermute | solution.py:584
  45.6 4.6 %collective-permute-start.28 = (f32[8,128]{1,0:T(8,128)S(1)}, f32[8,128]{1,0:T(8,128)S(1)}, u32[]{:S(2)}, u32[]{:S(2)}) collective-permute-start(f32[8,128]{1,0:T(8,128)S(1)} %shard_map.155), channel_id=1, source_target_pairs={{0,4},{1,5},{2,6},{3,7},{4,0},{5,1},{6,2},{7,3},{8,12},{9,13},{10,... | collective-permute-start | bytes 12296 | tf_op jit(solution)/shard_map/ppermute | solution.py:584
  46.1 5.5 %collective-permute-start.29 = (f32[8,128]{1,0:T(8,128)S(1)}, f32[8,128]{1,0:T(8,128)S(1)}, u32[]{:S(2)}, u32[]{:S(2)}) collective-permute-start(f32[8,128]{1,0:T(8,128)S(1)} %shard_map.155), channel_id=1, source_target_pairs={{0,6},{1,7},{2,4},{3,5},{4,2},{5,3},{6,0},{7,1},{8,14},{9,15},{10,... | collective-permute-start | bytes 12296 | tf_op jit(solution)/shard_map/ppermute | solution.py:584
  54.0 4.5 %collective-permute-start.31 = (f32[8,128]{1,0:T(8,128)S(1)}, f32[8,128]{1,0:T(8,128)S(1)}, u32[]{:S(2)}, u32[]{:S(2)}) collective-permute-start(f32[8,128]{1,0:T(8,128)S(1)} %get-tuple-element.98), channel_id=1, source_target_pairs={{0,24},{1,25},{2,26},{3,27},{4,28},{5,29},{6,30},{7,31},{8,16},{9,... | collective-permute-start | bytes 12296 | tf_op jit(solution)/shard_map/ppermute | solution.py:544
  61.0 4.5 %collective-permute-start.35 = (f32[8,128]{1,0:T(8,128)S(1)}, f32[8,128]{1,0:T(8,128)S(1)}, u32[]{:S(2)}, u32[]{:S(2)}) collective-permute-start(f32[8,128]{1,0:T(8,128)S(1)} %get-tuple-element.100), channel_id=1, source_target_pairs={{0,24},{1,25},{2,26},{3,27},{4,28},{5,29},{6,30},{7,31},{8,16},{9,... | collective-permute-start | bytes 12296 | tf_op jit(solution)/shard_map/ppermute | solution.py:544
  66.9 4.5 %collective-permute-start.39 = (f32[8,128]{1,0:T(8,128)S(1)}, f32[8,128]{1,0:T(8,128)S(1)}, u32[]{:S(2)}, u32[]{:S(2)}) collective-permute-start(f32[8,128]{1,0:T(8,128)S(1)} %get-tuple-element.103), channel_id=1, source_target_pairs={{0,24},{1,25},{2,26},{3,27},{4,28},{5,29},{6,30},{7,31},{8,16},{9,... | collective-permute-start | bytes 12296 | tf_op jit(solution)/shard_map/ppermute | solution.py:544
  73.9 4.6 %collective-permute-start.43 = (f32[8,128]{1,0:T(8,128)S(1)}, f32[8,128]{1,0:T(8,128)S(1)}, u32[]{:S(2)}, u32[]{:S(2)}) collective-permute-start(f32[8,128]{1,0:T(8,128)S(1)} %get-tuple-element.106), channel_id=1, source_target_pairs={{0,24},{1,25},{2,26},{3,27},{4,28},{5,29},{6,30},{7,31},{8,16},{9,... | collective-permute-start | bytes 12296 | tf_op jit(solution)/shard_map/ppermute | solution.py:544
  79.9 5.6 %collective-permute-start.47 = (f32[8,128]{1,0:T(8,128)S(1)}, f32[8,128]{1,0:T(8,128)S(1)}, u32[]{:S(2)}, u32[]{:S(2)}) collective-permute-start(f32[8,128]{1,0:T(8,128)S(1)} %get-tuple-element.108), channel_id=1, source_target_pairs={{0,24},{1,25},{2,26},{3,27},{4,28},{5,29},{6,30},{7,31},{8,16},{9,... | collective-permute-start | bytes 12296 | tf_op jit(solution)/shard_map/ppermute | solution.py:544
  86.8 4.6 %collective-permute-start.51 = (f32[8,128]{1,0:T(8,128)S(1)}, f32[8,128]{1,0:T(8,128)S(1)}, u32[]{:S(2)}, u32[]{:S(2)}) collective-permute-start(f32[8,128]{1,0:T(8,128)S(1)} %get-tuple-element.111), channel_id=1, source_target_pairs={{0,24},{1,25},{2,26},{3,27},{4,28},{5,29},{6,30},{7,31},{8,16},{9,... | collective-permute-start | bytes 12296 | tf_op jit(solution)/shard_map/ppermute | solution.py:544
  92.8 5.6 %collective-permute-start.55 = (f32[8,128]{1,0:T(8,128)S(1)}, f32[8,128]{1,0:T(8,128)S(1)}, u32[]{:S(2)}, u32[]{:S(2)}) collective-permute-start(f32[8,128]{1,0:T(8,128)S(1)} %get-tuple-element.114), channel_id=1, source_target_pairs={{0,24},{1,25},{2,26},{3,27},{4,28},{5,29},{6,30},{7,31},{8,16},{9,... | collective-permute-start | bytes 12296 | tf_op jit(solution)/shard_map/ppermute | solution.py:544
  (42 other events, 139.0 us)

commit v7 on v6

--- a/solution.py
+++ b/solution.py
@@ -49,7 +49,7 @@
 
 
 def halo_lines(arrivals, edge_ref):
-    s_odd, p_odd, s_even, p_even, which = [r[...] for r in arrivals]
+    s_odd, s_even, p_odd, p_even, which = [r[...] for r in arrivals]
     upper = tile_iota(0) < 4
     even = jnp.where(upper, s_even, p_even)
     odd = jnp.where(upper, s_odd, p_odd)
@@ -446,8 +446,9 @@
 
 def coarse_solve(group, *refs):
     (v_ref, c_ref, m_ref, x2_ref, w_ref, agg_ref, s_ref, xo_ref, out_ref, b_ref, x_ref, d_ref, pad_ref) = refs[-13:]
-    for odd, piece in enumerate(refs[:-13]):
-        for t, place in enumerate(range(odd, group, 2)):
+    first = [0] + list(range(group - 1, 1, -2))
+    for swapped, piece in enumerate(refs[:-13]):
+        for t, place in enumerate([m ^ swapped for m in first]):
             for j in range(4):
                 b_ref[j, pl.ds(place, 1), :] = piece[t, pl.ds(j, 1), :]
     blocks = group // SUBS
@@ -549,13 +550,13 @@
     def span_odd(a, b):
         return (a, odd(b)) if 0 <= odd(b) < count else (a ^ 1, b)
 
-    return [
-        swap(lambda a, b: (odd(a) % slabs, b)),
-        swap(span_odd),
-        swap(lambda a, b: (a ^ 1, b)),
-        swap(lambda a, b: (a, b ^ 1)),
-        which,
+    partners = [
+        lambda a, b: (odd(a) % slabs, b),
+        lambda a, b: (a ^ 1, b),
+        span_odd,
+        lambda a, b: (a, b ^ 1),
     ]
+    return [swap(partner) for partner in partners] + [which]
 
 
 def halo_choice(a, b, count):
@@ -591,8 +592,9 @@
 
 
 def span_gather(mesh, value):
-    even = jnp.stack([value] + [span_swap(mesh, value, m) for m in range(2, mesh.shape["span"], 2)])
-    return [even, span_swap(mesh, even, 1)]
+    masks = range(mesh.shape["span"] - 1, 1, -2)
+    held = jnp.stack([value] + [span_swap(mesh, value, m) for m in masks])
+    return [held, span_swap(mesh, held, 1)]
 
 
 def per_device(mesh, right_side, fine_values, fine_columns, fine_sends, fine_order, fine_weights, middle_values, middle_columns, middle_sends, middle_order, middle_weights, coarsest_values, coarsest_columns):
@@ -683,9 +685,9 @@
         pieces3 = span_stage(mesh, pieces3, out)
     resid = fine_part(x1)
     b2, x2, out = call(
-        fine_restrict,
+        lambda *refs: fine_restrict(*(refs[2:4] + refs[:2] + refs[4:])),
         [vec2, vec2, tile],
-        arrived + [resid, v1, c1, w1, place1, m2, send2],
+        arrived[2:4] + arrived[:2] + arrived[4:] + [resid, v1, c1, w1, place1, m2, send2],
         [edge, vmem(4, lines, LANES), pad2],
     )
     d2 = x2

time: 100 us -> 99.4 us (level)
  waiting for transfers between devices: 22 us -> 16.6 us
  starting transfers between devices: 57.2 us -> 61.6 us
    ppermute x52, starting transfers between devices: 49.5 us -> 55.2 us  [swap(): return lax.ppermute(out, AXES, pairs)]
    ppermute x52, waiting for transfers between devices: 19.2 us -> 13.8 us  [swap(): return lax.ppermute(out, AXES, pairs)]
    ppermute x7, starting transfers between devices: 7.63 us -> 6.37 us  [span_swap(): return lax.ppermute(value, AXES, pairs)]
  transfers between devices with their start and end apart: 59 -> 59, of which waited for: 26 -> 22; matrix products, arithmetic and copies ran while one was open for 0% -> 0% of each run, Pallas kernels for 14% -> 14%
where the time goes in v7:
time: 99.4 us; the launch traced here: 99.2 us
  starting transfers between devices  61.6 us (62%)
  Pallas kernels  19.8 us (20%)
  waiting for transfers between devices  16.6 us (17%)
  between operations  1.02 us (1%)
    ppermute x52, starting transfers between devices, swap(): return lax.ppermute(out, AXES, pairs)  55.2 us
    pallas_call x28, Pallas kernels, call(): pl.pallas_call(body, out_shape=shapes, in_specs=specs, out_specs=[pl.Bloc...  19.8 us
    ppermute x52, waiting for transfers between devices, swap(): return lax.ppermute(out, AXES, pairs)  13.8 us
    ppermute x7, starting transfers between devices, span_swap(): return lax.ppermute(value, AXES, pairs)  6.37 us
    ppermute x7, waiting for transfers between devices, span_swap(): return lax.ppermute(value, AXES, pairs)  2.77 us
  transfers between devices with their start and end apart: 59, of which 22 were waited for; matrix products, arithmetic and copies ran while one was open for 0% of the time, Pallas kernels for 14%

profile of v7, /device:TPU:0, one launch (start us, length us, event | category | flops | bytes accessed | tf_op | source)
XLA Modules:
  0.0 99.2 jit_solution(10248620016441829923)
XLA Ops:
  1.9 4.0 %collective-permute-start = (f32[8,128]{1,0:T(8,128)S(1)}, f32[8,128]{1,0:T(8,128)S(1)}, u32[]{:S(2)}, u32[]{:S(2)}) collective-permute-start(f32[8,128]{1,0:T(8,128)S(1)} %get-tuple-element.60._), channel_id=1, source_target_pairs={{0,24},{1,25},{2,26},{3,27},{4,28},{5,29},{6,30},{7,31},{8,16},{9,... | collective-permute-start | bytes 12296 | tf_op jit(solution)/shard_map/ppermute | solution.py:545
  6.4 1.5 %collective-permute-start.2 = (f32[8,128]{1,0:T(8,128)S(1)}, f32[8,128]{1,0:T(8,128)S(1)}, u32[]{:S(2)}, u32[]{:S(2)}) collective-permute-start(f32[8,128]{1,0:T(8,128)S(1)} %get-tuple-element.60._), channel_id=1, source_target_pairs={{0,8},{1,2},{2,1},{3,4},{4,3},{5,6},{6,5},{7,15},{8,0},{9,10},{10,... | collective-permute-start | bytes 12296 | tf_op jit(solution)/shard_map/ppermute | solution.py:545
  8.1 2.6 %collective-permute-start.20 = (f32[1,136,128]{2,1,0:T(8,128)S(1)}, f32[1,136,128]{2,1,0:T(8,128)S(1)}, u32[]{:S(2)}, u32[]{:S(2)}) collective-permute-start(f32[1,136,128]{2,1,0:T(8,128)S(1)} %get-tuple-element.88.refs_1_), channel_id=1, source_target_pairs={{0,4},{1,5},{2,6},{3,7},{4,0},{5,1},{6,2},{7,3},{8,12},{9,13},{10,... | collective-permute-start | bytes 208904 | tf_op jit(solution)/shard_map/ppermute | solution.py:585
  11.2 1.5 %shard_map.142.refs_5_ = f32[4,16,128]{2,1,0:T(8,128)S(1)} custom-call(f32[4,16,128]{2,1,0:T(8,128)S(1)} %get-tuple-element.61.x_ref.refs_9_.refs_10_, f32[4,16,128]{2,1,0:T(8,128)S(1)} %get-tuple-element.62.b_ref, f32[8,4,4,16,128]{4,3,2,1,0:T(8,128)S(1)} %shard_map.141.v_ref.refs_6_, s32[8,16,128]{2,1,0:T(8,128)S(1)} %get-tuple-element.63.c_ref.refs_7_), custom_call_target="tpu_custom_call" | custom-call | tf_op jit(solution)/shard_map/pallas_call | solution.py:507
  15.1 1.5 %collective-permute-start.6 = (f32[8,128]{1,0:T(8,128)S(1)}, f32[8,128]{1,0:T(8,128)S(1)}, u32[]{:S(2)}, u32[]{:S(2)}) collective-permute-start(f32[8,128]{1,0:T(8,128)S(1)} %get-tuple-element.66._), channel_id=1, source_target_pairs={{0,8},{1,2},{2,1},{3,4},{4,3},{5,6},{6,5},{7,15},{8,0},{9,10},{10,... | collective-permute-start | bytes 12296 | tf_op jit(solution)/shard_map/ppermute | solution.py:545
  16.6 1.5 %shard_map.144.refs_5_ = f32[4,16,128]{2,1,0:T(8,128)S(1)} custom-call(f32[4,16,128]{2,1,0:T(8,128)S(1)} %get-tuple-element.67.x_ref.refs_9_, f32[4,16,128]{2,1,0:T(8,128)S(1)} %get-tuple-element.62.b_ref, f32[8,4,4,16,128]{4,3,2,1,0:T(8,128)S(1)} %shard_map.141.v_ref.refs_6_, s32[8,16,128]{2,1,0:T(8,128)S(1)} %get-tuple-element.63.c_ref.refs_7_), custom_call_target="tpu_custom_call" | custom-call | tf_op jit(solution)/shard_map/pallas_call | solution.py:507
  19.1 2.5 %collective-permute-start.10 = (f32[8,128]{1,0:T(8,128)S(1)}, f32[8,128]{1,0:T(8,128)S(1)}, u32[]{:S(2)}, u32[]{:S(2)}) collective-permute-start(f32[8,128]{1,0:T(8,128)S(1)} %get-tuple-element.70), channel_id=1, source_target_pairs={{0,24},{1,25},{2,26},{3,27},{4,28},{5,29},{6,30},{7,31},{8,16},{9,... | collective-permute-start | bytes 12296 | tf_op jit(solution)/shard_map/ppermute | solution.py:545
  22.2 1.5 %collective-permute-start.8 = (f32[8,128]{1,0:T(8,128)S(1)}, f32[8,128]{1,0:T(8,128)S(1)}, u32[]{:S(2)}, u32[]{:S(2)}) collective-permute-start(f32[8,128]{1,0:T(8,128)S(1)} %get-tuple-element.70), channel_id=1, source_target_pairs={{0,8},{1,2},{2,1},{3,4},{4,3},{5,6},{6,5},{7,15},{8,0},{9,10},{10,... | collective-permute-start | bytes 12296 | tf_op jit(solution)/shard_map/ppermute | solution.py:545
  24.2 1.5 %shard_map.147.refs_5_ = f32[4,16,128]{2,1,0:T(8,128)S(1)} custom-call(f32[4,16,128]{2,1,0:T(8,128)S(1)} %get-tuple-element.71.x_ref.refs_11_, f32[4,16,128]{2,1,0:T(8,128)S(1)} %get-tuple-element.62.b_ref, f32[8,4,4,16,128]{4,3,2,1,0:T(8,128)S(1)} %shard_map.141.v_ref.refs_6_, s32[8,16,128]{2,1,0:T(8,128)S(1)} %get-tuple-element.63.c_ref.refs_7_), custom_call_target="tpu_custom_call" | custom-call | tf_op jit(solution)/shard_map/pallas_call | solution.py:507
  26.5 1.5 %collective-permute-start.12 = (f32[8,128]{1,0:T(8,128)S(1)}, f32[8,128]{1,0:T(8,128)S(1)}, u32[]{:S(2)}, u32[]{:S(2)}) collective-permute-start(f32[8,128]{1,0:T(8,128)S(1)} %get-tuple-element.75._), channel_id=1, source_target_pairs={{0,24},{1,25},{2,26},{3,27},{4,28},{5,29},{6,30},{7,31},{8,16},{9,... | collective-permute-start | bytes 12296 | tf_op jit(solution)/shard_map/ppermute | solution.py:545
  32.5 2.4 %collective-permute-start.16 = (f32[8,128]{1,0:T(8,128)S(1)}, f32[8,128]{1,0:T(8,128)S(1)}, u32[]{:S(2)}, u32[]{:S(2)}) collective-permute-start(f32[8,128]{1,0:T(8,128)S(1)} %get-tuple-element.80._.refs_5_), channel_id=1, source_target_pairs={{0,24},{1,25},{2,26},{3,27},{4,28},{5,29},{6,30},{7,31},{8,16},{9,... | collective-permute-start | bytes 12296 | tf_op jit(solution)/shard_map/ppermute | solution.py:545
  35.5 1.5 %collective-permute-start.18 = (f32[8,128]{1,0:T(8,128)S(1)}, f32[8,128]{1,0:T(8,128)S(1)}, u32[]{:S(2)}, u32[]{:S(2)}) collective-permute-start(f32[8,128]{1,0:T(8,128)S(1)} %get-tuple-element.80._.refs_5_), channel_id=1, source_target_pairs={{0,8},{1,2},{2,1},{3,4},{4,3},{5,6},{6,5},{7,15},{8,0},{9,10},{10,... | collective-permute-start | bytes 12296 | tf_op jit(solution)/shard_map/ppermute | solution.py:545
  46.3 2.1 %collective-permute-start.29 = (f32[8,128]{1,0:T(8,128)S(1)}, f32[8,128]{1,0:T(8,128)S(1)}, u32[]{:S(2)}, u32[]{:S(2)}) collective-permute-start(f32[8,128]{1,0:T(8,128)S(1)} %shard_map.155), channel_id=1, source_target_pairs={{0,3},{1,2},{2,1},{3,0},{4,7},{5,6},{6,5},{7,4},{8,11},{9,10},{10,... | collective-permute-start | bytes 12296 | tf_op jit(solution)/shard_map/ppermute | solution.py:585
  48.4 1.9 %collective-permute-done.27 = f32[8,128]{1,0:T(8,128)S(1)} collective-permute-done((f32[8,128]{1,0:T(8,128)S(1)}, f32[8,128]{1,0:T(8,128)S(1)}, u32[]{:S(2)}, u32[]{:S(2)}) %collective-permute-start.27) | collective-permute-done | bytes 4128 | tf_op jit(solution)/shard_map/ppermute | solution.py:585
  53.0 2.4 %collective-permute-start.31 = (f32[8,128]{1,0:T(8,128)S(1)}, f32[8,128]{1,0:T(8,128)S(1)}, u32[]{:S(2)}, u32[]{:S(2)}) collective-permute-start(f32[8,128]{1,0:T(8,128)S(1)} %get-tuple-element.98), channel_id=1, source_target_pairs={{0,24},{1,25},{2,26},{3,27},{4,28},{5,29},{6,30},{7,31},{8,16},{9,... | collective-permute-start | bytes 12296 | tf_op jit(solution)/shard_map/ppermute | solution.py:545
  56.0 1.5 %collective-permute-start.33 = (f32[8,128]{1,0:T(8,128)S(1)}, f32[8,128]{1,0:T(8,128)S(1)}, u32[]{:S(2)}, u32[]{:S(2)}) collective-permute-start(f32[8,128]{1,0:T(8,128)S(1)} %get-tuple-element.98), channel_id=1, source_target_pairs={{0,8},{1,2},{2,1},{3,4},{4,3},{5,6},{6,5},{7,15},{8,0},{9,10},{10,... | collective-permute-start | bytes 12296 | tf_op jit(solution)/shard_map/ppermute | solution.py:545
  65.9 2.4 %collective-permute-start.39 = (f32[8,128]{1,0:T(8,128)S(1)}, f32[8,128]{1,0:T(8,128)S(1)}, u32[]{:S(2)}, u32[]{:S(2)}) collective-permute-start(f32[8,128]{1,0:T(8,128)S(1)} %get-tuple-element.103), channel_id=1, source_target_pairs={{0,24},{1,25},{2,26},{3,27},{4,28},{5,29},{6,30},{7,31},{8,16},{9,... | collective-permute-start | bytes 12296 | tf_op jit(solution)/shard_map/ppermute | solution.py:545
  70.4 1.5 %collective-permute-done.40.refs_1_ = f32[8,128]{1,0:T(8,128)S(1)} collective-permute-done((f32[8,128]{1,0:T(8,128)S(1)}, f32[8,128]{1,0:T(8,128)S(1)}, u32[]{:S(2)}, u32[]{:S(2)}) %collective-permute-start.40) | collective-permute-done | bytes 4128 | tf_op jit(solution)/shard_map/ppermute | solution.py:545
  76.5 1.5 %shard_map.160.refs_5_ = f32[4,16,128]{2,1,0:T(8,128)S(1)} custom-call(f32[4,16,128]{2,1,0:T(8,128)S(1)} %get-tuple-element.107.x_ref.refs_9_.refs_10_, f32[4,16,128]{2,1,0:T(8,128)S(1)} %get-tuple-element.62.b_ref, f32[8,4,4,16,128]{4,3,2,1,0:T(8,128)S(1)} %shard_map.141.v_ref.refs_6_, s32[8,16,128]{2,1,0:T(8,128)S(1)} %get-tuple-element.63.c_ref.refs_7_), custom_call_target="tpu_custom_call" | custom-call | tf_op jit(solution)/shard_map/pallas_call | solution.py:507
  78.9 2.4 %collective-permute-start.47 = (f32[8,128]{1,0:T(8,128)S(1)}, f32[8,128]{1,0:T(8,128)S(1)}, u32[]{:S(2)}, u32[]{:S(2)}) collective-permute-start(f32[8,128]{1,0:T(8,128)S(1)} %get-tuple-element.108), channel_id=1, source_target_pairs={{0,24},{1,25},{2,26},{3,27},{4,28},{5,29},{6,30},{7,31},{8,16},{9,... | collective-permute-start | bytes 12296 | tf_op jit(solution)/shard_map/ppermute | solution.py:545
  83.4 1.5 %shard_map.162.refs_5_ = f32[4,16,128]{2,1,0:T(8,128)S(1)} custom-call(f32[4,16,128]{2,1,0:T(8,128)S(1)} %get-tuple-element.109.x_ref.refs_9_, f32[4,16,128]{2,1,0:T(8,128)S(1)} %get-tuple-element.62.b_ref, f32[8,4,4,16,128]{4,3,2,1,0:T(8,128)S(1)} %shard_map.141.v_ref.refs_6_, s32[8,16,128]{2,1,0:T(8,128)S(1)} %get-tuple-element.63.c_ref.refs_7_), custom_call_target="tpu_custom_call" | custom-call | tf_op jit(solution)/shard_map/pallas_call | solution.py:507
  89.3 1.5 %shard_map.164.refs_5_ = f32[4,16,128]{2,1,0:T(8,128)S(1)} custom-call(f32[4,16,128]{2,1,0:T(8,128)S(1)} %get-tuple-element.112.x_ref.refs_9_, f32[4,16,128]{2,1,0:T(8,128)S(1)} %get-tuple-element.62.b_ref, f32[8,4,4,16,128]{4,3,2,1,0:T(8,128)S(1)} %shard_map.141.v_ref.refs_6_, s32[8,16,128]{2,1,0:T(8,128)S(1)} %get-tuple-element.63.c_ref.refs_7_), custom_call_target="tpu_custom_call" | custom-call | tf_op jit(solution)/shard_map/pallas_call | solution.py:507
  91.8 2.4 %collective-permute-start.55 = (f32[8,128]{1,0:T(8,128)S(1)}, f32[8,128]{1,0:T(8,128)S(1)}, u32[]{:S(2)}, u32[]{:S(2)}) collective-permute-start(f32[8,128]{1,0:T(8,128)S(1)} %get-tuple-element.114), channel_id=1, source_target_pairs={{0,24},{1,25},{2,26},{3,27},{4,28},{5,29},{6,30},{7,31},{8,16},{9,... | collective-permute-start | bytes 12296 | tf_op jit(solution)/shard_map/ppermute | solution.py:545
  96.3 1.5 %shard_map.166.refs_5_ = f32[4,16,128]{2,1,0:T(8,128)S(1)} custom-call(f32[4,16,128]{2,1,0:T(8,128)S(1)} %get-tuple-element.115.x_ref.refs_8_, f32[4,16,128]{2,1,0:T(8,128)S(1)} %get-tuple-element.62.b_ref, f32[8,4,4,16,128]{4,3,2,1,0:T(8,128)S(1)} %shard_map.141.v_ref.refs_6_, s32[8,16,128]{2,1,0:T(8,128)S(1)} %get-tuple-element.63.c_ref.refs_7_), custom_call_target="tpu_custom_call" | custom-call | tf_op jit(solution)/shard_map/pallas_call | solution.py:507
  (144 shorter events, 51.8 us)
Async XLA Ops:
  1.9 10.8 %collective-permute-start = (f32[8,128]{1,0:T(8,128)S(1)}, f32[8,128]{1,0:T(8,128)S(1)}, u32[]{:S(2)}, u32[]{:S(2)}) collective-permute-start(f32[8,128]{1,0:T(8,128)S(1)} %get-tuple-element.60._), channel_id=1, source_target_pairs={{0,24},{1,25},{2,26},{3,27},{4,28},{5,29},{6,30},{7,31},{8,16},{9,... | collective-permute-start | bytes 12296 | tf_op jit(solution)/shard_map/ppermute | solution.py:545
  5.9 6.8 %collective-permute-start.1 = (f32[8,128]{1,0:T(8,128)S(1)}, f32[8,128]{1,0:T(8,128)S(1)}, u32[]{:S(2)}, u32[]{:S(2)}) collective-permute-start(f32[8,128]{1,0:T(8,128)S(1)} %get-tuple-element.60._), channel_id=1, source_target_pairs={{0,8},{1,9},{2,10},{3,11},{4,12},{5,13},{6,14},{7,15},{8,0},{9,1},... | collective-permute-start | bytes 12296 | tf_op jit(solution)/shard_map/ppermute | solution.py:545
  6.4 6.3 %collective-permute-start.2 = (f32[8,128]{1,0:T(8,128)S(1)}, f32[8,128]{1,0:T(8,128)S(1)}, u32[]{:S(2)}, u32[]{:S(2)}) collective-permute-start(f32[8,128]{1,0:T(8,128)S(1)} %get-tuple-element.60._), channel_id=1, source_target_pairs={{0,8},{1,2},{2,1},{3,4},{4,3},{5,6},{6,5},{7,15},{8,0},{9,10},{10,... | collective-permute-start | bytes 12296 | tf_op jit(solution)/shard_map/ppermute | solution.py:545
  7.9 4.8 %collective-permute-start.3 = (f32[8,128]{1,0:T(8,128)S(1)}, f32[8,128]{1,0:T(8,128)S(1)}, u32[]{:S(2)}, u32[]{:S(2)}) collective-permute-start(f32[8,128]{1,0:T(8,128)S(1)} %get-tuple-element.60._), channel_id=1, source_target_pairs={{0,1},{1,0},{2,3},{3,2},{4,5},{5,4},{6,7},{7,6},{8,9},{9,8},{10,11... | collective-permute-start | bytes 12296 | tf_op jit(solution)/shard_map/ppermute | solution.py:545
  8.1 10.9 %collective-permute-start.20 = (f32[1,136,128]{2,1,0:T(8,128)S(1)}, f32[1,136,128]{2,1,0:T(8,128)S(1)}, u32[]{:S(2)}, u32[]{:S(2)}) collective-permute-start(f32[1,136,128]{2,1,0:T(8,128)S(1)} %get-tuple-element.88.refs_1_), channel_id=1, source_target_pairs={{0,4},{1,5},{2,6},{3,7},{4,0},{5,1},{6,2},{7,3},{8,12},{9,13},{10,... | collective-permute-start | bytes 208904 | tf_op jit(solution)/shard_map/ppermute | solution.py:585
  13.1 5.1 %collective-permute-start.4 = (f32[8,128]{1,0:T(8,128)S(1)}, f32[8,128]{1,0:T(8,128)S(1)}, u32[]{:S(2)}, u32[]{:S(2)}) collective-permute-start(f32[8,128]{1,0:T(8,128)S(1)} %get-tuple-element.66._), channel_id=1, source_target_pairs={{0,24},{1,25},{2,26},{3,27},{4,28},{5,29},{6,30},{7,31},{8,16},{9,... | collective-permute-start | bytes 12296 | tf_op jit(solution)/shard_map/ppermute | solution.py:545
  14.5 3.7 %collective-permute-start.5 = (f32[8,128]{1,0:T(8,128)S(1)}, f32[8,128]{1,0:T(8,128)S(1)}, u32[]{:S(2)}, u32[]{:S(2)}) collective-permute-start(f32[8,128]{1,0:T(8,128)S(1)} %get-tuple-element.66._), channel_id=1, source_target_pairs={{0,8},{1,9},{2,10},{3,11},{4,12},{5,13},{6,14},{7,15},{8,0},{9,1},... | collective-permute-start | bytes 12296 | tf_op jit(solution)/shard_map/ppermute | solution.py:545
  19.0 7.3 %collective-permute-start.21 = (f32[2,136,128]{2,1,0:T(8,128)S(1)}, f32[2,136,128]{2,1,0:T(8,128)S(1)}, u32[]{:S(2)}, u32[]{:S(2)}) collective-permute-start(f32[2,136,128]{2,1,0:T(8,128)S(1)} %pad_maximum_fusion.1), channel_id=1, source_target_pairs={{0,2},{1,3},{2,0},{3,1},{4,6},{5,7},{6,4},{7,5},{8,10},{9,11},{10,... | collective-permute-start | bytes 417800 | tf_op jit(solution)/shard_map/ppermute | solution.py:585
  19.1 6.6 %collective-permute-start.10 = (f32[8,128]{1,0:T(8,128)S(1)}, f32[8,128]{1,0:T(8,128)S(1)}, u32[]{:S(2)}, u32[]{:S(2)}) collective-permute-start(f32[8,128]{1,0:T(8,128)S(1)} %get-tuple-element.70), channel_id=1, source_target_pairs={{0,24},{1,25},{2,26},{3,27},{4,28},{5,29},{6,30},{7,31},{8,16},{9,... | collective-permute-start | bytes 12296 | tf_op jit(solution)/shard_map/ppermute | solution.py:545
  21.6 4.1 %collective-permute-start.11 = (f32[8,128]{1,0:T(8,128)S(1)}, f32[8,128]{1,0:T(8,128)S(1)}, u32[]{:S(2)}, u32[]{:S(2)}) collective-permute-start(f32[8,128]{1,0:T(8,128)S(1)} %get-tuple-element.70), channel_id=1, source_target_pairs={{0,8},{1,9},{2,10},{3,11},{4,12},{5,13},{6,14},{7,15},{8,0},{9,1},... | collective-permute-start | bytes 12296 | tf_op jit(solution)/shard_map/ppermute | solution.py:545
  26.4 10.7 %collective-permute-start.22 = (f32[4,136,128]{2,1,0:T(8,128)S(1)}, f32[4,136,128]{2,1,0:T(8,128)S(1)}, u32[]{:S(2)}, u32[]{:S(2)}) collective-permute-start(f32[4,136,128]{2,1,0:T(8,128)S(1)} %pad_maximum_fusion), channel_id=1, source_target_pairs={{0,1},{1,0},{2,3},{3,2},{4,5},{5,4},{6,7},{7,6},{8,9},{9,8},{10,11... | collective-permute-start | bytes 835592 | tf_op jit(solution)/shard_map/ppermute | solution.py:585
  26.5 4.6 %collective-permute-start.12 = (f32[8,128]{1,0:T(8,128)S(1)}, f32[8,128]{1,0:T(8,128)S(1)}, u32[]{:S(2)}, u32[]{:S(2)}) collective-permute-start(f32[8,128]{1,0:T(8,128)S(1)} %get-tuple-element.75._), channel_id=1, source_target_pairs={{0,24},{1,25},{2,26},{3,27},{4,28},{5,29},{6,30},{7,31},{8,16},{9,... | collective-permute-start | bytes 12296 | tf_op jit(solution)/shard_map/ppermute | solution.py:545
  32.5 5.1 %collective-permute-start.16 = (f32[8,128]{1,0:T(8,128)S(1)}, f32[8,128]{1,0:T(8,128)S(1)}, u32[]{:S(2)}, u32[]{:S(2)}) collective-permute-start(f32[8,128]{1,0:T(8,128)S(1)} %get-tuple-element.80._.refs_5_), channel_id=1, source_target_pairs={{0,24},{1,25},{2,26},{3,27},{4,28},{5,29},{6,30},{7,31},{8,16},{9,... | collective-permute-start | bytes 12296 | tf_op jit(solution)/shard_map/ppermute | solution.py:545
  39.4 4.5 %collective-permute-start.23 = (f32[8,128]{1,0:T(8,128)S(1)}, f32[8,128]{1,0:T(8,128)S(1)}, u32[]{:S(2)}, u32[]{:S(2)}) collective-permute-start(f32[8,128]{1,0:T(8,128)S(1)} %get-tuple-element.92._), channel_id=1, source_target_pairs={{0,24},{1,25},{2,26},{3,27},{4,28},{5,29},{6,30},{7,31},{8,16},{9,... | collective-permute-start | bytes 12296 | tf_op jit(solution)/shard_map/ppermute | solution.py:545
  45.4 4.9 %collective-permute-start.27 = (f32[8,128]{1,0:T(8,128)S(1)}, f32[8,128]{1,0:T(8,128)S(1)}, u32[]{:S(2)}, u32[]{:S(2)}) collective-permute-start(f32[8,128]{1,0:T(8,128)S(1)} %shard_map.155), channel_id=1, source_target_pairs={{0,7},{1,6},{2,5},{3,4},{4,3},{5,2},{6,1},{7,0},{8,15},{9,14},{10,... | collective-permute-start | bytes 12296 | tf_op jit(solution)/shard_map/ppermute | solution.py:585
  45.5 4.8 %collective-permute-start.28 = (f32[8,128]{1,0:T(8,128)S(1)}, f32[8,128]{1,0:T(8,128)S(1)}, u32[]{:S(2)}, u32[]{:S(2)}) collective-permute-start(f32[8,128]{1,0:T(8,128)S(1)} %shard_map.155), channel_id=1, source_target_pairs={{0,5},{1,4},{2,7},{3,6},{4,1},{5,0},{6,3},{7,2},{8,13},{9,12},{10,... | collective-permute-start | bytes 12296 | tf_op jit(solution)/shard_map/ppermute | solution.py:585
  46.3 4.0 %collective-permute-start.29 = (f32[8,128]{1,0:T(8,128)S(1)}, f32[8,128]{1,0:T(8,128)S(1)}, u32[]{:S(2)}, u32[]{:S(2)}) collective-permute-start(f32[8,128]{1,0:T(8,128)S(1)} %shard_map.155), channel_id=1, source_target_pairs={{0,3},{1,2},{2,1},{3,0},{4,7},{5,6},{6,5},{7,4},{8,11},{9,10},{10,... | collective-permute-start | bytes 12296 | tf_op jit(solution)/shard_map/ppermute | solution.py:585
  53.0 5.1 %collective-permute-start.31 = (f32[8,128]{1,0:T(8,128)S(1)}, f32[8,128]{1,0:T(8,128)S(1)}, u32[]{:S(2)}, u32[]{:S(2)}) collective-permute-start(f32[8,128]{1,0:T(8,128)S(1)} %get-tuple-element.98), channel_id=1, source_target_pairs={{0,24},{1,25},{2,26},{3,27},{4,28},{5,29},{6,30},{7,31},{8,16},{9,... | collective-permute-start | bytes 12296 | tf_op jit(solution)/shard_map/ppermute | solution.py:545
  60.0 4.5 %collective-permute-start.35 = (f32[8,128]{1,0:T(8,128)S(1)}, f32[8,128]{1,0:T(8,128)S(1)}, u32[]{:S(2)}, u32[]{:S(2)}) collective-permute-start(f32[8,128]{1,0:T(8,128)S(1)} %get-tuple-element.100), channel_id=1, source_target_pairs={{0,24},{1,25},{2,26},{3,27},{4,28},{5,29},{6,30},{7,31},{8,16},{9,... | collective-permute-start | bytes 12296 | tf_op jit(solution)/shard_map/ppermute | solution.py:545
  65.9 4.5 %collective-permute-start.39 = (f32[8,128]{1,0:T(8,128)S(1)}, f32[8,128]{1,0:T(8,128)S(1)}, u32[]{:S(2)}, u32[]{:S(2)}) collective-permute-start(f32[8,128]{1,0:T(8,128)S(1)} %get-tuple-element.103), channel_id=1, source_target_pairs={{0,24},{1,25},{2,26},{3,27},{4,28},{5,29},{6,30},{7,31},{8,16},{9,... | collective-permute-start | bytes 12296 | tf_op jit(solution)/shard_map/ppermute | solution.py:545
  72.9 5.0 %collective-permute-start.43 = (f32[8,128]{1,0:T(8,128)S(1)}, f32[8,128]{1,0:T(8,128)S(1)}, u32[]{:S(2)}, u32[]{:S(2)}) collective-permute-start(f32[8,128]{1,0:T(8,128)S(1)} %get-tuple-element.106), channel_id=1, source_target_pairs={{0,24},{1,25},{2,26},{3,27},{4,28},{5,29},{6,30},{7,31},{8,16},{9,... | collective-permute-start | bytes 12296 | tf_op jit(solution)/shard_map/ppermute | solution.py:545
  78.9 6.0 %collective-permute-start.47 = (f32[8,128]{1,0:T(8,128)S(1)}, f32[8,128]{1,0:T(8,128)S(1)}, u32[]{:S(2)}, u32[]{:S(2)}) collective-permute-start(f32[8,128]{1,0:T(8,128)S(1)} %get-tuple-element.108), channel_id=1, source_target_pairs={{0,24},{1,25},{2,26},{3,27},{4,28},{5,29},{6,30},{7,31},{8,16},{9,... | collective-permute-start | bytes 12296 | tf_op jit(solution)/shard_map/ppermute | solution.py:545
  85.8 5.0 %collective-permute-start.51 = (f32[8,128]{1,0:T(8,128)S(1)}, f32[8,128]{1,0:T(8,128)S(1)}, u32[]{:S(2)}, u32[]{:S(2)}) collective-permute-start(f32[8,128]{1,0:T(8,128)S(1)} %get-tuple-element.111), channel_id=1, source_target_pairs={{0,24},{1,25},{2,26},{3,27},{4,28},{5,29},{6,30},{7,31},{8,16},{9,... | collective-permute-start | bytes 12296 | tf_op jit(solution)/shard_map/ppermute | solution.py:545
  91.8 6.0 %collective-permute-start.55 = (f32[8,128]{1,0:T(8,128)S(1)}, f32[8,128]{1,0:T(8,128)S(1)}, u32[]{:S(2)}, u32[]{:S(2)}) collective-permute-start(f32[8,128]{1,0:T(8,128)S(1)} %get-tuple-element.114), channel_id=1, source_target_pairs={{0,24},{1,25},{2,26},{3,27},{4,28},{5,29},{6,30},{7,31},{8,16},{9,... | collective-permute-start | bytes 12296 | tf_op jit(solution)/shard_map/ppermute | solution.py:545
  (42 other events, 134.3 us)

commit v8 on v7

--- a/solution.py
+++ b/solution.py
@@ -335,15 +335,27 @@
     )
 
 
-def middle_residual(arrivals, b_ref, x_ref, v_ref, c_ref, edge_ref):
-    halo_lines(arrivals, edge_ref)
+def middle_local(x_ref, v_ref, c_ref, a_ref):
     acc = [jnp.zeros((SUBS, LANES), F32) for _ in range(4)]
     for j in range(4):
         source = [wide(x_ref[j, pl.ds(r, 1), :]) for r in range(4)]
-        source += [wide(edge_ref[pl.ds(4 * e + j, 1), :]) for e in range(2)]
         for kp in range(NNZ // 2):
             col = c_ref[kp]
             got = pick_lines(source, col >> 7, col & (LANES - 1))
+            for i in range(4):
+                acc[i] = acc[i] + v_ref[kp, i, j] * got
+    for i in range(4):
+        a_ref[i] = acc[i]
+
+
+def middle_residual(arrivals, b_ref, a_ref, v_ref, c_ref, edge_ref):
+    halo_lines(arrivals, edge_ref)
+    acc = [a_ref[i] for i in range(4)]
+    for j in range(4):
+        source = [wide(edge_ref[pl.ds(4 * e + j, 1), :]) for e in range(2)]
+        for kp in range(NNZ // 2):
+            col = c_ref[kp]
+            got = pick_lines(source, col >> 7, col & (LANES - 1), 4)
             for i in range(4):
                 acc[i] = acc[i] + v_ref[kp, i, j] * got
     return [b_ref[i] - duplicate(acc[i]) for i in range(4)]
@@ -363,10 +375,10 @@
 
 def middle_step(factors, last, *refs):
     arrivals = refs[:5]
-    b_ref, m_ref, x_ref, d_ref, v_ref, c_ref, s_ref, xo_ref, out_ref = refs[5:14]
-    do_ref = refs[14] if last is False else None
+    b_ref, a_ref, m_ref, x_ref, d_ref, v_ref, c_ref, s_ref, xo_ref, out_ref = refs[5:15]
+    do_ref = refs[15] if last is False else None
     edge_ref, pad_ref = refs[-2:]
-    resid = middle_residual(arrivals, b_ref, x_ref, v_ref, c_ref, edge_ref)
+    resid = middle_residual(arrivals, b_ref, a_ref, v_ref, c_ref, edge_ref)
     xs, ds = middle_update(factors, resid, m_ref, x_ref, d_ref)
     for i in range(4):
         xo_ref[i] = xs[i]
@@ -378,8 +390,8 @@
 
 def middle_restrict(*refs):
     arrivals = refs[:5]
-    b_ref, x_ref, v_ref, c_ref, w_ref, p_ref, out_ref, edge_ref, line_ref = refs[5:]
-    resid = middle_residual(arrivals, b_ref, x_ref, v_ref, c_ref, edge_ref)
+    b_ref, a_ref, v_ref, c_ref, w_ref, p_ref, out_ref, edge_ref, line_ref = refs[5:]
+    resid = middle_residual(arrivals, b_ref, a_ref, v_ref, c_ref, edge_ref)
     place = p_ref[...]
     high, lane = place >> 7, place & (LANES - 1)
     for j in range(4):
@@ -397,9 +409,9 @@
 
 def middle_prolong(factors, *refs):
     arrivals = refs[:5]
-    (b_ref, m_ref, x_ref, d_ref, v_ref, c_ref, x1_ref, w_ref, agg_ref, s_ref, xo_ref, out_ref, edge_ref, line_ref, pad_ref) = refs[5:]
+    (b_ref, a_ref, m_ref, x_ref, d_ref, v_ref, c_ref, x1_ref, w_ref, agg_ref, s_ref, xo_ref, out_ref, edge_ref, line_ref, pad_ref) = refs[5:]
     lines = x1_ref.shape[1]
-    resid = middle_residual(arrivals, b_ref, x_ref, v_ref, c_ref, edge_ref)
+    resid = middle_residual(arrivals, b_ref, a_ref, v_ref, c_ref, edge_ref)
     xs, _ = middle_update(factors, resid, m_ref, x_ref, d_ref)
     for j in range(4):
         line_ref[j] = xs[j]
@@ -680,9 +692,6 @@
     x1, d1, out = fine_next(2, arrived, resid, x1, d1, [m2])
 
     arrived = exchange(mesh, out, choice)
-    stages = len(span_places(group)) - 1
-    for _ in range(stages - 2):
-        pieces3 = span_stage(mesh, pieces3, out)
     resid = fine_part(x1)
     b2, x2, out = call(
         lambda *refs: fine_restrict(*(refs[2:4] + refs[:2] + refs[4:])),
@@ -692,8 +701,11 @@
     )
     d2 = x2
 
+    def middle_part(x):
+        return call(middle_local, vec2, [x, v2, c2])
+
     def middle_next(which, arrived, x, d, after=()):
-        args = arrived + [b2, m2, x, d, v2, c2, send2]
+        args = arrived + [b2, middle_part(x), m2, x, d, v2, c2, send2]
         last = which == KSM - 1
         result = call(
             lambda *refs: middle_step(
@@ -707,7 +719,8 @@
         return result[0], (None if last else result[2]), result[1]
 
     arrived = exchange(mesh, out, choice)
-    pieces3 = span_stage(mesh, pieces3, out)
+    for _ in range(len(span_places(group)) - 3):
+        pieces3 = span_stage(mesh, pieces3, out)
     v2, c2 = call(
         middle_blocks,
         [shape(NNZ // 2, 4, 4, SUBS, LANES), shape(NNZ // 2, SUBS, LANES, dtype=I32)],
@@ -727,24 +740,25 @@
         [native_rows(middle_weights), middle_order, middle_order.reshape(-1, LANES), out],
         free=(3,),
     )
-    v3, c3, m3 = call(
-        lambda *refs: coarse_tables(group, *refs),
-        [shape(NNZ, 4, 4, group, LANES), shape(NNZ, group, LANES, dtype=I32), shape(4, group, LANES)],
-        [me.reshape(1)] + pieces3 + [out],
-        [vmem(group, NNZ * 17, LANES)],
-        free=(1 + len(pieces3),),
-        smem=(0,),
-    )
-    x2, d2, out = middle_next(2, arrived, x2, d2, [agg2, m3])
+    pieces3 = span_stage(mesh, pieces3, out)
+    x2, d2, out = middle_next(2, arrived, x2, d2, [agg2])
 
     arrived = exchange(mesh, out, choice)
     agg1 = call(fine_inverse, shape(lines, LANES, dtype=I32), [fine_order, out], free=(1,))
     rhs3 = call(
         lambda *refs: middle_restrict(*(refs[:11] + refs[12:])),
         tile,
-        arrived + [b2, x2, v2, c2, w2, place2, agg1],
+        arrived + [b2, middle_part(x2), v2, c2, w2, place2, agg1],
         [edge, vmem(4, SUBS, LANES)],
         free=(11,),
+    )
+    v3, c3, m3 = call(
+        lambda *refs: coarse_tables(group, *refs),
+        [shape(NNZ, 4, 4, group, LANES), shape(NNZ, group, LANES, dtype=I32), shape(4, group, LANES)],
+        [me.reshape(1)] + pieces3 + [rhs3],
+        [vmem(group, NNZ * 17, LANES)],
+        free=(1 + len(pieces3),),
+        smem=(0,),
     )
     vec3 = vmem(4, group, LANES)
     x2, out = call(
@@ -761,7 +775,7 @@
     x1, out = call(
         lambda *refs: middle_prolong(factors[2], *refs),
         [vec1, tile],
-        arrived + [b2, m2, x2, d2, v2, c2, x1, w1, agg1, send1],
+        arrived + [b2, middle_part(x2), m2, x2, d2, v2, c2, x1, w1, agg1, send1],
         [edge, vmem(4, SUBS, LANES), pad1],
     )
     d1 = x1

time: 99.4 us -> 98.8 us (level)
  waiting for transfers between devices: 16.6 us -> 14.7 us
    ppermute x52, waiting for transfers between devices: 13.8 us -> 12.3 us  [swap(): return lax.ppermute(out, AXES, pairs)]
    pallas_call x28 -> x34, Pallas kernels: 19.8 us -> 20.4 us  [call(): pl.pallas_call(body, out_shape=shapes, in_specs=specs, out_specs=[pl.Bloc...]
  transfers between devices with their start and end apart: 59 -> 59, of which waited for: 22 -> 23; matrix products, arithmetic and copies ran while one was open for 0% -> 0% of each run, Pallas kernels for 14% -> 15%
where the time goes in v8:
time: 98.8 us; the launch traced here: 98.6 us
  starting transfers between devices  61.7 us (62%)
  Pallas kernels  20.4 us (21%)
  waiting for transfers between devices  14.7 us (15%)
  between operations  1.02 us (1%)
    ppermute x52, starting transfers between devices, swap(): return lax.ppermute(out, AXES, pairs)  55.3 us
    pallas_call x34, Pallas kernels, call(): pl.pallas_call(body, out_shape=shapes, in_specs=specs, out_specs=[pl.Bloc...  20.4 us
    ppermute x52, waiting for transfers between devices, swap(): return lax.ppermute(out, AXES, pairs)  12.3 us
    ppermute x7, starting transfers between devices, span_swap(): return lax.ppermute(value, AXES, pairs)  6.38 us
    ppermute x7, waiting for transfers between devices, span_swap(): return lax.ppermute(value, AXES, pairs)  2.36 us
  transfers between devices with their start and end apart: 59, of which 23 were waited for; matrix products, arithmetic and copies ran while one was open for 0% of the time, Pallas kernels for 15%

profile of v8, /device:TPU:0, one launch (start us, length us, event | category | flops | bytes accessed | tf_op | source)
XLA Modules:
  0.0 98.6 jit_solution(14888591650867555054)
XLA Ops:
  1.9 4.0 %collective-permute-start = (f32[8,128]{1,0:T(8,128)S(1)}, f32[8,128]{1,0:T(8,128)S(1)}, u32[]{:S(2)}, u32[]{:S(2)}) collective-permute-start(f32[8,128]{1,0:T(8,128)S(1)} %get-tuple-element.60._), channel_id=1, source_target_pairs={{0,24},{1,25},{2,26},{3,27},{4,28},{5,29},{6,30},{7,31},{8,16},{9,... | collective-permute-start | bytes 12296 | tf_op jit(solution)/shard_map/ppermute | solution.py:557
  6.4 1.5 %collective-permute-start.2 = (f32[8,128]{1,0:T(8,128)S(1)}, f32[8,128]{1,0:T(8,128)S(1)}, u32[]{:S(2)}, u32[]{:S(2)}) collective-permute-start(f32[8,128]{1,0:T(8,128)S(1)} %get-tuple-element.60._), channel_id=1, source_target_pairs={{0,8},{1,2},{2,1},{3,4},{4,3},{5,6},{6,5},{7,15},{8,0},{9,10},{10,... | collective-permute-start | bytes 12296 | tf_op jit(solution)/shard_map/ppermute | solution.py:557
  8.1 2.6 %collective-permute-start.28 = (f32[1,136,128]{2,1,0:T(8,128)S(1)}, f32[1,136,128]{2,1,0:T(8,128)S(1)}, u32[]{:S(2)}, u32[]{:S(2)}) collective-permute-start(f32[1,136,128]{2,1,0:T(8,128)S(1)} %get-tuple-element.92.refs_1_), channel_id=1, source_target_pairs={{0,4},{1,5},{2,6},{3,7},{4,0},{5,1},{6,2},{7,3},{8,12},{9,13},{10,... | collective-permute-start | bytes 208904 | tf_op jit(solution)/shard_map/ppermute | solution.py:597
  11.2 1.5 %shard_map.142.refs_5_ = f32[4,16,128]{2,1,0:T(8,128)S(1)} custom-call(f32[4,16,128]{2,1,0:T(8,128)S(1)} %get-tuple-element.61.x_ref.refs_9_.refs_10_, f32[4,16,128]{2,1,0:T(8,128)S(1)} %get-tuple-element.62.b_ref, f32[8,4,4,16,128]{4,3,2,1,0:T(8,128)S(1)} %shard_map.141.v_ref.refs_6_, s32[8,16,128]{2,1,0:T(8,128)S(1)} %get-tuple-element.63.c_ref.refs_7_), custom_call_target="tpu_custom_call" | custom-call | tf_op jit(solution)/shard_map/pallas_call | solution.py:519
  15.1 1.5 %collective-permute-start.6 = (f32[8,128]{1,0:T(8,128)S(1)}, f32[8,128]{1,0:T(8,128)S(1)}, u32[]{:S(2)}, u32[]{:S(2)}) collective-permute-start(f32[8,128]{1,0:T(8,128)S(1)} %get-tuple-element.66._), channel_id=1, source_target_pairs={{0,8},{1,2},{2,1},{3,4},{4,3},{5,6},{6,5},{7,15},{8,0},{9,10},{10,... | collective-permute-start | bytes 12296 | tf_op jit(solution)/shard_map/ppermute | solution.py:557
  16.6 1.5 %shard_map.144.refs_5_ = f32[4,16,128]{2,1,0:T(8,128)S(1)} custom-call(f32[4,16,128]{2,1,0:T(8,128)S(1)} %get-tuple-element.67.x_ref.refs_9_, f32[4,16,128]{2,1,0:T(8,128)S(1)} %get-tuple-element.62.b_ref, f32[8,4,4,16,128]{4,3,2,1,0:T(8,128)S(1)} %shard_map.141.v_ref.refs_6_, s32[8,16,128]{2,1,0:T(8,128)S(1)} %get-tuple-element.63.c_ref.refs_7_), custom_call_target="tpu_custom_call" | custom-call | tf_op jit(solution)/shard_map/pallas_call | solution.py:519
  19.0 2.5 %collective-permute-start.10 = (f32[8,128]{1,0:T(8,128)S(1)}, f32[8,128]{1,0:T(8,128)S(1)}, u32[]{:S(2)}, u32[]{:S(2)}) collective-permute-start(f32[8,128]{1,0:T(8,128)S(1)} %get-tuple-element.70), channel_id=1, source_target_pairs={{0,24},{1,25},{2,26},{3,27},{4,28},{5,29},{6,30},{7,31},{8,16},{9,... | collective-permute-start | bytes 12296 | tf_op jit(solution)/shard_map/ppermute | solution.py:557
  22.0 1.5 %collective-permute-start.8 = (f32[8,128]{1,0:T(8,128)S(1)}, f32[8,128]{1,0:T(8,128)S(1)}, u32[]{:S(2)}, u32[]{:S(2)}) collective-permute-start(f32[8,128]{1,0:T(8,128)S(1)} %get-tuple-element.70), channel_id=1, source_target_pairs={{0,8},{1,2},{2,1},{3,4},{4,3},{5,6},{6,5},{7,15},{8,0},{9,10},{10,... | collective-permute-start | bytes 12296 | tf_op jit(solution)/shard_map/ppermute | solution.py:557
  23.5 1.5 %shard_map.147.refs_5_ = f32[4,16,128]{2,1,0:T(8,128)S(1)} custom-call(f32[4,16,128]{2,1,0:T(8,128)S(1)} %get-tuple-element.71.x_ref.refs_12_, f32[4,16,128]{2,1,0:T(8,128)S(1)} %get-tuple-element.62.b_ref, f32[8,4,4,16,128]{4,3,2,1,0:T(8,128)S(1)} %shard_map.141.v_ref.refs_6_, s32[8,16,128]{2,1,0:T(8,128)S(1)} %get-tuple-element.63.c_ref.refs_7_), custom_call_target="tpu_custom_call" | custom-call | tf_op jit(solution)/shard_map/pallas_call | solution.py:519
  26.3 1.5 %collective-permute-start.12 = (f32[8,128]{1,0:T(8,128)S(1)}, f32[8,128]{1,0:T(8,128)S(1)}, u32[]{:S(2)}, u32[]{:S(2)}) collective-permute-start(f32[8,128]{1,0:T(8,128)S(1)} %get-tuple-element.75._), channel_id=1, source_target_pairs={{0,24},{1,25},{2,26},{3,27},{4,28},{5,29},{6,30},{7,31},{8,16},{9,... | collective-permute-start | bytes 12296 | tf_op jit(solution)/shard_map/ppermute | solution.py:557
  28.3 1.5 %collective-permute-start.14 = (f32[8,128]{1,0:T(8,128)S(1)}, f32[8,128]{1,0:T(8,128)S(1)}, u32[]{:S(2)}, u32[]{:S(2)}) collective-permute-start(f32[8,128]{1,0:T(8,128)S(1)} %get-tuple-element.75._), channel_id=1, source_target_pairs={{0,8},{1,2},{2,1},{3,4},{4,3},{5,6},{6,5},{7,15},{8,0},{9,10},{10,... | collective-permute-start | bytes 12296 | tf_op jit(solution)/shard_map/ppermute | solution.py:557
  32.3 2.5 %collective-permute-start.16 = (f32[8,128]{1,0:T(8,128)S(1)}, f32[8,128]{1,0:T(8,128)S(1)}, u32[]{:S(2)}, u32[]{:S(2)}) collective-permute-start(f32[8,128]{1,0:T(8,128)S(1)} %get-tuple-element.80._), channel_id=1, source_target_pairs={{0,24},{1,25},{2,26},{3,27},{4,28},{5,29},{6,30},{7,31},{8,16},{9,... | collective-permute-start | bytes 12296 | tf_op jit(solution)/shard_map/ppermute | solution.py:557
  35.4 1.5 %collective-permute-start.18 = (f32[8,128]{1,0:T(8,128)S(1)}, f32[8,128]{1,0:T(8,128)S(1)}, u32[]{:S(2)}, u32[]{:S(2)}) collective-permute-start(f32[8,128]{1,0:T(8,128)S(1)} %get-tuple-element.80._), channel_id=1, source_target_pairs={{0,8},{1,2},{2,1},{3,4},{4,3},{5,6},{6,5},{7,15},{8,0},{9,10},{10,... | collective-permute-start | bytes 12296 | tf_op jit(solution)/shard_map/ppermute | solution.py:557
  41.2 1.5 %collective-permute-start.22 = (f32[8,128]{1,0:T(8,128)S(1)}, f32[8,128]{1,0:T(8,128)S(1)}, u32[]{:S(2)}, u32[]{:S(2)}) collective-permute-start(f32[8,128]{1,0:T(8,128)S(1)} %get-tuple-element.84._), channel_id=1, source_target_pairs={{0,8},{1,2},{2,1},{3,4},{4,3},{5,6},{6,5},{7,15},{8,0},{9,10},{10,... | collective-permute-start | bytes 12296 | tf_op jit(solution)/shard_map/ppermute | solution.py:557
  48.0 1.9 %collective-permute-done.24 = f32[8,128]{1,0:T(8,128)S(1)} collective-permute-done((f32[8,128]{1,0:T(8,128)S(1)}, f32[8,128]{1,0:T(8,128)S(1)}, u32[]{:S(2)}, u32[]{:S(2)}) %collective-permute-start.24) | collective-permute-done | bytes 4128 | tf_op jit(solution)/shard_map/ppermute | solution.py:597
  52.7 2.5 %collective-permute-start.31 = (f32[8,128]{1,0:T(8,128)S(1)}, f32[8,128]{1,0:T(8,128)S(1)}, u32[]{:S(2)}, u32[]{:S(2)}) collective-permute-start(f32[8,128]{1,0:T(8,128)S(1)} %get-tuple-element.98), channel_id=1, source_target_pairs={{0,24},{1,25},{2,26},{3,27},{4,28},{5,29},{6,30},{7,31},{8,16},{9,... | collective-permute-start | bytes 12296 | tf_op jit(solution)/shard_map/ppermute | solution.py:557
  55.7 1.5 %collective-permute-start.33 = (f32[8,128]{1,0:T(8,128)S(1)}, f32[8,128]{1,0:T(8,128)S(1)}, u32[]{:S(2)}, u32[]{:S(2)}) collective-permute-start(f32[8,128]{1,0:T(8,128)S(1)} %get-tuple-element.98), channel_id=1, source_target_pairs={{0,8},{1,2},{2,1},{3,4},{4,3},{5,6},{6,5},{7,15},{8,0},{9,10},{10,... | collective-permute-start | bytes 12296 | tf_op jit(solution)/shard_map/ppermute | solution.py:557
  65.4 2.5 %collective-permute-start.39 = (f32[8,128]{1,0:T(8,128)S(1)}, f32[8,128]{1,0:T(8,128)S(1)}, u32[]{:S(2)}, u32[]{:S(2)}) collective-permute-start(f32[8,128]{1,0:T(8,128)S(1)} %get-tuple-element.103), channel_id=1, source_target_pairs={{0,24},{1,25},{2,26},{3,27},{4,28},{5,29},{6,30},{7,31},{8,16},{9,... | collective-permute-start | bytes 12296 | tf_op jit(solution)/shard_map/ppermute | solution.py:557
  75.8 1.5 %shard_map.166.refs_5_ = f32[4,16,128]{2,1,0:T(8,128)S(1)} custom-call(f32[4,16,128]{2,1,0:T(8,128)S(1)} %get-tuple-element.107.x_ref.refs_9_.refs_10_, f32[4,16,128]{2,1,0:T(8,128)S(1)} %get-tuple-element.62.b_ref, f32[8,4,4,16,128]{4,3,2,1,0:T(8,128)S(1)} %shard_map.141.v_ref.refs_6_, s32[8,16,128]{2,1,0:T(8,128)S(1)} %get-tuple-element.63.c_ref.refs_7_), custom_call_target="tpu_custom_call" | custom-call | tf_op jit(solution)/shard_map/pallas_call | solution.py:519
  78.3 2.5 %collective-permute-start.47 = (f32[8,128]{1,0:T(8,128)S(1)}, f32[8,128]{1,0:T(8,128)S(1)}, u32[]{:S(2)}, u32[]{:S(2)}) collective-permute-start(f32[8,128]{1,0:T(8,128)S(1)} %get-tuple-element.108), channel_id=1, source_target_pairs={{0,24},{1,25},{2,26},{3,27},{4,28},{5,29},{6,30},{7,31},{8,16},{9,... | collective-permute-start | bytes 12296 | tf_op jit(solution)/shard_map/ppermute | solution.py:557
  82.8 1.5 %shard_map.168.refs_5_ = f32[4,16,128]{2,1,0:T(8,128)S(1)} custom-call(f32[4,16,128]{2,1,0:T(8,128)S(1)} %get-tuple-element.109.x_ref.refs_9_, f32[4,16,128]{2,1,0:T(8,128)S(1)} %get-tuple-element.62.b_ref, f32[8,4,4,16,128]{4,3,2,1,0:T(8,128)S(1)} %shard_map.141.v_ref.refs_6_, s32[8,16,128]{2,1,0:T(8,128)S(1)} %get-tuple-element.63.c_ref.refs_7_), custom_call_target="tpu_custom_call" | custom-call | tf_op jit(solution)/shard_map/pallas_call | solution.py:519
  88.7 1.5 %shard_map.170.refs_5_ = f32[4,16,128]{2,1,0:T(8,128)S(1)} custom-call(f32[4,16,128]{2,1,0:T(8,128)S(1)} %get-tuple-element.112.x_ref.refs_9_, f32[4,16,128]{2,1,0:T(8,128)S(1)} %get-tuple-element.62.b_ref, f32[8,4,4,16,128]{4,3,2,1,0:T(8,128)S(1)} %shard_map.141.v_ref.refs_6_, s32[8,16,128]{2,1,0:T(8,128)S(1)} %get-tuple-element.63.c_ref.refs_7_), custom_call_target="tpu_custom_call" | custom-call | tf_op jit(solution)/shard_map/pallas_call | solution.py:519
  91.2 2.5 %collective-permute-start.55 = (f32[8,128]{1,0:T(8,128)S(1)}, f32[8,128]{1,0:T(8,128)S(1)}, u32[]{:S(2)}, u32[]{:S(2)}) collective-permute-start(f32[8,128]{1,0:T(8,128)S(1)} %get-tuple-element.114), channel_id=1, source_target_pairs={{0,24},{1,25},{2,26},{3,27},{4,28},{5,29},{6,30},{7,31},{8,16},{9,... | collective-permute-start | bytes 12296 | tf_op jit(solution)/shard_map/ppermute | solution.py:557
  95.6 1.5 %shard_map.172.refs_5_ = f32[4,16,128]{2,1,0:T(8,128)S(1)} custom-call(f32[4,16,128]{2,1,0:T(8,128)S(1)} %get-tuple-element.115.x_ref.refs_8_, f32[4,16,128]{2,1,0:T(8,128)S(1)} %get-tuple-element.62.b_ref, f32[8,4,4,16,128]{4,3,2,1,0:T(8,128)S(1)} %shard_map.141.v_ref.refs_6_, s32[8,16,128]{2,1,0:T(8,128)S(1)} %get-tuple-element.63.c_ref.refs_7_), custom_call_target="tpu_custom_call" | custom-call | tf_op jit(solution)/shard_map/pallas_call | solution.py:519
  (150 shorter events, 51.8 us)
Async XLA Ops:
  1.9 10.8 %collective-permute-start = (f32[8,128]{1,0:T(8,128)S(1)}, f32[8,128]{1,0:T(8,128)S(1)}, u32[]{:S(2)}, u32[]{:S(2)}) collective-permute-start(f32[8,128]{1,0:T(8,128)S(1)} %get-tuple-element.60._), channel_id=1, source_target_pairs={{0,24},{1,25},{2,26},{3,27},{4,28},{5,29},{6,30},{7,31},{8,16},{9,... | collective-permute-start | bytes 12296 | tf_op jit(solution)/shard_map/ppermute | solution.py:557
  5.9 6.8 %collective-permute-start.1 = (f32[8,128]{1,0:T(8,128)S(1)}, f32[8,128]{1,0:T(8,128)S(1)}, u32[]{:S(2)}, u32[]{:S(2)}) collective-permute-start(f32[8,128]{1,0:T(8,128)S(1)} %get-tuple-element.60._), channel_id=1, source_target_pairs={{0,8},{1,9},{2,10},{3,11},{4,12},{5,13},{6,14},{7,15},{8,0},{9,1},... | collective-permute-start | bytes 12296 | tf_op jit(solution)/shard_map/ppermute | solution.py:557
  6.4 6.3 %collective-permute-start.2 = (f32[8,128]{1,0:T(8,128)S(1)}, f32[8,128]{1,0:T(8,128)S(1)}, u32[]{:S(2)}, u32[]{:S(2)}) collective-permute-start(f32[8,128]{1,0:T(8,128)S(1)} %get-tuple-element.60._), channel_id=1, source_target_pairs={{0,8},{1,2},{2,1},{3,4},{4,3},{5,6},{6,5},{7,15},{8,0},{9,10},{10,... | collective-permute-start | bytes 12296 | tf_op jit(solution)/shard_map/ppermute | solution.py:557
  7.9 4.8 %collective-permute-start.3 = (f32[8,128]{1,0:T(8,128)S(1)}, f32[8,128]{1,0:T(8,128)S(1)}, u32[]{:S(2)}, u32[]{:S(2)}) collective-permute-start(f32[8,128]{1,0:T(8,128)S(1)} %get-tuple-element.60._), channel_id=1, source_target_pairs={{0,1},{1,0},{2,3},{3,2},{4,5},{5,4},{6,7},{7,6},{8,9},{9,8},{10,11... | collective-permute-start | bytes 12296 | tf_op jit(solution)/shard_map/ppermute | solution.py:557
  8.1 18.1 %collective-permute-start.28 = (f32[1,136,128]{2,1,0:T(8,128)S(1)}, f32[1,136,128]{2,1,0:T(8,128)S(1)}, u32[]{:S(2)}, u32[]{:S(2)}) collective-permute-start(f32[1,136,128]{2,1,0:T(8,128)S(1)} %get-tuple-element.92.refs_1_), channel_id=1, source_target_pairs={{0,4},{1,5},{2,6},{3,7},{4,0},{5,1},{6,2},{7,3},{8,12},{9,13},{10,... | collective-permute-start | bytes 208904 | tf_op jit(solution)/shard_map/ppermute | solution.py:597
  13.1 5.1 %collective-permute-start.4 = (f32[8,128]{1,0:T(8,128)S(1)}, f32[8,128]{1,0:T(8,128)S(1)}, u32[]{:S(2)}, u32[]{:S(2)}) collective-permute-start(f32[8,128]{1,0:T(8,128)S(1)} %get-tuple-element.66._), channel_id=1, source_target_pairs={{0,24},{1,25},{2,26},{3,27},{4,28},{5,29},{6,30},{7,31},{8,16},{9,... | collective-permute-start | bytes 12296 | tf_op jit(solution)/shard_map/ppermute | solution.py:557
  14.5 3.7 %collective-permute-start.5 = (f32[8,128]{1,0:T(8,128)S(1)}, f32[8,128]{1,0:T(8,128)S(1)}, u32[]{:S(2)}, u32[]{:S(2)}) collective-permute-start(f32[8,128]{1,0:T(8,128)S(1)} %get-tuple-element.66._), channel_id=1, source_target_pairs={{0,8},{1,9},{2,10},{3,11},{4,12},{5,13},{6,14},{7,15},{8,0},{9,1},... | collective-permute-start | bytes 12296 | tf_op jit(solution)/shard_map/ppermute | solution.py:557
  19.0 6.0 %collective-permute-start.10 = (f32[8,128]{1,0:T(8,128)S(1)}, f32[8,128]{1,0:T(8,128)S(1)}, u32[]{:S(2)}, u32[]{:S(2)}) collective-permute-start(f32[8,128]{1,0:T(8,128)S(1)} %get-tuple-element.70), channel_id=1, source_target_pairs={{0,24},{1,25},{2,26},{3,27},{4,28},{5,29},{6,30},{7,31},{8,16},{9,... | collective-permute-start | bytes 12296 | tf_op jit(solution)/shard_map/ppermute | solution.py:557
  21.5 3.6 %collective-permute-start.11 = (f32[8,128]{1,0:T(8,128)S(1)}, f32[8,128]{1,0:T(8,128)S(1)}, u32[]{:S(2)}, u32[]{:S(2)}) collective-permute-start(f32[8,128]{1,0:T(8,128)S(1)} %get-tuple-element.70), channel_id=1, source_target_pairs={{0,8},{1,9},{2,10},{3,11},{4,12},{5,13},{6,14},{7,15},{8,0},{9,1},... | collective-permute-start | bytes 12296 | tf_op jit(solution)/shard_map/ppermute | solution.py:557
  22.0 3.6 %collective-permute-start.8 = (f32[8,128]{1,0:T(8,128)S(1)}, f32[8,128]{1,0:T(8,128)S(1)}, u32[]{:S(2)}, u32[]{:S(2)}) collective-permute-start(f32[8,128]{1,0:T(8,128)S(1)} %get-tuple-element.70), channel_id=1, source_target_pairs={{0,8},{1,2},{2,1},{3,4},{4,3},{5,6},{6,5},{7,15},{8,0},{9,10},{10,... | collective-permute-start | bytes 12296 | tf_op jit(solution)/shard_map/ppermute | solution.py:557
  26.2 6.0 %collective-permute-start.29 = (f32[2,136,128]{2,1,0:T(8,128)S(1)}, f32[2,136,128]{2,1,0:T(8,128)S(1)}, u32[]{:S(2)}, u32[]{:S(2)}) collective-permute-start(f32[2,136,128]{2,1,0:T(8,128)S(1)} %pad_maximum_fusion.1), channel_id=1, source_target_pairs={{0,2},{1,3},{2,0},{3,1},{4,6},{5,7},{6,4},{7,5},{8,10},{9,11},{10,... | collective-permute-start | bytes 417800 | tf_op jit(solution)/shard_map/ppermute | solution.py:597
  26.3 4.6 %collective-permute-start.12 = (f32[8,128]{1,0:T(8,128)S(1)}, f32[8,128]{1,0:T(8,128)S(1)}, u32[]{:S(2)}, u32[]{:S(2)}) collective-permute-start(f32[8,128]{1,0:T(8,128)S(1)} %get-tuple-element.75._), channel_id=1, source_target_pairs={{0,24},{1,25},{2,26},{3,27},{4,28},{5,29},{6,30},{7,31},{8,16},{9,... | collective-permute-start | bytes 12296 | tf_op jit(solution)/shard_map/ppermute | solution.py:557
  32.2 18.4 %collective-permute-start.30 = (f32[4,136,128]{2,1,0:T(8,128)S(1)}, f32[4,136,128]{2,1,0:T(8,128)S(1)}, u32[]{:S(2)}, u32[]{:S(2)}) collective-permute-start(f32[4,136,128]{2,1,0:T(8,128)S(1)} %pad_maximum_fusion), channel_id=1, source_target_pairs={{0,1},{1,0},{2,3},{3,2},{4,5},{5,4},{6,7},{7,6},{8,9},{9,8},{10,11... | collective-permute-start | bytes 835592 | tf_op jit(solution)/shard_map/ppermute | solution.py:597
  32.3 5.6 %collective-permute-start.16 = (f32[8,128]{1,0:T(8,128)S(1)}, f32[8,128]{1,0:T(8,128)S(1)}, u32[]{:S(2)}, u32[]{:S(2)}) collective-permute-start(f32[8,128]{1,0:T(8,128)S(1)} %get-tuple-element.80._), channel_id=1, source_target_pairs={{0,24},{1,25},{2,26},{3,27},{4,28},{5,29},{6,30},{7,31},{8,16},{9,... | collective-permute-start | bytes 12296 | tf_op jit(solution)/shard_map/ppermute | solution.py:557
  39.2 4.5 %collective-permute-start.20 = (f32[8,128]{1,0:T(8,128)S(1)}, f32[8,128]{1,0:T(8,128)S(1)}, u32[]{:S(2)}, u32[]{:S(2)}) collective-permute-start(f32[8,128]{1,0:T(8,128)S(1)} %get-tuple-element.84._), channel_id=1, source_target_pairs={{0,24},{1,25},{2,26},{3,27},{4,28},{5,29},{6,30},{7,31},{8,16},{9,... | collective-permute-start | bytes 12296 | tf_op jit(solution)/shard_map/ppermute | solution.py:557
  45.1 4.9 %collective-permute-start.24 = (f32[8,128]{1,0:T(8,128)S(1)}, f32[8,128]{1,0:T(8,128)S(1)}, u32[]{:S(2)}, u32[]{:S(2)}) collective-permute-start(f32[8,128]{1,0:T(8,128)S(1)} %shard_map.157.refs_5_), channel_id=1, source_target_pairs={{0,7},{1,6},{2,5},{3,4},{4,3},{5,2},{6,1},{7,0},{8,15},{9,14},{10,... | collective-permute-start | bytes 12296 | tf_op jit(solution)/shard_map/ppermute | solution.py:597
  45.1 4.8 %collective-permute-start.25 = (f32[8,128]{1,0:T(8,128)S(1)}, f32[8,128]{1,0:T(8,128)S(1)}, u32[]{:S(2)}, u32[]{:S(2)}) collective-permute-start(f32[8,128]{1,0:T(8,128)S(1)} %shard_map.157.refs_5_), channel_id=1, source_target_pairs={{0,5},{1,4},{2,7},{3,6},{4,1},{5,0},{6,3},{7,2},{8,13},{9,12},{10,... | collective-permute-start | bytes 12296 | tf_op jit(solution)/shard_map/ppermute | solution.py:597
  52.7 5.3 %collective-permute-start.31 = (f32[8,128]{1,0:T(8,128)S(1)}, f32[8,128]{1,0:T(8,128)S(1)}, u32[]{:S(2)}, u32[]{:S(2)}) collective-permute-start(f32[8,128]{1,0:T(8,128)S(1)} %get-tuple-element.98), channel_id=1, source_target_pairs={{0,24},{1,25},{2,26},{3,27},{4,28},{5,29},{6,30},{7,31},{8,16},{9,... | collective-permute-start | bytes 12296 | tf_op jit(solution)/shard_map/ppermute | solution.py:557
  59.5 4.5 %collective-permute-start.35 = (f32[8,128]{1,0:T(8,128)S(1)}, f32[8,128]{1,0:T(8,128)S(1)}, u32[]{:S(2)}, u32[]{:S(2)}) collective-permute-start(f32[8,128]{1,0:T(8,128)S(1)} %get-tuple-element.100), channel_id=1, source_target_pairs={{0,24},{1,25},{2,26},{3,27},{4,28},{5,29},{6,30},{7,31},{8,16},{9,... | collective-permute-start | bytes 12296 | tf_op jit(solution)/shard_map/ppermute | solution.py:557
  65.4 4.7 %collective-permute-start.39 = (f32[8,128]{1,0:T(8,128)S(1)}, f32[8,128]{1,0:T(8,128)S(1)}, u32[]{:S(2)}, u32[]{:S(2)}) collective-permute-start(f32[8,128]{1,0:T(8,128)S(1)} %get-tuple-element.103), channel_id=1, source_target_pairs={{0,24},{1,25},{2,26},{3,27},{4,28},{5,29},{6,30},{7,31},{8,16},{9,... | collective-permute-start | bytes 12296 | tf_op jit(solution)/shard_map/ppermute | solution.py:557
  72.3 5.0 %collective-permute-start.43 = (f32[8,128]{1,0:T(8,128)S(1)}, f32[8,128]{1,0:T(8,128)S(1)}, u32[]{:S(2)}, u32[]{:S(2)}) collective-permute-start(f32[8,128]{1,0:T(8,128)S(1)} %get-tuple-element.106), channel_id=1, source_target_pairs={{0,24},{1,25},{2,26},{3,27},{4,28},{5,29},{6,30},{7,31},{8,16},{9,... | collective-permute-start | bytes 12296 | tf_op jit(solution)/shard_map/ppermute | solution.py:557
  78.3 6.0 %collective-permute-start.47 = (f32[8,128]{1,0:T(8,128)S(1)}, f32[8,128]{1,0:T(8,128)S(1)}, u32[]{:S(2)}, u32[]{:S(2)}) collective-permute-start(f32[8,128]{1,0:T(8,128)S(1)} %get-tuple-element.108), channel_id=1, source_target_pairs={{0,24},{1,25},{2,26},{3,27},{4,28},{5,29},{6,30},{7,31},{8,16},{9,... | collective-permute-start | bytes 12296 | tf_op jit(solution)/shard_map/ppermute | solution.py:557
  85.2 5.0 %collective-permute-start.51 = (f32[8,128]{1,0:T(8,128)S(1)}, f32[8,128]{1,0:T(8,128)S(1)}, u32[]{:S(2)}, u32[]{:S(2)}) collective-permute-start(f32[8,128]{1,0:T(8,128)S(1)} %get-tuple-element.111), channel_id=1, source_target_pairs={{0,24},{1,25},{2,26},{3,27},{4,28},{5,29},{6,30},{7,31},{8,16},{9,... | collective-permute-start | bytes 12296 | tf_op jit(solution)/shard_map/ppermute | solution.py:557
  91.2 6.0 %collective-permute-start.55 = (f32[8,128]{1,0:T(8,128)S(1)}, f32[8,128]{1,0:T(8,128)S(1)}, u32[]{:S(2)}, u32[]{:S(2)}) collective-permute-start(f32[8,128]{1,0:T(8,128)S(1)} %get-tuple-element.114), channel_id=1, source_target_pairs={{0,24},{1,25},{2,26},{3,27},{4,28},{5,29},{6,30},{7,31},{8,16},{9,... | collective-permute-start | bytes 12296 | tf_op jit(solution)/shard_map/ppermute | solution.py:557
  (42 other events, 126.7 us)

commit v9 on v8

--- a/solution.py
+++ b/solution.py
@@ -113,24 +113,26 @@
     )
 
 
-def fine_prepare(v_ref, _, vo_ref):
-    lines = vo_ref.shape[3]
-    halves = lines // SUBS
-
-    def body(ki, carry):
-        k, i = ki // 4, ki % 4
-        for j in range(4):
-            for h in range(halves):
-                start = ki * (lines * 4) + h * SUBS * 4 + j
-                vo_ref[k, i, j, pl.ds(h * SUBS, SUBS), :] = v_ref[
-                    pl.ds(start, SUBS, stride=4), :
-                ]
-        return carry
-
-    lax.fori_loop(0, NNZ * 4, body, 0)
+def fine_first(x_ref, b_ref, v_ref, c_ref, r_ref, vo_ref, line_ref):
+    lines = x_ref.shape[1]
+
+    def values(k, i, j, h):
+        start = ((k * 4 + i) * lines + h * SUBS) * 4 + j
+        tile = v_ref[pl.ds(start, SUBS, stride=4), :]
+        vo_ref[k, i, j, pl.ds(h * SUBS, SUBS), :] = tile
+        return tile
+
+    fine_product(values, x_ref, b_ref, c_ref, r_ref, line_ref)
 
 
 def fine_local(x_ref, b_ref, v_ref, c_ref, r_ref, line_ref):
+    def values(k, i, j, h):
+        return v_ref[k, i, j, pl.ds(h * SUBS, SUBS), :]
+
+    fine_product(values, x_ref, b_ref, c_ref, r_ref, line_ref)
+
+
+def fine_product(values, x_ref, b_ref, c_ref, r_ref, line_ref):
     lines = x_ref.shape[1]
     halves = lines // SUBS
     for j in range(4):
@@ -142,7 +144,7 @@
         for i in range(4):
             total = b_ref[i, rows, :]
             for j in range(4):
-                total = total - v_ref[0, i, j, rows, :] * x_ref[j, rows, :]
+                total = total - values(0, i, j, h) * x_ref[j, rows, :]
             acc.append(total)
 
     def body(k, acc):
@@ -154,7 +156,7 @@
             for j in range(4):
                 got = pick_lines([line_ref[j, r] for r in range(lines)], high, lane)
                 for i in range(4):
-                    acc[4 * h + i] = acc[4 * h + i] - v_ref[k, i, j, rows, :] * got
+                    acc[4 * h + i] = acc[4 * h + i] - values(k, i, j, h) * got
         return tuple(acc)
 
     acc = lax.fori_loop(1, NNZ, body, tuple(acc))
@@ -597,10 +599,22 @@
     return lax.ppermute(value, AXES, pairs)
 
 
-def span_stage(mesh, pieces, out):
-    pieces, _ = lax.optimization_barrier((pieces, out))
-    held = jnp.concatenate(pieces)
-    return pieces + [span_swap(mesh, held, mesh.shape["span"] // 2 // held.shape[0])]
+def span_stage(mesh, held, out):
+    held, _ = lax.optimization_barrier((held, out))
+    return span_swap(mesh, held, mesh.shape["span"] // 2 // held.shape[0])
+
+
+def join_kernel(*refs):
+    place = 0
+    for piece in refs[:-1]:
+        for t in range(piece.shape[0]):
+            refs[-1][place] = piece[t]
+            place += 1
+
+
+def join(pieces):
+    count = sum(piece.shape[0] for piece in pieces)
+    return call(join_kernel, shape(count, *pieces[0].shape[1:]), pieces)
 
 
 def span_gather(mesh, value):
@@ -653,7 +667,15 @@
         hbm=range(len(starts)),
     )
     d1 = x1
-    v1 = call(fine_prepare, shape(NNZ, 4, 4, lines, LANES), [values1, out], free=(1,))
+
+    arrived = exchange(mesh, out, choice)
+    pieces3 = [own3, span_stage(mesh, own3, out)]
+    resid, v1 = call(
+        fine_first,
+        [vec1, shape(NNZ, 4, 4, lines, LANES)],
+        [x1, b1, values1, c1],
+        [vmem(4, lines, SUBS, LANES)],
+    )
 
     def fine_part(x):
         return call(fine_local, vec1, [x, b1, v1, c1], [vmem(4, lines, SUBS, LANES)])
@@ -672,9 +694,6 @@
         )
         return result[0], (None if last else result[2]), result[1]
 
-    arrived = exchange(mesh, out, choice)
-    pieces3 = span_stage(mesh, [own3], out)
-    resid = fine_part(x1)
     x1, d1, out = fine_next(1, arrived, resid, x1, d1)
 
     arrived = exchange(mesh, out, choice)
@@ -693,11 +712,13 @@
 
     arrived = exchange(mesh, out, choice)
     resid = fine_part(x1)
+    held3 = join(pieces3)
     b2, x2, out = call(
-        lambda *refs: fine_restrict(*(refs[2:4] + refs[:2] + refs[4:])),
+        lambda *refs: fine_restrict(*(refs[2:4] + refs[:2] + refs[4:12] + refs[13:])),
         [vec2, vec2, tile],
-        arrived[2:4] + arrived[:2] + arrived[4:] + [resid, v1, c1, w1, place1, m2, send2],
+        arrived[2:4] + arrived[:2] + arrived[4:] + [resid, v1, c1, w1, place1, m2, send2, held3],
         [edge, vmem(4, lines, LANES), pad2],
+        free=(12,),
     )
     d2 = x2
 
@@ -719,8 +740,10 @@
         return result[0], (None if last else result[2]), result[1]
 
     arrived = exchange(mesh, out, choice)
-    for _ in range(len(span_places(group)) - 3):
-        pieces3 = span_stage(mesh, pieces3, out)
+    for _ in range(len(span_places(group)) - 4):
+        pieces3.append(span_stage(mesh, held3, out))
+        held3 = join(pieces3)
+    pieces3.append(span_stage(mesh, held3, out))
     v2, c2 = call(
         middle_blocks,
         [shape(NNZ // 2, 4, 4, SUBS, LANES), shape(NNZ // 2, SUBS, LANES, dtype=I32)],
@@ -740,18 +763,19 @@
         [native_rows(middle_weights), middle_order, middle_order.reshape(-1, LANES), out],
         free=(3,),
     )
-    pieces3 = span_stage(mesh, pieces3, out)
     x2, d2, out = middle_next(2, arrived, x2, d2, [agg2])
 
     arrived = exchange(mesh, out, choice)
+    held3 = join(pieces3)
     agg1 = call(fine_inverse, shape(lines, LANES, dtype=I32), [fine_order, out], free=(1,))
     rhs3 = call(
-        lambda *refs: middle_restrict(*(refs[:11] + refs[12:])),
+        lambda *refs: middle_restrict(*(refs[:11] + refs[13:])),
         tile,
-        arrived + [b2, middle_part(x2), v2, c2, w2, place2, agg1],
+        arrived + [b2, middle_part(x2), v2, c2, w2, place2, agg1, held3],
         [edge, vmem(4, SUBS, LANES)],
-        free=(11,),
-    )
+        free=(11, 12),
+    )
+    pieces3.append(span_stage(mesh, held3, rhs3))
     v3, c3, m3 = call(
         lambda *refs: coarse_tables(group, *refs),
         [shape(NNZ, 4, 4, group, LANES), shape(NNZ, group, LANES, dtype=I32), shape(4, group, LANES)],

time: 98.8 us -> 98.6 us (level)
    pallas_call x34 -> x35, Pallas kernels: 20.4 us -> 20.1 us  [call(): pl.pallas_call(body, out_shape=shapes, in_specs=specs, out_specs=[pl.Bloc...]
  transfers between devices with their start and end apart: 59 -> 59, of which waited for: 23 -> 24; matrix products, arithmetic and copies ran while one was open for 0% -> 0% of each run, Pallas kernels for 15% -> 14%
where the time goes in v9:
time: 98.6 us; the launch traced here: 98.4 us
  starting transfers between devices  62 us (63%)
  Pallas kernels  20.1 us (20%)
  waiting for transfers between devices  14.5 us (15%)
  between operations  1.03 us (1%)
    ppermute x52, starting transfers between devices, swap(): return lax.ppermute(out, AXES, pairs)  55 us
    pallas_call x35, Pallas kernels, call(): pl.pallas_call(body, out_shape=shapes, in_specs=specs, out_specs=[pl.Bloc...  20.1 us
    ppermute x52, waiting for transfers between devices, swap(): return lax.ppermute(out, AXES, pairs)  12.5 us
    ppermute x7, starting transfers between devices, span_swap(): return lax.ppermute(value, AXES, pairs)  6.99 us
    ppermute x7, waiting for transfers between devices, span_swap(): return lax.ppermute(value, AXES, pairs)  2.02 us
  transfers between devices with their start and end apart: 59, of which 24 were waited for; matrix products, arithmetic and copies ran while one was open for 0% of the time, Pallas kernels for 14%

profile of v9, /device:TPU:0, one launch (start us, length us, event | category | flops | bytes accessed | tf_op | source)
XLA Modules:
  0.0 98.4 jit_solution(13619147066439237342)
XLA Ops:
  1.9 4.0 %collective-permute-start = (f32[8,128]{1,0:T(8,128)S(1)}, f32[8,128]{1,0:T(8,128)S(1)}, u32[]{:S(2)}, u32[]{:S(2)}) collective-permute-start(f32[8,128]{1,0:T(8,128)S(1)} %get-tuple-element.59), channel_id=1, source_target_pairs={{0,24},{1,25},{2,26},{3,27},{4,28},{5,29},{6,30},{7,31},{8,16},{9,... | collective-permute-start | bytes 12296 | tf_op jit(solution)/shard_map/ppermute | solution.py:559
  6.4 1.5 %collective-permute-start.2 = (f32[8,128]{1,0:T(8,128)S(1)}, f32[8,128]{1,0:T(8,128)S(1)}, u32[]{:S(2)}, u32[]{:S(2)}) collective-permute-start(f32[8,128]{1,0:T(8,128)S(1)} %get-tuple-element.59), channel_id=1, source_target_pairs={{0,8},{1,2},{2,1},{3,4},{4,3},{5,6},{6,5},{7,15},{8,0},{9,10},{10,... | collective-permute-start | bytes 12296 | tf_op jit(solution)/shard_map/ppermute | solution.py:559
  8.1 2.6 %collective-permute-start.12 = (f32[1,136,128]{2,1,0:T(8,128)S(1)}, f32[1,136,128]{2,1,0:T(8,128)S(1)}, u32[]{:S(2)}, u32[]{:S(2)}) collective-permute-start(f32[1,136,128]{2,1,0:T(8,128)S(1)} %get-tuple-element.77.refs_0_.refs_1_), channel_id=1, source_target_pairs={{0,4},{1,5},{2,6},{3,7},{4,0},{5,1},{6,2},{7,3},{8,12},{9,13},{10,... | collective-permute-start | bytes 208904 | tf_op jit(solution)/shard_map/ppermute | solution.py:599
  10.8 1.5 %shard_map.141 = (f32[4,16,128]{2,1,0:T(8,128)S(1)}, f32[8,4,4,16,128]{4,3,2,1,0:T(8,128)S(1)}) custom-call(f32[4,16,128]{2,1,0:T(8,128)S(1)} %get-tuple-element.60.x_ref.refs_9_.refs_10_, f32[4,16,128]{2,1,0:T(8,128)S(1)} %get-tuple-element.61.b_ref, f32[2048,128]{1,0:T(8,128)S(1)} %bitcast.54, s32[8,16,128]{2,1,0:T(8,128)S(1)} %get-tuple-element.62.c_ref.refs_7_), custom_call_target="tpu_custom_call" | custom-call | tf_op jit(solution)/shard_map/pallas_call | solution.py:521
  14.7 1.5 %collective-permute-start.6 = (f32[8,128]{1,0:T(8,128)S(1)}, f32[8,128]{1,0:T(8,128)S(1)}, u32[]{:S(2)}, u32[]{:S(2)}) collective-permute-start(f32[8,128]{1,0:T(8,128)S(1)} %get-tuple-element.67._), channel_id=1, source_target_pairs={{0,8},{1,2},{2,1},{3,4},{4,3},{5,6},{6,5},{7,15},{8,0},{9,10},{10,... | collective-permute-start | bytes 12296 | tf_op jit(solution)/shard_map/ppermute | solution.py:559
  16.2 1.5 %shard_map.143.refs_5_ = f32[4,16,128]{2,1,0:T(8,128)S(1)} custom-call(f32[4,16,128]{2,1,0:T(8,128)S(1)} %get-tuple-element.68.x_ref.refs_9_, f32[4,16,128]{2,1,0:T(8,128)S(1)} %get-tuple-element.61.b_ref, f32[8,4,4,16,128]{4,3,2,1,0:T(8,128)S(1)} %get-tuple-element.64.refs_6_.v_ref, s32[8,16,128]{2,1,0:T(8,128)S(1)} %get-tuple-element.62.c_ref.refs_7_), custom_call_target="tpu_custom_call" | custom-call | tf_op jit(solution)/shard_map/pallas_call | solution.py:521
  18.7 2.5 %collective-permute-start.10 = (f32[8,128]{1,0:T(8,128)S(1)}, f32[8,128]{1,0:T(8,128)S(1)}, u32[]{:S(2)}, u32[]{:S(2)}) collective-permute-start(f32[8,128]{1,0:T(8,128)S(1)} %get-tuple-element.71), channel_id=1, source_target_pairs={{0,24},{1,25},{2,26},{3,27},{4,28},{5,29},{6,30},{7,31},{8,16},{9,... | collective-permute-start | bytes 12296 | tf_op jit(solution)/shard_map/ppermute | solution.py:559
  21.7 1.5 %collective-permute-start.8 = (f32[8,128]{1,0:T(8,128)S(1)}, f32[8,128]{1,0:T(8,128)S(1)}, u32[]{:S(2)}, u32[]{:S(2)}) collective-permute-start(f32[8,128]{1,0:T(8,128)S(1)} %get-tuple-element.71), channel_id=1, source_target_pairs={{0,8},{1,2},{2,1},{3,4},{4,3},{5,6},{6,5},{7,15},{8,0},{9,10},{10,... | collective-permute-start | bytes 12296 | tf_op jit(solution)/shard_map/ppermute | solution.py:559
  23.2 1.5 %shard_map.146.refs_5_ = f32[4,16,128]{2,1,0:T(8,128)S(1)} custom-call(f32[4,16,128]{2,1,0:T(8,128)S(1)} %get-tuple-element.72.x_ref.refs_12_, f32[4,16,128]{2,1,0:T(8,128)S(1)} %get-tuple-element.61.b_ref, f32[8,4,4,16,128]{4,3,2,1,0:T(8,128)S(1)} %get-tuple-element.64.refs_6_.v_ref, s32[8,16,128]{2,1,0:T(8,128)S(1)} %get-tuple-element.62.c_ref.refs_7_), custom_call_target="tpu_custom_call" | custom-call | tf_op jit(solution)/shard_map/pallas_call | solution.py:521
  25.9 1.5 %collective-permute-start.13 = (f32[8,128]{1,0:T(8,128)S(1)}, f32[8,128]{1,0:T(8,128)S(1)}, u32[]{:S(2)}, u32[]{:S(2)}) collective-permute-start(f32[8,128]{1,0:T(8,128)S(1)} %get-tuple-element.78._), channel_id=1, source_target_pairs={{0,24},{1,25},{2,26},{3,27},{4,28},{5,29},{6,30},{7,31},{8,16},{9,... | collective-permute-start | bytes 12296 | tf_op jit(solution)/shard_map/ppermute | solution.py:559
  27.9 1.5 %collective-permute-start.15 = (f32[8,128]{1,0:T(8,128)S(1)}, f32[8,128]{1,0:T(8,128)S(1)}, u32[]{:S(2)}, u32[]{:S(2)}) collective-permute-start(f32[8,128]{1,0:T(8,128)S(1)} %get-tuple-element.78._), channel_id=1, source_target_pairs={{0,8},{1,2},{2,1},{3,4},{4,3},{5,6},{6,5},{7,15},{8,0},{9,10},{10,... | collective-permute-start | bytes 12296 | tf_op jit(solution)/shard_map/ppermute | solution.py:559
  31.8 2.5 %collective-permute-start.17 = (f32[8,128]{1,0:T(8,128)S(1)}, f32[8,128]{1,0:T(8,128)S(1)}, u32[]{:S(2)}, u32[]{:S(2)}) collective-permute-start(f32[8,128]{1,0:T(8,128)S(1)} %get-tuple-element.83._), channel_id=1, source_target_pairs={{0,24},{1,25},{2,26},{3,27},{4,28},{5,29},{6,30},{7,31},{8,16},{9,... | collective-permute-start | bytes 12296 | tf_op jit(solution)/shard_map/ppermute | solution.py:559
  34.8 1.5 %collective-permute-start.19 = (f32[8,128]{1,0:T(8,128)S(1)}, f32[8,128]{1,0:T(8,128)S(1)}, u32[]{:S(2)}, u32[]{:S(2)}) collective-permute-start(f32[8,128]{1,0:T(8,128)S(1)} %get-tuple-element.83._), channel_id=1, source_target_pairs={{0,8},{1,2},{2,1},{3,4},{4,3},{5,6},{6,5},{7,15},{8,0},{9,10},{10,... | collective-permute-start | bytes 12296 | tf_op jit(solution)/shard_map/ppermute | solution.py:559
  40.6 1.5 %collective-permute-start.23 = (f32[8,128]{1,0:T(8,128)S(1)}, f32[8,128]{1,0:T(8,128)S(1)}, u32[]{:S(2)}, u32[]{:S(2)}) collective-permute-start(f32[8,128]{1,0:T(8,128)S(1)} %get-tuple-element.87._), channel_id=1, source_target_pairs={{0,8},{1,2},{2,1},{3,4},{4,3},{5,6},{6,5},{7,15},{8,0},{9,10},{10,... | collective-permute-start | bytes 12296 | tf_op jit(solution)/shard_map/ppermute | solution.py:559
  46.0 2.7 %collective-permute-start.28 = (f32[8,128]{1,0:T(8,128)S(1)}, f32[8,128]{1,0:T(8,128)S(1)}, u32[]{:S(2)}, u32[]{:S(2)}) collective-permute-start(f32[8,128]{1,0:T(8,128)S(1)} %shard_map.158.refs_5_), channel_id=1, source_target_pairs={{0,3},{1,2},{2,1},{3,0},{4,7},{5,6},{6,5},{7,4},{8,11},{9,10},{10,... | collective-permute-start | bytes 12296 | tf_op jit(solution)/shard_map/ppermute | solution.py:599
  52.5 2.5 %collective-permute-start.31 = (f32[8,128]{1,0:T(8,128)S(1)}, f32[8,128]{1,0:T(8,128)S(1)}, u32[]{:S(2)}, u32[]{:S(2)}) collective-permute-start(f32[8,128]{1,0:T(8,128)S(1)} %get-tuple-element.96), channel_id=1, source_target_pairs={{0,24},{1,25},{2,26},{3,27},{4,28},{5,29},{6,30},{7,31},{8,16},{9,... | collective-permute-start | bytes 12296 | tf_op jit(solution)/shard_map/ppermute | solution.py:559
  55.5 1.5 %collective-permute-start.33 = (f32[8,128]{1,0:T(8,128)S(1)}, f32[8,128]{1,0:T(8,128)S(1)}, u32[]{:S(2)}, u32[]{:S(2)}) collective-permute-start(f32[8,128]{1,0:T(8,128)S(1)} %get-tuple-element.96), channel_id=1, source_target_pairs={{0,8},{1,2},{2,1},{3,4},{4,3},{5,6},{6,5},{7,15},{8,0},{9,10},{10,... | collective-permute-start | bytes 12296 | tf_op jit(solution)/shard_map/ppermute | solution.py:559
  65.2 2.5 %collective-permute-start.39 = (f32[8,128]{1,0:T(8,128)S(1)}, f32[8,128]{1,0:T(8,128)S(1)}, u32[]{:S(2)}, u32[]{:S(2)}) collective-permute-start(f32[8,128]{1,0:T(8,128)S(1)} %get-tuple-element.101), channel_id=1, source_target_pairs={{0,24},{1,25},{2,26},{3,27},{4,28},{5,29},{6,30},{7,31},{8,16},{9,... | collective-permute-start | bytes 12296 | tf_op jit(solution)/shard_map/ppermute | solution.py:559
  75.6 1.5 %shard_map.167.refs_5_ = f32[4,16,128]{2,1,0:T(8,128)S(1)} custom-call(f32[4,16,128]{2,1,0:T(8,128)S(1)} %get-tuple-element.105.x_ref.refs_9_.refs_10_, f32[4,16,128]{2,1,0:T(8,128)S(1)} %get-tuple-element.61.b_ref, f32[8,4,4,16,128]{4,3,2,1,0:T(8,128)S(1)} %get-tuple-element.64.refs_6_.v_ref, s32[8,16,128]{2,1,0:T(8,128)S(1)} %get-tuple-element.62.c_ref.refs_7_), custom_call_target="tpu_custom_call" | custom-call | tf_op jit(solution)/shard_map/pallas_call | solution.py:521
  78.1 2.5 %collective-permute-start.47 = (f32[8,128]{1,0:T(8,128)S(1)}, f32[8,128]{1,0:T(8,128)S(1)}, u32[]{:S(2)}, u32[]{:S(2)}) collective-permute-start(f32[8,128]{1,0:T(8,128)S(1)} %get-tuple-element.106), channel_id=1, source_target_pairs={{0,24},{1,25},{2,26},{3,27},{4,28},{5,29},{6,30},{7,31},{8,16},{9,... | collective-permute-start | bytes 12296 | tf_op jit(solution)/shard_map/ppermute | solution.py:559
  82.6 1.5 %shard_map.169.refs_5_ = f32[4,16,128]{2,1,0:T(8,128)S(1)} custom-call(f32[4,16,128]{2,1,0:T(8,128)S(1)} %get-tuple-element.107.x_ref.refs_9_, f32[4,16,128]{2,1,0:T(8,128)S(1)} %get-tuple-element.61.b_ref, f32[8,4,4,16,128]{4,3,2,1,0:T(8,128)S(1)} %get-tuple-element.64.refs_6_.v_ref, s32[8,16,128]{2,1,0:T(8,128)S(1)} %get-tuple-element.62.c_ref.refs_7_), custom_call_target="tpu_custom_call" | custom-call | tf_op jit(solution)/shard_map/pallas_call | solution.py:521
  88.5 1.5 %shard_map.171.refs_5_ = f32[4,16,128]{2,1,0:T(8,128)S(1)} custom-call(f32[4,16,128]{2,1,0:T(8,128)S(1)} %get-tuple-element.110.x_ref.refs_9_, f32[4,16,128]{2,1,0:T(8,128)S(1)} %get-tuple-element.61.b_ref, f32[8,4,4,16,128]{4,3,2,1,0:T(8,128)S(1)} %get-tuple-element.64.refs_6_.v_ref, s32[8,16,128]{2,1,0:T(8,128)S(1)} %get-tuple-element.62.c_ref.refs_7_), custom_call_target="tpu_custom_call" | custom-call | tf_op jit(solution)/shard_map/pallas_call | solution.py:521
  91.0 2.5 %collective-permute-start.55 = (f32[8,128]{1,0:T(8,128)S(1)}, f32[8,128]{1,0:T(8,128)S(1)}, u32[]{:S(2)}, u32[]{:S(2)}) collective-permute-start(f32[8,128]{1,0:T(8,128)S(1)} %get-tuple-element.112), channel_id=1, source_target_pairs={{0,24},{1,25},{2,26},{3,27},{4,28},{5,29},{6,30},{7,31},{8,16},{9,... | collective-permute-start | bytes 12296 | tf_op jit(solution)/shard_map/ppermute | solution.py:559
  95.4 1.5 %shard_map.173.refs_5_ = f32[4,16,128]{2,1,0:T(8,128)S(1)} custom-call(f32[4,16,128]{2,1,0:T(8,128)S(1)} %get-tuple-element.113.x_ref.refs_8_, f32[4,16,128]{2,1,0:T(8,128)S(1)} %get-tuple-element.61.b_ref, f32[8,4,4,16,128]{4,3,2,1,0:T(8,128)S(1)} %get-tuple-element.64.refs_6_.v_ref, s32[8,16,128]{2,1,0:T(8,128)S(1)} %get-tuple-element.62.c_ref.refs_7_), custom_call_target="tpu_custom_call" | custom-call | tf_op jit(solution)/shard_map/pallas_call | solution.py:521
  (149 shorter events, 50.9 us)
Async XLA Ops:
  1.9 10.4 %collective-permute-start = (f32[8,128]{1,0:T(8,128)S(1)}, f32[8,128]{1,0:T(8,128)S(1)}, u32[]{:S(2)}, u32[]{:S(2)}) collective-permute-start(f32[8,128]{1,0:T(8,128)S(1)} %get-tuple-element.59), channel_id=1, source_target_pairs={{0,24},{1,25},{2,26},{3,27},{4,28},{5,29},{6,30},{7,31},{8,16},{9,... | collective-permute-start | bytes 12296 | tf_op jit(solution)/shard_map/ppermute | solution.py:559
  5.9 6.5 %collective-permute-start.1 = (f32[8,128]{1,0:T(8,128)S(1)}, f32[8,128]{1,0:T(8,128)S(1)}, u32[]{:S(2)}, u32[]{:S(2)}) collective-permute-start(f32[8,128]{1,0:T(8,128)S(1)} %get-tuple-element.59), channel_id=1, source_target_pairs={{0,8},{1,9},{2,10},{3,11},{4,12},{5,13},{6,14},{7,15},{8,0},{9,1},... | collective-permute-start | bytes 12296 | tf_op jit(solution)/shard_map/ppermute | solution.py:559
  6.4 6.0 %collective-permute-start.2 = (f32[8,128]{1,0:T(8,128)S(1)}, f32[8,128]{1,0:T(8,128)S(1)}, u32[]{:S(2)}, u32[]{:S(2)}) collective-permute-start(f32[8,128]{1,0:T(8,128)S(1)} %get-tuple-element.59), channel_id=1, source_target_pairs={{0,8},{1,2},{2,1},{3,4},{4,3},{5,6},{6,5},{7,15},{8,0},{9,10},{10,... | collective-permute-start | bytes 12296 | tf_op jit(solution)/shard_map/ppermute | solution.py:559
  7.9 4.5 %collective-permute-start.3 = (f32[8,128]{1,0:T(8,128)S(1)}, f32[8,128]{1,0:T(8,128)S(1)}, u32[]{:S(2)}, u32[]{:S(2)}) collective-permute-start(f32[8,128]{1,0:T(8,128)S(1)} %get-tuple-element.59), channel_id=1, source_target_pairs={{0,1},{1,0},{2,3},{3,2},{4,5},{5,4},{6,7},{7,6},{8,9},{9,8},{10,11... | collective-permute-start | bytes 12296 | tf_op jit(solution)/shard_map/ppermute | solution.py:559
  8.1 16.6 %collective-permute-start.12 = (f32[1,136,128]{2,1,0:T(8,128)S(1)}, f32[1,136,128]{2,1,0:T(8,128)S(1)}, u32[]{:S(2)}, u32[]{:S(2)}) collective-permute-start(f32[1,136,128]{2,1,0:T(8,128)S(1)} %get-tuple-element.77.refs_0_.refs_1_), channel_id=1, source_target_pairs={{0,4},{1,5},{2,6},{3,7},{4,0},{5,1},{6,2},{7,3},{8,12},{9,13},{10,... | collective-permute-start | bytes 208904 | tf_op jit(solution)/shard_map/ppermute | solution.py:599
  12.7 5.1 %collective-permute-start.4 = (f32[8,128]{1,0:T(8,128)S(1)}, f32[8,128]{1,0:T(8,128)S(1)}, u32[]{:S(2)}, u32[]{:S(2)}) collective-permute-start(f32[8,128]{1,0:T(8,128)S(1)} %get-tuple-element.67._), channel_id=1, source_target_pairs={{0,24},{1,25},{2,26},{3,27},{4,28},{5,29},{6,30},{7,31},{8,16},{9,... | collective-permute-start | bytes 12296 | tf_op jit(solution)/shard_map/ppermute | solution.py:559
  14.2 3.7 %collective-permute-start.5 = (f32[8,128]{1,0:T(8,128)S(1)}, f32[8,128]{1,0:T(8,128)S(1)}, u32[]{:S(2)}, u32[]{:S(2)}) collective-permute-start(f32[8,128]{1,0:T(8,128)S(1)} %get-tuple-element.67._), channel_id=1, source_target_pairs={{0,8},{1,9},{2,10},{3,11},{4,12},{5,13},{6,14},{7,15},{8,0},{9,1},... | collective-permute-start | bytes 12296 | tf_op jit(solution)/shard_map/ppermute | solution.py:559
  14.7 3.6 %collective-permute-start.6 = (f32[8,128]{1,0:T(8,128)S(1)}, f32[8,128]{1,0:T(8,128)S(1)}, u32[]{:S(2)}, u32[]{:S(2)}) collective-permute-start(f32[8,128]{1,0:T(8,128)S(1)} %get-tuple-element.67._), channel_id=1, source_target_pairs={{0,8},{1,2},{2,1},{3,4},{4,3},{5,6},{6,5},{7,15},{8,0},{9,10},{10,... | collective-permute-start | bytes 12296 | tf_op jit(solution)/shard_map/ppermute | solution.py:559
  18.7 6.0 %collective-permute-start.10 = (f32[8,128]{1,0:T(8,128)S(1)}, f32[8,128]{1,0:T(8,128)S(1)}, u32[]{:S(2)}, u32[]{:S(2)}) collective-permute-start(f32[8,128]{1,0:T(8,128)S(1)} %get-tuple-element.71), channel_id=1, source_target_pairs={{0,24},{1,25},{2,26},{3,27},{4,28},{5,29},{6,30},{7,31},{8,16},{9,... | collective-permute-start | bytes 12296 | tf_op jit(solution)/shard_map/ppermute | solution.py:559
  25.9 16.7 %collective-permute-start.25 = (f32[2,136,128]{2,1,0:T(8,128)S(1)}, f32[2,136,128]{2,1,0:T(8,128)S(1)}, u32[]{:S(2)}, u32[]{:S(2)}) collective-permute-start(f32[2,136,128]{2,1,0:T(8,128)S(1)} %shard_map.147.refs_12_), channel_id=1, source_target_pairs={{0,2},{1,3},{2,0},{3,1},{4,6},{5,7},{6,4},{7,5},{8,10},{9,11},{10,... | collective-permute-start | bytes 417800 | tf_op jit(solution)/shard_map/ppermute | solution.py:599
  25.9 4.6 %collective-permute-start.13 = (f32[8,128]{1,0:T(8,128)S(1)}, f32[8,128]{1,0:T(8,128)S(1)}, u32[]{:S(2)}, u32[]{:S(2)}) collective-permute-start(f32[8,128]{1,0:T(8,128)S(1)} %get-tuple-element.78._), channel_id=1, source_target_pairs={{0,24},{1,25},{2,26},{3,27},{4,28},{5,29},{6,30},{7,31},{8,16},{9,... | collective-permute-start | bytes 12296 | tf_op jit(solution)/shard_map/ppermute | solution.py:559
  31.8 5.6 %collective-permute-start.17 = (f32[8,128]{1,0:T(8,128)S(1)}, f32[8,128]{1,0:T(8,128)S(1)}, u32[]{:S(2)}, u32[]{:S(2)}) collective-permute-start(f32[8,128]{1,0:T(8,128)S(1)} %get-tuple-element.83._), channel_id=1, source_target_pairs={{0,24},{1,25},{2,26},{3,27},{4,28},{5,29},{6,30},{7,31},{8,16},{9,... | collective-permute-start | bytes 12296 | tf_op jit(solution)/shard_map/ppermute | solution.py:559
  38.6 4.5 %collective-permute-start.21 = (f32[8,128]{1,0:T(8,128)S(1)}, f32[8,128]{1,0:T(8,128)S(1)}, u32[]{:S(2)}, u32[]{:S(2)}) collective-permute-start(f32[8,128]{1,0:T(8,128)S(1)} %get-tuple-element.87._), channel_id=1, source_target_pairs={{0,24},{1,25},{2,26},{3,27},{4,28},{5,29},{6,30},{7,31},{8,16},{9,... | collective-permute-start | bytes 12296 | tf_op jit(solution)/shard_map/ppermute | solution.py:559
  44.5 5.7 %collective-permute-start.30 = (f32[4,136,128]{2,1,0:T(8,128)S(1)}, f32[4,136,128]{2,1,0:T(8,128)S(1)}, u32[]{:S(2)}, u32[]{:S(2)}) collective-permute-start(f32[4,136,128]{2,1,0:T(8,128)S(1)} %shard_map.157.refs_12_), channel_id=1, source_target_pairs={{0,1},{1,0},{2,3},{3,2},{4,5},{5,4},{6,7},{7,6},{8,9},{9,8},{10,11... | collective-permute-start | bytes 835592 | tf_op jit(solution)/shard_map/ppermute | solution.py:599
  44.5 4.9 %collective-permute-start.26 = (f32[8,128]{1,0:T(8,128)S(1)}, f32[8,128]{1,0:T(8,128)S(1)}, u32[]{:S(2)}, u32[]{:S(2)}) collective-permute-start(f32[8,128]{1,0:T(8,128)S(1)} %shard_map.158.refs_5_), channel_id=1, source_target_pairs={{0,7},{1,6},{2,5},{3,4},{4,3},{5,2},{6,1},{7,0},{8,15},{9,14},{10,... | collective-permute-start | bytes 12296 | tf_op jit(solution)/shard_map/ppermute | solution.py:599
  44.6 4.8 %collective-permute-start.27 = (f32[8,128]{1,0:T(8,128)S(1)}, f32[8,128]{1,0:T(8,128)S(1)}, u32[]{:S(2)}, u32[]{:S(2)}) collective-permute-start(f32[8,128]{1,0:T(8,128)S(1)} %shard_map.158.refs_5_), channel_id=1, source_target_pairs={{0,5},{1,4},{2,7},{3,6},{4,1},{5,0},{6,3},{7,2},{8,13},{9,12},{10,... | collective-permute-start | bytes 12296 | tf_op jit(solution)/shard_map/ppermute | solution.py:599
  46.0 4.0 %collective-permute-start.28 = (f32[8,128]{1,0:T(8,128)S(1)}, f32[8,128]{1,0:T(8,128)S(1)}, u32[]{:S(2)}, u32[]{:S(2)}) collective-permute-start(f32[8,128]{1,0:T(8,128)S(1)} %shard_map.158.refs_5_), channel_id=1, source_target_pairs={{0,3},{1,2},{2,1},{3,0},{4,7},{5,6},{6,5},{7,4},{8,11},{9,10},{10,... | collective-permute-start | bytes 12296 | tf_op jit(solution)/shard_map/ppermute | solution.py:599
  52.5 5.1 %collective-permute-start.31 = (f32[8,128]{1,0:T(8,128)S(1)}, f32[8,128]{1,0:T(8,128)S(1)}, u32[]{:S(2)}, u32[]{:S(2)}) collective-permute-start(f32[8,128]{1,0:T(8,128)S(1)} %get-tuple-element.96), channel_id=1, source_target_pairs={{0,24},{1,25},{2,26},{3,27},{4,28},{5,29},{6,30},{7,31},{8,16},{9,... | collective-permute-start | bytes 12296 | tf_op jit(solution)/shard_map/ppermute | solution.py:559
  59.3 4.5 %collective-permute-start.35 = (f32[8,128]{1,0:T(8,128)S(1)}, f32[8,128]{1,0:T(8,128)S(1)}, u32[]{:S(2)}, u32[]{:S(2)}) collective-permute-start(f32[8,128]{1,0:T(8,128)S(1)} %get-tuple-element.98), channel_id=1, source_target_pairs={{0,24},{1,25},{2,26},{3,27},{4,28},{5,29},{6,30},{7,31},{8,16},{9,... | collective-permute-start | bytes 12296 | tf_op jit(solution)/shard_map/ppermute | solution.py:559
  65.2 4.7 %collective-permute-start.39 = (f32[8,128]{1,0:T(8,128)S(1)}, f32[8,128]{1,0:T(8,128)S(1)}, u32[]{:S(2)}, u32[]{:S(2)}) collective-permute-start(f32[8,128]{1,0:T(8,128)S(1)} %get-tuple-element.101), channel_id=1, source_target_pairs={{0,24},{1,25},{2,26},{3,27},{4,28},{5,29},{6,30},{7,31},{8,16},{9,... | collective-permute-start | bytes 12296 | tf_op jit(solution)/shard_map/ppermute | solution.py:559
  72.1 5.0 %collective-permute-start.43 = (f32[8,128]{1,0:T(8,128)S(1)}, f32[8,128]{1,0:T(8,128)S(1)}, u32[]{:S(2)}, u32[]{:S(2)}) collective-permute-start(f32[8,128]{1,0:T(8,128)S(1)} %get-tuple-element.104), channel_id=1, source_target_pairs={{0,24},{1,25},{2,26},{3,27},{4,28},{5,29},{6,30},{7,31},{8,16},{9,... | collective-permute-start | bytes 12296 | tf_op jit(solution)/shard_map/ppermute | solution.py:559
  78.1 6.0 %collective-permute-start.47 = (f32[8,128]{1,0:T(8,128)S(1)}, f32[8,128]{1,0:T(8,128)S(1)}, u32[]{:S(2)}, u32[]{:S(2)}) collective-permute-start(f32[8,128]{1,0:T(8,128)S(1)} %get-tuple-element.106), channel_id=1, source_target_pairs={{0,24},{1,25},{2,26},{3,27},{4,28},{5,29},{6,30},{7,31},{8,16},{9,... | collective-permute-start | bytes 12296 | tf_op jit(solution)/shard_map/ppermute | solution.py:559
  85.0 5.0 %collective-permute-start.51 = (f32[8,128]{1,0:T(8,128)S(1)}, f32[8,128]{1,0:T(8,128)S(1)}, u32[]{:S(2)}, u32[]{:S(2)}) collective-permute-start(f32[8,128]{1,0:T(8,128)S(1)} %get-tuple-element.109), channel_id=1, source_target_pairs={{0,24},{1,25},{2,26},{3,27},{4,28},{5,29},{6,30},{7,31},{8,16},{9,... | collective-permute-start | bytes 12296 | tf_op jit(solution)/shard_map/ppermute | solution.py:559
  91.0 6.0 %collective-permute-start.55 = (f32[8,128]{1,0:T(8,128)S(1)}, f32[8,128]{1,0:T(8,128)S(1)}, u32[]{:S(2)}, u32[]{:S(2)}) collective-permute-start(f32[8,128]{1,0:T(8,128)S(1)} %get-tuple-element.112), channel_id=1, source_target_pairs={{0,24},{1,25},{2,26},{3,27},{4,28},{5,29},{6,30},{7,31},{8,16},{9,... | collective-permute-start | bytes 12296 | tf_op jit(solution)/shard_map/ppermute | solution.py:559
  (42 other events, 127.0 us)

commit v10 on v9

--- a/solution.py
+++ b/solution.py
@@ -53,6 +53,11 @@
     upper = tile_iota(0) < 4
     even = jnp.where(upper, s_even, p_even)
     odd = jnp.where(upper, s_odd, p_odd)
+    edge_ref[...] = jnp.where(which == 1, even, jnp.where(which == 2, odd, 0.0))
+
+
+def edge_lines(arrivals, edge_ref):
+    odd, even, which = [r[...] for r in arrivals]
     edge_ref[...] = jnp.where(which == 1, even, jnp.where(which == 2, odd, 0.0))
 
 
@@ -165,34 +170,42 @@
             r_ref[i, pl.ds(h * SUBS, SUBS), :] = acc[4 * h + i]
 
 
-def fine_remote(arrivals, r_ref, v_ref, c_ref, edge_ref):
+def fine_remote(arrivals, r_ref, v_ref, c_ref, edge_ref, axis):
     lines = r_ref.shape[1]
     halves = lines // SUBS
-    halo_lines(arrivals, edge_ref)
-    edges = [[wide(edge_ref[pl.ds(4 * e + j, 1), :]) for e in range(2)] for j in range(4)]
+    edge_lines(arrivals, edge_ref)
+    edges = [wide(edge_ref[pl.ds(4 * axis + j, 1), :]) for j in range(4)]
     result = []
     for h in range(halves):
         rows = pl.ds(h * SUBS, SUBS)
         acc = [r_ref[i, rows, :] for i in range(4)]
         for k in range(1, NNZ):
             col = c_ref[k, rows, :]
-            high, lane = col >> 7, col & (LANES - 1)
+            here, lane = (col >> 7) == lines + axis, col & (LANES - 1)
             for j in range(4):
-                got = pick_lines(edges[j], high, lane, lines)
+                got = jnp.where(here, pick(edges[j], lane), 0.0)
                 for i in range(4):
                     acc[i] = acc[i] - v_ref[k, i, j, rows, :] * got
         result.append(acc)
     return result
 
 
+def fine_stream(*refs):
+    r_ref, v_ref, c_ref, ro_ref, edge_ref = refs[3:]
+    resid = fine_remote(refs[:3], r_ref, v_ref, c_ref, edge_ref, 0)
+    for h, acc in enumerate(resid):
+        for i in range(4):
+            ro_ref[i, pl.ds(h * SUBS, SUBS), :] = acc[i]
+
+
 def fine_step(factors, last, *refs):
-    arrivals = refs[:5]
-    r_ref, v_ref, c_ref, m_ref, x_ref, d_ref, s_ref, xo_ref, out_ref = refs[5:14]
-    do_ref = refs[14] if last is False else None
+    arrivals = refs[:3]
+    r_ref, v_ref, c_ref, m_ref, x_ref, d_ref, s_ref, xo_ref, out_ref = refs[3:12]
+    do_ref = refs[12] if last is False else None
     edge_ref, pad_ref = refs[-2:]
     keep, gain = factors
     lines = r_ref.shape[1]
-    resid = fine_remote(arrivals, r_ref, v_ref, c_ref, edge_ref)
+    resid = fine_remote(arrivals, r_ref, v_ref, c_ref, edge_ref, 1)
     for h in range(lines // SUBS):
         rows = pl.ds(h * SUBS, SUBS)
         for i in range(4):
@@ -211,10 +224,10 @@
 
 
 def fine_finish(*refs):
-    arrivals = refs[:5]
-    r_ref, v_ref, c_ref, x_ref, so_ref, ro_ref, edge_ref = refs[5:]
+    arrivals = refs[:3]
+    r_ref, v_ref, c_ref, x_ref, so_ref, ro_ref, edge_ref = refs[3:]
     lines = r_ref.shape[1]
-    resid = fine_remote(arrivals, r_ref, v_ref, c_ref, edge_ref)
+    resid = fine_remote(arrivals, r_ref, v_ref, c_ref, edge_ref, 1)
     for h in range(lines // SUBS):
         for i in range(4):
             native = pl.ds(h * SUBS * 4 + i, SUBS, stride=4)
@@ -223,10 +236,10 @@
 
 
 def fine_restrict(*refs):
-    arrivals = refs[:5]
-    (r_ref, v_ref, c_ref, w_ref, p_ref, m2_ref, s2_ref, b2_ref, x2_ref, out_ref, edge_ref, line_ref, pad_ref) = refs[5:]
+    arrivals = refs[:3]
+    (r_ref, v_ref, c_ref, w_ref, p_ref, m2_ref, s2_ref, b2_ref, x2_ref, out_ref, edge_ref, line_ref, pad_ref) = refs[3:]
     lines = r_ref.shape[1]
-    resid = fine_remote(arrivals, r_ref, v_ref, c_ref, edge_ref)
+    resid = fine_remote(arrivals, r_ref, v_ref, c_ref, edge_ref, 1)
     for h in range(lines // SUBS):
         rows = pl.ds(h * SUBS, SUBS)
         for j in range(4):
@@ -586,7 +599,7 @@
     places = [[0]]
     mask = group // 2
     while mask:
-        places.append([mask ^ m for piece in places for m in piece])
+        places.append([(mask | 1) ^ m for piece in places for m in piece])
         mask //= 2
     return places
 
@@ -601,7 +614,7 @@
 
 def span_stage(mesh, held, out):
     held, _ = lax.optimization_barrier((held, out))
-    return span_swap(mesh, held, mesh.shape["span"] // 2 // held.shape[0])
+    return span_swap(mesh, held, mesh.shape["span"] // 2 // held.shape[0] | 1)
 
 
 def join_kernel(*refs):
@@ -680,8 +693,11 @@
     def fine_part(x):
         return call(fine_local, vec1, [x, b1, v1, c1], [vmem(4, lines, SUBS, LANES)])
 
+    def fine_half(arrived, resid):
+        return call(fine_stream, vec1, arrived[:2] + arrived[4:] + [resid, v1, c1], [edge])
+
     def fine_next(which, arrived, resid, x, d, after=()):
-        args = arrived + [resid, v1, c1, m1, x, d, send1]
+        args = arrived[2:] + [fine_half(arrived, resid), v1, c1, m1, x, d, send1]
         last = which == KSM - 1
         result = call(
             lambda *refs: fine_step(
@@ -714,11 +730,11 @@
     resid = fine_part(x1)
     held3 = join(pieces3)
     b2, x2, out = call(
-        lambda *refs: fine_restrict(*(refs[2:4] + refs[:2] + refs[4:12] + refs[13:])),
+        lambda *refs: fine_restrict(*(refs[:10] + refs[11:])),
         [vec2, vec2, tile],
-        arrived[2:4] + arrived[:2] + arrived[4:] + [resid, v1, c1, w1, place1, m2, send2, held3],
+        arrived[2:] + [fine_half(arrived, resid), v1, c1, w1, place1, m2, send2, held3],
         [edge, vmem(4, lines, LANES), pad2],
-        free=(12,),
+        free=(10,),
     )
     d2 = x2
 
@@ -810,7 +826,8 @@
     arrived = exchange(mesh, out, choice)
     resid = fine_part(x1)
     rows = shape(4 * lines, LANES)
-    solved, left = call(fine_finish, [rows, rows], arrived + [resid, v1, c1, x1], [edge])
+    resid = fine_half(arrived, resid)
+    solved, left = call(fine_finish, [rows, rows], arrived[2:] + [resid, v1, c1, x1], [edge])
     return from_native(solved, lines), from_native(left, lines)
 
 

time: 98.6 us -> 98.3 us (level)
    pallas_call x35 -> x42, Pallas kernels: 20.1 us -> 21 us  [call(): pl.pallas_call(body, out_shape=shapes, in_specs=specs, out_specs=[pl.Bloc...]
  transfers between devices with their start and end apart: 59 -> 59, of which waited for: 24 -> 24; matrix products, arithmetic and copies ran while one was open for 0% -> 0% of each run, Pallas kernels for 14% -> 16%
where the time goes in v10:
time: 98.3 us; the launch traced here: 98.1 us
  starting transfers between devices  61.6 us (63%)
  Pallas kernels  21 us (21%)
  waiting for transfers between devices  13.7 us (14%)
  between operations  1.07 us (1%)
    ppermute x52, starting transfers between devices, swap(): return lax.ppermute(out, AXES, pairs)  55 us
    pallas_call x42, Pallas kernels, call(): pl.pallas_call(body, out_shape=shapes, in_specs=specs, out_specs=[pl.Bloc...  21 us
    ppermute x52, waiting for transfers between devices, swap(): return lax.ppermute(out, AXES, pairs)  11.7 us
    ppermute x7, starting transfers between devices, span_swap(): return lax.ppermute(value, AXES, pairs)  6.6 us
    ppermute x7, waiting for transfers between devices, span_swap(): return lax.ppermute(value, AXES, pairs)  2.02 us
  transfers between devices with their start and end apart: 59, of which 24 were waited for; matrix products, arithmetic and copies ran while one was open for 0% of the time, Pallas kernels for 16%

profile of v10, /device:TPU:0, one launch (start us, length us, event | category | flops | bytes accessed | tf_op | source)
XLA Modules:
  0.0 98.1 jit_solution(15833708931954807836)
XLA Ops:
  1.9 4.0 %collective-permute-start.2 = (f32[8,128]{1,0:T(8,128)S(1)}, f32[8,128]{1,0:T(8,128)S(1)}, u32[]{:S(2)}, u32[]{:S(2)}) collective-permute-start(f32[8,128]{1,0:T(8,128)S(1)} %get-tuple-element.59), channel_id=1, source_target_pairs={{0,24},{1,25},{2,26},{3,27},{4,28},{5,29},{6,30},{7,31},{8,16},{9,... | collective-permute-start | bytes 12296 | tf_op jit(solution)/shard_map/ppermute | solution.py:572
  6.4 1.5 %collective-permute-start = (f32[8,128]{1,0:T(8,128)S(1)}, f32[8,128]{1,0:T(8,128)S(1)}, u32[]{:S(2)}, u32[]{:S(2)}) collective-permute-start(f32[8,128]{1,0:T(8,128)S(1)} %get-tuple-element.59), channel_id=1, source_target_pairs={{0,8},{1,2},{2,1},{3,4},{4,3},{5,6},{6,5},{7,15},{8,0},{9,10},{10,... | collective-permute-start | bytes 12296 | tf_op jit(solution)/shard_map/ppermute | solution.py:572
  8.1 2.2 %collective-permute-start.12 = (f32[1,136,128]{2,1,0:T(8,128)S(1)}, f32[1,136,128]{2,1,0:T(8,128)S(1)}, u32[]{:S(2)}, u32[]{:S(2)}) collective-permute-start(f32[1,136,128]{2,1,0:T(8,128)S(1)} %get-tuple-element.77.refs_0_.refs_1_), channel_id=1, source_target_pairs={{0,5},{1,4},{2,7},{3,6},{4,1},{5,0},{6,3},{7,2},{8,13},{9,12},{10,... | collective-permute-start | bytes 208904 | tf_op jit(solution)/shard_map/ppermute | solution.py:612
  10.5 1.5 %shard_map.141 = (f32[4,16,128]{2,1,0:T(8,128)S(1)}, f32[8,4,4,16,128]{4,3,2,1,0:T(8,128)S(1)}) custom-call(f32[4,16,128]{2,1,0:T(8,128)S(1)} %get-tuple-element.60.x_ref.refs_7_.refs_8_, f32[4,16,128]{2,1,0:T(8,128)S(1)} %get-tuple-element.61.b_ref, f32[2048,128]{1,0:T(8,128)S(1)} %bitcast.54, s32[8,16,128]{2,1,0:T(8,128)S(1)} %get-tuple-element.62.c_ref.refs_5_), custom_call_target="tpu_custom_call" | custom-call | tf_op jit(solution)/shard_map/pallas_call | solution.py:534
  12.5 1.5 %collective-permute-start.6 = (f32[8,128]{1,0:T(8,128)S(1)}, f32[8,128]{1,0:T(8,128)S(1)}, u32[]{:S(2)}, u32[]{:S(2)}) collective-permute-start(f32[8,128]{1,0:T(8,128)S(1)} %get-tuple-element.67._), channel_id=1, source_target_pairs={{0,24},{1,25},{2,26},{3,27},{4,28},{5,29},{6,30},{7,31},{8,16},{9,... | collective-permute-start | bytes 12296 | tf_op jit(solution)/shard_map/ppermute | solution.py:572
  14.5 1.5 %collective-permute-start.4 = (f32[8,128]{1,0:T(8,128)S(1)}, f32[8,128]{1,0:T(8,128)S(1)}, u32[]{:S(2)}, u32[]{:S(2)}) collective-permute-start(f32[8,128]{1,0:T(8,128)S(1)} %get-tuple-element.67._), channel_id=1, source_target_pairs={{0,8},{1,2},{2,1},{3,4},{4,3},{5,6},{6,5},{7,15},{8,0},{9,10},{10,... | collective-permute-start | bytes 12296 | tf_op jit(solution)/shard_map/ppermute | solution.py:572
  16.0 1.5 %shard_map.144.refs_3_ = f32[4,16,128]{2,1,0:T(8,128)S(1)} custom-call(f32[4,16,128]{2,1,0:T(8,128)S(1)} %get-tuple-element.68.x_ref.refs_7_, f32[4,16,128]{2,1,0:T(8,128)S(1)} %get-tuple-element.61.b_ref, f32[8,4,4,16,128]{4,3,2,1,0:T(8,128)S(1)} %get-tuple-element.64.refs_4_.v_ref, s32[8,16,128]{2,1,0:T(8,128)S(1)} %get-tuple-element.62.c_ref.refs_5_), custom_call_target="tpu_custom_call" | custom-call | tf_op jit(solution)/shard_map/pallas_call | solution.py:534
  18.4 2.5 %collective-permute-start.10 = (f32[8,128]{1,0:T(8,128)S(1)}, f32[8,128]{1,0:T(8,128)S(1)}, u32[]{:S(2)}, u32[]{:S(2)}) collective-permute-start(f32[8,128]{1,0:T(8,128)S(1)} %get-tuple-element.71), channel_id=1, source_target_pairs={{0,24},{1,25},{2,26},{3,27},{4,28},{5,29},{6,30},{7,31},{8,16},{9,... | collective-permute-start | bytes 12296 | tf_op jit(solution)/shard_map/ppermute | solution.py:572
  21.5 1.5 %collective-permute-start.8 = (f32[8,128]{1,0:T(8,128)S(1)}, f32[8,128]{1,0:T(8,128)S(1)}, u32[]{:S(2)}, u32[]{:S(2)}) collective-permute-start(f32[8,128]{1,0:T(8,128)S(1)} %get-tuple-element.71), channel_id=1, source_target_pairs={{0,8},{1,2},{2,1},{3,4},{4,3},{5,6},{6,5},{7,15},{8,0},{9,10},{10,... | collective-permute-start | bytes 12296 | tf_op jit(solution)/shard_map/ppermute | solution.py:572
  23.0 1.5 %shard_map.148.refs_3_ = f32[4,16,128]{2,1,0:T(8,128)S(1)} custom-call(f32[4,16,128]{2,1,0:T(8,128)S(1)} %get-tuple-element.72.x_ref.refs_12_, f32[4,16,128]{2,1,0:T(8,128)S(1)} %get-tuple-element.61.b_ref, f32[8,4,4,16,128]{4,3,2,1,0:T(8,128)S(1)} %get-tuple-element.64.refs_4_.v_ref, s32[8,16,128]{2,1,0:T(8,128)S(1)} %get-tuple-element.62.c_ref.refs_5_), custom_call_target="tpu_custom_call" | custom-call | tf_op jit(solution)/shard_map/pallas_call | solution.py:534
  25.6 1.5 %collective-permute-start.13 = (f32[8,128]{1,0:T(8,128)S(1)}, f32[8,128]{1,0:T(8,128)S(1)}, u32[]{:S(2)}, u32[]{:S(2)}) collective-permute-start(f32[8,128]{1,0:T(8,128)S(1)} %get-tuple-element.78._), channel_id=1, source_target_pairs={{0,24},{1,25},{2,26},{3,27},{4,28},{5,29},{6,30},{7,31},{8,16},{9,... | collective-permute-start | bytes 12296 | tf_op jit(solution)/shard_map/ppermute | solution.py:572
  27.7 1.5 %collective-permute-start.15 = (f32[8,128]{1,0:T(8,128)S(1)}, f32[8,128]{1,0:T(8,128)S(1)}, u32[]{:S(2)}, u32[]{:S(2)}) collective-permute-start(f32[8,128]{1,0:T(8,128)S(1)} %get-tuple-element.78._), channel_id=1, source_target_pairs={{0,8},{1,2},{2,1},{3,4},{4,3},{5,6},{6,5},{7,15},{8,0},{9,10},{10,... | collective-permute-start | bytes 12296 | tf_op jit(solution)/shard_map/ppermute | solution.py:572
  31.5 2.5 %collective-permute-start.17 = (f32[8,128]{1,0:T(8,128)S(1)}, f32[8,128]{1,0:T(8,128)S(1)}, u32[]{:S(2)}, u32[]{:S(2)}) collective-permute-start(f32[8,128]{1,0:T(8,128)S(1)} %get-tuple-element.83._), channel_id=1, source_target_pairs={{0,24},{1,25},{2,26},{3,27},{4,28},{5,29},{6,30},{7,31},{8,16},{9,... | collective-permute-start | bytes 12296 | tf_op jit(solution)/shard_map/ppermute | solution.py:572
  34.5 1.5 %collective-permute-start.19 = (f32[8,128]{1,0:T(8,128)S(1)}, f32[8,128]{1,0:T(8,128)S(1)}, u32[]{:S(2)}, u32[]{:S(2)}) collective-permute-start(f32[8,128]{1,0:T(8,128)S(1)} %get-tuple-element.83._), channel_id=1, source_target_pairs={{0,8},{1,2},{2,1},{3,4},{4,3},{5,6},{6,5},{7,15},{8,0},{9,10},{10,... | collective-permute-start | bytes 12296 | tf_op jit(solution)/shard_map/ppermute | solution.py:572
  45.5 3.0 %collective-permute-start.28 = (f32[8,128]{1,0:T(8,128)S(1)}, f32[8,128]{1,0:T(8,128)S(1)}, u32[]{:S(2)}, u32[]{:S(2)}) collective-permute-start(f32[8,128]{1,0:T(8,128)S(1)} %shard_map.161.refs_5_), channel_id=1, source_target_pairs={{0,3},{1,2},{2,1},{3,0},{4,7},{5,6},{6,5},{7,4},{8,11},{9,10},{10,... | collective-permute-start | bytes 12296 | tf_op jit(solution)/shard_map/ppermute | solution.py:612
  52.3 2.5 %collective-permute-start.31 = (f32[8,128]{1,0:T(8,128)S(1)}, f32[8,128]{1,0:T(8,128)S(1)}, u32[]{:S(2)}, u32[]{:S(2)}) collective-permute-start(f32[8,128]{1,0:T(8,128)S(1)} %get-tuple-element.96), channel_id=1, source_target_pairs={{0,24},{1,25},{2,26},{3,27},{4,28},{5,29},{6,30},{7,31},{8,16},{9,... | collective-permute-start | bytes 12296 | tf_op jit(solution)/shard_map/ppermute | solution.py:572
  64.9 2.5 %collective-permute-start.39 = (f32[8,128]{1,0:T(8,128)S(1)}, f32[8,128]{1,0:T(8,128)S(1)}, u32[]{:S(2)}, u32[]{:S(2)}) collective-permute-start(f32[8,128]{1,0:T(8,128)S(1)} %get-tuple-element.101), channel_id=1, source_target_pairs={{0,24},{1,25},{2,26},{3,27},{4,28},{5,29},{6,30},{7,31},{8,16},{9,... | collective-permute-start | bytes 12296 | tf_op jit(solution)/shard_map/ppermute | solution.py:572
  75.4 1.5 %shard_map.170.refs_3_ = f32[4,16,128]{2,1,0:T(8,128)S(1)} custom-call(f32[4,16,128]{2,1,0:T(8,128)S(1)} %get-tuple-element.105.x_ref.refs_7_.refs_8_, f32[4,16,128]{2,1,0:T(8,128)S(1)} %get-tuple-element.61.b_ref, f32[8,4,4,16,128]{4,3,2,1,0:T(8,128)S(1)} %get-tuple-element.64.refs_4_.v_ref, s32[8,16,128]{2,1,0:T(8,128)S(1)} %get-tuple-element.62.c_ref.refs_5_), custom_call_target="tpu_custom_call" | custom-call | tf_op jit(solution)/shard_map/pallas_call | solution.py:534
  77.8 2.5 %collective-permute-start.49 = (f32[8,128]{1,0:T(8,128)S(1)}, f32[8,128]{1,0:T(8,128)S(1)}, u32[]{:S(2)}, u32[]{:S(2)}) collective-permute-start(f32[8,128]{1,0:T(8,128)S(1)} %get-tuple-element.106), channel_id=1, source_target_pairs={{0,24},{1,25},{2,26},{3,27},{4,28},{5,29},{6,30},{7,31},{8,16},{9,... | collective-permute-start | bytes 12296 | tf_op jit(solution)/shard_map/ppermute | solution.py:572
  82.3 1.5 %shard_map.173.refs_3_ = f32[4,16,128]{2,1,0:T(8,128)S(1)} custom-call(f32[4,16,128]{2,1,0:T(8,128)S(1)} %get-tuple-element.107.x_ref.refs_7_, f32[4,16,128]{2,1,0:T(8,128)S(1)} %get-tuple-element.61.b_ref, f32[8,4,4,16,128]{4,3,2,1,0:T(8,128)S(1)} %get-tuple-element.64.refs_4_.v_ref, s32[8,16,128]{2,1,0:T(8,128)S(1)} %get-tuple-element.62.c_ref.refs_5_), custom_call_target="tpu_custom_call" | custom-call | tf_op jit(solution)/shard_map/pallas_call | solution.py:534
  84.7 1.5 %collective-permute-start.53 = (f32[8,128]{1,0:T(8,128)S(1)}, f32[8,128]{1,0:T(8,128)S(1)}, u32[]{:S(2)}, u32[]{:S(2)}) collective-permute-start(f32[8,128]{1,0:T(8,128)S(1)} %get-tuple-element.109), channel_id=1, source_target_pairs={{0,24},{1,25},{2,26},{3,27},{4,28},{5,29},{6,30},{7,31},{8,16},{9,... | collective-permute-start | bytes 12296 | tf_op jit(solution)/shard_map/ppermute | solution.py:572
  88.3 1.5 %shard_map.176.refs_3_ = f32[4,16,128]{2,1,0:T(8,128)S(1)} custom-call(f32[4,16,128]{2,1,0:T(8,128)S(1)} %get-tuple-element.110.x_ref.refs_7_, f32[4,16,128]{2,1,0:T(8,128)S(1)} %get-tuple-element.61.b_ref, f32[8,4,4,16,128]{4,3,2,1,0:T(8,128)S(1)} %get-tuple-element.64.refs_4_.v_ref, s32[8,16,128]{2,1,0:T(8,128)S(1)} %get-tuple-element.62.c_ref.refs_5_), custom_call_target="tpu_custom_call" | custom-call | tf_op jit(solution)/shard_map/pallas_call | solution.py:534
  90.7 2.5 %collective-permute-start.57 = (f32[8,128]{1,0:T(8,128)S(1)}, f32[8,128]{1,0:T(8,128)S(1)}, u32[]{:S(2)}, u32[]{:S(2)}) collective-permute-start(f32[8,128]{1,0:T(8,128)S(1)} %get-tuple-element.112), channel_id=1, source_target_pairs={{0,24},{1,25},{2,26},{3,27},{4,28},{5,29},{6,30},{7,31},{8,16},{9,... | collective-permute-start | bytes 12296 | tf_op jit(solution)/shard_map/ppermute | solution.py:572
  95.2 1.5 %shard_map.179.refs_3_ = f32[4,16,128]{2,1,0:T(8,128)S(1)} custom-call(f32[4,16,128]{2,1,0:T(8,128)S(1)} %get-tuple-element.113.x_ref.refs_6_, f32[4,16,128]{2,1,0:T(8,128)S(1)} %get-tuple-element.61.b_ref, f32[8,4,4,16,128]{4,3,2,1,0:T(8,128)S(1)} %get-tuple-element.64.refs_4_.v_ref, s32[8,16,128]{2,1,0:T(8,128)S(1)} %get-tuple-element.62.c_ref.refs_5_), custom_call_target="tpu_custom_call" | custom-call | tf_op jit(solution)/shard_map/pallas_call | solution.py:534
  (156 shorter events, 50.5 us)
Async XLA Ops:
  1.9 10.0 %collective-permute-start.2 = (f32[8,128]{1,0:T(8,128)S(1)}, f32[8,128]{1,0:T(8,128)S(1)}, u32[]{:S(2)}, u32[]{:S(2)}) collective-permute-start(f32[8,128]{1,0:T(8,128)S(1)} %get-tuple-element.59), channel_id=1, source_target_pairs={{0,24},{1,25},{2,26},{3,27},{4,28},{5,29},{6,30},{7,31},{8,16},{9,... | collective-permute-start | bytes 12296 | tf_op jit(solution)/shard_map/ppermute | solution.py:572
  5.9 6.1 %collective-permute-start.3 = (f32[8,128]{1,0:T(8,128)S(1)}, f32[8,128]{1,0:T(8,128)S(1)}, u32[]{:S(2)}, u32[]{:S(2)}) collective-permute-start(f32[8,128]{1,0:T(8,128)S(1)} %get-tuple-element.59), channel_id=1, source_target_pairs={{0,8},{1,9},{2,10},{3,11},{4,12},{5,13},{6,14},{7,15},{8,0},{9,1},... | collective-permute-start | bytes 12296 | tf_op jit(solution)/shard_map/ppermute | solution.py:572
  6.4 5.7 %collective-permute-start = (f32[8,128]{1,0:T(8,128)S(1)}, f32[8,128]{1,0:T(8,128)S(1)}, u32[]{:S(2)}, u32[]{:S(2)}) collective-permute-start(f32[8,128]{1,0:T(8,128)S(1)} %get-tuple-element.59), channel_id=1, source_target_pairs={{0,8},{1,2},{2,1},{3,4},{4,3},{5,6},{6,5},{7,15},{8,0},{9,10},{10,... | collective-permute-start | bytes 12296 | tf_op jit(solution)/shard_map/ppermute | solution.py:572
  7.9 4.3 %collective-permute-start.1 = (f32[8,128]{1,0:T(8,128)S(1)}, f32[8,128]{1,0:T(8,128)S(1)}, u32[]{:S(2)}, u32[]{:S(2)}) collective-permute-start(f32[8,128]{1,0:T(8,128)S(1)} %get-tuple-element.59), channel_id=1, source_target_pairs={{0,1},{1,0},{2,3},{3,2},{4,5},{5,4},{6,7},{7,6},{8,9},{9,8},{10,11... | collective-permute-start | bytes 12296 | tf_op jit(solution)/shard_map/ppermute | solution.py:572
  8.1 16.6 %collective-permute-start.12 = (f32[1,136,128]{2,1,0:T(8,128)S(1)}, f32[1,136,128]{2,1,0:T(8,128)S(1)}, u32[]{:S(2)}, u32[]{:S(2)}) collective-permute-start(f32[1,136,128]{2,1,0:T(8,128)S(1)} %get-tuple-element.77.refs_0_.refs_1_), channel_id=1, source_target_pairs={{0,5},{1,4},{2,7},{3,6},{4,1},{5,0},{6,3},{7,2},{8,13},{9,12},{10,... | collective-permute-start | bytes 208904 | tf_op jit(solution)/shard_map/ppermute | solution.py:612
  12.5 5.2 %collective-permute-start.6 = (f32[8,128]{1,0:T(8,128)S(1)}, f32[8,128]{1,0:T(8,128)S(1)}, u32[]{:S(2)}, u32[]{:S(2)}) collective-permute-start(f32[8,128]{1,0:T(8,128)S(1)} %get-tuple-element.67._), channel_id=1, source_target_pairs={{0,24},{1,25},{2,26},{3,27},{4,28},{5,29},{6,30},{7,31},{8,16},{9,... | collective-permute-start | bytes 12296 | tf_op jit(solution)/shard_map/ppermute | solution.py:572
  14.0 3.7 %collective-permute-start.7 = (f32[8,128]{1,0:T(8,128)S(1)}, f32[8,128]{1,0:T(8,128)S(1)}, u32[]{:S(2)}, u32[]{:S(2)}) collective-permute-start(f32[8,128]{1,0:T(8,128)S(1)} %get-tuple-element.67._), channel_id=1, source_target_pairs={{0,8},{1,9},{2,10},{3,11},{4,12},{5,13},{6,14},{7,15},{8,0},{9,1},... | collective-permute-start | bytes 12296 | tf_op jit(solution)/shard_map/ppermute | solution.py:572
  14.5 3.6 %collective-permute-start.4 = (f32[8,128]{1,0:T(8,128)S(1)}, f32[8,128]{1,0:T(8,128)S(1)}, u32[]{:S(2)}, u32[]{:S(2)}) collective-permute-start(f32[8,128]{1,0:T(8,128)S(1)} %get-tuple-element.67._), channel_id=1, source_target_pairs={{0,8},{1,2},{2,1},{3,4},{4,3},{5,6},{6,5},{7,15},{8,0},{9,10},{10,... | collective-permute-start | bytes 12296 | tf_op jit(solution)/shard_map/ppermute | solution.py:572
  18.4 6.1 %collective-permute-start.10 = (f32[8,128]{1,0:T(8,128)S(1)}, f32[8,128]{1,0:T(8,128)S(1)}, u32[]{:S(2)}, u32[]{:S(2)}) collective-permute-start(f32[8,128]{1,0:T(8,128)S(1)} %get-tuple-element.71), channel_id=1, source_target_pairs={{0,24},{1,25},{2,26},{3,27},{4,28},{5,29},{6,30},{7,31},{8,16},{9,... | collective-permute-start | bytes 12296 | tf_op jit(solution)/shard_map/ppermute | solution.py:572
  25.6 16.7 %collective-permute-start.25 = (f32[2,136,128]{2,1,0:T(8,128)S(1)}, f32[2,136,128]{2,1,0:T(8,128)S(1)}, u32[]{:S(2)}, u32[]{:S(2)}) collective-permute-start(f32[2,136,128]{2,1,0:T(8,128)S(1)} %shard_map.150.refs_10_), channel_id=1, source_target_pairs={{0,3},{1,2},{2,1},{3,0},{4,7},{5,6},{6,5},{7,4},{8,11},{9,10},{10,... | collective-permute-start | bytes 417800 | tf_op jit(solution)/shard_map/ppermute | solution.py:612
  25.6 4.6 %collective-permute-start.13 = (f32[8,128]{1,0:T(8,128)S(1)}, f32[8,128]{1,0:T(8,128)S(1)}, u32[]{:S(2)}, u32[]{:S(2)}) collective-permute-start(f32[8,128]{1,0:T(8,128)S(1)} %get-tuple-element.78._), channel_id=1, source_target_pairs={{0,24},{1,25},{2,26},{3,27},{4,28},{5,29},{6,30},{7,31},{8,16},{9,... | collective-permute-start | bytes 12296 | tf_op jit(solution)/shard_map/ppermute | solution.py:572
  31.5 5.5 %collective-permute-start.17 = (f32[8,128]{1,0:T(8,128)S(1)}, f32[8,128]{1,0:T(8,128)S(1)}, u32[]{:S(2)}, u32[]{:S(2)}) collective-permute-start(f32[8,128]{1,0:T(8,128)S(1)} %get-tuple-element.83._), channel_id=1, source_target_pairs={{0,24},{1,25},{2,26},{3,27},{4,28},{5,29},{6,30},{7,31},{8,16},{9,... | collective-permute-start | bytes 12296 | tf_op jit(solution)/shard_map/ppermute | solution.py:572
  38.4 4.5 %collective-permute-start.21 = (f32[8,128]{1,0:T(8,128)S(1)}, f32[8,128]{1,0:T(8,128)S(1)}, u32[]{:S(2)}, u32[]{:S(2)}) collective-permute-start(f32[8,128]{1,0:T(8,128)S(1)} %get-tuple-element.87._), channel_id=1, source_target_pairs={{0,24},{1,25},{2,26},{3,27},{4,28},{5,29},{6,30},{7,31},{8,16},{9,... | collective-permute-start | bytes 12296 | tf_op jit(solution)/shard_map/ppermute | solution.py:572
  44.2 5.7 %collective-permute-start.30 = (f32[4,136,128]{2,1,0:T(8,128)S(1)}, f32[4,136,128]{2,1,0:T(8,128)S(1)}, u32[]{:S(2)}, u32[]{:S(2)}) collective-permute-start(f32[4,136,128]{2,1,0:T(8,128)S(1)} %shard_map.160.refs_12_), channel_id=1, source_target_pairs={{0,1},{1,0},{2,3},{3,2},{4,5},{5,4},{6,7},{7,6},{8,9},{9,8},{10,11... | collective-permute-start | bytes 835592 | tf_op jit(solution)/shard_map/ppermute | solution.py:612
  44.3 4.9 %collective-permute-start.26 = (f32[8,128]{1,0:T(8,128)S(1)}, f32[8,128]{1,0:T(8,128)S(1)}, u32[]{:S(2)}, u32[]{:S(2)}) collective-permute-start(f32[8,128]{1,0:T(8,128)S(1)} %shard_map.161.refs_5_), channel_id=1, source_target_pairs={{0,7},{1,6},{2,5},{3,4},{4,3},{5,2},{6,1},{7,0},{8,15},{9,14},{10,... | collective-permute-start | bytes 12296 | tf_op jit(solution)/shard_map/ppermute | solution.py:612
  44.4 4.8 %collective-permute-start.27 = (f32[8,128]{1,0:T(8,128)S(1)}, f32[8,128]{1,0:T(8,128)S(1)}, u32[]{:S(2)}, u32[]{:S(2)}) collective-permute-start(f32[8,128]{1,0:T(8,128)S(1)} %shard_map.161.refs_5_), channel_id=1, source_target_pairs={{0,5},{1,4},{2,7},{3,6},{4,1},{5,0},{6,3},{7,2},{8,13},{9,12},{10,... | collective-permute-start | bytes 12296 | tf_op jit(solution)/shard_map/ppermute | solution.py:612
  45.5 4.3 %collective-permute-start.28 = (f32[8,128]{1,0:T(8,128)S(1)}, f32[8,128]{1,0:T(8,128)S(1)}, u32[]{:S(2)}, u32[]{:S(2)}) collective-permute-start(f32[8,128]{1,0:T(8,128)S(1)} %shard_map.161.refs_5_), channel_id=1, source_target_pairs={{0,3},{1,2},{2,1},{3,0},{4,7},{5,6},{6,5},{7,4},{8,11},{9,10},{10,... | collective-permute-start | bytes 12296 | tf_op jit(solution)/shard_map/ppermute | solution.py:612
  52.3 5.1 %collective-permute-start.31 = (f32[8,128]{1,0:T(8,128)S(1)}, f32[8,128]{1,0:T(8,128)S(1)}, u32[]{:S(2)}, u32[]{:S(2)}) collective-permute-start(f32[8,128]{1,0:T(8,128)S(1)} %get-tuple-element.96), channel_id=1, source_target_pairs={{0,24},{1,25},{2,26},{3,27},{4,28},{5,29},{6,30},{7,31},{8,16},{9,... | collective-permute-start | bytes 12296 | tf_op jit(solution)/shard_map/ppermute | solution.py:572
  59.1 4.5 %collective-permute-start.35 = (f32[8,128]{1,0:T(8,128)S(1)}, f32[8,128]{1,0:T(8,128)S(1)}, u32[]{:S(2)}, u32[]{:S(2)}) collective-permute-start(f32[8,128]{1,0:T(8,128)S(1)} %get-tuple-element.98), channel_id=1, source_target_pairs={{0,24},{1,25},{2,26},{3,27},{4,28},{5,29},{6,30},{7,31},{8,16},{9,... | collective-permute-start | bytes 12296 | tf_op jit(solution)/shard_map/ppermute | solution.py:572
  64.9 4.7 %collective-permute-start.39 = (f32[8,128]{1,0:T(8,128)S(1)}, f32[8,128]{1,0:T(8,128)S(1)}, u32[]{:S(2)}, u32[]{:S(2)}) collective-permute-start(f32[8,128]{1,0:T(8,128)S(1)} %get-tuple-element.101), channel_id=1, source_target_pairs={{0,24},{1,25},{2,26},{3,27},{4,28},{5,29},{6,30},{7,31},{8,16},{9,... | collective-permute-start | bytes 12296 | tf_op jit(solution)/shard_map/ppermute | solution.py:572
  71.9 5.0 %collective-permute-start.45 = (f32[8,128]{1,0:T(8,128)S(1)}, f32[8,128]{1,0:T(8,128)S(1)}, u32[]{:S(2)}, u32[]{:S(2)}) collective-permute-start(f32[8,128]{1,0:T(8,128)S(1)} %get-tuple-element.104), channel_id=1, source_target_pairs={{0,24},{1,25},{2,26},{3,27},{4,28},{5,29},{6,30},{7,31},{8,16},{9,... | collective-permute-start | bytes 12296 | tf_op jit(solution)/shard_map/ppermute | solution.py:572
  77.8 6.1 %collective-permute-start.49 = (f32[8,128]{1,0:T(8,128)S(1)}, f32[8,128]{1,0:T(8,128)S(1)}, u32[]{:S(2)}, u32[]{:S(2)}) collective-permute-start(f32[8,128]{1,0:T(8,128)S(1)} %get-tuple-element.106), channel_id=1, source_target_pairs={{0,24},{1,25},{2,26},{3,27},{4,28},{5,29},{6,30},{7,31},{8,16},{9,... | collective-permute-start | bytes 12296 | tf_op jit(solution)/shard_map/ppermute | solution.py:572
  84.7 5.1 %collective-permute-start.53 = (f32[8,128]{1,0:T(8,128)S(1)}, f32[8,128]{1,0:T(8,128)S(1)}, u32[]{:S(2)}, u32[]{:S(2)}) collective-permute-start(f32[8,128]{1,0:T(8,128)S(1)} %get-tuple-element.109), channel_id=1, source_target_pairs={{0,24},{1,25},{2,26},{3,27},{4,28},{5,29},{6,30},{7,31},{8,16},{9,... | collective-permute-start | bytes 12296 | tf_op jit(solution)/shard_map/ppermute | solution.py:572
  90.7 6.1 %collective-permute-start.57 = (f32[8,128]{1,0:T(8,128)S(1)}, f32[8,128]{1,0:T(8,128)S(1)}, u32[]{:S(2)}, u32[]{:S(2)}) collective-permute-start(f32[8,128]{1,0:T(8,128)S(1)} %get-tuple-element.112), channel_id=1, source_target_pairs={{0,24},{1,25},{2,26},{3,27},{4,28},{5,29},{6,30},{7,31},{8,16},{9,... | collective-permute-start | bytes 12296 | tf_op jit(solution)/shard_map/ppermute | solution.py:572
  (42 other events, 126.4 us)

commit v11 on v10

--- a/solution.py
+++ b/solution.py
@@ -694,7 +694,10 @@
         return call(fine_local, vec1, [x, b1, v1, c1], [vmem(4, lines, SUBS, LANES)])
 
     def fine_half(arrived, resid):
-        return call(fine_stream, vec1, arrived[:2] + arrived[4:] + [resid, v1, c1], [edge])
+        args = [arrived[0], arrived[3], arrived[1], arrived[4], resid, v1, c1]
+        return call(
+            lambda *refs: fine_stream(*(refs[:1] + refs[2:])), vec1, args, [edge], free=(1,)
+        )
 
     def fine_next(which, arrived, resid, x, d, after=()):
         args = arrived[2:] + [fine_half(arrived, resid), v1, c1, m1, x, d, send1]

time: 98.3 us -> 98.8 us (level)
  transfers between devices with their start and end apart: 59 -> 59, of which waited for: 24 -> 24; matrix products, arithmetic and copies ran while one was open for 0% -> 0% of each run, Pallas kernels for 16% -> 15%
where the time goes in v11:
time: 98.8 us; the launch traced here: 98.6 us
  starting transfers between devices  62 us (63%)
  Pallas kernels  21 us (21%)
  waiting for transfers between devices  13.7 us (14%)
  between operations  1.14 us (1%)
    ppermute x52, starting transfers between devices, swap(): return lax.ppermute(out, AXES, pairs)  55.2 us
    pallas_call x42, Pallas kernels, call(): pl.pallas_call(body, out_shape=shapes, in_specs=specs, out_specs=[pl.Bloc...  21 us
    ppermute x52, waiting for transfers between devices, swap(): return lax.ppermute(out, AXES, pairs)  11.7 us
    ppermute x7, starting transfers between devices, span_swap(): return lax.ppermute(value, AXES, pairs)  6.8 us
    ppermute x7, waiting for transfers between devices, span_swap(): return lax.ppermute(value, AXES, pairs)  2.02 us
  transfers between devices with their start and end apart: 59, of which 24 were waited for; matrix products, arithmetic and copies ran while one was open for 0% of the time, Pallas kernels for 15%

profile of v11, /device:TPU:0, one launch (start us, length us, event | category | flops | bytes accessed | tf_op | source)
XLA Modules:
  0.0 98.6 jit_solution(15928834549413224488)
XLA Ops:
  2.5 3.5 %collective-permute-start.2 = (f32[8,128]{1,0:T(8,128)S(1)}, f32[8,128]{1,0:T(8,128)S(1)}, u32[]{:S(2)}, u32[]{:S(2)}) collective-permute-start(f32[8,128]{1,0:T(8,128)S(1)} %get-tuple-element.59), channel_id=1, source_target_pairs={{0,24},{1,25},{2,26},{3,27},{4,28},{5,29},{6,30},{7,31},{8,16},{9,... | collective-permute-start | bytes 12296 | tf_op jit(solution)/shard_map/ppermute | solution.py:572
  6.5 1.5 %collective-permute-start = (f32[8,128]{1,0:T(8,128)S(1)}, f32[8,128]{1,0:T(8,128)S(1)}, u32[]{:S(2)}, u32[]{:S(2)}) collective-permute-start(f32[8,128]{1,0:T(8,128)S(1)} %get-tuple-element.59), channel_id=1, source_target_pairs={{0,8},{1,2},{2,1},{3,4},{4,3},{5,6},{6,5},{7,15},{8,0},{9,10},{10,... | collective-permute-start | bytes 12296 | tf_op jit(solution)/shard_map/ppermute | solution.py:572
  8.0 2.4 %collective-permute-start.12 = (f32[1,136,128]{2,1,0:T(8,128)S(1)}, f32[1,136,128]{2,1,0:T(8,128)S(1)}, u32[]{:S(2)}, u32[]{:S(2)}) collective-permute-start(f32[1,136,128]{2,1,0:T(8,128)S(1)} %get-tuple-element.77.refs_0_.refs_1_), channel_id=1, source_target_pairs={{0,5},{1,4},{2,7},{3,6},{4,1},{5,0},{6,3},{7,2},{8,13},{9,12},{10,... | collective-permute-start | bytes 208904 | tf_op jit(solution)/shard_map/ppermute | solution.py:612
  10.5 1.5 %shard_map.141 = (f32[4,16,128]{2,1,0:T(8,128)S(1)}, f32[8,4,4,16,128]{4,3,2,1,0:T(8,128)S(1)}) custom-call(f32[4,16,128]{2,1,0:T(8,128)S(1)} %get-tuple-element.60.x_ref.refs_7_.refs_8_, f32[4,16,128]{2,1,0:T(8,128)S(1)} %get-tuple-element.61.b_ref, f32[2048,128]{1,0:T(8,128)S(1)} %bitcast.54, s32[8,16,128]{2,1,0:T(8,128)S(1)} %get-tuple-element.62.c_ref.refs_6_.refs_5_), custom_call_target="tpu_custom_call" | custom-call | tf_op jit(solution)/shard_map/pallas_call | solution.py:534
  12.7 1.5 %collective-permute-start.6 = (f32[8,128]{1,0:T(8,128)S(1)}, f32[8,128]{1,0:T(8,128)S(1)}, u32[]{:S(2)}, u32[]{:S(2)}) collective-permute-start(f32[8,128]{1,0:T(8,128)S(1)} %get-tuple-element.67._), channel_id=1, source_target_pairs={{0,24},{1,25},{2,26},{3,27},{4,28},{5,29},{6,30},{7,31},{8,16},{9,... | collective-permute-start | bytes 12296 | tf_op jit(solution)/shard_map/ppermute | solution.py:572
  14.7 1.5 %collective-permute-start.4 = (f32[8,128]{1,0:T(8,128)S(1)}, f32[8,128]{1,0:T(8,128)S(1)}, u32[]{:S(2)}, u32[]{:S(2)}) collective-permute-start(f32[8,128]{1,0:T(8,128)S(1)} %get-tuple-element.67._), channel_id=1, source_target_pairs={{0,8},{1,2},{2,1},{3,4},{4,3},{5,6},{6,5},{7,15},{8,0},{9,10},{10,... | collective-permute-start | bytes 12296 | tf_op jit(solution)/shard_map/ppermute | solution.py:572
  16.2 1.5 %shard_map.144.refs_4_ = f32[4,16,128]{2,1,0:T(8,128)S(1)} custom-call(f32[4,16,128]{2,1,0:T(8,128)S(1)} %get-tuple-element.68.x_ref.refs_7_, f32[4,16,128]{2,1,0:T(8,128)S(1)} %get-tuple-element.61.b_ref, f32[8,4,4,16,128]{4,3,2,1,0:T(8,128)S(1)} %get-tuple-element.64.refs_5_.refs_4_.v_ref, s32[8,16,128]{2,1,0:T(8,128)S(1)} %get-tuple-element.62.c_ref.refs_6_.refs_5_), custom_call_target="tpu_custom_call" | custom-call | tf_op jit(solution)/shard_map/pallas_call | solution.py:534
  18.6 2.5 %collective-permute-start.10 = (f32[8,128]{1,0:T(8,128)S(1)}, f32[8,128]{1,0:T(8,128)S(1)}, u32[]{:S(2)}, u32[]{:S(2)}) collective-permute-start(f32[8,128]{1,0:T(8,128)S(1)} %get-tuple-element.71), channel_id=1, source_target_pairs={{0,24},{1,25},{2,26},{3,27},{4,28},{5,29},{6,30},{7,31},{8,16},{9,... | collective-permute-start | bytes 12296 | tf_op jit(solution)/shard_map/ppermute | solution.py:572
  21.6 1.5 %collective-permute-start.8 = (f32[8,128]{1,0:T(8,128)S(1)}, f32[8,128]{1,0:T(8,128)S(1)}, u32[]{:S(2)}, u32[]{:S(2)}) collective-permute-start(f32[8,128]{1,0:T(8,128)S(1)} %get-tuple-element.71), channel_id=1, source_target_pairs={{0,8},{1,2},{2,1},{3,4},{4,3},{5,6},{6,5},{7,15},{8,0},{9,10},{10,... | collective-permute-start | bytes 12296 | tf_op jit(solution)/shard_map/ppermute | solution.py:572
  23.1 1.5 %shard_map.148.refs_4_ = f32[4,16,128]{2,1,0:T(8,128)S(1)} custom-call(f32[4,16,128]{2,1,0:T(8,128)S(1)} %get-tuple-element.72.x_ref.refs_12_, f32[4,16,128]{2,1,0:T(8,128)S(1)} %get-tuple-element.61.b_ref, f32[8,4,4,16,128]{4,3,2,1,0:T(8,128)S(1)} %get-tuple-element.64.refs_5_.refs_4_.v_ref, s32[8,16,128]{2,1,0:T(8,128)S(1)} %get-tuple-element.62.c_ref.refs_6_.refs_5_), custom_call_target="tpu_custom_call" | custom-call | tf_op jit(solution)/shard_map/pallas_call | solution.py:534
  25.8 1.5 %collective-permute-start.13 = (f32[8,128]{1,0:T(8,128)S(1)}, f32[8,128]{1,0:T(8,128)S(1)}, u32[]{:S(2)}, u32[]{:S(2)}) collective-permute-start(f32[8,128]{1,0:T(8,128)S(1)} %get-tuple-element.78._), channel_id=1, source_target_pairs={{0,24},{1,25},{2,26},{3,27},{4,28},{5,29},{6,30},{7,31},{8,16},{9,... | collective-permute-start | bytes 12296 | tf_op jit(solution)/shard_map/ppermute | solution.py:572
  27.8 1.5 %collective-permute-start.15 = (f32[8,128]{1,0:T(8,128)S(1)}, f32[8,128]{1,0:T(8,128)S(1)}, u32[]{:S(2)}, u32[]{:S(2)}) collective-permute-start(f32[8,128]{1,0:T(8,128)S(1)} %get-tuple-element.78._), channel_id=1, source_target_pairs={{0,8},{1,2},{2,1},{3,4},{4,3},{5,6},{6,5},{7,15},{8,0},{9,10},{10,... | collective-permute-start | bytes 12296 | tf_op jit(solution)/shard_map/ppermute | solution.py:572
  31.7 2.5 %collective-permute-start.17 = (f32[8,128]{1,0:T(8,128)S(1)}, f32[8,128]{1,0:T(8,128)S(1)}, u32[]{:S(2)}, u32[]{:S(2)}) collective-permute-start(f32[8,128]{1,0:T(8,128)S(1)} %get-tuple-element.83._), channel_id=1, source_target_pairs={{0,24},{1,25},{2,26},{3,27},{4,28},{5,29},{6,30},{7,31},{8,16},{9,... | collective-permute-start | bytes 12296 | tf_op jit(solution)/shard_map/ppermute | solution.py:572
  45.7 3.0 %collective-permute-start.28 = (f32[8,128]{1,0:T(8,128)S(1)}, f32[8,128]{1,0:T(8,128)S(1)}, u32[]{:S(2)}, u32[]{:S(2)}) collective-permute-start(f32[8,128]{1,0:T(8,128)S(1)} %shard_map.161.refs_5_), channel_id=1, source_target_pairs={{0,3},{1,2},{2,1},{3,0},{4,7},{5,6},{6,5},{7,4},{8,11},{9,10},{10,... | collective-permute-start | bytes 12296 | tf_op jit(solution)/shard_map/ppermute | solution.py:612
  52.4 2.5 %collective-permute-start.31 = (f32[8,128]{1,0:T(8,128)S(1)}, f32[8,128]{1,0:T(8,128)S(1)}, u32[]{:S(2)}, u32[]{:S(2)}) collective-permute-start(f32[8,128]{1,0:T(8,128)S(1)} %get-tuple-element.96), channel_id=1, source_target_pairs={{0,24},{1,25},{2,26},{3,27},{4,28},{5,29},{6,30},{7,31},{8,16},{9,... | collective-permute-start | bytes 12296 | tf_op jit(solution)/shard_map/ppermute | solution.py:572
  65.1 2.5 %collective-permute-start.39 = (f32[8,128]{1,0:T(8,128)S(1)}, f32[8,128]{1,0:T(8,128)S(1)}, u32[]{:S(2)}, u32[]{:S(2)}) collective-permute-start(f32[8,128]{1,0:T(8,128)S(1)} %get-tuple-element.101), channel_id=1, source_target_pairs={{0,24},{1,25},{2,26},{3,27},{4,28},{5,29},{6,30},{7,31},{8,16},{9,... | collective-permute-start | bytes 12296 | tf_op jit(solution)/shard_map/ppermute | solution.py:572
  72.1 1.5 %collective-permute-start.45 = (f32[8,128]{1,0:T(8,128)S(1)}, f32[8,128]{1,0:T(8,128)S(1)}, u32[]{:S(2)}, u32[]{:S(2)}) collective-permute-start(f32[8,128]{1,0:T(8,128)S(1)} %get-tuple-element.104), channel_id=1, source_target_pairs={{0,24},{1,25},{2,26},{3,27},{4,28},{5,29},{6,30},{7,31},{8,16},{9,... | collective-permute-start | bytes 12296 | tf_op jit(solution)/shard_map/ppermute | solution.py:572
  75.6 1.5 %shard_map.170.refs_4_ = f32[4,16,128]{2,1,0:T(8,128)S(1)} custom-call(f32[4,16,128]{2,1,0:T(8,128)S(1)} %get-tuple-element.105.x_ref.refs_7_.refs_8_, f32[4,16,128]{2,1,0:T(8,128)S(1)} %get-tuple-element.61.b_ref, f32[8,4,4,16,128]{4,3,2,1,0:T(8,128)S(1)} %get-tuple-element.64.refs_5_.refs_4_.v_ref, s32[8,16,128]{2,1,0:T(8,128)S(1)} %get-tuple-element.62.c_ref.refs_6_.refs_5_), custom_call_target="tpu_custom_call" | custom-call | tf_op jit(solution)/shard_map/pallas_call | solution.py:534
  78.1 2.5 %collective-permute-start.49 = (f32[8,128]{1,0:T(8,128)S(1)}, f32[8,128]{1,0:T(8,128)S(1)}, u32[]{:S(2)}, u32[]{:S(2)}) collective-permute-start(f32[8,128]{1,0:T(8,128)S(1)} %get-tuple-element.106), channel_id=1, source_target_pairs={{0,24},{1,25},{2,26},{3,27},{4,28},{5,29},{6,30},{7,31},{8,16},{9,... | collective-permute-start | bytes 12296 | tf_op jit(solution)/shard_map/ppermute | solution.py:572
  82.6 1.5 %shard_map.173.refs_4_ = f32[4,16,128]{2,1,0:T(8,128)S(1)} custom-call(f32[4,16,128]{2,1,0:T(8,128)S(1)} %get-tuple-element.107.x_ref.refs_7_, f32[4,16,128]{2,1,0:T(8,128)S(1)} %get-tuple-element.61.b_ref, f32[8,4,4,16,128]{4,3,2,1,0:T(8,128)S(1)} %get-tuple-element.64.refs_5_.refs_4_.v_ref, s32[8,16,128]{2,1,0:T(8,128)S(1)} %get-tuple-element.62.c_ref.refs_6_.refs_5_), custom_call_target="tpu_custom_call" | custom-call | tf_op jit(solution)/shard_map/pallas_call | solution.py:534
  85.1 1.5 %collective-permute-start.53 = (f32[8,128]{1,0:T(8,128)S(1)}, f32[8,128]{1,0:T(8,128)S(1)}, u32[]{:S(2)}, u32[]{:S(2)}) collective-permute-start(f32[8,128]{1,0:T(8,128)S(1)} %get-tuple-element.109), channel_id=1, source_target_pairs={{0,24},{1,25},{2,26},{3,27},{4,28},{5,29},{6,30},{7,31},{8,16},{9,... | collective-permute-start | bytes 12296 | tf_op jit(solution)/shard_map/ppermute | solution.py:572
  88.7 1.5 %shard_map.176.refs_4_ = f32[4,16,128]{2,1,0:T(8,128)S(1)} custom-call(f32[4,16,128]{2,1,0:T(8,128)S(1)} %get-tuple-element.110.x_ref.refs_7_, f32[4,16,128]{2,1,0:T(8,128)S(1)} %get-tuple-element.61.b_ref, f32[8,4,4,16,128]{4,3,2,1,0:T(8,128)S(1)} %get-tuple-element.64.refs_5_.refs_4_.v_ref, s32[8,16,128]{2,1,0:T(8,128)S(1)} %get-tuple-element.62.c_ref.refs_6_.refs_5_), custom_call_target="tpu_custom_call" | custom-call | tf_op jit(solution)/shard_map/pallas_call | solution.py:534
  91.1 2.5 %collective-permute-start.57 = (f32[8,128]{1,0:T(8,128)S(1)}, f32[8,128]{1,0:T(8,128)S(1)}, u32[]{:S(2)}, u32[]{:S(2)}) collective-permute-start(f32[8,128]{1,0:T(8,128)S(1)} %get-tuple-element.112), channel_id=1, source_target_pairs={{0,24},{1,25},{2,26},{3,27},{4,28},{5,29},{6,30},{7,31},{8,16},{9,... | collective-permute-start | bytes 12296 | tf_op jit(solution)/shard_map/ppermute | solution.py:572
  95.7 1.5 %shard_map.179.refs_4_ = f32[4,16,128]{2,1,0:T(8,128)S(1)} custom-call(f32[4,16,128]{2,1,0:T(8,128)S(1)} %get-tuple-element.113.x_ref.refs_6_, f32[4,16,128]{2,1,0:T(8,128)S(1)} %get-tuple-element.61.b_ref, f32[8,4,4,16,128]{4,3,2,1,0:T(8,128)S(1)} %get-tuple-element.64.refs_5_.refs_4_.v_ref, s32[8,16,128]{2,1,0:T(8,128)S(1)} %get-tuple-element.62.c_ref.refs_6_.refs_5_), custom_call_target="tpu_custom_call" | custom-call | tf_op jit(solution)/shard_map/pallas_call | solution.py:534
  (156 shorter events, 51.1 us)
Async XLA Ops:
  1.9 10.1 %collective-permute-start.1 = (f32[8,128]{1,0:T(8,128)S(1)}, f32[8,128]{1,0:T(8,128)S(1)}, u32[]{:S(2)}, u32[]{:S(2)}) collective-permute-start(f32[8,128]{1,0:T(8,128)S(1)} %get-tuple-element.59), channel_id=1, source_target_pairs={{0,1},{1,0},{2,3},{3,2},{4,5},{5,4},{6,7},{7,6},{8,9},{9,8},{10,11... | collective-permute-start | bytes 12296 | tf_op jit(solution)/shard_map/ppermute | solution.py:572
  2.5 9.6 %collective-permute-start.2 = (f32[8,128]{1,0:T(8,128)S(1)}, f32[8,128]{1,0:T(8,128)S(1)}, u32[]{:S(2)}, u32[]{:S(2)}) collective-permute-start(f32[8,128]{1,0:T(8,128)S(1)} %get-tuple-element.59), channel_id=1, source_target_pairs={{0,24},{1,25},{2,26},{3,27},{4,28},{5,29},{6,30},{7,31},{8,16},{9,... | collective-permute-start | bytes 12296 | tf_op jit(solution)/shard_map/ppermute | solution.py:572
  6.0 6.1 %collective-permute-start.3 = (f32[8,128]{1,0:T(8,128)S(1)}, f32[8,128]{1,0:T(8,128)S(1)}, u32[]{:S(2)}, u32[]{:S(2)}) collective-permute-start(f32[8,128]{1,0:T(8,128)S(1)} %get-tuple-element.59), channel_id=1, source_target_pairs={{0,8},{1,9},{2,10},{3,11},{4,12},{5,13},{6,14},{7,15},{8,0},{9,1},... | collective-permute-start | bytes 12296 | tf_op jit(solution)/shard_map/ppermute | solution.py:572
  6.5 5.8 %collective-permute-start = (f32[8,128]{1,0:T(8,128)S(1)}, f32[8,128]{1,0:T(8,128)S(1)}, u32[]{:S(2)}, u32[]{:S(2)}) collective-permute-start(f32[8,128]{1,0:T(8,128)S(1)} %get-tuple-element.59), channel_id=1, source_target_pairs={{0,8},{1,2},{2,1},{3,4},{4,3},{5,6},{6,5},{7,15},{8,0},{9,10},{10,... | collective-permute-start | bytes 12296 | tf_op jit(solution)/shard_map/ppermute | solution.py:572
  8.0 16.9 %collective-permute-start.12 = (f32[1,136,128]{2,1,0:T(8,128)S(1)}, f32[1,136,128]{2,1,0:T(8,128)S(1)}, u32[]{:S(2)}, u32[]{:S(2)}) collective-permute-start(f32[1,136,128]{2,1,0:T(8,128)S(1)} %get-tuple-element.77.refs_0_.refs_1_), channel_id=1, source_target_pairs={{0,5},{1,4},{2,7},{3,6},{4,1},{5,0},{6,3},{7,2},{8,13},{9,12},{10,... | collective-permute-start | bytes 208904 | tf_op jit(solution)/shard_map/ppermute | solution.py:612
  12.6 5.3 %collective-permute-start.5 = (f32[8,128]{1,0:T(8,128)S(1)}, f32[8,128]{1,0:T(8,128)S(1)}, u32[]{:S(2)}, u32[]{:S(2)}) collective-permute-start(f32[8,128]{1,0:T(8,128)S(1)} %get-tuple-element.67._), channel_id=1, source_target_pairs={{0,1},{1,0},{2,3},{3,2},{4,5},{5,4},{6,7},{7,6},{8,9},{9,8},{10,11... | collective-permute-start | bytes 12296 | tf_op jit(solution)/shard_map/ppermute | solution.py:572
  12.7 5.2 %collective-permute-start.6 = (f32[8,128]{1,0:T(8,128)S(1)}, f32[8,128]{1,0:T(8,128)S(1)}, u32[]{:S(2)}, u32[]{:S(2)}) collective-permute-start(f32[8,128]{1,0:T(8,128)S(1)} %get-tuple-element.67._), channel_id=1, source_target_pairs={{0,24},{1,25},{2,26},{3,27},{4,28},{5,29},{6,30},{7,31},{8,16},{9,... | collective-permute-start | bytes 12296 | tf_op jit(solution)/shard_map/ppermute | solution.py:572
  18.6 6.1 %collective-permute-start.10 = (f32[8,128]{1,0:T(8,128)S(1)}, f32[8,128]{1,0:T(8,128)S(1)}, u32[]{:S(2)}, u32[]{:S(2)}) collective-permute-start(f32[8,128]{1,0:T(8,128)S(1)} %get-tuple-element.71), channel_id=1, source_target_pairs={{0,24},{1,25},{2,26},{3,27},{4,28},{5,29},{6,30},{7,31},{8,16},{9,... | collective-permute-start | bytes 12296 | tf_op jit(solution)/shard_map/ppermute | solution.py:572
  25.8 16.7 %collective-permute-start.25 = (f32[2,136,128]{2,1,0:T(8,128)S(1)}, f32[2,136,128]{2,1,0:T(8,128)S(1)}, u32[]{:S(2)}, u32[]{:S(2)}) collective-permute-start(f32[2,136,128]{2,1,0:T(8,128)S(1)} %shard_map.150.refs_10_), channel_id=1, source_target_pairs={{0,3},{1,2},{2,1},{3,0},{4,7},{5,6},{6,5},{7,4},{8,11},{9,10},{10,... | collective-permute-start | bytes 417800 | tf_op jit(solution)/shard_map/ppermute | solution.py:612
  25.8 4.6 %collective-permute-start.13 = (f32[8,128]{1,0:T(8,128)S(1)}, f32[8,128]{1,0:T(8,128)S(1)}, u32[]{:S(2)}, u32[]{:S(2)}) collective-permute-start(f32[8,128]{1,0:T(8,128)S(1)} %get-tuple-element.78._), channel_id=1, source_target_pairs={{0,24},{1,25},{2,26},{3,27},{4,28},{5,29},{6,30},{7,31},{8,16},{9,... | collective-permute-start | bytes 12296 | tf_op jit(solution)/shard_map/ppermute | solution.py:572
  31.7 5.5 %collective-permute-start.17 = (f32[8,128]{1,0:T(8,128)S(1)}, f32[8,128]{1,0:T(8,128)S(1)}, u32[]{:S(2)}, u32[]{:S(2)}) collective-permute-start(f32[8,128]{1,0:T(8,128)S(1)} %get-tuple-element.83._), channel_id=1, source_target_pairs={{0,24},{1,25},{2,26},{3,27},{4,28},{5,29},{6,30},{7,31},{8,16},{9,... | collective-permute-start | bytes 12296 | tf_op jit(solution)/shard_map/ppermute | solution.py:572
  44.4 5.7 %collective-permute-start.30 = (f32[4,136,128]{2,1,0:T(8,128)S(1)}, f32[4,136,128]{2,1,0:T(8,128)S(1)}, u32[]{:S(2)}, u32[]{:S(2)}) collective-permute-start(f32[4,136,128]{2,1,0:T(8,128)S(1)} %shard_map.160.refs_12_), channel_id=1, source_target_pairs={{0,1},{1,0},{2,3},{3,2},{4,5},{5,4},{6,7},{7,6},{8,9},{9,8},{10,11... | collective-permute-start | bytes 835592 | tf_op jit(solution)/shard_map/ppermute | solution.py:612
  44.4 4.9 %collective-permute-start.26 = (f32[8,128]{1,0:T(8,128)S(1)}, f32[8,128]{1,0:T(8,128)S(1)}, u32[]{:S(2)}, u32[]{:S(2)}) collective-permute-start(f32[8,128]{1,0:T(8,128)S(1)} %shard_map.161.refs_5_), channel_id=1, source_target_pairs={{0,7},{1,6},{2,5},{3,4},{4,3},{5,2},{6,1},{7,0},{8,15},{9,14},{10,... | collective-permute-start | bytes 12296 | tf_op jit(solution)/shard_map/ppermute | solution.py:612
  44.5 4.8 %collective-permute-start.27 = (f32[8,128]{1,0:T(8,128)S(1)}, f32[8,128]{1,0:T(8,128)S(1)}, u32[]{:S(2)}, u32[]{:S(2)}) collective-permute-start(f32[8,128]{1,0:T(8,128)S(1)} %shard_map.161.refs_5_), channel_id=1, source_target_pairs={{0,5},{1,4},{2,7},{3,6},{4,1},{5,0},{6,3},{7,2},{8,13},{9,12},{10,... | collective-permute-start | bytes 12296 | tf_op jit(solution)/shard_map/ppermute | solution.py:612
  52.4 5.1 %collective-permute-start.31 = (f32[8,128]{1,0:T(8,128)S(1)}, f32[8,128]{1,0:T(8,128)S(1)}, u32[]{:S(2)}, u32[]{:S(2)}) collective-permute-start(f32[8,128]{1,0:T(8,128)S(1)} %get-tuple-element.96), channel_id=1, source_target_pairs={{0,24},{1,25},{2,26},{3,27},{4,28},{5,29},{6,30},{7,31},{8,16},{9,... | collective-permute-start | bytes 12296 | tf_op jit(solution)/shard_map/ppermute | solution.py:572
  65.1 4.7 %collective-permute-start.39 = (f32[8,128]{1,0:T(8,128)S(1)}, f32[8,128]{1,0:T(8,128)S(1)}, u32[]{:S(2)}, u32[]{:S(2)}) collective-permute-start(f32[8,128]{1,0:T(8,128)S(1)} %get-tuple-element.101), channel_id=1, source_target_pairs={{0,24},{1,25},{2,26},{3,27},{4,28},{5,29},{6,30},{7,31},{8,16},{9,... | collective-permute-start | bytes 12296 | tf_op jit(solution)/shard_map/ppermute | solution.py:572
  72.0 5.1 %collective-permute-start.44 = (f32[8,128]{1,0:T(8,128)S(1)}, f32[8,128]{1,0:T(8,128)S(1)}, u32[]{:S(2)}, u32[]{:S(2)}) collective-permute-start(f32[8,128]{1,0:T(8,128)S(1)} %get-tuple-element.104), channel_id=1, source_target_pairs={{0,1},{1,0},{2,3},{3,2},{4,5},{5,4},{6,7},{7,6},{8,9},{9,8},{10,11... | collective-permute-start | bytes 12296 | tf_op jit(solution)/shard_map/ppermute | solution.py:572
  72.1 5.1 %collective-permute-start.45 = (f32[8,128]{1,0:T(8,128)S(1)}, f32[8,128]{1,0:T(8,128)S(1)}, u32[]{:S(2)}, u32[]{:S(2)}) collective-permute-start(f32[8,128]{1,0:T(8,128)S(1)} %get-tuple-element.104), channel_id=1, source_target_pairs={{0,24},{1,25},{2,26},{3,27},{4,28},{5,29},{6,30},{7,31},{8,16},{9,... | collective-permute-start | bytes 12296 | tf_op jit(solution)/shard_map/ppermute | solution.py:572
  78.0 6.1 %collective-permute-start.48 = (f32[8,128]{1,0:T(8,128)S(1)}, f32[8,128]{1,0:T(8,128)S(1)}, u32[]{:S(2)}, u32[]{:S(2)}) collective-permute-start(f32[8,128]{1,0:T(8,128)S(1)} %get-tuple-element.106), channel_id=1, source_target_pairs={{0,1},{1,0},{2,3},{3,2},{4,5},{5,4},{6,7},{7,6},{8,9},{9,8},{10,11... | collective-permute-start | bytes 12296 | tf_op jit(solution)/shard_map/ppermute | solution.py:572
  78.1 6.1 %collective-permute-start.49 = (f32[8,128]{1,0:T(8,128)S(1)}, f32[8,128]{1,0:T(8,128)S(1)}, u32[]{:S(2)}, u32[]{:S(2)}) collective-permute-start(f32[8,128]{1,0:T(8,128)S(1)} %get-tuple-element.106), channel_id=1, source_target_pairs={{0,24},{1,25},{2,26},{3,27},{4,28},{5,29},{6,30},{7,31},{8,16},{9,... | collective-permute-start | bytes 12296 | tf_op jit(solution)/shard_map/ppermute | solution.py:572
  85.1 5.1 %collective-permute-start.52 = (f32[8,128]{1,0:T(8,128)S(1)}, f32[8,128]{1,0:T(8,128)S(1)}, u32[]{:S(2)}, u32[]{:S(2)}) collective-permute-start(f32[8,128]{1,0:T(8,128)S(1)} %get-tuple-element.109), channel_id=1, source_target_pairs={{0,1},{1,0},{2,3},{3,2},{4,5},{5,4},{6,7},{7,6},{8,9},{9,8},{10,11... | collective-permute-start | bytes 12296 | tf_op jit(solution)/shard_map/ppermute | solution.py:572
  85.1 5.1 %collective-permute-start.53 = (f32[8,128]{1,0:T(8,128)S(1)}, f32[8,128]{1,0:T(8,128)S(1)}, u32[]{:S(2)}, u32[]{:S(2)}) collective-permute-start(f32[8,128]{1,0:T(8,128)S(1)} %get-tuple-element.109), channel_id=1, source_target_pairs={{0,24},{1,25},{2,26},{3,27},{4,28},{5,29},{6,30},{7,31},{8,16},{9,... | collective-permute-start | bytes 12296 | tf_op jit(solution)/shard_map/ppermute | solution.py:572
  91.1 6.1 %collective-permute-start.56 = (f32[8,128]{1,0:T(8,128)S(1)}, f32[8,128]{1,0:T(8,128)S(1)}, u32[]{:S(2)}, u32[]{:S(2)}) collective-permute-start(f32[8,128]{1,0:T(8,128)S(1)} %get-tuple-element.112), channel_id=1, source_target_pairs={{0,1},{1,0},{2,3},{3,2},{4,5},{5,4},{6,7},{7,6},{8,9},{9,8},{10,11... | collective-permute-start | bytes 12296 | tf_op jit(solution)/shard_map/ppermute | solution.py:572
  91.1 6.1 %collective-permute-start.57 = (f32[8,128]{1,0:T(8,128)S(1)}, f32[8,128]{1,0:T(8,128)S(1)}, u32[]{:S(2)}, u32[]{:S(2)}) collective-permute-start(f32[8,128]{1,0:T(8,128)S(1)} %get-tuple-element.112), channel_id=1, source_target_pairs={{0,24},{1,25},{2,26},{3,27},{4,28},{5,29},{6,30},{7,31},{8,16},{9,... | collective-permute-start | bytes 12296 | tf_op jit(solution)/shard_map/ppermute | solution.py:572
  (42 other events, 137.3 us)
